TPU v7x, 32 devices: a whole 2x2x4 slice. The times are simulated.
32 devices in a mesh: rcv: 8 (over z, y), ref: 4 (over x, core).
Axes of the slice: x: 2, y: 2, z: 4, core: 2. Of those that a mesh axis runs over, the one named last changes fastest.
Arguments:
- receiver_spectra: bfloat16 [64, 8192], P('rcv', 'ref'), may hold values from -6 to 6
- reference_spectra: bfloat16 [8192, 1024], P('rcv', 'ref'), may hold values from -6 to 6
- receiver_counts: int32 [64], P('rcv'), may hold values from 1 to 16
- reference_counts: int32 [1024], P('ref'), may hold values from 1 to 16
- column_station: int32 [1024], P('ref'), may hold values from 0 to 1023, as said below
- lag_window: int32 [2, 64, 1024], P(None, 'rcv', 'ref'), may hold values from 0 to 256, as said below
- observed: bfloat16 [64, 1024, 512], P('rcv', 'ref'), may hold values from 0.19921875 to 2
Outputs:
- receiver_grad: float32 [64, 8192], P('rcv', 'ref')
- reference_grad: float32 [8192, 1024], P('rcv', 'ref')
Inputs may be any that keep to these rules, and one draw needn't show every extreme that they name: `receiver_counts`: number of valid leading segments of each station. `column_station`: A permutation of the 1024 reference stations that maps each block of 256 consecutive pair columns onto the same block of stations. lag_window[0] is a first lag below 256; lag_window[1] is a number of lags from 64 to 256.
All inputs are finite; a program needn't handle non-finite values.
Results may differ from a plain program's by a relative error of at most 0.0014.
Values may be sent and summed in bfloat16 or wider, within the bound.
No kernel may reach another device: no remote copies, remote signals or barrier semaphores. Data moves between devices by JAX's collectives and lax.ppermute only.
A program may use at most 64 MiB of HBM per device.

v0:
```python
import functools
import math

import jax
import jax.numpy as jnp
import numpy as np
from jax import lax
from jax.experimental import pallas as pl
from jax.experimental.pallas import tpu as pltpu
from jax.sharding import PartitionSpec as P

L = 512
S = 16
F = 256

env_floor = 0.05
misfit_scale = 0.03125
GROUP = 4
LANES = 128
FB = LANES // (2 * S)


def lag_tables(freq_total, lag_total):
    half = lag_total // 2
    freq_ids = np.arange(freq_total)[:, None]
    phase = 2.0 * np.pi * (freq_ids * np.arange(half)[None, :] % lag_total) / lag_total
    cosine = np.cos(phase) / math.sqrt(freq_total)
    sine = np.sin(phase) / math.sqrt(freq_total)
    back = [np.concatenate([cosine[p::2], sine[p::2]], axis=1) for p in (0, 1)]
    ahead = [np.concatenate([cosine[p::2].T, sine[p::2].T], axis=1) for p in (0, 1)]
    return [jnp.asarray(t.astype(np.float32)).astype(jnp.bfloat16) for t in ahead + back]


def nt(a, b):
    return lax.dot_general(a, b, (((1,), (1,)), ((), ())), preferred_element_type=jnp.float32)


def nn(a, b):
    return jnp.dot(a, b, preferred_element_type=jnp.float32)


def tn(a, b):
    return lax.dot_general(a, b, (((0,), (0,)), ((), ())), preferred_element_type=jnp.float32)


def pair_kernel(
    v_ref, u_ref, e_ref, invn_ref, eye_ref, ye_ref, yo_ref, ze_ref, zo_ref, w_ref, r_ref, x_ref
):
    src_total, col_total, k_own = v_ref.shape
    irec = u_ref.shape[0] // 2
    jj_total = LANES // (2 * irec)
    jp_total = col_total // jj_total
    ref_total, _, k_quarter = r_ref.shape
    k_total = src_total * k_own
    half_f = k_total // (4 * S)
    freq_total = 2 * half_f
    blocks = k_total // LANES
    own_blocks = k_own // LANES
    quarter_blocks = k_quarter // LANES

    group_ids = lax.broadcasted_iota(jnp.int32, (jp_total, LANES), 1) // (2 * S)

    def lanes_of(fb, per):
        return fb // per, pl.multiple_of(fb % per * LANES, LANES)

    def v_block(fb):
        src, off = lanes_of(fb, own_blocks)
        parts = [
            v_ref[src, jj * jp_total : (jj + 1) * jp_total, pl.ds(off, LANES)]
            for jj in range(jj_total)
        ]
        zero = jnp.zeros((jp_total, LANES), jnp.bfloat16)
        rows = [
            jnp.concatenate([jnp.where(group_ids == f, part, zero) for part in parts], axis=1)
            for f in range(FB)
        ]
        return jnp.concatenate(rows, axis=0)

    def u_block(fb):
        off = pl.multiple_of(fb * LANES, LANES)
        zero = jnp.zeros((irec, LANES), jnp.bfloat16)
        rows = []
        for q in range(2):
            part = u_ref[q * irec : (q + 1) * irec, pl.ds(off, LANES)]
            for jj in range(jj_total):
                rows.append(
                    jnp.concatenate([part if k == jj else zero for k in range(jj_total)], axis=1)
                )
        return jnp.concatenate(rows, axis=0)

    def place(fb, f):
        return pl.ds((f % 2) * half_f + fb * (FB // 2) + f // 2, jp_total, stride=freq_total)

    def forward(fb, _):
        out = nt(v_block(fb), u_block(fb))
        scale = invn_ref[...]
        for f in range(FB):
            x_ref[place(fb, f), :] = out[f * jp_total : (f + 1) * jp_total] * scale
        return 0

    lax.fori_loop(0, blocks, forward, 0, unroll=4)

    lane_ids = lax.broadcasted_iota(jnp.int32, (1, LANES), 1)
    sign = jnp.where(lane_ids < LANES // 2, -1.0, 1.0).astype(jnp.float32)
    width = 2

    def pairs(step, _):
        cols = [step * width + k for k in range(width)]
        rhs_e, rhs_o, obs = [], [], []
        for jp in cols:
            x = x_ref[pl.ds(pl.multiple_of(jp * freq_total, freq_total), freq_total), :]
            x = x.astype(jnp.bfloat16).astype(jnp.float32)
            turned = pltpu.roll(x, LANES // 2, 1) * sign
            rhs_e.append(jnp.concatenate([x[:half_f], turned[:half_f]], axis=0))
            rhs_o.append(jnp.concatenate([x[half_f:], turned[half_f:]], axis=0))
            rows = [e_ref[:, jj * jp_total + jp].astype(jnp.float32) for jj in range(jj_total)]
            rows = [r.reshape(irec, r.shape[-1]) for r in rows]
            obs.append(jnp.concatenate(rows * 2, axis=0))
        rhs_e = jnp.concatenate(rhs_e, axis=1).astype(jnp.bfloat16)
        rhs_o = jnp.concatenate(rhs_o, axis=1).astype(jnp.bfloat16)
        even = nn(ye_ref[...], rhs_e)
        odd = nn(yo_ref[...], rhs_o)
        seen = nt(eye_ref[...], jnp.concatenate(obs, axis=0).astype(jnp.bfloat16))
        g_e, g_o = [], []
        for k in range(width):
            lanes = slice(k * LANES, (k + 1) * LANES)
            e, d0, d1 = seen[:, lanes], even[:, lanes], odd[:, lanes]
            high = e < 0.0
            d = d0 + jnp.where(high, d1, -d1)
            power = d * d
            power = power + pltpu.roll(power, LANES // 2, 1) + env_floor
            g = d * (1.0 - jnp.abs(e) * lax.rsqrt(power)) * misfit_scale
            g = jnp.where(e == 0.0, 0.0, g)
            turned = -pltpu.roll(g, LANES // 2, 1) * sign
            g_e.append(jnp.concatenate([g, turned], axis=0))
            g_o.append(
                jnp.concatenate([jnp.where(high, g, -g), jnp.where(high, turned, -turned)], axis=0)
            )
        z_e = nn(ze_ref[...], jnp.concatenate(g_e, axis=1).astype(jnp.bfloat16))
        z_o = nn(zo_ref[...], jnp.concatenate(g_o, axis=1).astype(jnp.bfloat16))
        for k, jp in enumerate(cols):
            lanes = slice(k * LANES, (k + 1) * LANES)
            scale = invn_ref[pl.ds(jp, 1), :]
            base = pl.multiple_of(jp * freq_total, freq_total)
            x_ref[pl.ds(base, half_f), :] = z_e[:, lanes] * scale
            x_ref[pl.ds(base + half_f, half_f), :] = z_o[:, lanes] * scale
        return 0

    lax.fori_loop(0, jp_total // width, pairs, 0)

    first_part = lax.broadcasted_iota(jnp.int32, (irec, LANES), 1) % (2 * S) < S

    def backward(fb, _):
        z = jnp.concatenate([x_ref[place(fb, f), :] for f in range(FB)], axis=0)
        z = z.astype(jnp.bfloat16)
        w = nn(z, u_block(fb))
        src, off = lanes_of(fb, own_blocks)
        for jj in range(jj_total):
            lanes = slice(jj * LANES, (jj + 1) * LANES)
            total = w[:jp_total, lanes]
            for f in range(1, FB):
                total = jnp.where(group_ids == f, w[f * jp_total : (f + 1) * jp_total, lanes], total)
            w_ref[src, jj * jp_total : (jj + 1) * jp_total, pl.ds(off, LANES)] = total
        r = tn(z, v_block(fb))
        sums = []
        for q in range(2):
            total = None
            for jj in range(jj_total):
                begin = (q * jj_total + jj) * irec
                part = r[begin : begin + irec, jj * LANES : (jj + 1) * LANES]
                total = part if total is None else total + part
            sums.append(total)
        crossed = jnp.where(
            first_part, -pltpu.roll(sums[1], LANES - S, 1), pltpu.roll(sums[1], S, 1)
        )
        quarter, off = lanes_of(fb, quarter_blocks)
        r_ref[quarter, :, pl.ds(off, LANES)] = sums[0] + crossed
        return 0

    lax.fori_loop(0, blocks, backward, 0, unroll=4)


def shards(
    receiver_spectra,
    reference_spectra,
    receiver_counts,
    reference_counts,
    column_station,
    lag_window,
    observed,
    *,
    rcv_total,
    ref_total,
):
    row_total, k_quarter = receiver_spectra.shape
    k_own, col_total = reference_spectra.shape
    k_total = k_own * rcv_total
    lag_total = observed.shape[2]
    half = lag_total // 2
    members = math.gcd(GROUP, rcv_total)
    groups = [
        [begin + k for k in range(members)] for begin in range(0, rcv_total, members)
    ]
    irec = row_total * members
    cols = col_total // members
    jj_total = LANES // (2 * irec)
    jp_total = cols // jj_total
    bf16 = jnp.bfloat16

    seg_own = jnp.arange(k_own, dtype=jnp.int32) % S
    turned = reference_spectra.T
    turned = jnp.where(seg_own[None, :] < reference_counts[:, None], turned, jnp.zeros((), bf16))
    sent = jnp.broadcast_to(
        turned.reshape(1, members, cols, k_own), (rcv_total // members, members, cols, k_own)
    ).reshape(rcv_total, cols, k_own)
    v_all = lax.all_to_all(sent, "rcv", split_axis=0, concat_axis=0, tiled=True)

    local_order = column_station - lax.axis_index("ref") * col_total
    begin = lag_window[0][..., None]
    end = begin + lag_window[1][..., None]
    lag_ids = jnp.arange(half, dtype=jnp.int32)
    low = (lag_ids >= begin) & (lag_ids < end)
    high = (lag_ids + half >= begin) & (lag_ids + half < end)
    folded = jnp.where(
        low, observed[..., :half], jnp.where(high, -observed[..., half:], jnp.zeros((), bf16))
    )
    pick = (jnp.arange(col_total, dtype=jnp.int32)[:, None] == local_order[None, :]).astype(bf16)
    folded = jnp.transpose(folded, (1, 0, 2)).reshape(col_total, row_total * half)
    folded = jnp.dot(pick, folded, preferred_element_type=jnp.float32).astype(bf16)
    folded = folded.reshape(members, cols, row_total, half)
    e_all = lax.all_to_all(
        folded, "rcv", split_axis=0, concat_axis=0, axis_index_groups=groups, tiled=True
    )

    seg_quarter = jnp.arange(k_quarter, dtype=jnp.int32) % S
    masked = jnp.where(
        seg_quarter[None, :] < receiver_counts[:, None], receiver_spectra, jnp.zeros((), bf16)
    )
    counts = jnp.broadcast_to(receiver_counts.astype(bf16)[:, None], (row_total, LANES))
    own = jnp.concatenate([masked, counts], axis=1)
    near = lax.all_gather(own, "rcv", axis_index_groups=groups, axis=0, tiled=True)
    group_counts = near[:, k_quarter].astype(jnp.float32)
    u_all = lax.all_gather(near[:, :k_quarter], "ref", axis=1, tiled=True)
    parts = u_all.reshape(irec, k_total // (2 * S), 2, S)
    crossed = jnp.stack([parts[:, :, 1], -parts[:, :, 0]], axis=2).reshape(irec, k_total)
    u_rows = jnp.concatenate([u_all, crossed], axis=0)

    place = lax.axis_index("rcv") % members
    own_counts = lax.dynamic_slice_in_dim(reference_counts, place * cols, cols).astype(jnp.float32)
    least = jnp.minimum(
        own_counts.reshape(jj_total, jp_total).T[:, :, None], group_counts[None, None, :]
    )
    inverse = (1.0 / least).reshape(jp_total, jj_total * irec)
    inverse = jnp.concatenate([inverse, inverse], axis=1)

    tables = lag_tables(k_total // (2 * S), lag_total)
    eye = jnp.eye(half, dtype=bf16)
    w_part, r_part = pl.pallas_call(
        pair_kernel,
        out_shape=(
            jax.ShapeDtypeStruct((rcv_total, cols, k_own), jnp.float32),
            jax.ShapeDtypeStruct((ref_total, irec, k_quarter), jnp.float32),
        ),
        in_specs=[pl.BlockSpec(memory_space=pltpu.VMEM)] * 9,
        out_specs=[pl.BlockSpec(memory_space=pltpu.VMEM)] * 2,
        scratch_shapes=[pltpu.VMEM((jp_total * k_total // (2 * S), LANES), jnp.float32)],
        compiler_params=pltpu.CompilerParams(vmem_limit_bytes=48 * 1024 * 1024),
    )(v_all, u_rows, e_all, inverse, eye, *tables)

    got = lax.all_to_all(w_part, "rcv", split_axis=0, concat_axis=0, tiled=True)
    got = got.reshape(rcv_total // members, col_total, k_own).sum(axis=0)
    got = jnp.where(seg_own[None, :] < reference_counts[:, None], got, 0.0)
    reference_grad = got.T

    r_sum = lax.all_to_all(r_part, "ref", split_axis=0, concat_axis=0, tiled=True).sum(axis=0)
    r_sum = lax.all_to_all(
        r_sum.reshape(members, row_total, k_quarter),
        "rcv",
        split_axis=0,
        concat_axis=0,
        axis_index_groups=groups,
        tiled=True,
    ).sum(axis=0)
    receiver_grad = jnp.where(seg_quarter[None, :] < receiver_counts[:, None], r_sum, 0.0)
    return (receiver_grad, reference_grad)


def solution(mesh):
    return jax.shard_map(
        functools.partial(shards, rcv_total=mesh.shape["rcv"], ref_total=mesh.shape["ref"]),
        mesh=mesh,
        in_specs=(
            P("rcv", "ref"),
            P("rcv", "ref"),
            P("rcv"),
            P("ref"),
            P("ref"),
            P(None, "rcv", "ref"),
            P("rcv", "ref", None),
        ),
        out_specs=(P("rcv", "ref"), P("rcv", "ref")),
        check_vma=False,
    )
```

profile of v0, /device:TPU:0, one launch (start us, length us, event | category | flops | bytes accessed | tf_op | source)
XLA Modules:
  0.0 182.2 jit_solution(13213019854307707196)
XLA Ops:
  0.6 0.7 bitcast_add_fusion
  1.4 0.7 slice_bitcast_fusion
  2.1 1.7 fusion.10
  3.7 0.0 copy-start.15
  3.8 0.5 copy.39
  4.3 0.5 copy.38
  4.8 0.0 copy-done.15
  4.8 1.1 fusion.1
  5.9 0.5 convolution_convert_fusion
  6.4 0.0 copy-start.11
  6.4 0.0 copy-start.13
  6.4 0.0 copy-start.10
  6.4 0.0 copy-start.5
  6.4 1.3 copy.40
  7.7 5.2 %all-to-all-start.1 = ((bf16[4,64,8,256]{3,2,1,0:T(8,128)(2,1)}), bf16[4,64,8,256]{3,2,1,0:T(8,128)(2,1)S(1)}, u32[]{:S(2)}, u32[]{:S(2)}) async-start(bf16[4,64,8,256]{3,2,1,0:T(8,128)(2,1)} %bitcast.16), calls=%async_computation.1 | async-start | bytes 2097152 | tf_op jit(solution)/shard_map/all_to_all | solution.py:231
  13.0 0.0 copy-done.11
  13.0 0.1 dynamic-slice_convert_fusion
  13.0 0.1 reshape.85
  13.1 0.0 copy-done.13
  13.1 0.1 copy.36
  13.2 0.1 min.20
  13.3 0.1 min.21
  13.4 0.0 copy-done.10
  13.4 0.0 copy-start.6
  13.4 0.1 compare_select_fusion.2
  13.5 0.1 broadcast_in_dim.29
  13.6 0.4 copy-done.6
  14.0 20.0 %all_gather.6 = bf16[32,2176]{1,0:T(8,128)(2,1)S(1)} all-gather(bf16[8,2176]{1,0:T(8,128)(2,1)S(1)} %pad_maximum_fusion.2), channel_id=1, replica_groups={{0,4,8,12},{16,20,24,28},{1,5,9,13},{17,21,25,29},{2,6,10,14},{18,22,26..., dimensions={0}, use_global_device_ids=true | all-gather | bytes 174080 | tf_op jit(solution)/shard_map/all_gather | solution.py:241
  34.0 0.1 convert_reduce_fusion
  34.1 0.1 min.23
  34.2 0.0 copy-done.5
  34.2 0.2 copy.31
  34.4 7.2 %all_gather.7 = bf16[32,8192]{1,0:T(8,128)(2,1)S(1)} all-gather(bf16[32,2048]{1,0:T(8,128)(2,1)S(1)} %slice.32), channel_id=1, replica_groups=mesh['rcv'=8,'ref'=4] {'ref'}, dimensions={1}, use_global_device_ids=true | all-gather | bytes 655360 | tf_op jit(solution)/shard_map/all_gather | solution.py:243
  41.6 1.8 copy.32
  43.4 0.6 copy-done.8
  43.9 0.2 compare_select_fusion
  44.1 0.0 all-to-all-done.1.e_ref
  44.1 1.1 broadcast_in_dim.26
  45.2 0.0 copy-done.4
  45.2 4.2 %all-to-all-start = ((bf16[8,64,1024]{2,1,0:T(8,128)(2,1)}), bf16[8,64,1024]{2,1,0:T(8,128)(2,1)S(1)}, u32[]{:S(2)}, u32[]{:S(2)}) async-start(bf16[8,64,1024]{2,1,0:T(8,128)(2,1)} %bitcast.2), calls=%async_computation | async-start | bytes 2097152 | tf_op jit(solution)/shard_map/all_to_all | solution.py:216
  49.5 1.7 fusion.11
  51.2 1.7 pad_maximum_fusion
  53.0 2.6 %copy.33 = bf16[32,8192]{1,0:T(8,128)(2,1)} copy(bf16[32,8192]{0,1:T(8,128)(2,1)} %bitcast.27) | data formatting | bytes 1048576 | tf_op jit(solution)/shard_map/reshape | solution.py:245
  55.6 0.1 pad_maximum_fusion.3.invn_ref
  55.7 1.3 pad_maximum_fusion.1.u_ref
  57.0 18.8 %all-to-all-done.v_ref = bf16[8,64,1024]{2,1,0:T(8,128)(2,1)S(1)} async-done(((bf16[8,64,1024]{2,1,0:T(8,128)(2,1)}), bf16[8,64,1024]{2,1,0:T(8,128)(2,1)S(1)}, u32[]{:S(2)}, u32[]{:S(2)}) %all-to-all-start) | async-done | bytes 1048608 | tf_op jit(solution)/shard_map/all_to_all | solution.py:216
  75.8 0.0 copy-done
  75.8 0.0 copy-done.1
  75.8 0.9 copy-done.2
  76.7 0.9 copy-done.3
  77.6 27.2 %shard_map.122 = (f32[8,64,1024]{2,1,0:T(8,128)}, f32[4,32,2048]{2,1,0:T(8,128)S(1)}) custom-call(bf16[8,64,1024]{2,1,0:T(8,128)(2,1)S(1)} %all-to-all-done.v_ref, bf16[64,8192]{1,0:T(8,128)(2,1)S(1)} %pad_maximum_fusion.1.u_ref, bf16[4,64,8,256]{3,2,1,0:T(8,128)(2,1)S(1)} %all-to-all-done.1.e_ref, f32[32,128]{1,0:T(8,128)S(1)} %pad_maximum_fusion.3.invn_ref, ...), custom_call_target="tpu_custom_call" | custom-call | tf_op jit(solution)/shard_map/pallas_call | solution.py:258
  104.8 16.9 %all_to_all.25 = f32[4,32,2048]{2,1,0:T(8,128)S(1)} all-to-all(f32[4,32,2048]{2,1,0:T(8,128)S(1)} %get-tuple-element.4), channel_id=1, replica_groups=mesh['rcv'=8,'ref'=4] {'ref'}, dimensions={0} | all-to-all | bytes 2097152 | tf_op jit(solution)/shard_map/all_to_all | solution.py:275
  121.6 0.1 reduce_sum.29
  121.7 8.2 %all_to_all.26 = f32[4,8,2048]{2,1,0:T(8,128)S(1)} all-to-all(f32[4,8,2048]{2,1,0:T(8,128)S(1)} %bitcast.32), channel_id=1, replica_groups={{0,4,8,12},{16,20,24,28},{1,5,9,13},{17,21,25,29},{2,6,10,14},{18,22,26..., dimensions={0} | all-to-all | bytes 524288 | tf_op jit(solution)/shard_map/all_to_all | solution.py:276
  129.9 3.7 %all-to-all-start.4 = ((f32[8,64,1024]{2,1,0:T(8,128)}), f32[8,64,1024]{2,1,0:T(8,128)S(1)}, u32[]{:S(2)}, u32[]{:S(2)}) async-start(f32[8,64,1024]{2,1,0:T(8,128)} %get-tuple-element.5), calls=%async_computation.4 | async-start | bytes 4194304 | tf_op jit(solution)/shard_map/all_to_all | solution.py:270
  133.7 0.0 copy-start.9
  133.7 0.0 copy-start.12
  133.7 0.0 copy-done.7
  133.7 0.0 copy-done.14
  133.7 0.7 compare_select_fusion.1
  134.4 46.2 %all-to-all-done.4 = f32[8,64,1024]{2,1,0:T(8,128)S(1)} async-done(((f32[8,64,1024]{2,1,0:T(8,128)}), f32[8,64,1024]{2,1,0:T(8,128)S(1)}, u32[]{:S(2)}, u32[]{:S(2)}) %all-to-all-start.4) | async-done | bytes 2097184 | tf_op jit(solution)/shard_map/all_to_all | solution.py:270
  180.6 0.2 bitcast_reduce_fusion
  180.8 0.1 bitcast_select_fusion
  180.9 1.3 copy.37
  (21 shorter events, 0.1 us)
Async XLA Ops:
  3.7 1.1 copy-start.15
  6.4 6.6 %copy-start.11 = (s32[256]{0:T(256)S(1)}, s32[256]{0:T(256)}, u32[]{:S(2)}) copy-start(s32[256]{0:T(256)} %param.14) | copy-start | bytes 3076
  6.4 6.7 %copy-start.13 = (s32[8]{0:T(128)S(1)}, s32[8]{0:T(128)}, u32[]{:S(2)}) copy-start(s32[8]{0:T(128)} %param.13) | copy-start | bytes 100
  6.4 7.0 %copy-start.10 = (bf16[8,2048]{1,0:T(8,128)(2,1)S(1)}, bf16[8,2048]{1,0:T(8,128)(2,1)}, u32[]{:S(2)}) copy-start(bf16[8,2048]{1,0:T(8,128)(2,1)} %param.11) | copy-start | bytes 98308
  6.4 27.8 %copy-start.5 = (bf16[1024,256]{1,0:T(8,128)(2,1)S(1)}, bf16[1024,256]{1,0:T(8,128)(2,1)}, u32[]{:S(2)}) copy-start(bf16[1024,256]{1,0:T(8,128)(2,1)} %param.12) | copy-start | bytes 1572868
  7.7 36.4 %all-to-all-start.1 = ((bf16[4,64,8,256]{3,2,1,0:T(8,128)(2,1)}), bf16[4,64,8,256]{3,2,1,0:T(8,128)(2,1)S(1)}, u32[]{:S(2)}, u32[]{:S(2)}) async-start(bf16[4,64,8,256]{3,2,1,0:T(8,128)(2,1)} %bitcast.16), calls=%async_computation.1 | async-start | bytes 2097152 | tf_op jit(solution)/shard_map/all_to_all | solution.py:231
  13.4 0.6 copy-start.6
  41.6 3.6 %copy-start.4 = (bf16[32,8192]{1,0:T(8,128)(2,1)}, bf16[32,8192]{1,0:T(8,128)(2,1)S(1)}, u32[]{:S(2)}) copy-start(bf16[32,8192]{1,0:T(8,128)(2,1)S(1)} %all_gather.7) | copy-start | bytes 1572868
  43.4 0.6 copy-start.8
  45.2 30.5 %all-to-all-start = ((bf16[8,64,1024]{2,1,0:T(8,128)(2,1)}), bf16[8,64,1024]{2,1,0:T(8,128)(2,1)S(1)}, u32[]{:S(2)}, u32[]{:S(2)}) async-start(bf16[8,64,1024]{2,1,0:T(8,128)(2,1)} %bitcast.2), calls=%async_computation | async-start | bytes 2097152 | tf_op jit(solution)/shard_map/all_to_all | solution.py:216
  53.0 22.8 %copy-start = (bf16[128,512]{1,0:T(8,128)(2,1)S(1)}, bf16[128,512]{1,0:T(8,128)(2,1)}, u32[]{:S(2)}) copy-start(bf16[128,512]{1,0:T(8,128)(2,1)} %constant.73.zo_ref) | copy-start | bytes 393220
  53.0 22.8 %copy-start.1 = (bf16[128,512]{1,0:T(8,128)(2,1)S(1)}, bf16[128,512]{1,0:T(8,128)(2,1)}, u32[]{:S(2)}) copy-start(bf16[128,512]{1,0:T(8,128)(2,1)} %constant.72.ze_ref) | copy-start | bytes 393220
  75.8 0.9 copy-start.2
  76.7 0.9 copy-start.3
  129.9 3.8 %copy-start.7 = (s32[2048]{0:T(1024)S(1)}, s32[2048]{0:T(1024)}, u32[]{:S(2)}) copy-start(s32[2048]{0:T(1024)} %copy-done.6) | copy-start | bytes 24580
  129.9 3.8 %copy-start.14 = (s32[8]{0:T(128)S(1)}, s32[8]{0:T(128)}, u32[]{:S(2)}) copy-start(s32[8]{0:T(128)} %param.13) | copy-start | bytes 100
  129.9 50.7 %all-to-all-start.4 = ((f32[8,64,1024]{2,1,0:T(8,128)}), f32[8,64,1024]{2,1,0:T(8,128)S(1)}, u32[]{:S(2)}, u32[]{:S(2)}) async-start(f32[8,64,1024]{2,1,0:T(8,128)} %get-tuple-element.5), calls=%async_computation.4 | async-start | bytes 4194304 | tf_op jit(solution)/shard_map/all_to_all | solution.py:270
  133.7 47.1 %copy-start.9 = (s32[1024]{0:T(1024)S(1)}, s32[1024]{0:T(1024)}, u32[]{:S(2)}) copy-start(s32[1024]{0:T(1024)} %copy-done.8) | copy-start | bytes 12292
  133.7 47.1 %copy-start.12 = (s32[256]{0:T(256)S(1)}, s32[256]{0:T(256)}, u32[]{:S(2)}) copy-start(s32[256]{0:T(256)} %param.14) | copy-start | bytes 3076
where the time goes:
time: 183 us; the launch traced here: 182 us
  waiting for transfers between devices  65 us (36%)
  blocking collectives  52.2 us (29%)
  Pallas kernels  27.2 us (15%)
  local copies, waits for them, and re-layouts  15.1 us (8%)
  starting transfers between devices  13.2 us (7%)
  other arithmetic  8.19 us (4%)
    all_to_all x1, waiting for transfers between devices, shards(): got = lax.all_to_all(w_part, 'rcv', split_axis=0, concat_axis=0, tiled=True)  46.2 us
    pallas_call x1, Pallas kernels, shards(): pl.pallas_call(pair_kernel, out_shape=(jax.ShapeDtypeStruct((rcv_total, c...  27.2 us
    all_gather x1, blocking collectives, shards(): lax.all_gather(own, 'rcv', axis_index_groups=groups, axis=0, tiled=True)  20 us
    all_to_all x1, waiting for transfers between devices, shards(): v_all = lax.all_to_all(sent, 'rcv', split_axis=0, concat_axis=0, tiled=True)  18.8 us
    all_to_all x1, blocking collectives, shards(): lax.all_to_all(r_part, 'ref', split_axis=0, concat_axis=0, tiled=True)  16.9 us
    all_to_all x1, blocking collectives, shards(): lax.all_to_all(r_sum.reshape(members, row_total, k_quarter), 'rcv', split...  8.21 us
    all_gather x1, blocking collectives, shards(): u_all = lax.all_gather(near[:, :k_quarter], 'ref', axis=1, tiled=True)  7.16 us
    unnamed x37, local copies, waits for them, and re-layouts  6.73 us
  transfers between devices with their start and end apart: 3, of which 2 were waited for; matrix products, arithmetic and copies ran while one was open for 6% of the time, Pallas kernels for 0%

commit v1 on v0

--- a/solution.py
+++ b/solution.py
@@ -18,6 +18,8 @@
 GROUP = 4
 LANES = 128
 FB = LANES // (2 * S)
+WIDTH = 8
+FIXED = 32000.0
 
 
 def lag_tables(freq_total, lag_total):
@@ -44,13 +46,14 @@
 
 
 def pair_kernel(
-    v_ref, u_ref, e_ref, invn_ref, eye_ref, ye_ref, yo_ref, ze_ref, zo_ref, w_ref, r_ref, x_ref
+    c_ref, v_ref, u_ref, invn_ref, eye_ref, ye_ref, yo_ref, ze_ref, zo_ref, *rest
 ):
+    *e_refs, w_ref, r_ref, x_ref, urow_ref, code_ref = rest
     src_total, col_total, k_own = v_ref.shape
-    irec = u_ref.shape[0] // 2
+    ref_total, irec, k_quarter = u_ref.shape
+    member_rows = irec // len(e_refs)
     jj_total = LANES // (2 * irec)
     jp_total = col_total // jj_total
-    ref_total, _, k_quarter = r_ref.shape
     k_total = src_total * k_own
     half_f = k_total // (4 * S)
     freq_total = 2 * half_f
@@ -59,6 +62,8 @@
     quarter_blocks = k_quarter // LANES
 
     group_ids = lax.broadcasted_iota(jnp.int32, (jp_total, LANES), 1) // (2 * S)
+    first_part = lax.broadcasted_iota(jnp.int32, (irec, LANES), 1) % (2 * S) < S
+    me = c_ref[0]
 
     def lanes_of(fb, per):
         return fb // per, pl.multiple_of(fb % per * LANES, LANES)
@@ -76,36 +81,42 @@
         ]
         return jnp.concatenate(rows, axis=0)
 
-    def u_block(fb):
-        off = pl.multiple_of(fb * LANES, LANES)
+    def u_block(parts):
         zero = jnp.zeros((irec, LANES), jnp.bfloat16)
-        rows = []
-        for q in range(2):
-            part = u_ref[q * irec : (q + 1) * irec, pl.ds(off, LANES)]
-            for jj in range(jj_total):
-                rows.append(
-                    jnp.concatenate([part if k == jj else zero for k in range(jj_total)], axis=1)
-                )
-        return jnp.concatenate(rows, axis=0)
+        return jnp.concatenate(
+            [
+                jnp.concatenate([part if k == jj else zero for k in range(jj_total)], axis=1)
+                for part in parts
+                for jj in range(jj_total)
+            ],
+            axis=0,
+        )
 
     def place(fb, f):
         return pl.ds((f % 2) * half_f + fb * (FB // 2) + f // 2, jp_total, stride=freq_total)
 
     def forward(fb, _):
-        out = nt(v_block(fb), u_block(fb))
+        quarter, off = lanes_of(fb, quarter_blocks)
+        part = u_ref[quarter ^ me, :, pl.ds(off, LANES)]
+        wide = part.astype(jnp.float32)
+        crossed = jnp.where(first_part, pltpu.roll(wide, LANES - S, 1), -pltpu.roll(wide, S, 1))
+        crossed = crossed.astype(jnp.bfloat16)
+        lanes = pl.ds(pl.multiple_of(fb * LANES, LANES), LANES)
+        urow_ref[0, :, lanes] = part
+        urow_ref[1, :, lanes] = crossed
+        out = nt(v_block(fb), u_block([part, crossed]))
         scale = invn_ref[...]
         for f in range(FB):
             x_ref[place(fb, f), :] = out[f * jp_total : (f + 1) * jp_total] * scale
         return 0
 
-    lax.fori_loop(0, blocks, forward, 0, unroll=4)
+    lax.fori_loop(0, blocks, forward, 0, unroll=16)
 
     lane_ids = lax.broadcasted_iota(jnp.int32, (1, LANES), 1)
     sign = jnp.where(lane_ids < LANES // 2, -1.0, 1.0).astype(jnp.float32)
-    width = 2
 
     def pairs(step, _):
-        cols = [step * width + k for k in range(width)]
+        cols = [step * WIDTH + k for k in range(WIDTH)]
         rhs_e, rhs_o, obs = [], [], []
         for jp in cols:
             x = x_ref[pl.ds(pl.multiple_of(jp * freq_total, freq_total), freq_total), :]
@@ -113,8 +124,11 @@
             turned = pltpu.roll(x, LANES // 2, 1) * sign
             rhs_e.append(jnp.concatenate([x[:half_f], turned[:half_f]], axis=0))
             rhs_o.append(jnp.concatenate([x[half_f:], turned[half_f:]], axis=0))
-            rows = [e_ref[:, jj * jp_total + jp].astype(jnp.float32) for jj in range(jj_total)]
-            rows = [r.reshape(irec, r.shape[-1]) for r in rows]
+            rows = [
+                ref[jj * jp_total + jp].astype(jnp.float32)
+                for jj in range(jj_total)
+                for ref in e_refs
+            ]
             obs.append(jnp.concatenate(rows * 2, axis=0))
         rhs_e = jnp.concatenate(rhs_e, axis=1).astype(jnp.bfloat16)
         rhs_o = jnp.concatenate(rhs_o, axis=1).astype(jnp.bfloat16)
@@ -122,7 +136,7 @@
         odd = nn(yo_ref[...], rhs_o)
         seen = nt(eye_ref[...], jnp.concatenate(obs, axis=0).astype(jnp.bfloat16))
         g_e, g_o = [], []
-        for k in range(width):
+        for k in range(WIDTH):
             lanes = slice(k * LANES, (k + 1) * LANES)
             e, d0, d1 = seen[:, lanes], even[:, lanes], odd[:, lanes]
             high = e < 0.0
@@ -146,21 +160,27 @@
             x_ref[pl.ds(base + half_f, half_f), :] = z_o[:, lanes] * scale
         return 0
 
-    lax.fori_loop(0, jp_total // width, pairs, 0)
-
-    first_part = lax.broadcasted_iota(jnp.int32, (irec, LANES), 1) % (2 * S) < S
+    lax.fori_loop(0, jp_total // WIDTH, pairs, 0)
 
     def backward(fb, _):
         z = jnp.concatenate([x_ref[place(fb, f), :] for f in range(FB)], axis=0)
         z = z.astype(jnp.bfloat16)
-        w = nn(z, u_block(fb))
-        src, off = lanes_of(fb, own_blocks)
+        lanes = pl.ds(pl.multiple_of(fb * LANES, LANES), LANES)
+        w = nn(z, u_block([urow_ref[q, :, lanes] for q in range(2)]))
+        totals = []
         for jj in range(jj_total):
             lanes = slice(jj * LANES, (jj + 1) * LANES)
             total = w[:jp_total, lanes]
             for f in range(1, FB):
                 total = jnp.where(group_ids == f, w[f * jp_total : (f + 1) * jp_total, lanes], total)
-            w_ref[src, jj * jp_total : (jj + 1) * jp_total, pl.ds(off, LANES)] = total
+            totals.append(total)
+        total = jnp.concatenate(totals, axis=0)
+        largest = jnp.max(jnp.abs(total), axis=0, keepdims=True)
+        power = jnp.ceil(jnp.log2(jnp.maximum(largest, 1e-30)))
+        code_ref[pl.ds(fb, 1), :] = power
+        fixed = jnp.round(total * (jnp.exp2(-power) * FIXED)).astype(jnp.int32)
+        src, off = lanes_of(fb, own_blocks)
+        w_ref[src, :, pl.ds(off, LANES)] = fixed.astype(jnp.int16)
         r = tn(z, v_block(fb))
         sums = []
         for q in range(2):
@@ -177,7 +197,41 @@
         r_ref[quarter, :, pl.ds(off, LANES)] = sums[0] + crossed
         return 0
 
-    lax.fori_loop(0, blocks, backward, 0, unroll=4)
+    lax.fori_loop(0, blocks, backward, 0, unroll=16)
+
+    for src in range(src_total):
+        codes = code_ref[src * own_blocks : (src + 1) * own_blocks, :]
+        codes = jnp.concatenate(
+            [codes, jnp.zeros((col_total - own_blocks, LANES), jnp.float32)], axis=0
+        )
+        w_ref[src, :, k_own:] = codes.astype(jnp.int32).astype(jnp.int16)
+
+
+def join_kernel(got_ref, count_ref, out_ref):
+    src_total, cols, width = got_ref.shape
+    k_own, col_total = out_ref.shape
+    members = col_total // cols
+    seg_ids = lax.broadcasted_iota(jnp.int32, (LANES, col_total), 0) % S
+    inside = seg_ids < count_ref[...]
+    scales = []
+    for src in range(src_total):
+        codes = got_ref[src, :16, k_own:].astype(jnp.int32).astype(jnp.float32)
+        scales.append(jnp.exp2(codes) * (1.0 / FIXED))
+    for b in range(k_own // LANES):
+        rows = []
+        for m in range(members):
+            total = None
+            for src in range(m, src_total, members):
+                part = got_ref[src, :, b * LANES : (b + 1) * LANES]
+                part = part.astype(jnp.int32).astype(jnp.float32) * scales[src][b : b + 1]
+                total = part if total is None else total + part
+            rows.append(total)
+        whole = jnp.concatenate(rows, axis=0).T
+        out_ref[b * LANES : (b + 1) * LANES, :] = jnp.where(inside, whole, 0.0)
+
+
+def swap(x, axis, total, k):
+    return lax.ppermute(x, axis, [(r, r ^ k) for r in range(total)])
 
 
 def shards(
@@ -198,14 +252,26 @@
     lag_total = observed.shape[2]
     half = lag_total // 2
     members = math.gcd(GROUP, rcv_total)
-    groups = [
-        [begin + k for k in range(members)] for begin in range(0, rcv_total, members)
-    ]
     irec = row_total * members
     cols = col_total // members
     jj_total = LANES // (2 * irec)
     jp_total = cols // jj_total
     bf16 = jnp.bfloat16
+    mine = lax.axis_index("rcv") % members
+    quarter = lax.axis_index("ref")
+
+    seg_quarter = jnp.arange(k_quarter, dtype=jnp.int32) % S
+    masked = jnp.where(
+        seg_quarter[None, :] < receiver_counts[:, None], receiver_spectra, jnp.zeros((), bf16)
+    )
+    counts = jnp.broadcast_to(receiver_counts.astype(bf16)[:, None], (row_total, LANES))
+    own = jnp.concatenate([masked, counts], axis=1)
+    near = jnp.concatenate(
+        [own] + [swap(own, "rcv", rcv_total, k) for k in range(1, members)], axis=0
+    )
+    group_counts = near[:, k_quarter].astype(jnp.float32)
+    near = near[:, :k_quarter]
+    u_all = jnp.stack([near] + [swap(near, "ref", ref_total, k) for k in range(1, ref_total)])
 
     seg_own = jnp.arange(k_own, dtype=jnp.int32) % S
     turned = reference_spectra.T
@@ -215,7 +281,8 @@
     ).reshape(rcv_total, cols, k_own)
     v_all = lax.all_to_all(sent, "rcv", split_axis=0, concat_axis=0, tiled=True)
 
-    local_order = column_station - lax.axis_index("ref") * col_total
+    _, observed, lag_window = lax.optimization_barrier((sent, observed, lag_window))
+    local_order = column_station - quarter * col_total
     begin = lag_window[0][..., None]
     end = begin + lag_window[1][..., None]
     lag_ids = jnp.arange(half, dtype=jnp.int32)
@@ -228,25 +295,10 @@
     folded = jnp.transpose(folded, (1, 0, 2)).reshape(col_total, row_total * half)
     folded = jnp.dot(pick, folded, preferred_element_type=jnp.float32).astype(bf16)
     folded = folded.reshape(members, cols, row_total, half)
-    e_all = lax.all_to_all(
-        folded, "rcv", split_axis=0, concat_axis=0, axis_index_groups=groups, tiled=True
-    )
-
-    seg_quarter = jnp.arange(k_quarter, dtype=jnp.int32) % S
-    masked = jnp.where(
-        seg_quarter[None, :] < receiver_counts[:, None], receiver_spectra, jnp.zeros((), bf16)
-    )
-    counts = jnp.broadcast_to(receiver_counts.astype(bf16)[:, None], (row_total, LANES))
-    own = jnp.concatenate([masked, counts], axis=1)
-    near = lax.all_gather(own, "rcv", axis_index_groups=groups, axis=0, tiled=True)
-    group_counts = near[:, k_quarter].astype(jnp.float32)
-    u_all = lax.all_gather(near[:, :k_quarter], "ref", axis=1, tiled=True)
-    parts = u_all.reshape(irec, k_total // (2 * S), 2, S)
-    crossed = jnp.stack([parts[:, :, 1], -parts[:, :, 0]], axis=2).reshape(irec, k_total)
-    u_rows = jnp.concatenate([u_all, crossed], axis=0)
-
-    place = lax.axis_index("rcv") % members
-    own_counts = lax.dynamic_slice_in_dim(reference_counts, place * cols, cols).astype(jnp.float32)
+    share = [lax.dynamic_index_in_dim(folded, mine ^ k, 0, False) for k in range(members)]
+    e_all = share[:1] + [swap(share[k], "rcv", rcv_total, k) for k in range(1, members)]
+
+    own_counts = lax.dynamic_slice_in_dim(reference_counts, mine * cols, cols).astype(jnp.float32)
     least = jnp.minimum(
         own_counts.reshape(jj_total, jp_total).T[:, :, None], group_counts[None, None, :]
     )
@@ -255,32 +307,42 @@
 
     tables = lag_tables(k_total // (2 * S), lag_total)
     eye = jnp.eye(half, dtype=bf16)
+    vmem = pl.BlockSpec(memory_space=pltpu.VMEM)
     w_part, r_part = pl.pallas_call(
         pair_kernel,
         out_shape=(
-            jax.ShapeDtypeStruct((rcv_total, cols, k_own), jnp.float32),
+            jax.ShapeDtypeStruct((rcv_total, cols, k_own + LANES), jnp.int16),
             jax.ShapeDtypeStruct((ref_total, irec, k_quarter), jnp.float32),
         ),
-        in_specs=[pl.BlockSpec(memory_space=pltpu.VMEM)] * 9,
-        out_specs=[pl.BlockSpec(memory_space=pltpu.VMEM)] * 2,
-        scratch_shapes=[pltpu.VMEM((jp_total * k_total // (2 * S), LANES), jnp.float32)],
+        in_specs=[pl.BlockSpec(memory_space=pltpu.SMEM)] + [vmem] * (8 + members),
+        out_specs=[vmem] * 2,
+        scratch_shapes=[
+            pltpu.VMEM((jp_total * k_total // (2 * S), LANES), jnp.float32),
+            pltpu.VMEM((2, irec, k_total), bf16),
+            pltpu.VMEM((k_total // LANES, LANES), jnp.float32),
+        ],
         compiler_params=pltpu.CompilerParams(vmem_limit_bytes=48 * 1024 * 1024),
-    )(v_all, u_rows, e_all, inverse, eye, *tables)
+    )(quarter.reshape(1).astype(jnp.int32), v_all, u_all, inverse, eye, *tables, *e_all)
 
     got = lax.all_to_all(w_part, "rcv", split_axis=0, concat_axis=0, tiled=True)
-    got = got.reshape(rcv_total // members, col_total, k_own).sum(axis=0)
-    got = jnp.where(seg_own[None, :] < reference_counts[:, None], got, 0.0)
-    reference_grad = got.T
-
-    r_sum = lax.all_to_all(r_part, "ref", split_axis=0, concat_axis=0, tiled=True).sum(axis=0)
-    r_sum = lax.all_to_all(
-        r_sum.reshape(members, row_total, k_quarter),
-        "rcv",
-        split_axis=0,
-        concat_axis=0,
-        axis_index_groups=groups,
-        tiled=True,
-    ).sum(axis=0)
+    reference_grad = pl.pallas_call(
+        join_kernel,
+        out_shape=jax.ShapeDtypeStruct((k_own, col_total), jnp.float32),
+        in_specs=[vmem] * 2,
+        out_specs=vmem,
+        compiler_params=pltpu.CompilerParams(vmem_limit_bytes=32 * 1024 * 1024),
+    )(got, reference_counts.reshape(1, col_total))
+
+    parts = [
+        lax.dynamic_index_in_dim(r_part, quarter ^ k, 0, False) for k in range(ref_total)
+    ]
+    r_sum = parts[0]
+    for k in range(1, ref_total):
+        r_sum = r_sum + swap(parts[k], "ref", ref_total, k)
+    parts = [r_sum[k * row_total : (k + 1) * row_total] for k in range(members)]
+    r_sum = parts[0]
+    for k in range(1, members):
+        r_sum = r_sum + swap(parts[k], "rcv", rcv_total, k)
     receiver_grad = jnp.where(seg_quarter[None, :] < receiver_counts[:, None], r_sum, 0.0)
     return (receiver_grad, reference_grad)
 

time: 183 us -> 105 us (0.57)
  blocking collectives: 52.2 us -> 0 us
  waiting for transfers between devices: 65 us -> 35.3 us
  starting transfers between devices: 13.2 us -> 25.8 us
  Pallas kernels: 27.2 us -> 20 us
  local copies, waits for them, and re-layouts: 15.1 us -> 13 us
    all_to_all x1, waiting for transfers between devices: 46.2 us -> 4.05 us  [shards(): got = lax.all_to_all(w_part, 'rcv', split_axis=0, concat_axis=0, tiled=True)]
    ppermute x0 -> x15, waiting for transfers between devices: none -> 31.3 us  [swap(): return lax.ppermute(x, axis, [(r, r ^ k) for r in range(total)])]
    all_gather x2 -> x0, blocking collectives: 27.1 us -> none  [the longest x1 20 us: shards(): lax.all_gather(own, 'rcv', axis_index_groups=groups, axis=0, tiled=True)]
    all_to_all x2 -> x0, blocking collectives: 25.1 us -> none  [the longest x1 16.9 us: shards(): lax.all_to_all(r_part, 'ref', split_axis=0, concat_axis=0, tiled=True)]
    all_to_all x1, waiting for transfers between devices: 18.8 us -> 0.01 us  [shards(): v_all = lax.all_to_all(sent, 'rcv', split_axis=0, concat_axis=0, tiled=True)]
    ppermute x0 -> x15, starting transfers between devices: none -> 15.7 us  [swap(): return lax.ppermute(x, axis, [(r, r ^ k) for r in range(total)])]
    pallas_call x1, Pallas kernels: 27.2 us -> 18.6 us  [shards(): pl.pallas_call(pair_kernel, out_shape=(jax.ShapeDtypeStruct((rcv_total, c...]
    all_to_all x1 -> x0, starting transfers between devices: 5.25 us -> none  [shards(): lax.all_to_all(folded, 'rcv', split_axis=0, concat_axis=0, axis_index_gro...]
  transfers between devices with their start and end apart: 3 -> 17, of which waited for: 2 -> 10; matrix products, arithmetic and copies ran while one was open for 6% -> 14% of each run, Pallas kernels for 0% -> 0%
where the time goes in v1:
time: 105 us; the launch traced here: 104 us
  waiting for transfers between devices  35.3 us (34%)
  starting transfers between devices  25.8 us (25%)
  Pallas kernels  20 us (19%)
  local copies, waits for them, and re-layouts  13 us (12%)
  other arithmetic  8.59 us (8%)
    ppermute x15, waiting for transfers between devices, swap(): return lax.ppermute(x, axis, [(r, r ^ k) for r in range(total)])  31.3 us
    pallas_call x1, Pallas kernels, shards(): pl.pallas_call(pair_kernel, out_shape=(jax.ShapeDtypeStruct((rcv_total, c...  18.6 us
    ppermute x15, starting transfers between devices, swap(): return lax.ppermute(x, axis, [(r, r ^ k) for r in range(total)])  15.7 us
    unnamed x32, local copies, waits for them, and re-layouts  6.85 us
    all_to_all x1, starting transfers between devices, shards(): v_all = lax.all_to_all(sent, 'rcv', split_axis=0, concat_axis=0, tiled=True)  6.21 us
    all_to_all x1, waiting for transfers between devices, shards(): got = lax.all_to_all(w_part, 'rcv', split_axis=0, concat_axis=0, tiled=True)  4.05 us
    all_to_all x1, starting transfers between devices, shards(): got = lax.all_to_all(w_part, 'rcv', split_axis=0, concat_axis=0, tiled=True)  3.87 us
    optimization_barrier x1, local copies, waits for them, and re-layouts, shards(): lax.optimization_barrier((sent, observed, lag_window))  2.86 us
  transfers between devices with their start and end apart: 17, of which 10 were waited for; matrix products, arithmetic and copies ran while one was open for 14% of the time, Pallas kernels for 0%

profile of v1, /device:TPU:0, one launch (start us, length us, event | category | flops | bytes accessed | tf_op | source)
XLA Modules:
  0.0 104.2 jit_solution(6966202248188770726)
XLA Ops:
  0.6 0.7 convert_element_type.35
  1.3 0.8 compare_select_fusion.2
  2.2 0.1 broadcast_in_dim.25
  2.2 0.6 pad_maximum_fusion.2
  2.9 3.0 %collective-permute-start = (bf16[8,2176]{1,0:T(8,128)(2,1)}, bf16[8,2176]{1,0:T(8,128)(2,1)}, u32[]{:S(2)}, u32[]{:S(2)}) collective-permute-start(bf16[8,2176]{1,0:T(8,128)(2,1)} %pad_maximum_fusion.2), channel_id=1, source_target_pairs={{0,4},{4,0},{8,12},{12,8},{16,20},{20,16},{24,28},{28,24},{1,5},{5... | collective-permute-start | bytes 104456 | tf_op jit(solution)/shard_map/ppermute | solution.py:234
  5.8 1.6 %collective-permute-start.1 = (bf16[8,2176]{1,0:T(8,128)(2,1)}, bf16[8,2176]{1,0:T(8,128)(2,1)}, u32[]{:S(2)}, u32[]{:S(2)}) collective-permute-start(bf16[8,2176]{1,0:T(8,128)(2,1)} %pad_maximum_fusion.2), channel_id=1, source_target_pairs={{0,8},{4,12},{8,0},{12,4},{16,24},{20,28},{24,16},{28,20},{1,9},{5... | collective-permute-start | bytes 104456 | tf_op jit(solution)/shard_map/ppermute | solution.py:234
  7.4 0.0 collective-permute-start.2
  7.4 1.2 %copy.15 = bf16[1024,256]{0,1:T(8,128)(2,1)S(1)} copy(bf16[1024,256]{1,0:T(8,128)(2,1)} %param.12) | data formatting | bytes 1048576 | tf_op args[1]
  8.7 0.9 compare_select_fusion
  9.5 0.0 copy-start.12
  9.6 1.1 %broadcast_in_dim.23 = bf16[2,4,64,1024]{3,2,1,0:T(8,128)(2,1)} broadcast(bf16[4,64,1024]{2,1,0:T(8,128)(2,1)S(1)} %bitcast.49), dimensions={1,2,3} | broadcast | bytes 1572864 | tf_op jit(solution)/shard_map/broadcast_in_dim | solution.py:279
  10.7 6.2 %all-to-all-start = ((bf16[8,64,1024]{2,1,0:T(8,128)(2,1)}), bf16[8,64,1024]{2,1,0:T(8,128)(2,1)S(1)}, u32[]{:S(2)}, u32[]{:S(2)}) async-start(bf16[8,64,1024]{2,1,0:T(8,128)(2,1)} %bitcast.3), calls=%async_computation | async-start | bytes 2097152 | tf_op jit(solution)/shard_map/all_to_all | solution.py:282
  16.9 0.0 copy-start.14
  16.9 2.9 %copy.17 = bf16[8,256,512]{1,2,0:T(8,128)(2,1)S(1)} copy(bf16[8,256,512]{2,1,0:T(8,128)(2,1)} %param.17) | data formatting | bytes 4194304 | tf_op jit(solution)/shard_map/optimization_barrier | solution.py:284
  19.8 1.1 %fusion.1 = bf16[8,256,256]{1,2,0:T(8,128)(2,1)S(1)} fusion(bf16[8,256,512]{1,2,0:T(8,128)(2,1)S(1)} %copy.17, s32[8,256]{1,0:T(8,128)S(1)} %bitcast_add_fusion.1, s32[8,256]{1,0:T(8,128)S(1)} %slice_bitcast_fusion, s32[256]{0:T(256)S(1)} %iota_add_fusion), kind=kLoop, calls=%fused_computation.4 | loop fusion | flops 5767168 | bytes 3163136 | tf_op jit(solution)/shard_map/jit(_where)/select_n | solution.py:291
  20.9 0.5 convolution_convert_fusion
  21.4 0.0 copy-start.6
  21.4 0.3 copy.19
  21.7 0.9 dynamic-slice_bitcast_fusion.3
  22.6 2.0 %collective-permute-start.6 = (bf16[64,8,256]{2,1,0:T(8,128)(2,1)}, bf16[64,8,256]{2,1,0:T(8,128)(2,1)S(1)}, u32[]{:S(2)}, u32[]{:S(2)}) collective-permute-start(bf16[64,8,256]{2,1,0:T(8,128)(2,1)} %get-tuple-element.15), channel_id=1, source_target_pairs={{0,4},{4,0},{8,12},{12,8},{16,20},{20,16},{24,28},{28,24},{1,5},{5... | collective-permute-start | bytes 786440 | tf_op jit(solution)/shard_map/ppermute | solution.py:234
  24.6 1.5 %collective-permute-start.7 = (bf16[64,8,256]{2,1,0:T(8,128)(2,1)}, bf16[64,8,256]{2,1,0:T(8,128)(2,1)S(1)}, u32[]{:S(2)}, u32[]{:S(2)}) collective-permute-start(bf16[64,8,256]{2,1,0:T(8,128)(2,1)} %get-tuple-element.14), channel_id=1, source_target_pairs={{0,8},{4,12},{8,0},{12,4},{16,24},{20,28},{24,16},{28,20},{1,9},{5... | collective-permute-start | bytes 786440 | tf_op jit(solution)/shard_map/ppermute | solution.py:234
  26.1 0.1 dynamic-slice_convert_fusion
  26.2 0.1 reshape.76
  26.3 0.1 copy.16
  26.4 0.1 min.20
  26.5 0.1 min.21
  26.6 0.8 pad_maximum_fusion.1
  27.4 0.1 collective-permute-start.3
  27.5 1.6 %collective-permute-start.4 = (bf16[32,2048]{1,0:T(8,128)(2,1)S(1)}, bf16[32,2048]{1,0:T(8,128)(2,1)}, u32[]{:S(2)}, u32[]{:S(2)}) collective-permute-start(bf16[32,2048]{1,0:T(8,128)(2,1)S(1)} %get-tuple-element.21), channel_id=1, source_target_pairs={{0,2},{1,3},{2,0},{3,1},{4,6},{5,7},{6,4},{7,5},{8,10},{9,11},{10,... | collective-permute-start | bytes 393224 | tf_op jit(solution)/shard_map/ppermute | solution.py:234
  29.1 0.3 collective-permute-start.5
  29.4 0.8 convert_reduce_fusion
  30.2 0.1 min.23
  30.3 0.1 collective-permute-start.8
  30.4 0.1 pad_maximum_fusion.3.invn_ref
  30.4 3.6 %collective-permute-done.4 = bf16[32,2048]{1,0:T(8,128)(2,1)} collective-permute-done((bf16[32,2048]{1,0:T(8,128)(2,1)S(1)}, bf16[32,2048]{1,0:T(8,128)(2,1)}, u32[]{:S(2)}, u32[]{:S(2)}) %collective-permute-start.4) | collective-permute-done | bytes 131104 | tf_op jit(solution)/shard_map/ppermute | solution.py:234
  34.0 1.9 %collective-permute-done.5 = bf16[32,2048]{1,0:T(8,128)(2,1)} collective-permute-done((bf16[32,2048]{1,0:T(8,128)(2,1)S(1)}, bf16[32,2048]{1,0:T(8,128)(2,1)}, u32[]{:S(2)}, u32[]{:S(2)}) %collective-permute-start.5) | collective-permute-done | bytes 131104 | tf_op jit(solution)/shard_map/ppermute | solution.py:234
  35.9 1.0 pad_maximum_fusion.u_ref
  36.9 4.0 %collective-permute-done.7.rest_2_ = bf16[64,8,256]{2,1,0:T(8,128)(2,1)S(1)} collective-permute-done((bf16[64,8,256]{2,1,0:T(8,128)(2,1)}, bf16[64,8,256]{2,1,0:T(8,128)(2,1)S(1)}, u32[]{:S(2)}, u32[]{:S(2)}) %collective-permute-start.7) | collective-permute-done | bytes 262176 | tf_op jit(solution)/shard_map/ppermute | solution.py:234
  40.9 6.5 %collective-permute-done.8.rest_3_ = bf16[64,8,256]{2,1,0:T(8,128)(2,1)S(1)} collective-permute-done((bf16[64,8,256]{2,1,0:T(8,128)(2,1)S(1)}, bf16[64,8,256]{2,1,0:T(8,128)(2,1)S(1)}, u32[]{:S(2)}, u32[]{:S(2)}) %collective-permute-start.8) | collective-permute-done | bytes 262176 | tf_op jit(solution)/shard_map/ppermute | solution.py:234
  47.4 0.7 copy-done
  48.1 0.9 copy-done.1
  49.0 0.9 copy-done.2
  49.9 0.9 copy-done.3
  50.8 0.9 copy-done.4
  51.7 0.9 copy-done.5
  52.6 18.6 %shard_map.122 = (s16[8,64,1152]{2,1,0:T(8,128)(2,1)}, f32[4,32,2048]{2,1,0:T(8,128)S(1)}) custom-call(s32[1]{0:T(128)} %bitcast.c_ref, bf16[8,64,1024]{2,1,0:T(8,128)(2,1)S(1)} %all-to-all-done.v_ref, bf16[4,32,2048]{2,1,0:T(8,128)(2,1)S(1)} %pad_maximum_fusion.u_ref, f32[32,128]{1,0:T(8,128)S(1)} %pad_maximum_fusion.3.invn_ref, ...), custom_call_target="tpu_custom_call" | custom-call | tf_op jit(solution)/shard_map/pallas_call | solution.py:311
  71.3 3.9 %all-to-all-start.1 = ((s16[8,64,1152]{2,1,0:T(8,128)(2,1)}), s16[8,64,1152]{2,1,0:T(8,128)(2,1)S(1)}, u32[]{:S(2)}, u32[]{:S(2)}) async-start(s16[8,64,1152]{2,1,0:T(8,128)(2,1)} %get-tuple-element.9), calls=%async_computation.1 | async-start | bytes 2359296 | tf_op jit(solution)/shard_map/all_to_all | solution.py:327
  75.1 0.0 copy-start.13
  75.2 0.0 copy-start.7
  75.2 0.8 dynamic-slice_bitcast_fusion.2
  75.9 1.5 %collective-permute-start.10 = (f32[32,2048]{1,0:T(8,128)}, f32[32,2048]{1,0:T(8,128)S(1)}, u32[]{:S(2)}, u32[]{:S(2)}) collective-permute-start(f32[32,2048]{1,0:T(8,128)} %get-tuple-element.12), channel_id=1, source_target_pairs={{0,2},{1,3},{2,0},{3,1},{4,6},{5,7},{6,4},{7,5},{8,10},{9,11},{10,... | collective-permute-start | bytes 786440 | tf_op jit(solution)/shard_map/ppermute | solution.py:234
  77.4 0.6 collective-permute-start.9
  78.1 7.3 %collective-permute-done.10 = f32[32,2048]{1,0:T(8,128)S(1)} collective-permute-done((f32[32,2048]{1,0:T(8,128)}, f32[32,2048]{1,0:T(8,128)S(1)}, u32[]{:S(2)}, u32[]{:S(2)}) %collective-permute-start.10) | collective-permute-done | bytes 262176 | tf_op jit(solution)/shard_map/ppermute | solution.py:234
  85.4 2.1 %collective-permute-done.11 = f32[32,2048]{1,0:T(8,128)S(1)} collective-permute-done((f32[32,2048]{1,0:T(8,128)S(1)}, f32[32,2048]{1,0:T(8,128)S(1)}, u32[]{:S(2)}, u32[]{:S(2)}) %collective-permute-start.11) | collective-permute-done | bytes 262176 | tf_op jit(solution)/shard_map/ppermute | solution.py:234
  87.5 1.0 fusion.3
  88.5 1.7 %collective-permute-start.12 = (f32[8,2048]{1,0:T(8,128)S(1)}, f32[8,2048]{1,0:T(8,128)S(1)}, u32[]{:S(2)}, u32[]{:S(2)}) collective-permute-start(f32[8,2048]{1,0:T(8,128)S(1)} %get-tuple-element.17), channel_id=1, source_target_pairs={{0,4},{4,0},{8,12},{12,8},{16,20},{20,16},{24,28},{28,24},{1,5},{5... | collective-permute-start | bytes 196616 | tf_op jit(solution)/shard_map/ppermute | solution.py:234
  90.3 1.5 %collective-permute-start.13 = (f32[8,2048]{1,0:T(8,128)S(1)}, f32[8,2048]{1,0:T(8,128)S(1)}, u32[]{:S(2)}, u32[]{:S(2)}) collective-permute-start(f32[8,2048]{1,0:T(8,128)S(1)} %get-tuple-element.19), channel_id=1, source_target_pairs={{0,8},{4,12},{8,0},{12,4},{16,24},{20,28},{24,16},{28,20},{1,9},{5... | collective-permute-start | bytes 196616 | tf_op jit(solution)/shard_map/ppermute | solution.py:234
  91.7 0.3 collective-permute-start.14
  92.1 1.6 %collective-permute-done.12 = f32[8,2048]{1,0:T(8,128)S(1)} collective-permute-done((f32[8,2048]{1,0:T(8,128)S(1)}, f32[8,2048]{1,0:T(8,128)S(1)}, u32[]{:S(2)}, u32[]{:S(2)}) %collective-permute-start.12) | collective-permute-done | bytes 65568 | tf_op jit(solution)/shard_map/ppermute | solution.py:234
  93.7 1.6 %collective-permute-done.13 = f32[8,2048]{1,0:T(8,128)S(1)} collective-permute-done((f32[8,2048]{1,0:T(8,128)S(1)}, f32[8,2048]{1,0:T(8,128)S(1)}, u32[]{:S(2)}, u32[]{:S(2)}) %collective-permute-start.13) | collective-permute-done | bytes 65568 | tf_op jit(solution)/shard_map/ppermute | solution.py:234
  95.2 2.8 %collective-permute-done.14 = f32[8,2048]{1,0:T(8,128)S(1)} collective-permute-done((f32[8,2048]{1,0:T(8,128)S(1)}, f32[8,2048]{1,0:T(8,128)S(1)}, u32[]{:S(2)}, u32[]{:S(2)}) %collective-permute-start.14) | collective-permute-done | bytes 65568 | tf_op jit(solution)/shard_map/ppermute | solution.py:234
  98.1 0.7 compare_select_fusion.1
  98.8 4.1 %all-to-all-done.1.got_ref = s16[8,64,1152]{2,1,0:T(8,128)(2,1)S(1)} async-done(((s16[8,64,1152]{2,1,0:T(8,128)(2,1)}), s16[8,64,1152]{2,1,0:T(8,128)(2,1)S(1)}, u32[]{:S(2)}, u32[]{:S(2)}) %all-to-all-start.1) | async-done | bytes 1179680 | tf_op jit(solution)/shard_map/all_to_all | solution.py:327
  102.8 1.4 %shard_map.123 = f32[1024,256]{1,0:T(8,128)} custom-call(s16[8,64,1152]{2,1,0:T(8,128)(2,1)S(1)} %all-to-all-done.1.got_ref, s32[1,256]{1,0:T(1,128)S(1)} %bitcast.45), custom_call_target="tpu_custom_call" | custom-call | tf_op jit(solution)/shard_map/pallas_call | solution.py:328
  (38 shorter events, 0.2 us)
Async XLA Ops:
  0.6 6.8 %copy-start.10 = (s32[2048]{0:T(1024)}, s32[2048]{0:T(1024)S(1)}, u32[]{:S(2)}) copy-start(s32[2048]{0:T(1024)S(1)} %add_select_fusion) | copy-start | bytes 24580
  2.2 5.3 %copy-start.8 = (bf16[8,2048]{1,0:T(8,128)(2,1)}, bf16[8,2048]{1,0:T(8,128)(2,1)S(1)}, u32[]{:S(2)}) copy-start(bf16[8,2048]{1,0:T(8,128)(2,1)S(1)} %compare_select_fusion.2) | copy-start | bytes 98308
  2.9 23.7 %collective-permute-start = (bf16[8,2176]{1,0:T(8,128)(2,1)}, bf16[8,2176]{1,0:T(8,128)(2,1)}, u32[]{:S(2)}, u32[]{:S(2)}) collective-permute-start(bf16[8,2176]{1,0:T(8,128)(2,1)} %pad_maximum_fusion.2), channel_id=1, source_target_pairs={{0,4},{4,0},{8,12},{12,8},{16,20},{20,16},{24,28},{28,24},{1,5},{5... | collective-permute-start | bytes 104456 | tf_op jit(solution)/shard_map/ppermute | solution.py:234
  5.8 20.8 %collective-permute-start.1 = (bf16[8,2176]{1,0:T(8,128)(2,1)}, bf16[8,2176]{1,0:T(8,128)(2,1)}, u32[]{:S(2)}, u32[]{:S(2)}) collective-permute-start(bf16[8,2176]{1,0:T(8,128)(2,1)} %pad_maximum_fusion.2), channel_id=1, source_target_pairs={{0,8},{4,12},{8,0},{12,4},{16,24},{20,28},{24,16},{28,20},{1,9},{5... | collective-permute-start | bytes 104456 | tf_op jit(solution)/shard_map/ppermute | solution.py:234
  7.4 19.2 %collective-permute-start.2 = (bf16[8,2176]{1,0:T(8,128)(2,1)}, bf16[8,2176]{1,0:T(8,128)(2,1)}, u32[]{:S(2)}, u32[]{:S(2)}) collective-permute-start(bf16[8,2176]{1,0:T(8,128)(2,1)} %pad_maximum_fusion.2), channel_id=1, source_target_pairs={{0,12},{4,8},{8,4},{12,0},{16,28},{20,24},{24,20},{28,16},{1,13},{... | collective-permute-start | bytes 104456 | tf_op jit(solution)/shard_map/ppermute | solution.py:234
  9.5 7.3 %copy-start.12 = (s32[2,8,256]{2,1,0:T(8,128)S(1)}, s32[2,8,256]{2,1,0:T(8,128)}, u32[]{:S(2)}) copy-start(s32[2,8,256]{2,1,0:T(8,128)} %param.16) | copy-start | bytes 49156
  10.7 37.4 %all-to-all-start = ((bf16[8,64,1024]{2,1,0:T(8,128)(2,1)}), bf16[8,64,1024]{2,1,0:T(8,128)(2,1)S(1)}, u32[]{:S(2)}, u32[]{:S(2)}) async-start(bf16[8,64,1024]{2,1,0:T(8,128)(2,1)} %bitcast.3), calls=%async_computation | async-start | bytes 2097152 | tf_op jit(solution)/shard_map/all_to_all | solution.py:282
  16.9 2.9 %copy-start.14 = (s32[256]{0:T(256)S(1)}, s32[256]{0:T(256)}, u32[]{:S(2)}) copy-start(s32[256]{0:T(256)} %param.15) | copy-start | bytes 3076
  21.4 4.7 %copy-start.6 = (s32[256]{0:T(256)S(1)}, s32[256]{0:T(256)}, u32[]{:S(2)}) copy-start(s32[256]{0:T(256)} %param.14) | copy-start | bytes 3076
  21.7 4.9 %copy-start.9 = (bf16[8,2048]{1,0:T(8,128)(2,1)S(1)}, bf16[8,2048]{1,0:T(8,128)(2,1)}, u32[]{:S(2)}) copy-start(bf16[8,2048]{1,0:T(8,128)(2,1)} %copy-done.8) | copy-start | bytes 98308
  22.6 14.3 %collective-permute-start.6 = (bf16[64,8,256]{2,1,0:T(8,128)(2,1)}, bf16[64,8,256]{2,1,0:T(8,128)(2,1)S(1)}, u32[]{:S(2)}, u32[]{:S(2)}) collective-permute-start(bf16[64,8,256]{2,1,0:T(8,128)(2,1)} %get-tuple-element.15), channel_id=1, source_target_pairs={{0,4},{4,0},{8,12},{12,8},{16,20},{20,16},{24,28},{28,24},{1,5},{5... | collective-permute-start | bytes 786440 | tf_op jit(solution)/shard_map/ppermute | solution.py:234
  24.6 16.3 %collective-permute-start.7 = (bf16[64,8,256]{2,1,0:T(8,128)(2,1)}, bf16[64,8,256]{2,1,0:T(8,128)(2,1)S(1)}, u32[]{:S(2)}, u32[]{:S(2)}) collective-permute-start(bf16[64,8,256]{2,1,0:T(8,128)(2,1)} %get-tuple-element.14), channel_id=1, source_target_pairs={{0,8},{4,12},{8,0},{12,4},{16,24},{20,28},{24,16},{28,20},{1,9},{5... | collective-permute-start | bytes 786440 | tf_op jit(solution)/shard_map/ppermute | solution.py:234
  27.4 2.8 %collective-permute-start.3 = (bf16[32,2048]{1,0:T(8,128)(2,1)S(1)}, bf16[32,2048]{1,0:T(8,128)(2,1)S(1)}, u32[]{:S(2)}, u32[]{:S(2)}) collective-permute-start(bf16[32,2048]{1,0:T(8,128)(2,1)S(1)} %get-tuple-element.21), channel_id=1, source_target_pairs={{0,1},{1,0},{2,3},{3,2},{4,5},{5,4},{6,7},{7,6},{8,9},{9,8},{10,11... | collective-permute-start | bytes 393224 | tf_op jit(solution)/shard_map/ppermute | solution.py:234
  27.5 6.5 %collective-permute-start.4 = (bf16[32,2048]{1,0:T(8,128)(2,1)S(1)}, bf16[32,2048]{1,0:T(8,128)(2,1)}, u32[]{:S(2)}, u32[]{:S(2)}) collective-permute-start(bf16[32,2048]{1,0:T(8,128)(2,1)S(1)} %get-tuple-element.21), channel_id=1, source_target_pairs={{0,2},{1,3},{2,0},{3,1},{4,6},{5,7},{6,4},{7,5},{8,10},{9,11},{10,... | collective-permute-start | bytes 393224 | tf_op jit(solution)/shard_map/ppermute | solution.py:234
  29.1 6.8 %collective-permute-start.5 = (bf16[32,2048]{1,0:T(8,128)(2,1)S(1)}, bf16[32,2048]{1,0:T(8,128)(2,1)}, u32[]{:S(2)}, u32[]{:S(2)}) collective-permute-start(bf16[32,2048]{1,0:T(8,128)(2,1)S(1)} %get-tuple-element.21), channel_id=1, source_target_pairs={{0,3},{1,2},{2,1},{3,0},{4,7},{5,6},{6,5},{7,4},{8,11},{9,10},{10,... | collective-permute-start | bytes 393224 | tf_op jit(solution)/shard_map/ppermute | solution.py:234
  30.3 17.1 %collective-permute-start.8 = (bf16[64,8,256]{2,1,0:T(8,128)(2,1)S(1)}, bf16[64,8,256]{2,1,0:T(8,128)(2,1)S(1)}, u32[]{:S(2)}, u32[]{:S(2)}) collective-permute-start(bf16[64,8,256]{2,1,0:T(8,128)(2,1)S(1)} %get-tuple-element.13), channel_id=1, source_target_pairs={{0,12},{4,8},{8,4},{12,0},{16,28},{20,24},{24,20},{28,16},{1,13},{... | collective-permute-start | bytes 786440 | tf_op jit(solution)/shard_map/ppermute | solution.py:234
  47.4 0.7 copy-start
  48.1 1.0 copy-start.1
  49.0 0.9 copy-start.2
  49.9 0.9 copy-start.3
  50.8 0.9 copy-start.4
  51.7 0.9 copy-start.5
  71.3 31.6 %all-to-all-start.1 = ((s16[8,64,1152]{2,1,0:T(8,128)(2,1)}), s16[8,64,1152]{2,1,0:T(8,128)(2,1)S(1)}, u32[]{:S(2)}, u32[]{:S(2)}) async-start(s16[8,64,1152]{2,1,0:T(8,128)(2,1)} %get-tuple-element.9), calls=%async_computation.1 | async-start | bytes 2359296 | tf_op jit(solution)/shard_map/all_to_all | solution.py:327
  75.1 22.9 %copy-start.11 = (s32[2048]{0:T(1024)S(1)}, s32[2048]{0:T(1024)}, u32[]{:S(2)}) copy-start(s32[2048]{0:T(1024)} %copy-done.10) | copy-start | bytes 24580
  75.1 22.9 %copy-start.13 = (s32[8]{0:T(128)S(1)}, s32[8]{0:T(128)}, u32[]{:S(2)}) copy-start(s32[8]{0:T(128)} %param.13) | copy-start | bytes 100
  75.2 27.7 %copy-start.7 = (s32[256]{0:T(256)S(1)}, s32[256]{0:T(256)}, u32[]{:S(2)}) copy-start(s32[256]{0:T(256)} %param.14) | copy-start | bytes 3076
  75.9 9.4 %collective-permute-start.10 = (f32[32,2048]{1,0:T(8,128)}, f32[32,2048]{1,0:T(8,128)S(1)}, u32[]{:S(2)}, u32[]{:S(2)}) collective-permute-start(f32[32,2048]{1,0:T(8,128)} %get-tuple-element.12), channel_id=1, source_target_pairs={{0,2},{1,3},{2,0},{3,1},{4,6},{5,7},{6,4},{7,5},{8,10},{9,11},{10,... | collective-permute-start | bytes 786440 | tf_op jit(solution)/shard_map/ppermute | solution.py:234
  77.4 10.1 %collective-permute-start.11 = (f32[32,2048]{1,0:T(8,128)S(1)}, f32[32,2048]{1,0:T(8,128)S(1)}, u32[]{:S(2)}, u32[]{:S(2)}) collective-permute-start(f32[32,2048]{1,0:T(8,128)S(1)} %get-tuple-element.11), channel_id=1, source_target_pairs={{0,3},{1,2},{2,1},{3,0},{4,7},{5,6},{6,5},{7,4},{8,11},{9,10},{10,... | collective-permute-start | bytes 786440 | tf_op jit(solution)/shard_map/ppermute | solution.py:234
  77.4 10.1 %collective-permute-start.9 = (f32[32,2048]{1,0:T(8,128)S(1)}, f32[32,2048]{1,0:T(8,128)}, u32[]{:S(2)}, u32[]{:S(2)}) collective-permute-start(f32[32,2048]{1,0:T(8,128)S(1)} %get-tuple-element.10), channel_id=1, source_target_pairs={{0,1},{1,0},{2,3},{3,2},{4,5},{5,4},{6,7},{7,6},{8,9},{9,8},{10,11... | collective-permute-start | bytes 786440 | tf_op jit(solution)/shard_map/ppermute | solution.py:234
  88.5 5.1 %collective-permute-start.12 = (f32[8,2048]{1,0:T(8,128)S(1)}, f32[8,2048]{1,0:T(8,128)S(1)}, u32[]{:S(2)}, u32[]{:S(2)}) collective-permute-start(f32[8,2048]{1,0:T(8,128)S(1)} %get-tuple-element.17), channel_id=1, source_target_pairs={{0,4},{4,0},{8,12},{12,8},{16,20},{20,16},{24,28},{28,24},{1,5},{5... | collective-permute-start | bytes 196616 | tf_op jit(solution)/shard_map/ppermute | solution.py:234
  90.3 5.0 %collective-permute-start.13 = (f32[8,2048]{1,0:T(8,128)S(1)}, f32[8,2048]{1,0:T(8,128)S(1)}, u32[]{:S(2)}, u32[]{:S(2)}) collective-permute-start(f32[8,2048]{1,0:T(8,128)S(1)} %get-tuple-element.19), channel_id=1, source_target_pairs={{0,8},{4,12},{8,0},{12,4},{16,24},{20,28},{24,16},{28,20},{1,9},{5... | collective-permute-start | bytes 196616 | tf_op jit(solution)/shard_map/ppermute | solution.py:234
  91.7 6.3 %collective-permute-start.14 = (f32[8,2048]{1,0:T(8,128)S(1)}, f32[8,2048]{1,0:T(8,128)S(1)}, u32[]{:S(2)}, u32[]{:S(2)}) collective-permute-start(f32[8,2048]{1,0:T(8,128)S(1)} %get-tuple-element.18), channel_id=1, source_target_pairs={{0,12},{4,8},{8,4},{12,0},{16,28},{20,24},{24,20},{28,16},{1,13},{... | collective-permute-start | bytes 196616 | tf_op jit(solution)/shard_map/ppermute | solution.py:234

commit v2 on v1

--- a/solution.py
+++ b/solution.py
@@ -19,6 +19,8 @@
 LANES = 128
 FB = LANES // (2 * S)
 WIDTH = 8
+CHUNKS = 2
+MOST_SWAPS = 8
 FIXED = 32000.0
 
 
@@ -45,13 +47,86 @@
     return lax.dot_general(a, b, (((0,), (0,)), ((), ())), preferred_element_type=jnp.float32)
 
 
-def pair_kernel(
-    c_ref, v_ref, u_ref, invn_ref, eye_ref, ye_ref, yo_ref, ze_ref, zo_ref, *rest
-):
-    *e_refs, w_ref, r_ref, x_ref, urow_ref, code_ref = rest
+def prepare_kernel(spectra_ref, counts_ref, rspectra_ref, rcounts_ref, eye_ref, u_ref, *v_refs):
+    k_own, col_total = spectra_ref.shape
+    chunk_total = len(v_refs)
+    rcv_total, cols, _ = v_refs[0].shape
+    members = col_total // (cols * chunk_total)
+    width = min(k_own, 2 * LANES)
+    counts = counts_ref[...]
+    for begin in range(0, k_own, width):
+        seg_ids = lax.broadcasted_iota(jnp.int32, (width, col_total), 0) % S
+        part = spectra_ref[begin : begin + width, :].astype(jnp.float32)
+        part = jnp.where(seg_ids < counts, part, 0.0).astype(jnp.bfloat16)
+        turned = nt(eye_ref[...], part).astype(jnp.bfloat16)
+        for c in range(chunk_total):
+            for m in range(members):
+                first = (m * chunk_total + c) * cols
+                rows = turned[first : first + cols]
+                for dest in range(m, rcv_total, members):
+                    v_refs[c][dest, :, begin : begin + width] = rows
+    rows, quarter = rspectra_ref.shape
+    seg_ids = lax.broadcasted_iota(jnp.int32, (rows, quarter), 1) % S
+    part = rspectra_ref[...].astype(jnp.float32)
+    part = jnp.where(seg_ids < rcounts_ref[...], part, 0.0)
+    u_ref[:, :quarter] = part.astype(jnp.bfloat16)
+    u_ref[:, quarter:] = jnp.broadcast_to(rcounts_ref[...], (rows, LANES)).astype(
+        jnp.float32
+    ).astype(jnp.bfloat16)
+
+
+def fold_kernel(c_ref, observed_ref, window_ref, order_ref, *rest):
+    *out_refs, line_ref = rest
+    row_total, col_total, lag_total = observed_ref.shape
+    half = lag_total // 2
+    cols = out_refs[0].shape[0]
+    members = col_total // (cols * CHUNKS)
+    window = jnp.concatenate([window_ref[0], window_ref[1]], axis=0).astype(jnp.float32).T
+    station = lax.broadcasted_iota(jnp.int32, (col_total, col_total), 0) + c_ref[1]
+    pick = jnp.where(station == order_ref[...], 1.0, 0.0).astype(jnp.bfloat16)
+    lag_ids = lax.broadcasted_iota(jnp.int32, (col_total, half), 1).astype(jnp.float32)
+    lines = col_total * row_total
+    for i in range(row_total):
+        begin = window[:, i : i + 1]
+        end = begin + window[:, row_total + i : row_total + i + 1]
+        values = observed_ref[i].astype(jnp.float32)
+        low = (lag_ids >= begin) & (lag_ids < end)
+        high = (lag_ids + half >= begin) & (lag_ids + half < end)
+        folded = jnp.where(low, values[:, :half], jnp.where(high, -values[:, half:], 0.0))
+        moved = nn(pick, folded.astype(jnp.bfloat16))
+        for h in range(half // LANES):
+            line_ref[pl.ds(h * lines + i, col_total, stride=row_total), :] = moved[
+                :, h * LANES : (h + 1) * LANES
+            ]
+    mine = c_ref[0]
+    for c in range(CHUNKS):
+        for k in range(members):
+            first = ((mine ^ k) * CHUNKS + c) * (cols * row_total)
+            for h in range(half // LANES):
+                begin = pl.multiple_of(h * lines + first, cols * row_total)
+                rows = line_ref[pl.ds(begin, cols * row_total), :]
+                out_refs[c * members + k][:, :, h * LANES : (h + 1) * LANES] = rows.reshape(
+                    cols, row_total, LANES
+                ).astype(jnp.bfloat16)
+
+
+def pair_kernel(n_v, n_e, n_r, *refs):
+    refs = list(refs)
+
+    def take(n):
+        taken = refs[:n]
+        del refs[:n]
+        return taken
+
+    (c_ref, invn_ref, eye_ref, ye_ref, yo_ref, ze_ref, zo_ref) = take(7)
+    v_from, e_from, u_from = take(n_v), take(n_e), take(n_r)
+    r_from = take(n_r) if len(refs) > n_r + 8 else []
+    (w_ref,) = take(1)
+    r_to = take(n_r)
+    x_ref, urow_ref, code_ref, v_ref, e_ref, r_ref, sems = refs
+
     src_total, col_total, k_own = v_ref.shape
-    ref_total, irec, k_quarter = u_ref.shape
-    member_rows = irec // len(e_refs)
+    ref_total, irec, k_quarter = r_ref.shape
     jj_total = LANES // (2 * irec)
     jp_total = col_total // jj_total
     k_total = src_total * k_own
@@ -61,9 +136,28 @@
     own_blocks = k_own // LANES
     quarter_blocks = k_quarter // LANES
 
+    me = c_ref[2]
+    quarter_me = c_ref[3]
+    v_copies, u_copies, e_copies, r_copies = [], [], [], []
+
+    def fetch(copies, src, dst):
+        slot = sum(map(len, (v_copies, u_copies, e_copies, r_copies)))
+        copy = pltpu.make_async_copy(src, dst, sems.at[slot])
+        copy.start()
+        copies.append(copy)
+
+    for k, ref in enumerate(u_from):
+        begin = pl.multiple_of((quarter_me ^ k) * k_quarter, k_quarter)
+        fetch(u_copies, ref, urow_ref.at[0, :, pl.ds(begin, k_quarter)])
+    for k, ref in enumerate(v_from):
+        fetch(v_copies, ref, v_ref if n_v == 1 else v_ref.at[me ^ k])
+    for k, ref in enumerate(e_from):
+        fetch(e_copies, ref, e_ref.at[k])
+    for k, ref in enumerate(r_from):
+        fetch(r_copies, ref, r_ref.at[quarter_me ^ k])
+
     group_ids = lax.broadcasted_iota(jnp.int32, (jp_total, LANES), 1) // (2 * S)
     first_part = lax.broadcasted_iota(jnp.int32, (irec, LANES), 1) % (2 * S) < S
-    me = c_ref[0]
 
     def lanes_of(fb, per):
         return fb // per, pl.multiple_of(fb % per * LANES, LANES)
@@ -96,13 +190,11 @@
         return pl.ds((f % 2) * half_f + fb * (FB // 2) + f // 2, jp_total, stride=freq_total)
 
     def forward(fb, _):
-        quarter, off = lanes_of(fb, quarter_blocks)
-        part = u_ref[quarter ^ me, :, pl.ds(off, LANES)]
+        lanes = pl.ds(pl.multiple_of(fb * LANES, LANES), LANES)
+        part = urow_ref[0, :, lanes]
         wide = part.astype(jnp.float32)
         crossed = jnp.where(first_part, pltpu.roll(wide, LANES - S, 1), -pltpu.roll(wide, S, 1))
         crossed = crossed.astype(jnp.bfloat16)
-        lanes = pl.ds(pl.multiple_of(fb * LANES, LANES), LANES)
-        urow_ref[0, :, lanes] = part
         urow_ref[1, :, lanes] = crossed
         out = nt(v_block(fb), u_block([part, crossed]))
         scale = invn_ref[...]
@@ -110,6 +202,8 @@
             x_ref[place(fb, f), :] = out[f * jp_total : (f + 1) * jp_total] * scale
         return 0
 
+    for copy in u_copies + v_copies:
+        copy.wait()
     lax.fori_loop(0, blocks, forward, 0, unroll=16)
 
     lane_ids = lax.broadcasted_iota(jnp.int32, (1, LANES), 1)
@@ -125,9 +219,9 @@
             rhs_e.append(jnp.concatenate([x[:half_f], turned[:half_f]], axis=0))
             rhs_o.append(jnp.concatenate([x[half_f:], turned[half_f:]], axis=0))
             rows = [
-                ref[jj * jp_total + jp].astype(jnp.float32)
+                e_ref[k, jj * jp_total + jp].astype(jnp.float32)
                 for jj in range(jj_total)
-                for ref in e_refs
+                for k in range(n_e)
             ]
             obs.append(jnp.concatenate(rows * 2, axis=0))
         rhs_e = jnp.concatenate(rhs_e, axis=1).astype(jnp.bfloat16)
@@ -160,6 +254,8 @@
             x_ref[pl.ds(base + half_f, half_f), :] = z_o[:, lanes] * scale
         return 0
 
+    for copy in e_copies:
+        copy.wait()
     lax.fori_loop(0, jp_total // WIDTH, pairs, 0)
 
     def backward(fb, _):
@@ -194,10 +290,20 @@
             first_part, -pltpu.roll(sums[1], LANES - S, 1), pltpu.roll(sums[1], S, 1)
         )
         quarter, off = lanes_of(fb, quarter_blocks)
-        r_ref[quarter, :, pl.ds(off, LANES)] = sums[0] + crossed
+        lanes = pl.ds(off, LANES)
+        total = sums[0] + crossed
+        r_ref[quarter, :, lanes] = r_ref[quarter, :, lanes] + total if r_from else total
         return 0
 
+    for copy in r_copies:
+        copy.wait()
     lax.fori_loop(0, blocks, backward, 0, unroll=16)
+    outs = [
+        pltpu.make_async_copy(r_ref.at[quarter_me ^ k], ref, sems.at[k])
+        for k, ref in enumerate(r_to)
+    ]
+    for copy in outs:
+        copy.start()
 
     for src in range(src_total):
         codes = code_ref[src * own_blocks : (src + 1) * own_blocks, :]
@@ -205,27 +311,34 @@
             [codes, jnp.zeros((col_total - own_blocks, LANES), jnp.float32)], axis=0
         )
         w_ref[src, :, k_own:] = codes.astype(jnp.int32).astype(jnp.int16)
-
-
-def join_kernel(got_ref, count_ref, out_ref):
-    src_total, cols, width = got_ref.shape
+    for copy in outs:
+        copy.wait()
+
+
+def join_kernel(count_ref, *refs):
+    *got_refs, out_ref = refs
+    src_total, cols, _ = got_refs[0].shape
     k_own, col_total = out_ref.shape
-    members = col_total // cols
+    members = col_total // (cols * len(got_refs))
     seg_ids = lax.broadcasted_iota(jnp.int32, (LANES, col_total), 0) % S
     inside = seg_ids < count_ref[...]
-    scales = []
-    for src in range(src_total):
-        codes = got_ref[src, :16, k_own:].astype(jnp.int32).astype(jnp.float32)
-        scales.append(jnp.exp2(codes) * (1.0 / FIXED))
+    scales = [
+        [
+            jnp.exp2(ref[src, :16, k_own:].astype(jnp.int32).astype(jnp.float32)) * (1.0 / FIXED)
+            for src in range(src_total)
+        ]
+        for ref in got_refs
+    ]
     for b in range(k_own // LANES):
         rows = []
         for m in range(members):
-            total = None
-            for src in range(m, src_total, members):
-                part = got_ref[src, :, b * LANES : (b + 1) * LANES]
-                part = part.astype(jnp.int32).astype(jnp.float32) * scales[src][b : b + 1]
-                total = part if total is None else total + part
-            rows.append(total)
+            for ref, scale in zip(got_refs, scales):
+                total = None
+                for src in range(m, src_total, members):
+                    part = ref[src, :, b * LANES : (b + 1) * LANES]
+                    part = part.astype(jnp.int32).astype(jnp.float32) * scale[src][b : b + 1]
+                    total = part if total is None else total + part
+                rows.append(total)
         whole = jnp.concatenate(rows, axis=0).T
         out_ref[b * LANES : (b + 1) * LANES, :] = jnp.where(inside, whole, 0.0)
 
@@ -253,96 +366,119 @@
     half = lag_total // 2
     members = math.gcd(GROUP, rcv_total)
     irec = row_total * members
-    cols = col_total // members
+    cols = col_total // (members * CHUNKS)
     jj_total = LANES // (2 * irec)
     jp_total = cols // jj_total
     bf16 = jnp.bfloat16
-    mine = lax.axis_index("rcv") % members
+    place = lax.axis_index("rcv")
+    mine = place % members
     quarter = lax.axis_index("ref")
-
-    seg_quarter = jnp.arange(k_quarter, dtype=jnp.int32) % S
-    masked = jnp.where(
-        seg_quarter[None, :] < receiver_counts[:, None], receiver_spectra, jnp.zeros((), bf16)
+    vmem = pl.BlockSpec(memory_space=pltpu.VMEM)
+    smem = pl.BlockSpec(memory_space=pltpu.SMEM)
+    hbm = pl.BlockSpec(memory_space=pl.ANY)
+    scalars = jnp.stack([mine, quarter * col_total, place, quarter]).astype(jnp.int32)
+
+    def params(mib):
+        return pltpu.CompilerParams(vmem_limit_bytes=mib * 1024 * 1024)
+
+    def cost(us):
+        return pl.CostEstimate(flops=us * 10**9, bytes_accessed=0, transcendentals=0)
+
+    u_own, *sent = pl.pallas_call(
+        prepare_kernel,
+        out_shape=[jax.ShapeDtypeStruct((row_total, k_quarter + LANES), bf16)]
+        + [jax.ShapeDtypeStruct((rcv_total, cols, k_own), bf16)] * CHUNKS,
+        in_specs=[vmem] * 5,
+        out_specs=[vmem] * (1 + CHUNKS),
+        compiler_params=params(24),
+    )(
+        reference_spectra,
+        reference_counts.reshape(1, col_total),
+        receiver_spectra,
+        receiver_counts.reshape(row_total, 1),
+        jnp.eye(col_total, dtype=bf16),
     )
-    counts = jnp.broadcast_to(receiver_counts.astype(bf16)[:, None], (row_total, LANES))
-    own = jnp.concatenate([masked, counts], axis=1)
+
+    def spread(x):
+        if rcv_total > MOST_SWAPS:
+            return [lax.all_to_all(x, "rcv", split_axis=0, concat_axis=0, tiled=True)]
+        parts = [lax.dynamic_index_in_dim(x, place ^ k, 0, False) for k in range(rcv_total)]
+        return parts[:1] + [swap(parts[k], "rcv", rcv_total, k) for k in range(1, rcv_total)]
+
+    v_all = [spread(x) for x in sent]
+
     near = jnp.concatenate(
-        [own] + [swap(own, "rcv", rcv_total, k) for k in range(1, members)], axis=0
+        [u_own] + [swap(u_own, "rcv", rcv_total, k) for k in range(1, members)], axis=0
     )
     group_counts = near[:, k_quarter].astype(jnp.float32)
     near = near[:, :k_quarter]
-    u_all = jnp.stack([near] + [swap(near, "ref", ref_total, k) for k in range(1, ref_total)])
-
-    seg_own = jnp.arange(k_own, dtype=jnp.int32) % S
-    turned = reference_spectra.T
-    turned = jnp.where(seg_own[None, :] < reference_counts[:, None], turned, jnp.zeros((), bf16))
-    sent = jnp.broadcast_to(
-        turned.reshape(1, members, cols, k_own), (rcv_total // members, members, cols, k_own)
-    ).reshape(rcv_total, cols, k_own)
-    v_all = lax.all_to_all(sent, "rcv", split_axis=0, concat_axis=0, tiled=True)
-
-    _, observed, lag_window = lax.optimization_barrier((sent, observed, lag_window))
-    local_order = column_station - quarter * col_total
-    begin = lag_window[0][..., None]
-    end = begin + lag_window[1][..., None]
-    lag_ids = jnp.arange(half, dtype=jnp.int32)
-    low = (lag_ids >= begin) & (lag_ids < end)
-    high = (lag_ids + half >= begin) & (lag_ids + half < end)
-    folded = jnp.where(
-        low, observed[..., :half], jnp.where(high, -observed[..., half:], jnp.zeros((), bf16))
-    )
-    pick = (jnp.arange(col_total, dtype=jnp.int32)[:, None] == local_order[None, :]).astype(bf16)
-    folded = jnp.transpose(folded, (1, 0, 2)).reshape(col_total, row_total * half)
-    folded = jnp.dot(pick, folded, preferred_element_type=jnp.float32).astype(bf16)
-    folded = folded.reshape(members, cols, row_total, half)
-    share = [lax.dynamic_index_in_dim(folded, mine ^ k, 0, False) for k in range(members)]
-    e_all = share[:1] + [swap(share[k], "rcv", rcv_total, k) for k in range(1, members)]
-
-    own_counts = lax.dynamic_slice_in_dim(reference_counts, mine * cols, cols).astype(jnp.float32)
-    least = jnp.minimum(
-        own_counts.reshape(jj_total, jp_total).T[:, :, None], group_counts[None, None, :]
-    )
-    inverse = (1.0 / least).reshape(jp_total, jj_total * irec)
-    inverse = jnp.concatenate([inverse, inverse], axis=1)
+    u_all = [near] + [swap(near, "ref", ref_total, k) for k in range(1, ref_total)]
+
+    folded = pl.pallas_call(
+        fold_kernel,
+        out_shape=[jax.ShapeDtypeStruct((cols, row_total, half), bf16)] * (CHUNKS * members),
+        in_specs=[smem] + [vmem] * 3,
+        out_specs=[vmem] * (CHUNKS * members),
+        scratch_shapes=[pltpu.VMEM((half // LANES * col_total * row_total, LANES), jnp.float32)],
+        compiler_params=params(32),
+        cost_estimate=cost(4),
+    )(scalars, observed, lag_window, column_station.reshape(1, col_total))
+    e_all = [
+        [
+            x if k == 0 else swap(x, "rcv", rcv_total, k)
+            for k, x in enumerate(folded[c * members : (c + 1) * members])
+        ]
+        for c in range(CHUNKS)
+    ]
 
     tables = lag_tables(k_total // (2 * S), lag_total)
     eye = jnp.eye(half, dtype=bf16)
-    vmem = pl.BlockSpec(memory_space=pltpu.VMEM)
-    w_part, r_part = pl.pallas_call(
-        pair_kernel,
-        out_shape=(
-            jax.ShapeDtypeStruct((rcv_total, cols, k_own + LANES), jnp.int16),
-            jax.ShapeDtypeStruct((ref_total, irec, k_quarter), jnp.float32),
-        ),
-        in_specs=[pl.BlockSpec(memory_space=pltpu.SMEM)] + [vmem] * (8 + members),
-        out_specs=[vmem] * 2,
-        scratch_shapes=[
-            pltpu.VMEM((jp_total * k_total // (2 * S), LANES), jnp.float32),
-            pltpu.VMEM((2, irec, k_total), bf16),
-            pltpu.VMEM((k_total // LANES, LANES), jnp.float32),
-        ],
-        compiler_params=pltpu.CompilerParams(vmem_limit_bytes=48 * 1024 * 1024),
-    )(quarter.reshape(1).astype(jnp.int32), v_all, u_all, inverse, eye, *tables, *e_all)
-
-    got = lax.all_to_all(w_part, "rcv", split_axis=0, concat_axis=0, tiled=True)
+    own_counts = lax.dynamic_slice_in_dim(
+        reference_counts, mine * (cols * CHUNKS), cols * CHUNKS
+    ).astype(jnp.float32)
+    r_all, got = [], []
+    for c in range(CHUNKS):
+        counts = own_counts[c * cols : (c + 1) * cols].reshape(jj_total, jp_total).T
+        least = jnp.minimum(counts[:, :, None], group_counts[None, None, :])
+        inverse = (1.0 / least).reshape(jp_total, jj_total * irec)
+        inverse = jnp.concatenate([inverse, inverse], axis=1)
+        operands = v_all[c] + e_all[c] + u_all + r_all
+        w_part, *r_all = pl.pallas_call(
+            functools.partial(pair_kernel, len(v_all[c]), members, ref_total),
+            out_shape=[jax.ShapeDtypeStruct((rcv_total, cols, k_own + LANES), jnp.int16)]
+            + [jax.ShapeDtypeStruct((irec, k_quarter), jnp.float32)] * ref_total,
+            in_specs=[smem] + [vmem] * 6 + [hbm] * len(operands),
+            out_specs=[vmem] + [hbm] * ref_total,
+            scratch_shapes=[
+                pltpu.VMEM((jp_total * k_total // (2 * S), LANES), jnp.float32),
+                pltpu.VMEM((2, irec, k_total), bf16),
+                pltpu.VMEM((k_total // LANES, LANES), jnp.float32),
+                pltpu.VMEM((rcv_total, cols, k_own), bf16),
+                pltpu.VMEM((members, cols, row_total, half), bf16),
+                pltpu.VMEM((ref_total, irec, k_quarter), jnp.float32),
+                pltpu.SemaphoreType.DMA((len(operands),)),
+            ],
+            compiler_params=params(48),
+            cost_estimate=cost(10),
+        )(scalars, inverse, eye, *tables, *operands)
+        got.append(lax.all_to_all(w_part, "rcv", split_axis=0, concat_axis=0, tiled=True))
+
     reference_grad = pl.pallas_call(
         join_kernel,
         out_shape=jax.ShapeDtypeStruct((k_own, col_total), jnp.float32),
-        in_specs=[vmem] * 2,
+        in_specs=[vmem] * (1 + CHUNKS),
         out_specs=vmem,
-        compiler_params=pltpu.CompilerParams(vmem_limit_bytes=32 * 1024 * 1024),
-    )(got, reference_counts.reshape(1, col_total))
-
-    parts = [
-        lax.dynamic_index_in_dim(r_part, quarter ^ k, 0, False) for k in range(ref_total)
-    ]
-    r_sum = parts[0]
+        compiler_params=params(32),
+    )(reference_counts.reshape(1, col_total), *got)
+
+    r_sum = r_all[0]
     for k in range(1, ref_total):
-        r_sum = r_sum + swap(parts[k], "ref", ref_total, k)
+        r_sum = r_sum + swap(r_all[k], "ref", ref_total, k)
     parts = [r_sum[k * row_total : (k + 1) * row_total] for k in range(members)]
     r_sum = parts[0]
     for k in range(1, members):
         r_sum = r_sum + swap(parts[k], "rcv", rcv_total, k)
+    seg_quarter = jnp.arange(k_quarter, dtype=jnp.int32) % S
     receiver_grad = jnp.where(seg_quarter[None, :] < receiver_counts[:, None], r_sum, 0.0)
     return (receiver_grad, reference_grad)
 

time: 105 us -> 130 us (1.24)
  starting transfers between devices: 25.8 us -> 50.9 us
  Pallas kernels: 20 us -> 37.1 us
  other arithmetic: 8.59 us -> 1.88 us
  waiting for transfers between devices: 35.3 us -> 29.7 us
  local copies, waits for them, and re-layouts: 13 us -> 9.37 us
    ppermute x15 -> x32, starting transfers between devices: 15.7 us -> 43.7 us  [swap(): return lax.ppermute(x, axis, [(r, r ^ k) for r in range(total)])]
    pallas_call x1 -> x4, Pallas kernels: 18.6 us -> 35.7 us  [the longest x2 33.2 us: shards(): pl.pallas_call(functools.partial(pair_kernel, len(v_all[c]), members, ref...]
    ppermute x15 -> x32, waiting for transfers between devices: 31.3 us -> 15.1 us  [swap(): return lax.ppermute(x, axis, [(r, r ^ k) for r in range(total)])]
    all_to_all x2, waiting for transfers between devices: 4.05 us -> 14.7 us  [shards(): lax.all_to_all(w_part, 'rcv', split_axis=0, concat_axis=0, tiled=True)]
    all_to_all x2, starting transfers between devices: 10.1 us -> 7.19 us  [shards(): lax.all_to_all(w_part, 'rcv', split_axis=0, concat_axis=0, tiled=True)]
    optimization_barrier x1 -> x0, local copies, waits for them, and re-layouts: 2.86 us -> none  [shards(): lax.optimization_barrier((sent, observed, lag_window))]
    select_n x4 -> x0, other arithmetic: 2.76 us -> none  [the longest x1 1.06 us: shards(): jnp.where(low, observed[..., :half], jnp.where(high, -observed[..., half:...]
    concatenate x2 -> x0, other arithmetic: 1.43 us -> none  [the longest x1 0.81 us: shards(): jnp.concatenate([own] + [swap(own, 'rcv', rcv_total, k) for k in range(1,...]
  transfers between devices with their start and end apart: 17 -> 34, of which waited for: 10 -> 8; matrix products, arithmetic and copies ran while one was open for 14% -> 4% of each run, Pallas kernels for 0% -> 14%
where the time goes in v2:
time: 130 us
  starting transfers between devices  50.9 us (39%)
  Pallas kernels  37.1 us (29%)
  waiting for transfers between devices  29.7 us (23%)
  local copies, waits for them, and re-layouts  9.37 us (7%)
  other arithmetic  1.88 us (1%)
    ppermute x32, starting transfers between devices, swap(): return lax.ppermute(x, axis, [(r, r ^ k) for r in range(total)])  43.7 us
    pallas_call x2, Pallas kernels, shards(): pl.pallas_call(functools.partial(pair_kernel, len(v_all[c]), members, ref...  33.2 us
    ppermute x32, waiting for transfers between devices, swap(): return lax.ppermute(x, axis, [(r, r ^ k) for r in range(total)])  15.1 us
    all_to_all x2, waiting for transfers between devices, shards(): lax.all_to_all(w_part, 'rcv', split_axis=0, concat_axis=0, tiled=True)  14.7 us
    all_to_all x2, starting transfers between devices, shards(): lax.all_to_all(w_part, 'rcv', split_axis=0, concat_axis=0, tiled=True)  7.19 us
    unnamed x27, local copies, waits for them, and re-layouts  7.04 us
  transfers between devices with their start and end apart: 34, of which 8 were waited for; matrix products, arithmetic and copies ran while one was open for 4% of the time, Pallas kernels for 14%

profile of v2, /device:TPU:0, one launch (start us, length us, event | category | flops | bytes accessed | tf_op | source)
XLA Modules:
  0.0 129.8 jit_solution(373348118671660894)
XLA Ops:
  0.7 0.7 copy.17.rcounts_ref
  1.4 1.0 copy-done
  2.4 0.8 copy-done.1
  3.2 0.7 copy-done.2
  3.9 0.3 shard_map.122
  4.2 3.0 %collective-permute-start = (bf16[8,2176]{1,0:T(8,128)(2,1)S(1)}, bf16[8,2176]{1,0:T(8,128)(2,1)}, u32[]{:S(2)}, u32[]{:S(2)}) collective-permute-start(bf16[8,2176]{1,0:T(8,128)(2,1)S(1)} %get-tuple-element.23), channel_id=1, source_target_pairs={{0,4},{4,0},{8,12},{12,8},{16,20},{20,16},{24,28},{28,24},{1,5},{5... | collective-permute-start | bytes 104456 | tf_op jit(solution)/shard_map/ppermute | solution.py:347
  7.2 1.6 %collective-permute-start.1 = (bf16[8,2176]{1,0:T(8,128)(2,1)S(1)}, bf16[8,2176]{1,0:T(8,128)(2,1)}, u32[]{:S(2)}, u32[]{:S(2)}) collective-permute-start(bf16[8,2176]{1,0:T(8,128)(2,1)S(1)} %get-tuple-element.23), channel_id=1, source_target_pairs={{0,8},{4,12},{8,0},{12,4},{16,24},{20,28},{24,16},{28,20},{1,9},{5... | collective-permute-start | bytes 104456 | tf_op jit(solution)/shard_map/ppermute | solution.py:347
  8.9 2.0 %collective-permute-start.16 = (bf16[32,1024]{1,0:T(8,128)(2,1)S(1)}, bf16[32,1024]{1,0:T(8,128)(2,1)S(1)}, u32[]{:S(2)}, u32[]{:S(2)}) collective-permute-start(bf16[32,1024]{1,0:T(8,128)(2,1)S(1)} %get-tuple-element.50), channel_id=1, source_target_pairs={{0,4},{4,0},{8,12},{12,8},{16,20},{20,16},{24,28},{28,24},{1,5},{5... | collective-permute-start | bytes 196616 | tf_op jit(solution)/shard_map/ppermute | solution.py:347
  10.8 1.6 %collective-permute-start.17 = (bf16[32,1024]{1,0:T(8,128)(2,1)S(1)}, bf16[32,1024]{1,0:T(8,128)(2,1)S(1)}, u32[]{:S(2)}, u32[]{:S(2)}) collective-permute-start(bf16[32,1024]{1,0:T(8,128)(2,1)S(1)} %get-tuple-element.49), channel_id=1, source_target_pairs={{0,8},{4,12},{8,0},{12,4},{16,24},{20,28},{24,16},{28,20},{1,9},{5... | collective-permute-start | bytes 196616 | tf_op jit(solution)/shard_map/ppermute | solution.py:347
  12.4 0.8 dynamic-slice_convert_fusion
  13.2 0.1 fusion.8
  13.2 0.1 pad_add_fusion.c_ref.refs_0_
  13.3 1.6 %copy-done.4 = bf16[8,256,512]{2,1,0:T(8,128)(2,1)S(1)} copy-done((bf16[8,256,512]{2,1,0:T(8,128)(2,1)S(1)}, bf16[8,256,512]{2,1,0:T(8,128)(2,1)}, u32[]{:S(2)}) %copy-start.4) | copy-done | bytes 2097176
  14.9 0.7 copy-done.5
  15.6 0.7 copy-done.6
  16.3 2.2 %shard_map.123 = (bf16[32,8,256]{2,1,0:T(8,128)(2,1)S(1)}, bf16[32,8,256]{2,1,0:T(8,128)(2,1)S(1)}, bf16[32,8,256]{2,1,0:T(8,128)(2,1)S(1)}, bf16[32,8,256]{2,1,...) custom-call(s32[4]{0:T(128)S(1)} %pad_add_fusion.c_ref.refs_0_, ...), custom_call_target="tpu_custom_call" | custom-call | flops 4000000000 | tf_op jit(solution)/shard_map/pallas_call | solution.py:417
  18.5 0.7 dynamic-slice_bitcast_fusion.8
  19.2 0.1 slice.45
  19.3 0.1 copy.16
  19.4 0.1 min.34
  19.4 0.1 min.35
  19.5 0.1 slice.49
  19.6 0.1 copy.18
  19.7 0.1 min.40
  19.8 0.1 min.41
  19.9 0.8 constant_dynamic-update-slice_fusion.2
  20.7 3.0 %collective-permute-start.19 = (bf16[32,1024]{1,0:T(8,128)(2,1)S(1)}, bf16[32,1024]{1,0:T(8,128)(2,1)S(1)}, u32[]{:S(2)}, u32[]{:S(2)}) collective-permute-start(bf16[32,1024]{1,0:T(8,128)(2,1)S(1)} %get-tuple-element.47), channel_id=1, source_target_pairs={{0,16},{4,20},{8,24},{12,28},{16,0},{20,4},{24,8},{28,12},{1,17},{... | collective-permute-start | bytes 196616 | tf_op jit(solution)/shard_map/ppermute | solution.py:347
  23.6 0.8 constant_dynamic-update-slice_fusion.1
  24.4 1.3 collective-permute-start.20
  25.7 3.7 %collective-permute-start.21 = (bf16[32,1024]{1,0:T(8,128)(2,1)S(1)}, bf16[32,1024]{1,0:T(8,128)(2,1)S(1)}, u32[]{:S(2)}, u32[]{:S(2)}) collective-permute-start(bf16[32,1024]{1,0:T(8,128)(2,1)S(1)} %get-tuple-element.45), channel_id=1, source_target_pairs={{0,24},{4,28},{8,16},{12,20},{16,8},{20,12},{24,0},{28,4},{1,25},{... | collective-permute-start | bytes 196616 | tf_op jit(solution)/shard_map/ppermute | solution.py:347
  29.4 1.7 %collective-permute-start.3 = (bf16[32,1024]{1,0:T(8,128)(2,1)}, bf16[32,1024]{1,0:T(8,128)(2,1)S(1)}, u32[]{:S(2)}, u32[]{:S(2)}) collective-permute-start(bf16[32,1024]{1,0:T(8,128)(2,1)} %get-tuple-element.58), channel_id=1, source_target_pairs={{0,4},{4,0},{8,12},{12,8},{16,20},{20,16},{24,28},{28,24},{1,5},{5... | collective-permute-start | bytes 196616 | tf_op jit(solution)/shard_map/ppermute | solution.py:347
  31.1 0.1 convert_reduce_fusion
  31.2 0.1 min.37
  31.3 0.4 collective-permute-start.23
  31.7 1.7 %collective-permute-done.20.refs_12_ = bf16[32,1024]{1,0:T(8,128)(2,1)S(1)} collective-permute-done((bf16[32,1024]{1,0:T(8,128)(2,1)S(1)}, bf16[32,1024]{1,0:T(8,128)(2,1)S(1)}, u32[]{:S(2)}, u32[]{:S(2)}) %collective-permute-start.20) | collective-permute-done | bytes 65568 | tf_op jit(solution)/shard_map/ppermute | solution.py:347
  33.4 3.0 %collective-permute-start.5 = (bf16[32,1024]{1,0:T(8,128)(2,1)S(1)}, bf16[32,1024]{1,0:T(8,128)(2,1)S(1)}, u32[]{:S(2)}, u32[]{:S(2)}) collective-permute-start(bf16[32,1024]{1,0:T(8,128)(2,1)S(1)} %get-tuple-element.56), channel_id=1, source_target_pairs={{0,12},{4,8},{8,4},{12,0},{16,28},{20,24},{24,20},{28,16},{1,13},{... | collective-permute-start | bytes 196616 | tf_op jit(solution)/shard_map/ppermute | solution.py:347
  36.3 0.7 collective-permute-done.22.refs_14_
  37.0 0.9 collective-permute-start.6
  37.9 1.6 %collective-permute-start.7 = (bf16[32,1024]{1,0:T(8,128)(2,1)S(1)}, bf16[32,1024]{1,0:T(8,128)(2,1)S(1)}, u32[]{:S(2)}, u32[]{:S(2)}) collective-permute-start(bf16[32,1024]{1,0:T(8,128)(2,1)S(1)} %get-tuple-element.54), channel_id=1, source_target_pairs={{0,20},{4,16},{8,28},{12,24},{16,4},{20,0},{24,12},{28,8},{1,21},{... | collective-permute-start | bytes 196616 | tf_op jit(solution)/shard_map/ppermute | solution.py:347
  39.6 1.2 collective-permute-start.24
  40.7 2.2 %collective-permute-start.25 = (bf16[32,8,256]{2,1,0:T(8,128)(2,1)S(1)}, bf16[32,8,256]{2,1,0:T(8,128)(2,1)S(1)}, u32[]{:S(2)}, u32[]{:S(2)}) collective-permute-start(bf16[32,8,256]{2,1,0:T(8,128)(2,1)S(1)} %get-tuple-element.33), channel_id=1, source_target_pairs={{0,12},{4,8},{8,4},{12,0},{16,28},{20,24},{24,20},{28,16},{1,13},{... | collective-permute-start | bytes 393224 | tf_op jit(solution)/shard_map/ppermute | solution.py:347
  43.0 1.7 %collective-permute-done.7.refs_12_ = bf16[32,1024]{1,0:T(8,128)(2,1)S(1)} collective-permute-done((bf16[32,1024]{1,0:T(8,128)(2,1)S(1)}, bf16[32,1024]{1,0:T(8,128)(2,1)S(1)}, u32[]{:S(2)}, u32[]{:S(2)}) %collective-permute-start.7) | collective-permute-done | bytes 65568 | tf_op jit(solution)/shard_map/ppermute | solution.py:347
  44.7 1.5 %collective-permute-start.14 = (bf16[32,2048]{1,0:T(8,128)(2,1)S(1)}, bf16[32,2048]{1,0:T(8,128)(2,1)S(1)}, u32[]{:S(2)}, u32[]{:S(2)}) collective-permute-start(bf16[32,2048]{1,0:T(8,128)(2,1)S(1)} %slice.55.refs_19_), channel_id=1, source_target_pairs={{0,2},{1,3},{2,0},{3,1},{4,6},{5,7},{6,4},{7,5},{8,10},{9,11},{10,... | collective-permute-start | bytes 393224 | tf_op jit(solution)/shard_map/ppermute | solution.py:347
  46.2 0.1 pad_maximum_fusion.1.refs_1_
  46.3 0.1 pad_maximum_fusion.refs_1_
  46.4 2.0 %collective-permute-start.8 = (bf16[32,1024]{1,0:T(8,128)(2,1)S(1)}, bf16[32,1024]{1,0:T(8,128)(2,1)S(1)}, u32[]{:S(2)}, u32[]{:S(2)}) collective-permute-start(bf16[32,1024]{1,0:T(8,128)(2,1)S(1)} %get-tuple-element.53), channel_id=1, source_target_pairs={{0,24},{4,28},{8,16},{12,20},{16,8},{20,12},{24,0},{28,4},{1,25},{... | collective-permute-start | bytes 196616 | tf_op jit(solution)/shard_map/ppermute | solution.py:347
  48.3 4.1 %collective-permute-start.9 = (bf16[32,1024]{1,0:T(8,128)(2,1)S(1)}, bf16[32,1024]{1,0:T(8,128)(2,1)S(1)}, u32[]{:S(2)}, u32[]{:S(2)}) collective-permute-start(bf16[32,1024]{1,0:T(8,128)(2,1)S(1)} %get-tuple-element.52), channel_id=1, source_target_pairs={{0,28},{4,24},{8,20},{12,16},{16,12},{20,8},{24,4},{28,0},{1,29},{... | collective-permute-start | bytes 196616 | tf_op jit(solution)/shard_map/ppermute | solution.py:347
  52.5 3.4 %collective-permute-start.12 = (bf16[32,8,256]{2,1,0:T(8,128)(2,1)S(1)}, bf16[32,8,256]{2,1,0:T(8,128)(2,1)S(1)}, u32[]{:S(2)}, u32[]{:S(2)}) collective-permute-start(bf16[32,8,256]{2,1,0:T(8,128)(2,1)S(1)} %get-tuple-element.28), channel_id=1, source_target_pairs={{0,12},{4,8},{8,4},{12,0},{16,28},{20,24},{24,20},{28,16},{1,13},{... | collective-permute-start | bytes 393224 | tf_op jit(solution)/shard_map/ppermute | solution.py:347
  56.0 16.5 %shard_map.124 = (s16[8,32,1152]{2,1,0:T(8,128)(2,1)}, f32[32,2048]{1,0:T(8,128)S(1)}, f32[32,2048]{1,0:T(8,128)S(1)}, f32[32,2048]{1,0:T(8,128)S(1)}, f32[32,2048]{1,0:T(8,128)S(1)}) custom-call(s32[4]{0:T(128)S(1)} %pad_add_fusion.c_ref.refs_0_, f32[16,128]{1,0:T(8,128)S(1)} %pad_maximum_fusion.1.refs_1_, bf16[256,256]{1,0:T(8,128)(2,1)S(1)} %fusion.eye_ref.refs_2_, ...), custom_call_target="tpu_custom_call" | custom-call | flops 10000000000 | tf_op jit(solution)/shard_map/pallas_call | solution.py:446
  72.5 16.7 %shard_map.125 = (s16[8,32,1152]{2,1,0:T(8,128)(2,1)}, f32[32,2048]{1,0:T(8,128)S(1)}, f32[32,2048]{1,0:T(8,128)S(1)}, f32[32,2048]{1,0:T(8,128)S(1)}, f32[32,2048]{1,0:T(8,128)S(1)}) custom-call(s32[4]{0:T(128)S(1)} %pad_add_fusion.c_ref.refs_0_, f32[16,128]{1,0:T(8,128)S(1)} %pad_maximum_fusion.refs_1_, bf16[256,256]{1,0:T(8,128)(2,1)S(1)} %fusion.eye_ref.refs_2_, ...), custom_call_target="tpu_custom_call" | custom-call | flops 10000000000 | tf_op jit(solution)/shard_map/pallas_call | solution.py:446
  89.3 3.5 %all-to-all-start.1 = ((s16[8,32,1152]{2,1,0:T(8,128)(2,1)}), s16[8,32,1152]{2,1,0:T(8,128)(2,1)S(1)}, u32[]{:S(2)}, u32[]{:S(2)}) async-start(s16[8,32,1152]{2,1,0:T(8,128)(2,1)} %get-tuple-element.43), calls=%async_computation.1 | async-start | bytes 1179648 | tf_op jit(solution)/shard_map/all_to_all | solution.py:464
  92.9 1.5 %collective-permute-start.27 = (f32[32,2048]{1,0:T(8,128)S(1)}, f32[32,2048]{1,0:T(8,128)S(1)}, u32[]{:S(2)}, u32[]{:S(2)}) collective-permute-start(f32[32,2048]{1,0:T(8,128)S(1)} %get-tuple-element.40), channel_id=1, source_target_pairs={{0,2},{1,3},{2,0},{3,1},{4,6},{5,7},{6,4},{7,5},{8,10},{9,11},{10,... | collective-permute-start | bytes 786440 | tf_op jit(solution)/shard_map/ppermute | solution.py:347
  94.4 0.3 collective-permute-start.28
  94.8 14.0 %all-to-all-done.1.refs_1_ = s16[8,32,1152]{2,1,0:T(8,128)(2,1)S(1)} async-done(((s16[8,32,1152]{2,1,0:T(8,128)(2,1)}), s16[8,32,1152]{2,1,0:T(8,128)(2,1)S(1)}, u32[]{:S(2)}, u32[]{:S(2)}) %all-to-all-start.1) | async-done | bytes 589856 | tf_op jit(solution)/shard_map/all_to_all | solution.py:464
  108.7 3.6 %all-to-all-start = ((s16[8,32,1152]{2,1,0:T(8,128)(2,1)}), s16[8,32,1152]{2,1,0:T(8,128)(2,1)S(1)}, u32[]{:S(2)}, u32[]{:S(2)}) async-start(s16[8,32,1152]{2,1,0:T(8,128)(2,1)} %get-tuple-element.42), calls=%async_computation | async-start | bytes 1179648 | tf_op jit(solution)/shard_map/all_to_all | solution.py:464
  112.5 2.1 %collective-permute-start.29 = (f32[8,2048]{1,0:T(8,128)S(1)}, f32[8,2048]{1,0:T(8,128)S(1)}, u32[]{:S(2)}, u32[]{:S(2)}) collective-permute-start(f32[8,2048]{1,0:T(8,128)S(1)} %get-tuple-element.60), channel_id=1, source_target_pairs={{0,4},{4,0},{8,12},{12,8},{16,20},{20,16},{24,28},{28,24},{1,5},{5... | collective-permute-start | bytes 196616 | tf_op jit(solution)/shard_map/ppermute | solution.py:347
  114.6 1.5 %collective-permute-start.30 = (f32[8,2048]{1,0:T(8,128)S(1)}, f32[8,2048]{1,0:T(8,128)S(1)}, u32[]{:S(2)}, u32[]{:S(2)}) collective-permute-start(f32[8,2048]{1,0:T(8,128)S(1)} %get-tuple-element.62), channel_id=1, source_target_pairs={{0,8},{4,12},{8,0},{12,4},{16,24},{20,28},{24,16},{28,20},{1,9},{5... | collective-permute-start | bytes 196616 | tf_op jit(solution)/shard_map/ppermute | solution.py:347
  116.0 0.1 collective-permute-start.31
  116.1 3.7 %collective-permute-done.29 = f32[8,2048]{1,0:T(8,128)S(1)} collective-permute-done((f32[8,2048]{1,0:T(8,128)S(1)}, f32[8,2048]{1,0:T(8,128)S(1)}, u32[]{:S(2)}, u32[]{:S(2)}) %collective-permute-start.29) | collective-permute-done | bytes 65568 | tf_op jit(solution)/shard_map/ppermute | solution.py:347
  119.8 4.6 %collective-permute-done.30 = f32[8,2048]{1,0:T(8,128)S(1)} collective-permute-done((f32[8,2048]{1,0:T(8,128)S(1)}, f32[8,2048]{1,0:T(8,128)S(1)}, u32[]{:S(2)}, u32[]{:S(2)}) %collective-permute-start.30) | collective-permute-done | bytes 65568 | tf_op jit(solution)/shard_map/ppermute | solution.py:347
  124.4 2.6 %collective-permute-done.31 = f32[8,2048]{1,0:T(8,128)S(1)} collective-permute-done((f32[8,2048]{1,0:T(8,128)S(1)}, f32[8,2048]{1,0:T(8,128)S(1)}, u32[]{:S(2)}, u32[]{:S(2)}) %collective-permute-start.31) | collective-permute-done | bytes 65568 | tf_op jit(solution)/shard_map/ppermute | solution.py:347
  127.1 0.7 fusion.3
  127.8 0.7 all-to-all-done.refs_0_
  128.4 1.4 %shard_map.126 = f32[1024,256]{1,0:T(8,128)} custom-call(s32[1,256]{1,0:T(1,128)S(1)} %bitcast.42, s16[8,32,1152]{2,1,0:T(8,128)(2,1)S(1)} %all-to-all-done.refs_0_, s16[8,32,1152]{2,1,0:T(8,128)(2,1)S(1)} %all-to-all-done.1.refs_1_), custom_call_target="tpu_custom_call" | custom-call | tf_op jit(solution)/shard_map/pallas_call | solution.py:466
  (63 shorter events, 0.5 us)
Async XLA Ops:
  1.4 1.0 copy-start
  2.4 0.8 copy-start.1
  3.2 0.7 copy-start.2
  4.2 15.6 %collective-permute-start = (bf16[8,2176]{1,0:T(8,128)(2,1)S(1)}, bf16[8,2176]{1,0:T(8,128)(2,1)}, u32[]{:S(2)}, u32[]{:S(2)}) collective-permute-start(bf16[8,2176]{1,0:T(8,128)(2,1)S(1)} %get-tuple-element.23), channel_id=1, source_target_pairs={{0,4},{4,0},{8,12},{12,8},{16,20},{20,16},{24,28},{28,24},{1,5},{5... | collective-permute-start | bytes 104456 | tf_op jit(solution)/shard_map/ppermute | solution.py:347
  7.2 13.4 %collective-permute-start.1 = (bf16[8,2176]{1,0:T(8,128)(2,1)S(1)}, bf16[8,2176]{1,0:T(8,128)(2,1)}, u32[]{:S(2)}, u32[]{:S(2)}) collective-permute-start(bf16[8,2176]{1,0:T(8,128)(2,1)S(1)} %get-tuple-element.23), channel_id=1, source_target_pairs={{0,8},{4,12},{8,0},{12,4},{16,24},{20,28},{24,16},{28,20},{1,9},{5... | collective-permute-start | bytes 104456 | tf_op jit(solution)/shard_map/ppermute | solution.py:347
  8.8 15.6 %collective-permute-start.2 = (bf16[8,2176]{1,0:T(8,128)(2,1)S(1)}, bf16[8,2176]{1,0:T(8,128)(2,1)S(1)}, u32[]{:S(2)}, u32[]{:S(2)}) collective-permute-start(bf16[8,2176]{1,0:T(8,128)(2,1)S(1)} %get-tuple-element.23), channel_id=1, source_target_pairs={{0,12},{4,8},{8,4},{12,0},{16,28},{20,24},{24,20},{28,16},{1,13},{... | collective-permute-start | bytes 104456 | tf_op jit(solution)/shard_map/ppermute | solution.py:347
  8.9 16.9 %collective-permute-start.16 = (bf16[32,1024]{1,0:T(8,128)(2,1)S(1)}, bf16[32,1024]{1,0:T(8,128)(2,1)S(1)}, u32[]{:S(2)}, u32[]{:S(2)}) collective-permute-start(bf16[32,1024]{1,0:T(8,128)(2,1)S(1)} %get-tuple-element.50), channel_id=1, source_target_pairs={{0,4},{4,0},{8,12},{12,8},{16,20},{20,16},{24,28},{28,24},{1,5},{5... | collective-permute-start | bytes 196616 | tf_op jit(solution)/shard_map/ppermute | solution.py:347
  10.8 18.5 %collective-permute-start.17 = (bf16[32,1024]{1,0:T(8,128)(2,1)S(1)}, bf16[32,1024]{1,0:T(8,128)(2,1)S(1)}, u32[]{:S(2)}, u32[]{:S(2)}) collective-permute-start(bf16[32,1024]{1,0:T(8,128)(2,1)S(1)} %get-tuple-element.49), channel_id=1, source_target_pairs={{0,8},{4,12},{8,0},{12,4},{16,24},{20,28},{24,16},{28,20},{1,9},{5... | collective-permute-start | bytes 196616 | tf_op jit(solution)/shard_map/ppermute | solution.py:347
  13.3 1.6 %copy-start.4 = (bf16[8,256,512]{2,1,0:T(8,128)(2,1)S(1)}, bf16[8,256,512]{2,1,0:T(8,128)(2,1)}, u32[]{:S(2)}) copy-start(bf16[8,256,512]{2,1,0:T(8,128)(2,1)} %observed_ref.1) | copy-start | bytes 6291460
  14.9 0.7 copy-start.5
  15.6 0.7 copy-start.6
  16.3 39.6 %copy-start.7 = (bf16[256,256]{1,0:T(8,128)(2,1)S(1)}, bf16[256,256]{1,0:T(8,128)(2,1)}, u32[]{:S(2)}) copy-start(bf16[256,256]{1,0:T(8,128)(2,1)} %constant.104.refs_3_) | copy-start | bytes 393220
  16.3 39.6 %copy-start.8 = (bf16[256,256]{1,0:T(8,128)(2,1)S(1)}, bf16[256,256]{1,0:T(8,128)(2,1)}, u32[]{:S(2)}) copy-start(bf16[256,256]{1,0:T(8,128)(2,1)} %constant.105.refs_4_) | copy-start | bytes 393220
  16.3 39.6 %copy-start.9 = (bf16[128,512]{1,0:T(8,128)(2,1)S(1)}, bf16[128,512]{1,0:T(8,128)(2,1)}, u32[]{:S(2)}) copy-start(bf16[128,512]{1,0:T(8,128)(2,1)} %constant.106.refs_5_) | copy-start | bytes 393220
  16.3 39.6 %copy-start.10 = (bf16[128,512]{1,0:T(8,128)(2,1)S(1)}, bf16[128,512]{1,0:T(8,128)(2,1)}, u32[]{:S(2)}) copy-start(bf16[128,512]{1,0:T(8,128)(2,1)} %constant.107.refs_6_) | copy-start | bytes 393220
  19.9 9.6 %collective-permute-start.18 = (bf16[32,1024]{1,0:T(8,128)(2,1)S(1)}, bf16[32,1024]{1,0:T(8,128)(2,1)S(1)}, u32[]{:S(2)}, u32[]{:S(2)}) collective-permute-start(bf16[32,1024]{1,0:T(8,128)(2,1)S(1)} %get-tuple-element.48), channel_id=1, source_target_pairs={{0,12},{4,8},{8,4},{12,0},{16,28},{20,24},{24,20},{28,16},{1,13},{... | collective-permute-start | bytes 196616 | tf_op jit(solution)/shard_map/ppermute | solution.py:347
  20.7 10.6 %collective-permute-start.19 = (bf16[32,1024]{1,0:T(8,128)(2,1)S(1)}, bf16[32,1024]{1,0:T(8,128)(2,1)S(1)}, u32[]{:S(2)}, u32[]{:S(2)}) collective-permute-start(bf16[32,1024]{1,0:T(8,128)(2,1)S(1)} %get-tuple-element.47), channel_id=1, source_target_pairs={{0,16},{4,20},{8,24},{12,28},{16,0},{20,4},{24,8},{28,12},{1,17},{... | collective-permute-start | bytes 196616 | tf_op jit(solution)/shard_map/ppermute | solution.py:347
  24.4 8.9 %collective-permute-start.20 = (bf16[32,1024]{1,0:T(8,128)(2,1)S(1)}, bf16[32,1024]{1,0:T(8,128)(2,1)S(1)}, u32[]{:S(2)}, u32[]{:S(2)}) collective-permute-start(bf16[32,1024]{1,0:T(8,128)(2,1)S(1)} %get-tuple-element.46), channel_id=1, source_target_pairs={{0,20},{4,16},{8,28},{12,24},{16,4},{20,0},{24,12},{28,8},{1,21},{... | collective-permute-start | bytes 196616 | tf_op jit(solution)/shard_map/ppermute | solution.py:347
  25.7 7.6 %collective-permute-start.21 = (bf16[32,1024]{1,0:T(8,128)(2,1)S(1)}, bf16[32,1024]{1,0:T(8,128)(2,1)S(1)}, u32[]{:S(2)}, u32[]{:S(2)}) collective-permute-start(bf16[32,1024]{1,0:T(8,128)(2,1)S(1)} %get-tuple-element.45), channel_id=1, source_target_pairs={{0,24},{4,28},{8,16},{12,20},{16,8},{20,12},{24,0},{28,4},{1,25},{... | collective-permute-start | bytes 196616 | tf_op jit(solution)/shard_map/ppermute | solution.py:347
  29.4 7.6 %collective-permute-start.22 = (bf16[32,1024]{1,0:T(8,128)(2,1)S(1)}, bf16[32,1024]{1,0:T(8,128)(2,1)S(1)}, u32[]{:S(2)}, u32[]{:S(2)}) collective-permute-start(bf16[32,1024]{1,0:T(8,128)(2,1)S(1)} %get-tuple-element.44), channel_id=1, source_target_pairs={{0,28},{4,24},{8,20},{12,16},{16,12},{20,8},{24,4},{28,0},{1,29},{... | collective-permute-start | bytes 196616 | tf_op jit(solution)/shard_map/ppermute | solution.py:347
  29.4 8.5 %collective-permute-start.3 = (bf16[32,1024]{1,0:T(8,128)(2,1)}, bf16[32,1024]{1,0:T(8,128)(2,1)S(1)}, u32[]{:S(2)}, u32[]{:S(2)}) collective-permute-start(bf16[32,1024]{1,0:T(8,128)(2,1)} %get-tuple-element.58), channel_id=1, source_target_pairs={{0,4},{4,0},{8,12},{12,8},{16,20},{20,16},{24,28},{28,24},{1,5},{5... | collective-permute-start | bytes 196616 | tf_op jit(solution)/shard_map/ppermute | solution.py:347
  31.3 14.9 %collective-permute-start.23 = (bf16[32,8,256]{2,1,0:T(8,128)(2,1)S(1)}, bf16[32,8,256]{2,1,0:T(8,128)(2,1)S(1)}, u32[]{:S(2)}, u32[]{:S(2)}) collective-permute-start(bf16[32,8,256]{2,1,0:T(8,128)(2,1)S(1)} %get-tuple-element.31), channel_id=1, source_target_pairs={{0,4},{4,0},{8,12},{12,8},{16,20},{20,16},{24,28},{28,24},{1,5},{5... | collective-permute-start | bytes 393224 | tf_op jit(solution)/shard_map/ppermute | solution.py:347
  33.3 6.2 %collective-permute-start.4 = (bf16[32,1024]{1,0:T(8,128)(2,1)}, bf16[32,1024]{1,0:T(8,128)(2,1)S(1)}, u32[]{:S(2)}, u32[]{:S(2)}) collective-permute-start(bf16[32,1024]{1,0:T(8,128)(2,1)} %get-tuple-element.57), channel_id=1, source_target_pairs={{0,8},{4,12},{8,0},{12,4},{16,24},{20,28},{24,16},{28,20},{1,9},{5... | collective-permute-start | bytes 196616 | tf_op jit(solution)/shard_map/ppermute | solution.py:347
  33.4 7.4 %collective-permute-start.5 = (bf16[32,1024]{1,0:T(8,128)(2,1)S(1)}, bf16[32,1024]{1,0:T(8,128)(2,1)S(1)}, u32[]{:S(2)}, u32[]{:S(2)}) collective-permute-start(bf16[32,1024]{1,0:T(8,128)(2,1)S(1)} %get-tuple-element.56), channel_id=1, source_target_pairs={{0,12},{4,8},{8,4},{12,0},{16,28},{20,24},{24,20},{28,16},{1,13},{... | collective-permute-start | bytes 196616 | tf_op jit(solution)/shard_map/ppermute | solution.py:347
  37.0 6.0 %collective-permute-start.6 = (bf16[32,1024]{1,0:T(8,128)(2,1)S(1)}, bf16[32,1024]{1,0:T(8,128)(2,1)S(1)}, u32[]{:S(2)}, u32[]{:S(2)}) collective-permute-start(bf16[32,1024]{1,0:T(8,128)(2,1)S(1)} %get-tuple-element.55), channel_id=1, source_target_pairs={{0,16},{4,20},{8,24},{12,28},{16,0},{20,4},{24,8},{28,12},{1,17},{... | collective-permute-start | bytes 196616 | tf_op jit(solution)/shard_map/ppermute | solution.py:347
  37.9 6.8 %collective-permute-start.7 = (bf16[32,1024]{1,0:T(8,128)(2,1)S(1)}, bf16[32,1024]{1,0:T(8,128)(2,1)S(1)}, u32[]{:S(2)}, u32[]{:S(2)}) collective-permute-start(bf16[32,1024]{1,0:T(8,128)(2,1)S(1)} %get-tuple-element.54), channel_id=1, source_target_pairs={{0,20},{4,16},{8,28},{12,24},{16,4},{20,0},{24,12},{28,8},{1,21},{... | collective-permute-start | bytes 196616 | tf_op jit(solution)/shard_map/ppermute | solution.py:347
  39.6 6.8 %collective-permute-start.24 = (bf16[32,8,256]{2,1,0:T(8,128)(2,1)S(1)}, bf16[32,8,256]{2,1,0:T(8,128)(2,1)S(1)}, u32[]{:S(2)}, u32[]{:S(2)}) collective-permute-start(bf16[32,8,256]{2,1,0:T(8,128)(2,1)S(1)} %get-tuple-element.32), channel_id=1, source_target_pairs={{0,8},{4,12},{8,0},{12,4},{16,24},{20,28},{24,16},{28,20},{1,9},{5... | collective-permute-start | bytes 393224 | tf_op jit(solution)/shard_map/ppermute | solution.py:347
  40.7 7.6 %collective-permute-start.25 = (bf16[32,8,256]{2,1,0:T(8,128)(2,1)S(1)}, bf16[32,8,256]{2,1,0:T(8,128)(2,1)S(1)}, u32[]{:S(2)}, u32[]{:S(2)}) collective-permute-start(bf16[32,8,256]{2,1,0:T(8,128)(2,1)S(1)} %get-tuple-element.33), channel_id=1, source_target_pairs={{0,12},{4,8},{8,4},{12,0},{16,28},{20,24},{24,20},{28,16},{1,13},{... | collective-permute-start | bytes 393224 | tf_op jit(solution)/shard_map/ppermute | solution.py:347
  43.0 9.5 %collective-permute-start.13 = (bf16[32,2048]{1,0:T(8,128)(2,1)S(1)}, bf16[32,2048]{1,0:T(8,128)(2,1)S(1)}, u32[]{:S(2)}, u32[]{:S(2)}) collective-permute-start(bf16[32,2048]{1,0:T(8,128)(2,1)S(1)} %slice.55.refs_19_), channel_id=1, source_target_pairs={{0,1},{1,0},{2,3},{3,2},{4,5},{5,4},{6,7},{7,6},{8,9},{9,8},{10,11... | collective-permute-start | bytes 393224 | tf_op jit(solution)/shard_map/ppermute | solution.py:347
  44.7 7.7 %collective-permute-start.14 = (bf16[32,2048]{1,0:T(8,128)(2,1)S(1)}, bf16[32,2048]{1,0:T(8,128)(2,1)S(1)}, u32[]{:S(2)}, u32[]{:S(2)}) collective-permute-start(bf16[32,2048]{1,0:T(8,128)(2,1)S(1)} %slice.55.refs_19_), channel_id=1, source_target_pairs={{0,2},{1,3},{2,0},{3,1},{4,6},{5,7},{6,4},{7,5},{8,10},{9,11},{10,... | collective-permute-start | bytes 393224 | tf_op jit(solution)/shard_map/ppermute | solution.py:347
  46.2 6.3 %collective-permute-start.15 = (bf16[32,2048]{1,0:T(8,128)(2,1)S(1)}, bf16[32,2048]{1,0:T(8,128)(2,1)S(1)}, u32[]{:S(2)}, u32[]{:S(2)}) collective-permute-start(bf16[32,2048]{1,0:T(8,128)(2,1)S(1)} %slice.55.refs_19_), channel_id=1, source_target_pairs={{0,3},{1,2},{2,1},{3,0},{4,7},{5,6},{6,5},{7,4},{8,11},{9,10},{10,... | collective-permute-start | bytes 393224 | tf_op jit(solution)/shard_map/ppermute | solution.py:347
  46.4 26.1 %collective-permute-start.8 = (bf16[32,1024]{1,0:T(8,128)(2,1)S(1)}, bf16[32,1024]{1,0:T(8,128)(2,1)S(1)}, u32[]{:S(2)}, u32[]{:S(2)}) collective-permute-start(bf16[32,1024]{1,0:T(8,128)(2,1)S(1)} %get-tuple-element.53), channel_id=1, source_target_pairs={{0,24},{4,28},{8,16},{12,20},{16,8},{20,12},{24,0},{28,4},{1,25},{... | collective-permute-start | bytes 196616 | tf_op jit(solution)/shard_map/ppermute | solution.py:347
  48.3 24.2 %collective-permute-start.9 = (bf16[32,1024]{1,0:T(8,128)(2,1)S(1)}, bf16[32,1024]{1,0:T(8,128)(2,1)S(1)}, u32[]{:S(2)}, u32[]{:S(2)}) collective-permute-start(bf16[32,1024]{1,0:T(8,128)(2,1)S(1)} %get-tuple-element.52), channel_id=1, source_target_pairs={{0,28},{4,24},{8,20},{12,16},{16,12},{20,8},{24,4},{28,0},{1,29},{... | collective-permute-start | bytes 196616 | tf_op jit(solution)/shard_map/ppermute | solution.py:347
  52.4 20.1 %collective-permute-start.10 = (bf16[32,8,256]{2,1,0:T(8,128)(2,1)S(1)}, bf16[32,8,256]{2,1,0:T(8,128)(2,1)S(1)}, u32[]{:S(2)}, u32[]{:S(2)}) collective-permute-start(bf16[32,8,256]{2,1,0:T(8,128)(2,1)S(1)} %get-tuple-element.26), channel_id=1, source_target_pairs={{0,4},{4,0},{8,12},{12,8},{16,20},{20,16},{24,28},{28,24},{1,5},{5... | collective-permute-start | bytes 393224 | tf_op jit(solution)/shard_map/ppermute | solution.py:347
  52.5 20.1 %collective-permute-start.11 = (bf16[32,8,256]{2,1,0:T(8,128)(2,1)S(1)}, bf16[32,8,256]{2,1,0:T(8,128)(2,1)S(1)}, u32[]{:S(2)}, u32[]{:S(2)}) collective-permute-start(bf16[32,8,256]{2,1,0:T(8,128)(2,1)S(1)} %get-tuple-element.27), channel_id=1, source_target_pairs={{0,8},{4,12},{8,0},{12,4},{16,24},{20,28},{24,16},{28,20},{1,9},{5... | collective-permute-start | bytes 393224 | tf_op jit(solution)/shard_map/ppermute | solution.py:347
  52.5 20.0 %collective-permute-start.12 = (bf16[32,8,256]{2,1,0:T(8,128)(2,1)S(1)}, bf16[32,8,256]{2,1,0:T(8,128)(2,1)S(1)}, u32[]{:S(2)}, u32[]{:S(2)}) collective-permute-start(bf16[32,8,256]{2,1,0:T(8,128)(2,1)S(1)} %get-tuple-element.28), channel_id=1, source_target_pairs={{0,12},{4,8},{8,4},{12,0},{16,28},{20,24},{24,20},{28,16},{1,13},{... | collective-permute-start | bytes 393224 | tf_op jit(solution)/shard_map/ppermute | solution.py:347
  89.2 37.8 %copy-start.11 = (s32[8]{0:T(128)S(1)}, s32[8]{0:T(128)}, u32[]{:S(2)}) copy-start(s32[8]{0:T(128)} %param.13) | copy-start | bytes 100
  89.3 39.2 %copy-start.3 = (s32[256]{0:T(256)S(1)}, s32[256]{0:T(256)}, u32[]{:S(2)}) copy-start(s32[256]{0:T(256)} %param.14) | copy-start | bytes 3076
  89.3 19.5 %all-to-all-start.1 = ((s16[8,32,1152]{2,1,0:T(8,128)(2,1)}), s16[8,32,1152]{2,1,0:T(8,128)(2,1)S(1)}, u32[]{:S(2)}, u32[]{:S(2)}) async-start(s16[8,32,1152]{2,1,0:T(8,128)(2,1)} %get-tuple-element.43), calls=%async_computation.1 | async-start | bytes 1179648 | tf_op jit(solution)/shard_map/all_to_all | solution.py:464
  92.8 19.6 %collective-permute-start.26 = (f32[32,2048]{1,0:T(8,128)S(1)}, f32[32,2048]{1,0:T(8,128)S(1)}, u32[]{:S(2)}, u32[]{:S(2)}) collective-permute-start(f32[32,2048]{1,0:T(8,128)S(1)} %get-tuple-element.39), channel_id=1, source_target_pairs={{0,1},{1,0},{2,3},{3,2},{4,5},{5,4},{6,7},{7,6},{8,9},{9,8},{10,11... | collective-permute-start | bytes 786440 | tf_op jit(solution)/shard_map/ppermute | solution.py:347
  92.9 19.5 %collective-permute-start.27 = (f32[32,2048]{1,0:T(8,128)S(1)}, f32[32,2048]{1,0:T(8,128)S(1)}, u32[]{:S(2)}, u32[]{:S(2)}) collective-permute-start(f32[32,2048]{1,0:T(8,128)S(1)} %get-tuple-element.40), channel_id=1, source_target_pairs={{0,2},{1,3},{2,0},{3,1},{4,6},{5,7},{6,4},{7,5},{8,10},{9,11},{10,... | collective-permute-start | bytes 786440 | tf_op jit(solution)/shard_map/ppermute | solution.py:347
  94.4 18.0 %collective-permute-start.28 = (f32[32,2048]{1,0:T(8,128)S(1)}, f32[32,2048]{1,0:T(8,128)S(1)}, u32[]{:S(2)}, u32[]{:S(2)}) collective-permute-start(f32[32,2048]{1,0:T(8,128)S(1)} %get-tuple-element.41), channel_id=1, source_target_pairs={{0,3},{1,2},{2,1},{3,0},{4,7},{5,6},{6,5},{7,4},{8,11},{9,10},{10,... | collective-permute-start | bytes 786440 | tf_op jit(solution)/shard_map/ppermute | solution.py:347
  108.7 19.7 %all-to-all-start = ((s16[8,32,1152]{2,1,0:T(8,128)(2,1)}), s16[8,32,1152]{2,1,0:T(8,128)(2,1)S(1)}, u32[]{:S(2)}, u32[]{:S(2)}) async-start(s16[8,32,1152]{2,1,0:T(8,128)(2,1)} %get-tuple-element.42), calls=%async_computation | async-start | bytes 1179648 | tf_op jit(solution)/shard_map/all_to_all | solution.py:464
  112.5 7.4 %collective-permute-start.29 = (f32[8,2048]{1,0:T(8,128)S(1)}, f32[8,2048]{1,0:T(8,128)S(1)}, u32[]{:S(2)}, u32[]{:S(2)}) collective-permute-start(f32[8,2048]{1,0:T(8,128)S(1)} %get-tuple-element.60), channel_id=1, source_target_pairs={{0,4},{4,0},{8,12},{12,8},{16,20},{20,16},{24,28},{28,24},{1,5},{5... | collective-permute-start | bytes 196616 | tf_op jit(solution)/shard_map/ppermute | solution.py:347
  114.6 9.9 %collective-permute-start.30 = (f32[8,2048]{1,0:T(8,128)S(1)}, f32[8,2048]{1,0:T(8,128)S(1)}, u32[]{:S(2)}, u32[]{:S(2)}) collective-permute-start(f32[8,2048]{1,0:T(8,128)S(1)} %get-tuple-element.62), channel_id=1, source_target_pairs={{0,8},{4,12},{8,0},{12,4},{16,24},{20,28},{24,16},{28,20},{1,9},{5... | collective-permute-start | bytes 196616 | tf_op jit(solution)/shard_map/ppermute | solution.py:347
  116.0 11.0 %collective-permute-start.31 = (f32[8,2048]{1,0:T(8,128)S(1)}, f32[8,2048]{1,0:T(8,128)S(1)}, u32[]{:S(2)}, u32[]{:S(2)}) collective-permute-start(f32[8,2048]{1,0:T(8,128)S(1)} %get-tuple-element.61), channel_id=1, source_target_pairs={{0,12},{4,8},{8,4},{12,0},{16,28},{20,24},{24,20},{28,16},{1,13},{... | collective-permute-start | bytes 196616 | tf_op jit(solution)/shard_map/ppermute | solution.py:347

commit v3 on v2

--- a/solution.py
+++ b/solution.py
@@ -19,8 +19,8 @@
 LANES = 128
 FB = LANES // (2 * S)
 WIDTH = 8
-CHUNKS = 2
-MOST_SWAPS = 8
+CHUNKS = 1
+MOST_SWAPS = 1
 FIXED = 32000.0
 
 
@@ -47,24 +47,22 @@
     return lax.dot_general(a, b, (((0,), (0,)), ((), ())), preferred_element_type=jnp.float32)
 
 
-def prepare_kernel(spectra_ref, counts_ref, rspectra_ref, rcounts_ref, eye_ref, u_ref, *v_refs):
+def prepare_kernel(
+    spectra_from, counts_ref, rspectra_ref, rcounts_ref, eye_ref, u_ref, *rest
+):
+    *v_to, spectra_ref, turned_ref, in_sems, out_sems = rest
     k_own, col_total = spectra_ref.shape
-    chunk_total = len(v_refs)
-    rcv_total, cols, _ = v_refs[0].shape
+    chunk_total = len(v_to)
+    rcv_total, cols, _ = v_to[0].shape
     members = col_total // (cols * chunk_total)
     width = min(k_own, 2 * LANES)
-    counts = counts_ref[...]
-    for begin in range(0, k_own, width):
-        seg_ids = lax.broadcasted_iota(jnp.int32, (width, col_total), 0) % S
-        part = spectra_ref[begin : begin + width, :].astype(jnp.float32)
-        part = jnp.where(seg_ids < counts, part, 0.0).astype(jnp.bfloat16)
-        turned = nt(eye_ref[...], part).astype(jnp.bfloat16)
-        for c in range(chunk_total):
-            for m in range(members):
-                first = (m * chunk_total + c) * cols
-                rows = turned[first : first + cols]
-                for dest in range(m, rcv_total, members):
-                    v_refs[c][dest, :, begin : begin + width] = rows
+    copies = []
+    for n, begin in enumerate(range(0, k_own, width)):
+        rows = pl.ds(begin, width)
+        copies.append(
+            pltpu.make_async_copy(spectra_from.at[rows], spectra_ref.at[rows], in_sems.at[n])
+        )
+        copies[-1].start()
     rows, quarter = rspectra_ref.shape
     seg_ids = lax.broadcasted_iota(jnp.int32, (rows, quarter), 1) % S
     part = rspectra_ref[...].astype(jnp.float32)
@@ -73,10 +71,31 @@
     u_ref[:, quarter:] = jnp.broadcast_to(rcounts_ref[...], (rows, LANES)).astype(
         jnp.float32
     ).astype(jnp.bfloat16)
-
-
-def fold_kernel(c_ref, observed_ref, window_ref, order_ref, *rest):
-    *out_refs, line_ref = rest
+    counts = counts_ref[...]
+    seg_ids = lax.broadcasted_iota(jnp.int32, (width, col_total), 0) % S
+    for n, begin in enumerate(range(0, k_own, width)):
+        copies[n].wait()
+        part = spectra_ref[begin : begin + width, :].astype(jnp.float32)
+        part = jnp.where(seg_ids < counts, part, 0.0).astype(jnp.bfloat16)
+        turned_ref[:, begin : begin + width] = nt(eye_ref[...], part).astype(jnp.bfloat16)
+    copies = []
+    for c in range(chunk_total):
+        for dest in range(rcv_total):
+            first = (dest % members * chunk_total + c) * cols
+            copies.append(
+                pltpu.make_async_copy(
+                    turned_ref.at[pl.ds(first, cols)],
+                    v_to[c].at[dest],
+                    out_sems.at[c * rcv_total + dest],
+                )
+            )
+            copies[-1].start()
+    for copy in copies:
+        copy.wait()
+
+
+def fold_kernel(c_ref, observed_from, window_ref, order_ref, *rest):
+    *out_refs, observed_ref, line_ref, sems = rest
     row_total, col_total, lag_total = observed_ref.shape
     half = lag_total // 2
     cols = out_refs[0].shape[0]
@@ -86,7 +105,14 @@
     pick = jnp.where(station == order_ref[...], 1.0, 0.0).astype(jnp.bfloat16)
     lag_ids = lax.broadcasted_iota(jnp.int32, (col_total, half), 1).astype(jnp.float32)
     lines = col_total * row_total
+    copies = [
+        pltpu.make_async_copy(observed_from.at[i], observed_ref.at[i], sems.at[i])
+        for i in range(row_total)
+    ]
+    for copy in copies:
+        copy.start()
     for i in range(row_total):
+        copies[i].wait()
         begin = window[:, i : i + 1]
         end = begin + window[:, row_total + i : row_total + i + 1]
         values = observed_ref[i].astype(jnp.float32)
@@ -120,10 +146,10 @@
 
     (c_ref, invn_ref, eye_ref, ye_ref, yo_ref, ze_ref, zo_ref) = take(7)
     v_from, e_from, u_from = take(n_v), take(n_e), take(n_r)
-    r_from = take(n_r) if len(refs) > n_r + 8 else []
-    (w_ref,) = take(1)
+    r_from = take(n_r) if len(refs) > n_r + 12 else []
+    (w_to,) = take(1)
     r_to = take(n_r)
-    x_ref, urow_ref, code_ref, v_ref, e_ref, r_ref, sems = refs
+    x_ref, z_ref, u_ref, turned_ref, code_ref, v_ref, e_ref, r_ref, w_ref, sems, w_sems = refs
 
     src_total, col_total, k_own = v_ref.shape
     ref_total, irec, k_quarter = r_ref.shape
@@ -148,7 +174,7 @@
 
     for k, ref in enumerate(u_from):
         begin = pl.multiple_of((quarter_me ^ k) * k_quarter, k_quarter)
-        fetch(u_copies, ref, urow_ref.at[0, :, pl.ds(begin, k_quarter)])
+        fetch(u_copies, ref, u_ref.at[:, pl.ds(begin, k_quarter)])
     for k, ref in enumerate(v_from):
         fetch(v_copies, ref, v_ref if n_v == 1 else v_ref.at[me ^ k])
     for k, ref in enumerate(e_from):
@@ -191,11 +217,11 @@
 
     def forward(fb, _):
         lanes = pl.ds(pl.multiple_of(fb * LANES, LANES), LANES)
-        part = urow_ref[0, :, lanes]
+        part = u_ref[:, lanes]
         wide = part.astype(jnp.float32)
         crossed = jnp.where(first_part, pltpu.roll(wide, LANES - S, 1), -pltpu.roll(wide, S, 1))
         crossed = crossed.astype(jnp.bfloat16)
-        urow_ref[1, :, lanes] = crossed
+        turned_ref[:, lanes] = crossed
         out = nt(v_block(fb), u_block([part, crossed]))
         scale = invn_ref[...]
         for f in range(FB):
@@ -250,19 +276,19 @@
             lanes = slice(k * LANES, (k + 1) * LANES)
             scale = invn_ref[pl.ds(jp, 1), :]
             base = pl.multiple_of(jp * freq_total, freq_total)
-            x_ref[pl.ds(base, half_f), :] = z_e[:, lanes] * scale
-            x_ref[pl.ds(base + half_f, half_f), :] = z_o[:, lanes] * scale
+            z_ref[pl.ds(base, half_f), :] = z_e[:, lanes] * scale
+            z_ref[pl.ds(base + half_f, half_f), :] = z_o[:, lanes] * scale
         return 0
 
     for copy in e_copies:
         copy.wait()
     lax.fori_loop(0, jp_total // WIDTH, pairs, 0)
 
-    def backward(fb, _):
-        z = jnp.concatenate([x_ref[place(fb, f), :] for f in range(FB)], axis=0)
+    def backward(fb):
+        z = jnp.concatenate([z_ref[place(fb, f), :] for f in range(FB)], axis=0)
         z = z.astype(jnp.bfloat16)
         lanes = pl.ds(pl.multiple_of(fb * LANES, LANES), LANES)
-        w = nn(z, u_block([urow_ref[q, :, lanes] for q in range(2)]))
+        w = nn(z, u_block([u_ref[:, lanes], turned_ref[:, lanes]]))
         totals = []
         for jj in range(jj_total):
             lanes = slice(jj * LANES, (jj + 1) * LANES)
@@ -293,26 +319,34 @@
         lanes = pl.ds(off, LANES)
         total = sums[0] + crossed
         r_ref[quarter, :, lanes] = r_ref[quarter, :, lanes] + total if r_from else total
-        return 0
-
-    for copy in r_copies:
-        copy.wait()
-    lax.fori_loop(0, blocks, backward, 0, unroll=16)
-    outs = [
-        pltpu.make_async_copy(r_ref.at[quarter_me ^ k], ref, sems.at[k])
-        for k, ref in enumerate(r_to)
-    ]
-    for copy in outs:
-        copy.start()
-
-    for src in range(src_total):
-        codes = code_ref[src * own_blocks : (src + 1) * own_blocks, :]
+
+    def w_copy(src):
+        return pltpu.make_async_copy(w_ref.at[src], w_to.at[src], w_sems.at[src])
+
+    def from_owner(src, _):
+        for b in range(own_blocks):
+            backward(src * own_blocks + b)
+        codes = code_ref[pl.ds(src * own_blocks, own_blocks), :]
         codes = jnp.concatenate(
             [codes, jnp.zeros((col_total - own_blocks, LANES), jnp.float32)], axis=0
         )
         w_ref[src, :, k_own:] = codes.astype(jnp.int32).astype(jnp.int16)
+        w_copy(src).start()
+        return 0
+
+    for copy in r_copies:
+        copy.wait()
+    owners = src_total // ref_total
+    outs = []
+    for k, ref in enumerate(r_to):
+        begin = (quarter_me ^ k) * owners
+        lax.fori_loop(begin, begin + owners, from_owner, 0)
+        outs.append(pltpu.make_async_copy(r_ref.at[quarter_me ^ k], ref, sems.at[k]))
+        outs[-1].start()
     for copy in outs:
         copy.wait()
+    for src in range(src_total):
+        w_copy(src).wait()
 
 
 def join_kernel(count_ref, *refs):
@@ -388,8 +422,14 @@
         prepare_kernel,
         out_shape=[jax.ShapeDtypeStruct((row_total, k_quarter + LANES), bf16)]
         + [jax.ShapeDtypeStruct((rcv_total, cols, k_own), bf16)] * CHUNKS,
-        in_specs=[vmem] * 5,
-        out_specs=[vmem] * (1 + CHUNKS),
+        in_specs=[hbm] + [vmem] * 4,
+        out_specs=[vmem] + [hbm] * CHUNKS,
+        scratch_shapes=[
+            pltpu.VMEM((k_own, col_total), bf16),
+            pltpu.VMEM((col_total, k_own), bf16),
+            pltpu.SemaphoreType.DMA((k_own // min(k_own, 2 * LANES),)),
+            pltpu.SemaphoreType.DMA((CHUNKS * rcv_total,)),
+        ],
         compiler_params=params(24),
     )(
         reference_spectra,
@@ -417,9 +457,13 @@
     folded = pl.pallas_call(
         fold_kernel,
         out_shape=[jax.ShapeDtypeStruct((cols, row_total, half), bf16)] * (CHUNKS * members),
-        in_specs=[smem] + [vmem] * 3,
+        in_specs=[smem, hbm] + [vmem] * 2,
         out_specs=[vmem] * (CHUNKS * members),
-        scratch_shapes=[pltpu.VMEM((half // LANES * col_total * row_total, LANES), jnp.float32)],
+        scratch_shapes=[
+            pltpu.VMEM((row_total, col_total, lag_total), bf16),
+            pltpu.VMEM((half // LANES * col_total * row_total, LANES), jnp.float32),
+            pltpu.SemaphoreType.DMA((row_total,)),
+        ],
         compiler_params=params(32),
         cost_estimate=cost(4),
     )(scalars, observed, lag_window, column_station.reshape(1, col_total))
@@ -448,15 +492,19 @@
             out_shape=[jax.ShapeDtypeStruct((rcv_total, cols, k_own + LANES), jnp.int16)]
             + [jax.ShapeDtypeStruct((irec, k_quarter), jnp.float32)] * ref_total,
             in_specs=[smem] + [vmem] * 6 + [hbm] * len(operands),
-            out_specs=[vmem] + [hbm] * ref_total,
+            out_specs=[hbm] * (1 + ref_total),
             scratch_shapes=[
                 pltpu.VMEM((jp_total * k_total // (2 * S), LANES), jnp.float32),
-                pltpu.VMEM((2, irec, k_total), bf16),
+                pltpu.VMEM((jp_total * k_total // (2 * S), LANES), jnp.float32),
+                pltpu.VMEM((irec, k_total), bf16),
+                pltpu.VMEM((irec, k_total), bf16),
                 pltpu.VMEM((k_total // LANES, LANES), jnp.float32),
                 pltpu.VMEM((rcv_total, cols, k_own), bf16),
                 pltpu.VMEM((members, cols, row_total, half), bf16),
                 pltpu.VMEM((ref_total, irec, k_quarter), jnp.float32),
+                pltpu.VMEM((rcv_total, cols, k_own + LANES), jnp.int16),
                 pltpu.SemaphoreType.DMA((len(operands),)),
+                pltpu.SemaphoreType.DMA((rcv_total,)),
             ],
             compiler_params=params(48),
             cost_estimate=cost(10),

time: 130 us -> 110 us (0.85)
  starting transfers between devices: 50.9 us -> 28 us
  Pallas kernels: 37.1 us -> 27.7 us
  local copies, waits for them, and re-layouts: 9.37 us -> 16.2 us
  waiting for transfers between devices: 29.7 us -> 34.4 us
    ppermute x32 -> x15, starting transfers between devices: 43.7 us -> 18.8 us  [swap(): return lax.ppermute(x, axis, [(r, r ^ k) for r in range(total)])]
    ppermute x32 -> x15, waiting for transfers between devices: 15.1 us -> 28.9 us  [swap(): return lax.ppermute(x, axis, [(r, r ^ k) for r in range(total)])]
    pallas_call x2 -> x1, Pallas kernels: 33.2 us -> 19.7 us  [shards(): pl.pallas_call(functools.partial(pair_kernel, len(v_all[c]), members, ref...]
    all_to_all x2 -> x1, waiting for transfers between devices: 14.7 us -> 4 us  [shards(): lax.all_to_all(w_part, 'rcv', split_axis=0, concat_axis=0, tiled=True)]
    unnamed x27 -> x35, local copies, waits for them, and re-layouts: 7.04 us -> 13.4 us
    all_to_all x0 -> x1, starting transfers between devices: none -> 3.99 us  [spread(): return [lax.all_to_all(x, 'rcv', split_axis=0, concat_axis=0, tiled=True)]]
    pallas_call x1, Pallas kernels: 0.33 us -> 2.78 us  [shards(): pl.pallas_call(prepare_kernel, out_shape=[jax.ShapeDtypeStruct((row_total...]
    all_to_all x2 -> x1, starting transfers between devices: 7.19 us -> 5.25 us  [shards(): lax.all_to_all(w_part, 'rcv', split_axis=0, concat_axis=0, tiled=True)]
  transfers between devices with their start and end apart: 34 -> 17, of which waited for: 8 -> 10; matrix products, arithmetic and copies ran while one was open for 4% -> 5% of each run, Pallas kernels for 14% -> 4%
where the time goes in v3:
time: 110 us; the launch traced here: 109 us
  waiting for transfers between devices  34.4 us (31%)
  starting transfers between devices  28 us (25%)
  Pallas kernels  27.7 us (25%)
  local copies, waits for them, and re-layouts  16.2 us (15%)
  other arithmetic  1.85 us (2%)
    ppermute x15, waiting for transfers between devices, swap(): return lax.ppermute(x, axis, [(r, r ^ k) for r in range(total)])  28.9 us
    pallas_call x1, Pallas kernels, shards(): pl.pallas_call(functools.partial(pair_kernel, len(v_all[c]), members, ref...  19.7 us
    ppermute x15, starting transfers between devices, swap(): return lax.ppermute(x, axis, [(r, r ^ k) for r in range(total)])  18.8 us
    unnamed x35, local copies, waits for them, and re-layouts  13.4 us
    all_to_all x1, starting transfers between devices, shards(): lax.all_to_all(w_part, 'rcv', split_axis=0, concat_axis=0, tiled=True)  5.25 us
    all_to_all x1, waiting for transfers between devices, shards(): lax.all_to_all(w_part, 'rcv', split_axis=0, concat_axis=0, tiled=True)  4 us
    all_to_all x1, starting transfers between devices, spread(): return [lax.all_to_all(x, 'rcv', split_axis=0, concat_axis=0, tiled=True)]  3.99 us
    pallas_call x1, Pallas kernels, shards(): pl.pallas_call(fold_kernel, out_shape=[jax.ShapeDtypeStruct((cols, row_to...  3.88 us
  transfers between devices with their start and end apart: 17, of which 10 were waited for; matrix products, arithmetic and copies ran while one was open for 5% of the time, Pallas kernels for 4%

profile of v3, /device:TPU:0, one launch (start us, length us, event | category | flops | bytes accessed | tf_op | source)
XLA Modules:
  0.0 108.9 jit_solution(6887030731786125919)
XLA Ops:
  0.7 0.7 copy.16.rcounts_ref
  1.4 1.0 copy-done
  2.4 0.8 copy-done.1
  3.2 0.7 copy-done.2
  3.9 2.8 %shard_map.122 = (bf16[8,2176]{1,0:T(8,128)(2,1)S(1)}, bf16[8,64,1024]{2,1,0:T(8,128)(2,1)}) custom-call(bf16[1024,256]{1,0:T(8,128)(2,1)S(1)} %copy-done, s32[1,256]{1,0:T(1,128)S(1)} %bitcast.8, bf16[8,2048]{1,0:T(8,128)(2,1)S(1)} %copy-done.1, s32[8,1]{1,0:T(8,128)S(1)} %copy.16.rcounts_ref, bf16[256,256]{1,0:T(8,128)(2,1)S(1)} %fusion.eye_ref.refs_2_), custom_call_target="tpu_custom_call" | custom-call | tf_op jit(solution)/shard_map/pallas_call | solution.py:421
  6.7 3.0 %collective-permute-start = (bf16[8,2176]{1,0:T(8,128)(2,1)S(1)}, bf16[8,2176]{1,0:T(8,128)(2,1)S(1)}, u32[]{:S(2)}, u32[]{:S(2)}) collective-permute-start(bf16[8,2176]{1,0:T(8,128)(2,1)S(1)} %get-tuple-element.13), channel_id=1, source_target_pairs={{0,4},{4,0},{8,12},{12,8},{16,20},{20,16},{24,28},{28,24},{1,5},{5... | collective-permute-start | bytes 104456 | tf_op jit(solution)/shard_map/ppermute | solution.py:381
  9.7 1.6 %collective-permute-start.1 = (bf16[8,2176]{1,0:T(8,128)(2,1)S(1)}, bf16[8,2176]{1,0:T(8,128)(2,1)S(1)}, u32[]{:S(2)}, u32[]{:S(2)}) collective-permute-start(bf16[8,2176]{1,0:T(8,128)(2,1)S(1)} %get-tuple-element.13), channel_id=1, source_target_pairs={{0,8},{4,12},{8,0},{12,4},{16,24},{20,28},{24,16},{28,20},{1,9},{5... | collective-permute-start | bytes 104456 | tf_op jit(solution)/shard_map/ppermute | solution.py:381
  11.3 0.0 collective-permute-start.2
  11.3 0.1 pad_add_fusion.c_ref.refs_0_
  11.3 1.6 %copy-done.4 = bf16[8,256,512]{2,1,0:T(8,128)(2,1)S(1)} copy-done((bf16[8,256,512]{2,1,0:T(8,128)(2,1)S(1)}, bf16[8,256,512]{2,1,0:T(8,128)(2,1)}, u32[]{:S(2)}) %copy-start.4) | copy-done | bytes 2097176
  12.9 0.7 copy-done.7
  13.7 0.7 copy-done.8
  14.3 3.9 %shard_map.123 = (bf16[64,8,256]{2,1,0:T(8,128)(2,1)S(1)}, bf16[64,8,256]{2,1,0:T(8,128)(2,1)S(1)}, bf16[64,8,256]{2,1,0:T(8,128)(2,1)S(1)}, bf16[64,8,256]{2,1,0:T(8,128)(2,1)S(1)}) custom-call(s32[4]{0:T(128)S(1)} %pad_add_fusion.c_ref.refs_0_, bf16[8,256,512]{2,1,0:T(8,128)(2,1)S(1)} %copy-done.4, s32[2,8,256]{2,1,0:T(8,128)S(1)} %copy-done.7, ...), custom_call_target="tpu_custom_call" | custom-call | flops 4000000000 | tf_op jit(solution)/shard_map/pallas_call | solution.py:457
  18.2 2.0 %collective-permute-start.3 = (bf16[64,8,256]{2,1,0:T(8,128)(2,1)S(1)}, bf16[64,8,256]{2,1,0:T(8,128)(2,1)S(1)}, u32[]{:S(2)}, u32[]{:S(2)}) collective-permute-start(bf16[64,8,256]{2,1,0:T(8,128)(2,1)S(1)} %get-tuple-element.16), channel_id=1, source_target_pairs={{0,4},{4,0},{8,12},{12,8},{16,20},{20,16},{24,28},{28,24},{1,5},{5... | collective-permute-start | bytes 786440 | tf_op jit(solution)/shard_map/ppermute | solution.py:381
  20.2 1.6 %collective-permute-start.4 = (bf16[64,8,256]{2,1,0:T(8,128)(2,1)S(1)}, bf16[64,8,256]{2,1,0:T(8,128)(2,1)S(1)}, u32[]{:S(2)}, u32[]{:S(2)}) collective-permute-start(bf16[64,8,256]{2,1,0:T(8,128)(2,1)S(1)} %get-tuple-element.17), channel_id=1, source_target_pairs={{0,8},{4,12},{8,0},{12,4},{16,24},{20,28},{24,16},{28,20},{1,9},{5... | collective-permute-start | bytes 786440 | tf_op jit(solution)/shard_map/ppermute | solution.py:381
  21.8 4.0 %all-to-all-start = ((bf16[8,64,1024]{2,1,0:T(8,128)(2,1)}), bf16[8,64,1024]{2,1,0:T(8,128)(2,1)S(1)}, u32[]{:S(2)}, u32[]{:S(2)}) async-start(bf16[8,64,1024]{2,1,0:T(8,128)(2,1)} %get-tuple-element.14), calls=%async_computation | async-start | bytes 2097152 | tf_op jit(solution)/shard_map/all_to_all | solution.py:444
  25.8 0.6 constant_dynamic-update-slice_fusion.3
  26.4 0.0 collective-permute-done
  26.4 2.9 %collective-permute-start.5 = (bf16[64,8,256]{2,1,0:T(8,128)(2,1)S(1)}, bf16[64,8,256]{2,1,0:T(8,128)(2,1)S(1)}, u32[]{:S(2)}, u32[]{:S(2)}) collective-permute-start(bf16[64,8,256]{2,1,0:T(8,128)(2,1)S(1)} %get-tuple-element.18), channel_id=1, source_target_pairs={{0,12},{4,8},{8,4},{12,0},{16,28},{20,24},{24,20},{28,16},{1,13},{... | collective-permute-start | bytes 786440 | tf_op jit(solution)/shard_map/ppermute | solution.py:381
  29.3 0.6 constant_dynamic-update-slice_fusion.2
  29.9 0.6 constant_dynamic-update-slice_fusion.1
  30.6 0.0 collective-permute-done.2
  30.6 0.6 constant_dynamic-update-slice_fusion
  31.2 0.9 slice.25.refs_12_
  32.1 0.1 collective-permute-start.6
  32.2 0.1 dynamic-slice_convert_fusion
  32.3 0.1 reshape.36
  32.4 0.1 copy.15
  32.4 0.1 min.20
  32.5 0.1 min.21
  32.6 1.5 %collective-permute-start.7 = (bf16[32,2048]{1,0:T(8,128)(2,1)S(1)}, bf16[32,2048]{1,0:T(8,128)(2,1)S(1)}, u32[]{:S(2)}, u32[]{:S(2)}) collective-permute-start(bf16[32,2048]{1,0:T(8,128)(2,1)S(1)} %slice.25.refs_12_), channel_id=1, source_target_pairs={{0,2},{1,3},{2,0},{3,1},{4,6},{5,7},{6,4},{7,5},{8,10},{9,11},{10,... | collective-permute-start | bytes 393224 | tf_op jit(solution)/shard_map/ppermute | solution.py:381
  34.1 0.8 convert_reduce_fusion
  34.9 0.1 min.23
  35.0 0.0 collective-permute-done.6.refs_13_
  35.0 0.3 collective-permute-start.8
  35.4 0.1 pad_maximum_fusion.refs_1_
  35.5 3.5 %collective-permute-done.7.refs_14_ = bf16[32,2048]{1,0:T(8,128)(2,1)S(1)} collective-permute-done((bf16[32,2048]{1,0:T(8,128)(2,1)S(1)}, bf16[32,2048]{1,0:T(8,128)(2,1)S(1)}, u32[]{:S(2)}, u32[]{:S(2)}) %collective-permute-start.7) | collective-permute-done | bytes 131104 | tf_op jit(solution)/shard_map/ppermute | solution.py:381
  38.9 2.0 %collective-permute-done.8.refs_15_ = bf16[32,2048]{1,0:T(8,128)(2,1)S(1)} collective-permute-done((bf16[32,2048]{1,0:T(8,128)(2,1)S(1)}, bf16[32,2048]{1,0:T(8,128)(2,1)S(1)}, u32[]{:S(2)}, u32[]{:S(2)}) %collective-permute-start.8) | collective-permute-done | bytes 131104 | tf_op jit(solution)/shard_map/ppermute | solution.py:381
  40.9 0.6 copy-done.5
  41.6 7.1 %collective-permute-done.5.refs_11_ = bf16[64,8,256]{2,1,0:T(8,128)(2,1)S(1)} collective-permute-done((bf16[64,8,256]{2,1,0:T(8,128)(2,1)S(1)}, bf16[64,8,256]{2,1,0:T(8,128)(2,1)S(1)}, u32[]{:S(2)}, u32[]{:S(2)}) %collective-permute-start.5) | collective-permute-done | bytes 262176 | tf_op jit(solution)/shard_map/ppermute | solution.py:381
  48.7 1.4 %all-to-all-done.refs_7_ = bf16[8,64,1024]{2,1,0:T(8,128)(2,1)S(1)} async-done(((bf16[8,64,1024]{2,1,0:T(8,128)(2,1)}), bf16[8,64,1024]{2,1,0:T(8,128)(2,1)S(1)}, u32[]{:S(2)}, u32[]{:S(2)}) %all-to-all-start) | async-done | bytes 1048608 | tf_op jit(solution)/shard_map/all_to_all | solution.py:444
  50.2 0.9 copy-done.6
  51.1 0.9 copy-done.9
  52.0 0.9 copy-done.10
  52.9 0.9 copy-done.11
  53.8 0.9 copy-done.12
  54.7 0.9 copy-done.14
  55.6 19.7 %shard_map.124 = (s16[8,64,1152]{2,1,0:T(8,128)(2,1)}, f32[32,2048]{1,0:T(8,128)S(1)}, f32[32,2048]{1,0:T(8,128)S(1)}, f32[32,2048]{1,0:T(8,128)S(1)}, f32[32,2048]{1,0:T(8,128)S(1)}) custom-call(s32[4]{0:T(128)S(1)} %pad_add_fusion.c_ref.refs_0_, f32[32,128]{1,0:T(8,128)S(1)} %pad_maximum_fusion.refs_1_, bf16[256,256]{1,0:T(8,128)(2,1)S(1)} %fusion.eye_ref.refs_2_, ...), custom_call_target="tpu_custom_call" | custom-call | flops 10000000000 | tf_op jit(solution)/shard_map/pallas_call | solution.py:490
  75.3 5.2 %all-to-all-start.1 = ((s16[8,64,1152]{2,1,0:T(8,128)(2,1)}), s16[8,64,1152]{2,1,0:T(8,128)(2,1)S(1)}, u32[]{:S(2)}, u32[]{:S(2)}) async-start(s16[8,64,1152]{2,1,0:T(8,128)(2,1)} %get-tuple-element.23), calls=%async_computation.1 | async-start | bytes 2359296 | tf_op jit(solution)/shard_map/all_to_all | solution.py:512
  80.6 1.6 %collective-permute-start.10 = (f32[32,2048]{1,0:T(8,128)S(1)}, f32[32,2048]{1,0:T(8,128)S(1)}, u32[]{:S(2)}, u32[]{:S(2)}) collective-permute-start(f32[32,2048]{1,0:T(8,128)S(1)} %get-tuple-element.21), channel_id=1, source_target_pairs={{0,2},{1,3},{2,0},{3,1},{4,6},{5,7},{6,4},{7,5},{8,10},{9,11},{10,... | collective-permute-start | bytes 786440 | tf_op jit(solution)/shard_map/ppermute | solution.py:381
  82.2 0.0 collective-permute-start.11
  82.2 0.6 collective-permute-start.9
  82.8 6.1 %collective-permute-done.10 = f32[32,2048]{1,0:T(8,128)S(1)} collective-permute-done((f32[32,2048]{1,0:T(8,128)S(1)}, f32[32,2048]{1,0:T(8,128)S(1)}, u32[]{:S(2)}, u32[]{:S(2)}) %collective-permute-start.10) | collective-permute-done | bytes 262176 | tf_op jit(solution)/shard_map/ppermute | solution.py:381
  88.9 2.7 %collective-permute-done.11 = f32[32,2048]{1,0:T(8,128)S(1)} collective-permute-done((f32[32,2048]{1,0:T(8,128)S(1)}, f32[32,2048]{1,0:T(8,128)S(1)}, u32[]{:S(2)}, u32[]{:S(2)}) %collective-permute-start.11) | collective-permute-done | bytes 262176 | tf_op jit(solution)/shard_map/ppermute | solution.py:381
  91.6 0.1 add_add_fusion
  91.7 2.0 %collective-permute-start.12 = (f32[8,2048]{1,0:T(8,128)S(1)}, f32[8,2048]{1,0:T(8,128)S(1)}, u32[]{:S(2)}, u32[]{:S(2)}) collective-permute-start(f32[8,2048]{1,0:T(8,128)S(1)} %get-tuple-element.24), channel_id=1, source_target_pairs={{0,4},{4,0},{8,12},{12,8},{16,20},{20,16},{24,28},{28,24},{1,5},{5... | collective-permute-start | bytes 196616 | tf_op jit(solution)/shard_map/ppermute | solution.py:381
  93.7 1.5 %collective-permute-start.13 = (f32[8,2048]{1,0:T(8,128)S(1)}, f32[8,2048]{1,0:T(8,128)S(1)}, u32[]{:S(2)}, u32[]{:S(2)}) collective-permute-start(f32[8,2048]{1,0:T(8,128)S(1)} %get-tuple-element.26), channel_id=1, source_target_pairs={{0,8},{4,12},{8,0},{12,4},{16,24},{20,28},{24,16},{28,20},{1,9},{5... | collective-permute-start | bytes 196616 | tf_op jit(solution)/shard_map/ppermute | solution.py:381
  95.2 0.1 collective-permute-start.14
  95.3 1.8 %collective-permute-done.12 = f32[8,2048]{1,0:T(8,128)S(1)} collective-permute-done((f32[8,2048]{1,0:T(8,128)S(1)}, f32[8,2048]{1,0:T(8,128)S(1)}, u32[]{:S(2)}, u32[]{:S(2)}) %collective-permute-start.12) | collective-permute-done | bytes 65568 | tf_op jit(solution)/shard_map/ppermute | solution.py:381
  97.1 3.2 %collective-permute-done.13 = f32[8,2048]{1,0:T(8,128)S(1)} collective-permute-done((f32[8,2048]{1,0:T(8,128)S(1)}, f32[8,2048]{1,0:T(8,128)S(1)}, u32[]{:S(2)}, u32[]{:S(2)}) %collective-permute-start.13) | collective-permute-done | bytes 65568 | tf_op jit(solution)/shard_map/ppermute | solution.py:381
  100.3 2.4 %collective-permute-done.14 = f32[8,2048]{1,0:T(8,128)S(1)} collective-permute-done((f32[8,2048]{1,0:T(8,128)S(1)}, f32[8,2048]{1,0:T(8,128)S(1)}, u32[]{:S(2)}, u32[]{:S(2)}) %collective-permute-start.14) | collective-permute-done | bytes 65568 | tf_op jit(solution)/shard_map/ppermute | solution.py:381
  102.8 0.7 fusion.3
  103.5 4.0 %all-to-all-done.1.refs_0_ = s16[8,64,1152]{2,1,0:T(8,128)(2,1)S(1)} async-done(((s16[8,64,1152]{2,1,0:T(8,128)(2,1)}), s16[8,64,1152]{2,1,0:T(8,128)(2,1)S(1)}, u32[]{:S(2)}, u32[]{:S(2)}) %all-to-all-start.1) | async-done | bytes 1179680 | tf_op jit(solution)/shard_map/all_to_all | solution.py:512
  107.5 1.3 %shard_map.125 = f32[1024,256]{1,0:T(8,128)} custom-call(s32[1,256]{1,0:T(1,128)S(1)} %bitcast.9, s16[8,64,1152]{2,1,0:T(8,128)(2,1)S(1)} %all-to-all-done.1.refs_0_), custom_call_target="tpu_custom_call" | custom-call | tf_op jit(solution)/shard_map/pallas_call | solution.py:514
  (28 shorter events, 0.1 us)
Async XLA Ops:
  1.4 1.0 copy-start
  2.4 0.8 copy-start.1
  3.2 0.7 copy-start.2
  6.7 19.7 %collective-permute-start = (bf16[8,2176]{1,0:T(8,128)(2,1)S(1)}, bf16[8,2176]{1,0:T(8,128)(2,1)S(1)}, u32[]{:S(2)}, u32[]{:S(2)}) collective-permute-start(bf16[8,2176]{1,0:T(8,128)(2,1)S(1)} %get-tuple-element.13), channel_id=1, source_target_pairs={{0,4},{4,0},{8,12},{12,8},{16,20},{20,16},{24,28},{28,24},{1,5},{5... | collective-permute-start | bytes 104456 | tf_op jit(solution)/shard_map/ppermute | solution.py:381
  9.7 20.3 %collective-permute-start.1 = (bf16[8,2176]{1,0:T(8,128)(2,1)S(1)}, bf16[8,2176]{1,0:T(8,128)(2,1)S(1)}, u32[]{:S(2)}, u32[]{:S(2)}) collective-permute-start(bf16[8,2176]{1,0:T(8,128)(2,1)S(1)} %get-tuple-element.13), channel_id=1, source_target_pairs={{0,8},{4,12},{8,0},{12,4},{16,24},{20,28},{24,16},{28,20},{1,9},{5... | collective-permute-start | bytes 104456 | tf_op jit(solution)/shard_map/ppermute | solution.py:381
  11.3 19.3 %collective-permute-start.2 = (bf16[8,2176]{1,0:T(8,128)(2,1)S(1)}, bf16[8,2176]{1,0:T(8,128)(2,1)S(1)}, u32[]{:S(2)}, u32[]{:S(2)}) collective-permute-start(bf16[8,2176]{1,0:T(8,128)(2,1)S(1)} %get-tuple-element.13), channel_id=1, source_target_pairs={{0,12},{4,8},{8,4},{12,0},{16,28},{20,24},{24,20},{28,16},{1,13},{... | collective-permute-start | bytes 104456 | tf_op jit(solution)/shard_map/ppermute | solution.py:381
  11.3 1.6 %copy-start.4 = (bf16[8,256,512]{2,1,0:T(8,128)(2,1)S(1)}, bf16[8,256,512]{2,1,0:T(8,128)(2,1)}, u32[]{:S(2)}) copy-start(bf16[8,256,512]{2,1,0:T(8,128)(2,1)} %observed_from.1) | copy-start | bytes 6291460
  12.9 0.7 copy-start.7
  13.7 0.7 copy-start.8
  18.2 12.3 %copy-start.13 = (bf16[64,8,256]{2,1,0:T(8,128)(2,1)}, bf16[64,8,256]{2,1,0:T(8,128)(2,1)S(1)}, u32[]{:S(2)}) copy-start(bf16[64,8,256]{2,1,0:T(8,128)(2,1)S(1)} %get-tuple-element.15.refs_8_) | copy-start | bytes 786436
  18.2 23.3 %collective-permute-start.3 = (bf16[64,8,256]{2,1,0:T(8,128)(2,1)S(1)}, bf16[64,8,256]{2,1,0:T(8,128)(2,1)S(1)}, u32[]{:S(2)}, u32[]{:S(2)}) collective-permute-start(bf16[64,8,256]{2,1,0:T(8,128)(2,1)S(1)} %get-tuple-element.16), channel_id=1, source_target_pairs={{0,4},{4,0},{8,12},{12,8},{16,20},{20,16},{24,28},{28,24},{1,5},{5... | collective-permute-start | bytes 786440 | tf_op jit(solution)/shard_map/ppermute | solution.py:381
  20.2 21.4 %collective-permute-start.4 = (bf16[64,8,256]{2,1,0:T(8,128)(2,1)S(1)}, bf16[64,8,256]{2,1,0:T(8,128)(2,1)S(1)}, u32[]{:S(2)}, u32[]{:S(2)}) collective-permute-start(bf16[64,8,256]{2,1,0:T(8,128)(2,1)S(1)} %get-tuple-element.17), channel_id=1, source_target_pairs={{0,8},{4,12},{8,0},{12,4},{16,24},{20,28},{24,16},{28,20},{1,9},{5... | collective-permute-start | bytes 786440 | tf_op jit(solution)/shard_map/ppermute | solution.py:381
  21.8 10.4 %copy-start.3 = (s32[256]{0:T(256)S(1)}, s32[256]{0:T(256)}, u32[]{:S(2)}) copy-start(s32[256]{0:T(256)} %param.14) | copy-start | bytes 3076
  21.8 28.4 %all-to-all-start = ((bf16[8,64,1024]{2,1,0:T(8,128)(2,1)}), bf16[8,64,1024]{2,1,0:T(8,128)(2,1)S(1)}, u32[]{:S(2)}, u32[]{:S(2)}) async-start(bf16[8,64,1024]{2,1,0:T(8,128)(2,1)} %get-tuple-element.14), calls=%async_computation | async-start | bytes 2097152 | tf_op jit(solution)/shard_map/all_to_all | solution.py:444
  26.4 22.3 %collective-permute-start.5 = (bf16[64,8,256]{2,1,0:T(8,128)(2,1)S(1)}, bf16[64,8,256]{2,1,0:T(8,128)(2,1)S(1)}, u32[]{:S(2)}, u32[]{:S(2)}) collective-permute-start(bf16[64,8,256]{2,1,0:T(8,128)(2,1)S(1)} %get-tuple-element.18), channel_id=1, source_target_pairs={{0,12},{4,8},{8,4},{12,0},{16,28},{20,24},{24,20},{28,16},{1,13},{... | collective-permute-start | bytes 786440 | tf_op jit(solution)/shard_map/ppermute | solution.py:381
  32.1 2.9 %collective-permute-start.6 = (bf16[32,2048]{1,0:T(8,128)(2,1)S(1)}, bf16[32,2048]{1,0:T(8,128)(2,1)S(1)}, u32[]{:S(2)}, u32[]{:S(2)}) collective-permute-start(bf16[32,2048]{1,0:T(8,128)(2,1)S(1)} %slice.25.refs_12_), channel_id=1, source_target_pairs={{0,1},{1,0},{2,3},{3,2},{4,5},{5,4},{6,7},{7,6},{8,9},{9,8},{10,11... | collective-permute-start | bytes 393224 | tf_op jit(solution)/shard_map/ppermute | solution.py:381
  32.6 6.3 %collective-permute-start.7 = (bf16[32,2048]{1,0:T(8,128)(2,1)S(1)}, bf16[32,2048]{1,0:T(8,128)(2,1)S(1)}, u32[]{:S(2)}, u32[]{:S(2)}) collective-permute-start(bf16[32,2048]{1,0:T(8,128)(2,1)S(1)} %slice.25.refs_12_), channel_id=1, source_target_pairs={{0,2},{1,3},{2,0},{3,1},{4,6},{5,7},{6,4},{7,5},{8,10},{9,11},{10,... | collective-permute-start | bytes 393224 | tf_op jit(solution)/shard_map/ppermute | solution.py:381
  35.0 5.9 %collective-permute-start.8 = (bf16[32,2048]{1,0:T(8,128)(2,1)S(1)}, bf16[32,2048]{1,0:T(8,128)(2,1)S(1)}, u32[]{:S(2)}, u32[]{:S(2)}) collective-permute-start(bf16[32,2048]{1,0:T(8,128)(2,1)S(1)} %slice.25.refs_12_), channel_id=1, source_target_pairs={{0,3},{1,2},{2,1},{3,0},{4,7},{5,6},{6,5},{7,4},{8,11},{9,10},{10,... | collective-permute-start | bytes 393224 | tf_op jit(solution)/shard_map/ppermute | solution.py:381
  40.9 0.7 copy-start.5
  50.1 0.9 copy-start.6
  51.1 0.9 copy-start.9
  52.0 0.9 copy-start.10
  52.9 0.9 copy-start.11
  53.8 0.9 copy-start.12
  54.7 0.9 copy-start.14
  75.3 32.2 %all-to-all-start.1 = ((s16[8,64,1152]{2,1,0:T(8,128)(2,1)}), s16[8,64,1152]{2,1,0:T(8,128)(2,1)S(1)}, u32[]{:S(2)}, u32[]{:S(2)}) async-start(s16[8,64,1152]{2,1,0:T(8,128)(2,1)} %get-tuple-element.23), calls=%async_computation.1 | async-start | bytes 2359296 | tf_op jit(solution)/shard_map/all_to_all | solution.py:512
  80.6 22.2 %copy-start.15 = (s32[8]{0:T(128)S(1)}, s32[8]{0:T(128)}, u32[]{:S(2)}) copy-start(s32[8]{0:T(128)} %param.13) | copy-start | bytes 100
  80.6 8.3 %collective-permute-start.10 = (f32[32,2048]{1,0:T(8,128)S(1)}, f32[32,2048]{1,0:T(8,128)S(1)}, u32[]{:S(2)}, u32[]{:S(2)}) collective-permute-start(f32[32,2048]{1,0:T(8,128)S(1)} %get-tuple-element.21), channel_id=1, source_target_pairs={{0,2},{1,3},{2,0},{3,1},{4,6},{5,7},{6,4},{7,5},{8,10},{9,11},{10,... | collective-permute-start | bytes 786440 | tf_op jit(solution)/shard_map/ppermute | solution.py:381
  82.2 9.5 %collective-permute-start.11 = (f32[32,2048]{1,0:T(8,128)S(1)}, f32[32,2048]{1,0:T(8,128)S(1)}, u32[]{:S(2)}, u32[]{:S(2)}) collective-permute-start(f32[32,2048]{1,0:T(8,128)S(1)} %get-tuple-element.22), channel_id=1, source_target_pairs={{0,3},{1,2},{2,1},{3,0},{4,7},{5,6},{6,5},{7,4},{8,11},{9,10},{10,... | collective-permute-start | bytes 786440 | tf_op jit(solution)/shard_map/ppermute | solution.py:381
  82.2 9.5 %collective-permute-start.9 = (f32[32,2048]{1,0:T(8,128)S(1)}, f32[32,2048]{1,0:T(8,128)S(1)}, u32[]{:S(2)}, u32[]{:S(2)}) collective-permute-start(f32[32,2048]{1,0:T(8,128)S(1)} %get-tuple-element.20), channel_id=1, source_target_pairs={{0,1},{1,0},{2,3},{3,2},{4,5},{5,4},{6,7},{7,6},{8,9},{9,8},{10,11... | collective-permute-start | bytes 786440 | tf_op jit(solution)/shard_map/ppermute | solution.py:381
  91.7 5.4 %collective-permute-start.12 = (f32[8,2048]{1,0:T(8,128)S(1)}, f32[8,2048]{1,0:T(8,128)S(1)}, u32[]{:S(2)}, u32[]{:S(2)}) collective-permute-start(f32[8,2048]{1,0:T(8,128)S(1)} %get-tuple-element.24), channel_id=1, source_target_pairs={{0,4},{4,0},{8,12},{12,8},{16,20},{20,16},{24,28},{28,24},{1,5},{5... | collective-permute-start | bytes 196616 | tf_op jit(solution)/shard_map/ppermute | solution.py:381
  93.7 6.6 %collective-permute-start.13 = (f32[8,2048]{1,0:T(8,128)S(1)}, f32[8,2048]{1,0:T(8,128)S(1)}, u32[]{:S(2)}, u32[]{:S(2)}) collective-permute-start(f32[8,2048]{1,0:T(8,128)S(1)} %get-tuple-element.26), channel_id=1, source_target_pairs={{0,8},{4,12},{8,0},{12,4},{16,24},{20,28},{24,16},{28,20},{1,9},{5... | collective-permute-start | bytes 196616 | tf_op jit(solution)/shard_map/ppermute | solution.py:381
  95.2 7.6 %collective-permute-start.14 = (f32[8,2048]{1,0:T(8,128)S(1)}, f32[8,2048]{1,0:T(8,128)S(1)}, u32[]{:S(2)}, u32[]{:S(2)}) collective-permute-start(f32[8,2048]{1,0:T(8,128)S(1)} %get-tuple-element.25), channel_id=1, source_target_pairs={{0,12},{4,8},{8,4},{12,0},{16,28},{20,24},{24,20},{28,16},{1,13},{... | collective-permute-start | bytes 196616 | tf_op jit(solution)/shard_map/ppermute | solution.py:381

commit v4 on v1

v4 whole, which is shorter than its diff:
```python
import functools
import math

import jax
import jax.numpy as jnp
import numpy as np
from jax import lax
from jax.experimental import pallas as pl
from jax.experimental.pallas import tpu as pltpu
from jax.sharding import PartitionSpec as P

L = 512
S = 16
F = 256

env_floor = 0.05
misfit_scale = 0.03125
GROUP = 4
LANES = 128
FB = LANES // (2 * S)
WIDTH = 8
FIXED = 32000.0


def lag_tables(freq_total, lag_total):
    half = lag_total // 2
    freq_ids = np.arange(freq_total)[:, None]
    phase = 2.0 * np.pi * (freq_ids * np.arange(half)[None, :] % lag_total) / lag_total
    cosine = np.cos(phase) / math.sqrt(freq_total)
    sine = np.sin(phase) / math.sqrt(freq_total)
    back = [np.concatenate([cosine[p::2], sine[p::2]], axis=1) for p in (0, 1)]
    ahead = [np.concatenate([cosine[p::2].T, sine[p::2].T], axis=1) for p in (0, 1)]
    back = [np.concatenate([t[:, :half], t[:, half:]], axis=0) for t in back]
    whole = np.concatenate(ahead + back, axis=0)
    return jnp.asarray(whole.astype(np.float32)).astype(jnp.bfloat16)


def nt(a, b):
    return lax.dot_general(a, b, (((1,), (1,)), ((), ())), preferred_element_type=jnp.float32)


def nn(a, b):
    return jnp.dot(a, b, preferred_element_type=jnp.float32)


def tn(a, b):
    return lax.dot_general(a, b, (((0,), (0,)), ((), ())), preferred_element_type=jnp.float32)


def eye_of(size):
    rows = lax.broadcasted_iota(jnp.int32, (size, size), 0)
    lanes = lax.broadcasted_iota(jnp.int32, (size, size), 1)
    return jnp.where(rows == lanes, 1.0, 0.0).astype(jnp.bfloat16)


def turn_kernel(spectra_from, counts_from, v_to, spectra_ref, counts_ref, turned_ref, sems):
    k_own, col_total = spectra_ref.shape
    rcv_total, cols, _ = v_to.shape
    members = col_total // cols
    width = min(k_own, 2 * LANES)
    copies = [pltpu.make_async_copy(counts_from, counts_ref, sems.at[0])]
    for n, begin in enumerate(range(0, k_own, width)):
        rows = pl.ds(begin, width)
        copies.append(
            pltpu.make_async_copy(spectra_from.at[rows], spectra_ref.at[rows], sems.at[1 + n])
        )
    for copy in copies:
        copy.start()
    eye = eye_of(col_total)
    seg_ids = lax.broadcasted_iota(jnp.int32, (width, col_total), 0) % S
    copies[0].wait()
    inside = seg_ids < counts_ref[...]
    for n, begin in enumerate(range(0, k_own, width)):
        copies[1 + n].wait()
        part = spectra_ref[begin : begin + width, :].astype(jnp.float32)
        part = jnp.where(inside, part, 0.0).astype(jnp.bfloat16)
        turned_ref[:, begin : begin + width] = nt(eye, part).astype(jnp.bfloat16)
    copies = [
        pltpu.make_async_copy(
            turned_ref.at[pl.ds(dest % members * cols, cols)], v_to.at[dest], sems.at[dest]
        )
        for dest in range(rcv_total)
    ]
    for copy in copies:
        copy.start()
    for copy in copies:
        copy.wait()


def fold_kernel(c_ref, rcounts_ref, observed_from, rspectra_from, window_from, order_from, *rest):
    *out_to, observed_ref, rspectra_ref, window_ref, order_ref, line_ref, out_ref, sems, out_sems = (
        rest
    )
    row_total, col_total, lag_total = observed_ref.shape
    half = lag_total // 2
    members = len(out_to)
    cols = col_total // members
    lines = col_total * row_total
    quarter = rspectra_ref.shape[1]
    copies = [
        pltpu.make_async_copy(src, dst, sems.at[row_total + n])
        for n, (src, dst) in enumerate(
            [(window_from, window_ref), (order_from, order_ref), (rspectra_from, rspectra_ref)]
        )
    ] + [
        pltpu.make_async_copy(observed_from.at[i], observed_ref.at[i], sems.at[i])
        for i in range(row_total)
    ]
    for copy in copies:
        copy.start()
    for copy in copies[:3]:
        copy.wait()
    window = jnp.concatenate([window_ref[0], window_ref[1]], axis=0).astype(jnp.float32).T
    station = lax.broadcasted_iota(jnp.int32, (col_total, col_total), 0) + c_ref[1]
    pick = jnp.where(station == order_ref[...], 1.0, 0.0).astype(jnp.bfloat16)
    lag_ids = lax.broadcasted_iota(jnp.int32, (col_total, half), 1).astype(jnp.float32)
    for i in range(row_total):
        copies[3 + i].wait()
        begin = window[:, i : i + 1]
        end = begin + window[:, row_total + i : row_total + i + 1]
        values = observed_ref[i].astype(jnp.float32)
        low = (lag_ids >= begin) & (lag_ids < end)
        high = (lag_ids + half >= begin) & (lag_ids + half < end)
        folded = jnp.where(low, values[:, :half], jnp.where(high, -values[:, half:], 0.0))
        moved = nn(pick, folded.astype(jnp.bfloat16))
        for h in range(half // LANES):
            line_ref[pl.ds(h * lines + i, col_total, stride=row_total), :] = moved[
                :, h * LANES : (h + 1) * LANES
            ]
    row_ids = lax.broadcasted_iota(jnp.int32, (row_total, half), 0)
    counts = jnp.zeros((row_total, half), jnp.int32)
    for i in range(row_total):
        counts = jnp.where(row_ids == i, rcounts_ref[i], counts)
    seg_ids = lax.broadcasted_iota(jnp.int32, (row_total, half), 1) % S
    pieces = quarter // half
    for k in range(members):
        for n in range(pieces):
            part = rspectra_ref[:, n * half : (n + 1) * half].astype(jnp.float32)
            out_ref[k, cols + n] = jnp.where(seg_ids < counts, part, 0.0).astype(jnp.bfloat16)
        out_ref[k, cols + pieces] = counts.astype(jnp.float32).astype(jnp.bfloat16)
    mine = c_ref[0]
    copies = []
    for k in range(members):
        first = (mine ^ k) * (cols * row_total)
        for h in range(half // LANES):
            begin = pl.multiple_of(h * lines + first, cols * row_total)
            rows = line_ref[pl.ds(begin, cols * row_total), :]
            out_ref[k, :cols, :, h * LANES : (h + 1) * LANES] = rows.reshape(
                cols, row_total, LANES
            ).astype(jnp.bfloat16)
        copies.append(pltpu.make_async_copy(out_ref.at[k], out_to[k], out_sems.at[k]))
        copies[-1].start()
    for copy in copies:
        copy.wait()


def near_kernel(*refs):
    *parts, out_ref, sems = refs
    extra = out_ref.shape[1]
    copies = []
    for k, ref in enumerate(parts):
        rows = ref.at[pl.ds(ref.shape[0] - extra, extra)]
        copies.append(pltpu.make_async_copy(rows, out_ref.at[k], sems.at[k]))
        copies[-1].start()
    for copy in copies:
        copy.wait()


def pair_kernel(n_e, n_r, c_ref, invn_ref, table_ref, v_from, *refs):
    refs = list(refs)
    e_from, u_from = refs[:n_e], refs[n_e : n_e + n_r]
    w_to, *r_to = refs[n_e + n_r : n_e + 2 * n_r + 1]
    (
        x_ref, z_ref, plain_ref, turned_ref, code_ref, u_ref, v_ref, e_ref, r_ref, w_ref,
        sems, w_sems,
    ) = refs[n_e + 2 * n_r + 1 :]

    src_total, col_total, k_own = v_ref.shape
    ref_total, irec, k_quarter = r_ref.shape
    jj_total = LANES // (2 * irec)
    jp_total = col_total // jj_total
    k_total = src_total * k_own
    half_f = k_total // (4 * S)
    freq_total = 2 * half_f
    blocks = k_total // LANES
    own_blocks = k_own // LANES
    quarter_blocks = k_quarter // LANES

    quarter_me = c_ref[3]
    early = [pltpu.make_async_copy(v_from, v_ref, sems.at[0])]
    for k, ref in enumerate(u_from):
        early.append(pltpu.make_async_copy(ref, u_ref.at[quarter_me ^ k], sems.at[1 + k]))
    late = [
        pltpu.make_async_copy(ref.at[pl.ds(0, col_total)], e_ref.at[k], sems.at[1 + n_r + k])
        for k, ref in enumerate(e_from)
    ]
    for copy in early + late:
        copy.start()
    half = e_ref.shape[-1]
    eye = eye_of(half)
    table_y = [table_ref[p * half : (p + 1) * half, :] for p in range(2)]
    table_z = []
    for p in range(2):
        begin = 2 * half + p * 2 * half_f
        parts = [table_ref[begin + n * half_f : begin + (n + 1) * half_f, :] for n in range(2)]
        table_z.append(jnp.concatenate(parts, axis=1))

    group_ids = lax.broadcasted_iota(jnp.int32, (jp_total, LANES), 1) // (2 * S)
    first_part = lax.broadcasted_iota(jnp.int32, (irec, LANES), 1) % (2 * S) < S

    def lanes_of(fb, per):
        return fb // per, pl.multiple_of(fb % per * LANES, LANES)

    def v_block(fb):
        src, off = lanes_of(fb, own_blocks)
        parts = [
            v_ref[src, jj * jp_total : (jj + 1) * jp_total, pl.ds(off, LANES)]
            for jj in range(jj_total)
        ]
        zero = jnp.zeros((jp_total, LANES), jnp.bfloat16)
        rows = [
            jnp.concatenate([jnp.where(group_ids == f, part, zero) for part in parts], axis=1)
            for f in range(FB)
        ]
        return jnp.concatenate(rows, axis=0)

    def u_block(parts):
        zero = jnp.zeros((irec, LANES), jnp.bfloat16)
        return jnp.concatenate(
            [
                jnp.concatenate([part if k == jj else zero for k in range(jj_total)], axis=1)
                for part in parts
                for jj in range(jj_total)
            ],
            axis=0,
        )

    def place(fb, f):
        return pl.ds((f % 2) * half_f + fb * (FB // 2) + f // 2, jp_total, stride=freq_total)

    def forward(fb, _):
        lanes = pl.ds(pl.multiple_of(fb * LANES, LANES), LANES)
        quarter, off = lanes_of(fb, quarter_blocks)
        piece, off = off // half, pl.multiple_of(off % half, LANES)
        wide = u_ref[quarter, :, piece, :, pl.ds(off, LANES)].astype(jnp.float32)
        wide = wide.reshape(irec, LANES)
        part = wide.astype(jnp.bfloat16)
        plain_ref[:, lanes] = part
        crossed = jnp.where(first_part, pltpu.roll(wide, LANES - S, 1), -pltpu.roll(wide, S, 1))
        crossed = crossed.astype(jnp.bfloat16)
        turned_ref[:, lanes] = crossed
        out = nt(v_block(fb), u_block([part, crossed]))
        scale = invn_ref[...]
        for f in range(FB):
            x_ref[place(fb, f), :] = out[f * jp_total : (f + 1) * jp_total] * scale
        return 0

    for copy in early:
        copy.wait()
    lax.fori_loop(0, blocks, forward, 0, unroll=16)

    lane_ids = lax.broadcasted_iota(jnp.int32, (1, LANES), 1)
    sign = jnp.where(lane_ids < LANES // 2, -1.0, 1.0).astype(jnp.float32)

    sign = sign.astype(jnp.bfloat16)

    def pairs(step, _):
        cols = [step * WIDTH + k for k in range(WIDTH)]
        rhs_e, rhs_o, obs = [], [], []
        for jp in cols:
            x = x_ref[pl.ds(pl.multiple_of(jp * freq_total, freq_total), freq_total), :]
            plain = x.astype(jnp.bfloat16)
            turned = pltpu.roll(x, LANES // 2, 1).astype(jnp.bfloat16) * sign
            rhs_e.append(jnp.concatenate([plain[:half_f], turned[:half_f]], axis=0))
            rhs_o.append(jnp.concatenate([plain[half_f:], turned[half_f:]], axis=0))
            rows = [
                e_ref[:, jj * jp_total + jp].astype(jnp.float32).reshape(irec, half)
                for jj in range(jj_total)
            ]
            rows = jnp.concatenate(rows, axis=0).astype(jnp.bfloat16)
            obs += [rows, rows]
        even = nn(table_y[0], jnp.concatenate(rhs_e, axis=1))
        odd = nn(table_y[1], jnp.concatenate(rhs_o, axis=1))
        seen = nt(eye, jnp.concatenate(obs, axis=0))
        g_e, g_o = [], []
        for k in range(WIDTH):
            lanes = slice(k * LANES, (k + 1) * LANES)
            e, d0, d1 = seen[:, lanes], even[:, lanes], odd[:, lanes]
            d = jnp.where(e < 0.0, d0 + d1, d0 - d1)
            power = d * d
            power = power + (pltpu.roll(power, LANES // 2, 1) + env_floor)
            g = d * (1.0 - jnp.abs(e) * lax.rsqrt(power))
            side = jnp.where(e < 0.0, 1.0, jnp.where(e > 0.0, -1.0, 0.0)).astype(jnp.bfloat16)
            turned = pltpu.roll(g, LANES // 2, 1).astype(jnp.bfloat16)
            g_side = g.astype(jnp.bfloat16) * side
            t_side = turned * (side * -sign)
            g_e.append(jnp.concatenate([g_side * side, t_side * side], axis=0))
            g_o.append(jnp.concatenate([g_side, t_side], axis=0))
        z_e = nn(table_z[0], jnp.concatenate(g_e, axis=1))
        z_o = nn(table_z[1], jnp.concatenate(g_o, axis=1))
        for k, jp in enumerate(cols):
            lanes = slice(k * LANES, (k + 1) * LANES)
            scale = invn_ref[pl.ds(jp, 1), :] * misfit_scale
            base = pl.multiple_of(jp * freq_total, freq_total)
            z_ref[pl.ds(base, half_f), :] = z_e[:, lanes] * scale
            z_ref[pl.ds(base + half_f, half_f), :] = z_o[:, lanes] * scale
        return 0

    for copy in late:
        copy.wait()
    lax.fori_loop(0, jp_total // WIDTH, pairs, 0)

    def backward(fb):
        z = jnp.concatenate([z_ref[place(fb, f), :] for f in range(FB)], axis=0)
        z = z.astype(jnp.bfloat16)
        lanes = pl.ds(pl.multiple_of(fb * LANES, LANES), LANES)
        w = nn(z, u_block([plain_ref[:, lanes], turned_ref[:, lanes]]))
        totals = []
        for jj in range(jj_total):
            lanes = slice(jj * LANES, (jj + 1) * LANES)
            total = w[:jp_total, lanes]
            for f in range(1, FB):
                total = jnp.where(group_ids == f, w[f * jp_total : (f + 1) * jp_total, lanes], total)
            totals.append(total)
        total = jnp.concatenate(totals, axis=0)
        largest = jnp.max(jnp.abs(total), axis=0, keepdims=True)
        power = jnp.ceil(jnp.log2(jnp.maximum(largest, 1e-30)))
        code_ref[pl.ds(fb, 1), :] = power
        fixed = jnp.round(total * (jnp.exp2(-power) * FIXED)).astype(jnp.int32)
        src, off = lanes_of(fb, own_blocks)
        w_ref[src, :, pl.ds(off, LANES)] = fixed.astype(jnp.int16)
        r = tn(z, v_block(fb))
        sums = []
        for q in range(2):
            total = None
            for jj in range(jj_total):
                begin = (q * jj_total + jj) * irec
                part = r[begin : begin + irec, jj * LANES : (jj + 1) * LANES]
                total = part if total is None else total + part
            sums.append(total)
        crossed = jnp.where(
            first_part, -pltpu.roll(sums[1], LANES - S, 1), pltpu.roll(sums[1], S, 1)
        )
        quarter, off = lanes_of(fb, quarter_blocks)
        lanes = pl.ds(off, LANES)
        total = sums[0] + crossed
        r_ref[quarter, :, lanes] = total

    def w_copy(src):
        return pltpu.make_async_copy(w_ref.at[src], w_to.at[src], w_sems.at[src])

    def from_owner(src, _):
        for b in range(own_blocks):
            backward(src * own_blocks + b)
        codes = code_ref[pl.ds(src * own_blocks, own_blocks), :]
        codes = jnp.concatenate(
            [codes, jnp.zeros((col_total - own_blocks, LANES), jnp.float32)], axis=0
        )
        w_ref[src, :, k_own:] = codes.astype(jnp.int32).astype(jnp.int16)
        w_copy(src).start()
        return 0

    owners = src_total // ref_total
    outs = []
    for k, ref in enumerate(r_to):
        begin = (quarter_me ^ k) * owners
        lax.fori_loop(begin, begin + owners, from_owner, 0)
        outs.append(pltpu.make_async_copy(r_ref.at[quarter_me ^ k], ref, sems.at[k]))
        outs[-1].start()
    for copy in outs:
        copy.wait()
    for src in range(src_total):
        w_copy(src).wait()


def join_kernel(count_ref, got_ref, out_ref):
    src_total, cols, _ = got_ref.shape
    k_own, col_total = out_ref.shape
    members = col_total // cols
    seg_ids = lax.broadcasted_iota(jnp.int32, (LANES, col_total), 0) % S
    inside = seg_ids < count_ref[...]
    scales = [
        jnp.exp2(got_ref[src, :16, k_own:].astype(jnp.int32).astype(jnp.float32)) * (1.0 / FIXED)
        for src in range(src_total)
    ]
    for b in range(k_own // LANES):
        rows = []
        for m in range(members):
            total = None
            for src in range(m, src_total, members):
                part = got_ref[src, :, b * LANES : (b + 1) * LANES]
                part = part.astype(jnp.int32).astype(jnp.float32) * scales[src][b : b + 1]
                total = part if total is None else total + part
            rows.append(total)
        whole = jnp.concatenate(rows, axis=0).T
        out_ref[b * LANES : (b + 1) * LANES, :] = jnp.where(inside, whole, 0.0)


def swap(x, axis, total, k):
    return lax.ppermute(x, axis, [(r, r ^ k) for r in range(total)])


def shards(
    receiver_spectra,
    reference_spectra,
    receiver_counts,
    reference_counts,
    column_station,
    lag_window,
    observed,
    *,
    rcv_total,
    ref_total,
):
    row_total, k_quarter = receiver_spectra.shape
    k_own, col_total = reference_spectra.shape
    k_total = k_own * rcv_total
    lag_total = observed.shape[2]
    half = lag_total // 2
    members = math.gcd(GROUP, rcv_total)
    irec = row_total * members
    cols = col_total // members
    jj_total = LANES // (2 * irec)
    jp_total = cols // jj_total
    extra = k_quarter // half + 1
    bf16 = jnp.bfloat16
    place = lax.axis_index("rcv")
    mine = place % members
    quarter = lax.axis_index("ref")
    vmem = pl.BlockSpec(memory_space=pltpu.VMEM)
    smem = pl.BlockSpec(memory_space=pltpu.SMEM)
    hbm = pl.BlockSpec(memory_space=pl.ANY)
    scalars = jnp.stack([mine, quarter * col_total, place, quarter]).astype(jnp.int32)
    params = pltpu.CompilerParams(vmem_limit_bytes=32 * 1024 * 1024)
    free = pl.CostEstimate(flops=0, bytes_accessed=0, transcendentals=0)

    sent = pl.pallas_call(
        turn_kernel,
        out_shape=jax.ShapeDtypeStruct((rcv_total, cols, k_own), bf16),
        in_specs=[hbm] * 2,
        out_specs=hbm,
        scratch_shapes=[
            pltpu.VMEM((k_own, col_total), bf16),
            pltpu.VMEM((1, col_total), jnp.int32),
            pltpu.VMEM((col_total, k_own), bf16),
            pltpu.SemaphoreType.DMA((max(rcv_total, 1 + k_own // min(k_own, 2 * LANES)),)),
        ],
        compiler_params=params,
        cost_estimate=free,
    )(reference_spectra, reference_counts.reshape(1, col_total))
    v_all = lax.all_to_all(sent, "rcv", split_axis=0, concat_axis=0, tiled=True)

    _, observed = lax.optimization_barrier((sent, observed))
    shape = (cols + extra, row_total, half)
    folded = pl.pallas_call(
        fold_kernel,
        out_shape=[jax.ShapeDtypeStruct(shape, bf16)] * members,
        in_specs=[smem] * 2 + [hbm] * 4,
        out_specs=[hbm] * members,
        scratch_shapes=[
            pltpu.VMEM(observed.shape, bf16),
            pltpu.VMEM(receiver_spectra.shape, bf16),
            pltpu.VMEM(lag_window.shape, jnp.int32),
            pltpu.VMEM((1, col_total), jnp.int32),
            pltpu.VMEM((half // LANES * col_total * row_total, LANES), jnp.float32),
            pltpu.VMEM((members,) + shape, bf16),
            pltpu.SemaphoreType.DMA((row_total + 3,)),
            pltpu.SemaphoreType.DMA((members,)),
        ],
        compiler_params=params,
        cost_estimate=free,
    )(
        scalars,
        receiver_counts,
        observed,
        receiver_spectra,
        lag_window,
        column_station.reshape(1, col_total),
    )
    e_all = [folded[0]] + [swap(folded[k], "rcv", rcv_total, k) for k in range(1, members)]

    near = pl.pallas_call(
        near_kernel,
        out_shape=jax.ShapeDtypeStruct((members, extra, row_total, half), bf16),
        in_specs=[hbm] * members,
        out_specs=hbm,
        scratch_shapes=[pltpu.SemaphoreType.DMA((members,))],
        compiler_params=params,
        cost_estimate=free,
    )(*e_all)
    u_all = [near] + [swap(near, "ref", ref_total, k) for k in range(1, ref_total)]

    group_counts = near[:, extra - 1, :, 0].reshape(irec).astype(jnp.float32)
    own_counts = lax.dynamic_slice_in_dim(reference_counts, mine * cols, cols).astype(jnp.float32)
    counts = own_counts.reshape(jj_total, jp_total).T
    least = jnp.minimum(counts[:, :, None], group_counts[None, None, :])
    inverse = (1.0 / least).reshape(jp_total, jj_total * irec)
    inverse = jnp.concatenate([inverse, inverse], axis=1)

    table = lag_tables(k_total // (2 * S), lag_total)
    lines = jp_total * k_total // (2 * S)
    w_part, *r_all = pl.pallas_call(
        functools.partial(pair_kernel, members, ref_total),
        out_shape=[jax.ShapeDtypeStruct((rcv_total, cols, k_own + LANES), jnp.int16)]
        + [jax.ShapeDtypeStruct((irec, k_quarter), jnp.float32)] * ref_total,
        in_specs=[smem] + [vmem] * 2 + [hbm] * (1 + members + ref_total),
        out_specs=[hbm] * (1 + ref_total),
        scratch_shapes=[
            pltpu.VMEM((lines, LANES), jnp.float32),
            pltpu.VMEM((lines, LANES), jnp.float32),
            pltpu.VMEM((irec, k_total), bf16),
            pltpu.VMEM((irec, k_total), bf16),
            pltpu.VMEM((k_total // LANES, LANES), jnp.float32),
            pltpu.VMEM((ref_total,) + near.shape, bf16),
            pltpu.VMEM((rcv_total, cols, k_own), bf16),
            pltpu.VMEM((members, cols, row_total, half), bf16),
            pltpu.VMEM((ref_total, irec, k_quarter), jnp.float32),
            pltpu.VMEM((rcv_total, cols, k_own + LANES), jnp.int16),
            pltpu.SemaphoreType.DMA((1 + members + ref_total,)),
            pltpu.SemaphoreType.DMA((rcv_total,)),
        ],
        compiler_params=params,
        cost_estimate=free,
    )(scalars, inverse, table, v_all, *e_all, *u_all)

    got = lax.all_to_all(w_part, "rcv", split_axis=0, concat_axis=0, tiled=True)
    reference_grad = pl.pallas_call(
        join_kernel,
        out_shape=jax.ShapeDtypeStruct((k_own, col_total), jnp.float32),
        in_specs=[vmem] * 2,
        out_specs=vmem,
        compiler_params=params,
        cost_estimate=free,
    )(reference_counts.reshape(1, col_total), got)

    r_sum = r_all[0]
    for k in range(1, ref_total):
        r_sum = r_sum + swap(r_all[k], "ref", ref_total, k)
    parts = [r_sum[k * row_total : (k + 1) * row_total] for k in range(members)]
    r_sum = parts[0]
    for k in range(1, members):
        r_sum = r_sum + swap(parts[k], "rcv", rcv_total, k)
    seg_quarter = jnp.arange(k_quarter, dtype=jnp.int32) % S
    receiver_grad = jnp.where(seg_quarter[None, :] < receiver_counts[:, None], r_sum, 0.0)
    return (receiver_grad, reference_grad)


def solution(mesh):
    return jax.shard_map(
        functools.partial(shards, rcv_total=mesh.shape["rcv"], ref_total=mesh.shape["ref"]),
        mesh=mesh,
        in_specs=(
            P("rcv", "ref"),
            P("rcv", "ref"),
            P("rcv"),
            P("ref"),
            P("ref"),
            P(None, "rcv", "ref"),
            P("rcv", "ref", None),
        ),
        out_specs=(P("rcv", "ref"), P("rcv", "ref")),
        check_vma=False,
    )
```

time: 105 us -> 113 us (1.076)
  waiting for transfers between devices: 35.3 us -> 52.6 us
  Pallas kernels: 20 us -> 29.3 us
  other arithmetic: 8.59 us -> 1.11 us
  local copies, waits for them, and re-layouts: 13 us -> 5.96 us
  starting transfers between devices: 25.8 us -> 22.4 us
    ppermute x15 -> x12, waiting for transfers between devices: 31.3 us -> 48.6 us  [swap(): return lax.ppermute(x, axis, [(r, r ^ k) for r in range(total)])]
    pallas_call x1 -> x4, Pallas kernels: 18.6 us -> 28 us  [the longest x1 20.1 us: shards(): pl.pallas_call(functools.partial(pair_kernel, members, ref_total), out_sh...]
    ppermute x15 -> x12, starting transfers between devices: 15.7 us -> 11.2 us  [swap(): return lax.ppermute(x, axis, [(r, r ^ k) for r in range(total)])]
    optimization_barrier x1 -> x0, local copies, waits for them, and re-layouts: 2.86 us -> none  [shards(): lax.optimization_barrier((sent, observed, lag_window))]
    select_n x4 -> x0, other arithmetic: 2.76 us -> none  [the longest x1 1.06 us: shards(): jnp.where(low, observed[..., :half], jnp.where(high, -observed[..., half:...]
    squeeze x2 -> x0, local copies, waits for them, and re-layouts: 1.64 us -> none  [the longest x1 0.88 us: shards(): lax.dynamic_index_in_dim(folded, mine ^ k, 0, False)]
    unnamed x32 -> x34, local copies, waits for them, and re-layouts: 6.85 us -> 5.42 us
    concatenate x2 -> x0, other arithmetic: 1.43 us -> none  [the longest x1 0.81 us: shards(): jnp.concatenate([own] + [swap(own, 'rcv', rcv_total, k) for k in range(1,...]
  transfers between devices with their start and end apart: 17 -> 14, of which waited for: 10 -> 11; matrix products, arithmetic and copies ran while one was open for 14% -> 1% of each run, Pallas kernels for 0% -> 5%
where the time goes in v4:
time: 113 us; the launch traced here: 112 us
  waiting for transfers between devices  52.6 us (47%)
  Pallas kernels  29.3 us (26%)
  starting transfers between devices  22.4 us (20%)
  local copies, waits for them, and re-layouts  5.96 us (5%)
    ppermute x12, waiting for transfers between devices, swap(): return lax.ppermute(x, axis, [(r, r ^ k) for r in range(total)])  48.6 us
    pallas_call x1, Pallas kernels, shards(): pl.pallas_call(functools.partial(pair_kernel, members, ref_total), out_sh...  20.1 us
    ppermute x12, starting transfers between devices, swap(): return lax.ppermute(x, axis, [(r, r ^ k) for r in range(total)])  11.2 us
    all_to_all x1, starting transfers between devices, shards(): v_all = lax.all_to_all(sent, 'rcv', split_axis=0, concat_axis=0, tiled=True)  7.42 us
    unnamed x34, local copies, waits for them, and re-layouts  5.42 us
    pallas_call x1, Pallas kernels, shards(): pl.pallas_call(fold_kernel, out_shape=[jax.ShapeDtypeStruct(shape, bf16)]...  5 us
    all_to_all x1, waiting for transfers between devices, shards(): got = lax.all_to_all(w_part, 'rcv', split_axis=0, concat_axis=0, tiled=True)  3.95 us
    all_to_all x1, starting transfers between devices, shards(): got = lax.all_to_all(w_part, 'rcv', split_axis=0, concat_axis=0, tiled=True)  3.83 us
  transfers between devices with their start and end apart: 14, of which 11 were waited for; matrix products, arithmetic and copies ran while one was open for 1% of the time, Pallas kernels for 5%

profile of v4, /device:TPU:0, one launch (start us, length us, event | category | flops | bytes accessed | tf_op | source)
XLA Modules:
  0.0 112.2 jit_solution(3107966824721813556)
XLA Ops:
  0.6 1.0 copy-done.1
  1.7 0.7 copy-done.7
  2.4 2.7 %shard_map.95 = bf16[8,64,1024]{2,1,0:T(8,128)(2,1)} custom-call(bf16[1024,256]{1,0:T(8,128)(2,1)S(1)} %copy-done.1, s32[1,256]{1,0:T(1,128)S(1)} %bitcast.7), custom_call_target="tpu_custom_call" | custom-call | tf_op jit(solution)/shard_map/pallas_call | solution.py:437
  5.1 0.0 copy-start
  5.1 0.0 copy-start.5
  5.1 0.0 copy-start.9
  5.1 0.0 copy-start.10
  5.1 7.4 %all-to-all-start = ((bf16[8,64,1024]{2,1,0:T(8,128)(2,1)}), bf16[8,64,1024]{2,1,0:T(8,128)(2,1)S(1)}, u32[]{:S(2)}, u32[]{:S(2)}) async-start(bf16[8,64,1024]{2,1,0:T(8,128)(2,1)} %shard_map.95), calls=%async_computation | async-start | bytes 2097152 | tf_op jit(solution)/shard_map/all_to_all | solution.py:451
  12.6 0.1 pad_add_fusion.c_ref
  12.7 0.0 copy-done.6
  12.7 0.0 copy-done.9
  12.7 0.0 copy-done.10
  12.7 5.0 %shard_map.96 = (bf16[73,8,256]{2,1,0:T(8,128)(2,1)S(1)}, bf16[73,8,256]{2,1,0:T(8,128)(2,1)}, bf16[73,8,256]{2,1,0:T(8,128)(2,1)}, bf16[73,8,256]{2,1,0:T(8,128)(2,1)}) custom-call(s32[4]{0:T(128)S(1)} %pad_add_fusion.c_ref, s32[8]{0:T(128)S(1)} %copy-done.9, bf16[8,256,512]{2,1,0:T(8,128)(2,1)S(1)} %copy-done, bf16[8,2048]{1,0:T(8,128)(2,1)S(1)} %copy-done.5, ...), custom_call_target="tpu_custom_call" | custom-call | tf_op jit(solution)/shard_map/pallas_call | solution.py:455
  17.7 0.0 copy-start.2
  17.7 2.1 %collective-permute-start = (bf16[73,8,256]{2,1,0:T(8,128)(2,1)}, bf16[73,8,256]{2,1,0:T(8,128)(2,1)S(1)}, u32[]{:S(2)}, u32[]{:S(2)}) collective-permute-start(bf16[73,8,256]{2,1,0:T(8,128)(2,1)} %get-tuple-element.14), channel_id=1, source_target_pairs={{0,4},{4,0},{8,12},{12,8},{16,20},{20,16},{24,28},{28,24},{1,5},{5... | collective-permute-start | bytes 897032 | tf_op jit(solution)/shard_map/ppermute | solution.py:400
  19.8 1.5 %collective-permute-start.1 = (bf16[73,8,256]{2,1,0:T(8,128)(2,1)}, bf16[73,8,256]{2,1,0:T(8,128)(2,1)S(1)}, u32[]{:S(2)}, u32[]{:S(2)}) collective-permute-start(bf16[73,8,256]{2,1,0:T(8,128)(2,1)} %get-tuple-element.15), channel_id=1, source_target_pairs={{0,8},{4,12},{8,0},{12,4},{16,24},{20,28},{24,16},{28,20},{1,9},{5... | collective-permute-start | bytes 897032 | tf_op jit(solution)/shard_map/ppermute | solution.py:400
  21.2 0.1 collective-permute-start.2
  21.3 0.1 dynamic-slice_convert_fusion
  21.4 0.1 reshape.35
  21.5 0.1 copy.11
  21.6 0.1 min.20
  21.7 0.1 min.21
  21.8 11.0 %collective-permute-done.refs_1_ = bf16[73,8,256]{2,1,0:T(8,128)(2,1)S(1)} collective-permute-done((bf16[73,8,256]{2,1,0:T(8,128)(2,1)}, bf16[73,8,256]{2,1,0:T(8,128)(2,1)S(1)}, u32[]{:S(2)}, u32[]{:S(2)}) %collective-permute-start) | collective-permute-done | bytes 299040 | tf_op jit(solution)/shard_map/ppermute | solution.py:400
  32.8 6.1 %collective-permute-done.1.refs_2_ = bf16[73,8,256]{2,1,0:T(8,128)(2,1)S(1)} collective-permute-done((bf16[73,8,256]{2,1,0:T(8,128)(2,1)}, bf16[73,8,256]{2,1,0:T(8,128)(2,1)S(1)}, u32[]{:S(2)}, u32[]{:S(2)}) %collective-permute-start.1) | collective-permute-done | bytes 299040 | tf_op jit(solution)/shard_map/ppermute | solution.py:400
  38.9 6.6 %collective-permute-done.2.refs_3_ = bf16[73,8,256]{2,1,0:T(8,128)(2,1)S(1)} collective-permute-done((bf16[73,8,256]{2,1,0:T(8,128)(2,1)}, bf16[73,8,256]{2,1,0:T(8,128)(2,1)S(1)}, u32[]{:S(2)}, u32[]{:S(2)}) %collective-permute-start.2) | collective-permute-done | bytes 299040 | tf_op jit(solution)/shard_map/ppermute | solution.py:400
  45.5 0.2 shard_map.97.refs_4_
  45.7 0.1 collective-permute-start.3
  45.8 1.6 %collective-permute-start.4 = (bf16[4,9,8,256]{3,2,1,0:T(8,128)(2,1)S(1)}, bf16[4,9,8,256]{3,2,1,0:T(8,128)(2,1)S(1)}, u32[]{:S(2)}, u32[]{:S(2)}) collective-permute-start(bf16[4,9,8,256]{3,2,1,0:T(8,128)(2,1)S(1)} %shard_map.97.refs_4_), channel_id=1, source_target_pairs={{0,2},{1,3},{2,0},{3,1},{4,6},{5,7},{6,4},{7,5},{8,10},{9,11},{10,... | collective-permute-start | bytes 442376 | tf_op jit(solution)/shard_map/ppermute | solution.py:400
  47.3 0.3 collective-permute-start.5
  47.6 0.1 convert_reduce_fusion
  47.7 0.1 reshape.38
  47.8 0.1 min.23
  47.9 0.1 pad_maximum_fusion.invn_ref
  48.0 0.0 collective-permute-done.3.refs_5_
  48.0 4.5 %collective-permute-done.4.refs_6_ = bf16[4,9,8,256]{3,2,1,0:T(8,128)(2,1)S(1)} collective-permute-done((bf16[4,9,8,256]{3,2,1,0:T(8,128)(2,1)S(1)}, bf16[4,9,8,256]{3,2,1,0:T(8,128)(2,1)S(1)}, u32[]{:S(2)}, u32[]{:S(2)}) %collective-permute-start.4) | collective-permute-done | bytes 147488 | tf_op jit(solution)/shard_map/ppermute | solution.py:400
  52.5 0.6 copy-done.3
  53.1 1.7 %collective-permute-done.5.refs_7_ = bf16[4,9,8,256]{3,2,1,0:T(8,128)(2,1)} collective-permute-done((bf16[4,9,8,256]{3,2,1,0:T(8,128)(2,1)S(1)}, bf16[4,9,8,256]{3,2,1,0:T(8,128)(2,1)}, u32[]{:S(2)}, u32[]{:S(2)}) %collective-permute-start.5) | collective-permute-done | bytes 147488 | tf_op jit(solution)/shard_map/ppermute | solution.py:400
  54.9 0.0 all-to-all-done.v_from
  54.9 0.0 copy-done.2
  54.9 0.9 copy-done.4
  55.8 20.1 %shard_map.98 = (s16[8,64,1152]{2,1,0:T(8,128)(2,1)}, f32[32,2048]{1,0:T(8,128)S(1)}, f32[32,2048]{1,0:T(8,128)S(1)}, f32[32,2048]{1,0:T(8,128)S(1)}, f32[32,2048]{1,0:T(8,128)S(1)}) custom-call(s32[4]{0:T(128)S(1)} %pad_add_fusion.c_ref, f32[32,128]{1,0:T(8,128)S(1)} %pad_maximum_fusion.invn_ref, bf16[1024,256]{1,0:T(8,128)(2,1)S(1)} %copy-done.2, ...), custom_call_target="tpu_custom_call" | custom-call | tf_op jit(solution)/shard_map/pallas_call | solution.py:502
  75.8 0.0 copy-start.11
  75.8 0.7 copy-done.11
  76.5 0.7 copy-done.13
  77.2 0.7 copy-done.15
  78.0 3.8 %all-to-all-start.1 = ((s16[8,64,1152]{2,1,0:T(8,128)(2,1)}), s16[8,64,1152]{2,1,0:T(8,128)(2,1)S(1)}, u32[]{:S(2)}, u32[]{:S(2)}) async-start(s16[8,64,1152]{2,1,0:T(8,128)(2,1)} %get-tuple-element.21), calls=%async_computation.1 | async-start | bytes 2359296 | tf_op jit(solution)/shard_map/all_to_all | solution.py:526
  81.8 0.0 copy-done.16
  81.8 0.2 collective-permute-start.6
  82.0 0.0 copy-done.14
  82.0 1.5 %collective-permute-start.7 = (f32[32,2048]{1,0:T(8,128)S(1)}, f32[32,2048]{1,0:T(8,128)S(1)}, u32[]{:S(2)}, u32[]{:S(2)}) collective-permute-start(f32[32,2048]{1,0:T(8,128)S(1)} %copy-done.14), channel_id=1, source_target_pairs={{0,2},{1,3},{2,0},{3,1},{4,6},{5,7},{6,4},{7,5},{8,10},{9,11},{10,... | collective-permute-start | bytes 786440 | tf_op jit(solution)/shard_map/ppermute | solution.py:400
  83.5 0.2 collective-permute-start.8
  83.7 0.0 collective-permute-done.6
  83.7 7.4 %collective-permute-done.7 = f32[32,2048]{1,0:T(8,128)S(1)} collective-permute-done((f32[32,2048]{1,0:T(8,128)S(1)}, f32[32,2048]{1,0:T(8,128)S(1)}, u32[]{:S(2)}, u32[]{:S(2)}) %collective-permute-start.7) | collective-permute-done | bytes 262176 | tf_op jit(solution)/shard_map/ppermute | solution.py:400
  91.1 4.5 %collective-permute-done.8 = f32[32,2048]{1,0:T(8,128)S(1)} collective-permute-done((f32[32,2048]{1,0:T(8,128)S(1)}, f32[32,2048]{1,0:T(8,128)S(1)}, u32[]{:S(2)}, u32[]{:S(2)}) %collective-permute-start.8) | collective-permute-done | bytes 262176 | tf_op jit(solution)/shard_map/ppermute | solution.py:400
  95.6 0.1 add_add_fusion
  95.7 2.1 %collective-permute-start.10 = (f32[8,2048]{1,0:T(8,128)S(1)}, f32[8,2048]{1,0:T(8,128)S(1)}, u32[]{:S(2)}, u32[]{:S(2)}) collective-permute-start(f32[8,2048]{1,0:T(8,128)S(1)} %get-tuple-element.24), channel_id=1, source_target_pairs={{0,8},{4,12},{8,0},{12,4},{16,24},{20,28},{24,16},{28,20},{1,9},{5... | collective-permute-start | bytes 196616 | tf_op jit(solution)/shard_map/ppermute | solution.py:400
  97.9 1.5 %collective-permute-start.11 = (f32[8,2048]{1,0:T(8,128)S(1)}, f32[8,2048]{1,0:T(8,128)S(1)}, u32[]{:S(2)}, u32[]{:S(2)}) collective-permute-start(f32[8,2048]{1,0:T(8,128)S(1)} %get-tuple-element.23), channel_id=1, source_target_pairs={{0,12},{4,8},{8,4},{12,0},{16,28},{20,24},{24,20},{28,16},{1,13},{... | collective-permute-start | bytes 196616 | tf_op jit(solution)/shard_map/ppermute | solution.py:400
  99.3 0.1 collective-permute-start.9
  99.4 5.1 %collective-permute-done.10 = f32[8,2048]{1,0:T(8,128)S(1)} collective-permute-done((f32[8,2048]{1,0:T(8,128)S(1)}, f32[8,2048]{1,0:T(8,128)S(1)}, u32[]{:S(2)}, u32[]{:S(2)}) %collective-permute-start.10) | collective-permute-done | bytes 65568 | tf_op jit(solution)/shard_map/ppermute | solution.py:400
  104.5 1.4 %collective-permute-done.11 = f32[8,2048]{1,0:T(8,128)S(1)} collective-permute-done((f32[8,2048]{1,0:T(8,128)S(1)}, f32[8,2048]{1,0:T(8,128)S(1)}, u32[]{:S(2)}, u32[]{:S(2)}) %collective-permute-start.11) | collective-permute-done | bytes 65568 | tf_op jit(solution)/shard_map/ppermute | solution.py:400
  105.9 0.3 collective-permute-done.9
  106.2 0.7 fusion.2
  106.9 4.0 %all-to-all-done.1.got_ref = s16[8,64,1152]{2,1,0:T(8,128)(2,1)S(1)} async-done(((s16[8,64,1152]{2,1,0:T(8,128)(2,1)}), s16[8,64,1152]{2,1,0:T(8,128)(2,1)S(1)}, u32[]{:S(2)}, u32[]{:S(2)}) %all-to-all-start.1) | async-done | bytes 1179680 | tf_op jit(solution)/shard_map/all_to_all | solution.py:526
  110.9 1.3 %shard_map.99 = f32[1024,256]{1,0:T(8,128)} custom-call(s32[1,256]{1,0:T(1,128)S(1)} %bitcast.8, s16[8,64,1152]{2,1,0:T(8,128)(2,1)S(1)} %all-to-all-done.1.got_ref), custom_call_target="tpu_custom_call" | custom-call | tf_op jit(solution)/shard_map/pallas_call | solution.py:527
  (19 shorter events, 0.1 us)
Async XLA Ops:
  0.6 1.0 copy-start.1
  1.7 0.7 copy-start.7
  2.4 10.3 %copy-start.6 = (s32[2,8,256]{2,1,0:T(8,128)S(1)}, s32[2,8,256]{2,1,0:T(8,128)}, u32[]{:S(2)}) copy-start(s32[2,8,256]{2,1,0:T(8,128)} %window_from.1) | copy-start | bytes 49156
  5.1 7.6 %copy-start = (bf16[8,256,512]{2,1,0:T(8,128)(2,1)S(1)}, bf16[8,256,512]{2,1,0:T(8,128)(2,1)}, u32[]{:S(2)}) copy-start(bf16[8,256,512]{2,1,0:T(8,128)(2,1)} %observed_from) | copy-start | bytes 6291460
  5.1 7.6 %copy-start.5 = (bf16[8,2048]{1,0:T(8,128)(2,1)S(1)}, bf16[8,2048]{1,0:T(8,128)(2,1)}, u32[]{:S(2)}) copy-start(bf16[8,2048]{1,0:T(8,128)(2,1)} %rspectra_from.1) | copy-start | bytes 98308
  5.1 7.6 %copy-start.9 = (s32[8]{0:T(128)S(1)}, s32[8]{0:T(128)}, u32[]{:S(2)}) copy-start(s32[8]{0:T(128)} %rcounts_ref.1) | copy-start | bytes 100
  5.1 7.6 %copy-start.10 = (s32[256]{0:T(256)S(1)}, s32[256]{0:T(256)}, u32[]{:S(2)}) copy-start(s32[256]{0:T(256)} %param.12) | copy-start | bytes 3076
  5.1 49.7 %all-to-all-start = ((bf16[8,64,1024]{2,1,0:T(8,128)(2,1)}), bf16[8,64,1024]{2,1,0:T(8,128)(2,1)S(1)}, u32[]{:S(2)}, u32[]{:S(2)}) async-start(bf16[8,64,1024]{2,1,0:T(8,128)(2,1)} %shard_map.95), calls=%async_computation | async-start | bytes 2097152 | tf_op jit(solution)/shard_map/all_to_all | solution.py:451
  12.6 8.8 %copy-start.8 = (s32[256]{0:T(256)S(1)}, s32[256]{0:T(256)}, u32[]{:S(2)}) copy-start(s32[256]{0:T(256)} %param.11) | copy-start | bytes 3076
  17.7 37.2 %copy-start.2 = (bf16[1024,256]{1,0:T(8,128)(2,1)S(1)}, bf16[1024,256]{1,0:T(8,128)(2,1)}, u32[]{:S(2)}) copy-start(bf16[1024,256]{1,0:T(8,128)(2,1)} %constant.49.table_ref) | copy-start | bytes 1572868
  17.7 15.0 %collective-permute-start = (bf16[73,8,256]{2,1,0:T(8,128)(2,1)}, bf16[73,8,256]{2,1,0:T(8,128)(2,1)S(1)}, u32[]{:S(2)}, u32[]{:S(2)}) collective-permute-start(bf16[73,8,256]{2,1,0:T(8,128)(2,1)} %get-tuple-element.14), channel_id=1, source_target_pairs={{0,4},{4,0},{8,12},{12,8},{16,20},{20,16},{24,28},{28,24},{1,5},{5... | collective-permute-start | bytes 897032 | tf_op jit(solution)/shard_map/ppermute | solution.py:400
  19.8 19.1 %collective-permute-start.1 = (bf16[73,8,256]{2,1,0:T(8,128)(2,1)}, bf16[73,8,256]{2,1,0:T(8,128)(2,1)S(1)}, u32[]{:S(2)}, u32[]{:S(2)}) collective-permute-start(bf16[73,8,256]{2,1,0:T(8,128)(2,1)} %get-tuple-element.15), channel_id=1, source_target_pairs={{0,8},{4,12},{8,0},{12,4},{16,24},{20,28},{24,16},{28,20},{1,9},{5... | collective-permute-start | bytes 897032 | tf_op jit(solution)/shard_map/ppermute | solution.py:400
  21.2 24.2 %collective-permute-start.2 = (bf16[73,8,256]{2,1,0:T(8,128)(2,1)}, bf16[73,8,256]{2,1,0:T(8,128)(2,1)S(1)}, u32[]{:S(2)}, u32[]{:S(2)}) collective-permute-start(bf16[73,8,256]{2,1,0:T(8,128)(2,1)} %get-tuple-element.16), channel_id=1, source_target_pairs={{0,12},{4,8},{8,4},{12,0},{16,28},{20,24},{24,20},{28,16},{1,13},{... | collective-permute-start | bytes 897032 | tf_op jit(solution)/shard_map/ppermute | solution.py:400
  45.7 2.3 %collective-permute-start.3 = (bf16[4,9,8,256]{3,2,1,0:T(8,128)(2,1)S(1)}, bf16[4,9,8,256]{3,2,1,0:T(8,128)(2,1)S(1)}, u32[]{:S(2)}, u32[]{:S(2)}) collective-permute-start(bf16[4,9,8,256]{3,2,1,0:T(8,128)(2,1)S(1)} %shard_map.97.refs_4_), channel_id=1, source_target_pairs={{0,1},{1,0},{2,3},{3,2},{4,5},{5,4},{6,7},{7,6},{8,9},{9,8},{10,11... | collective-permute-start | bytes 442376 | tf_op jit(solution)/shard_map/ppermute | solution.py:400
  45.8 6.7 %collective-permute-start.4 = (bf16[4,9,8,256]{3,2,1,0:T(8,128)(2,1)S(1)}, bf16[4,9,8,256]{3,2,1,0:T(8,128)(2,1)S(1)}, u32[]{:S(2)}, u32[]{:S(2)}) collective-permute-start(bf16[4,9,8,256]{3,2,1,0:T(8,128)(2,1)S(1)} %shard_map.97.refs_4_), channel_id=1, source_target_pairs={{0,2},{1,3},{2,0},{3,1},{4,6},{5,7},{6,4},{7,5},{8,10},{9,11},{10,... | collective-permute-start | bytes 442376 | tf_op jit(solution)/shard_map/ppermute | solution.py:400
  47.3 7.5 %collective-permute-start.5 = (bf16[4,9,8,256]{3,2,1,0:T(8,128)(2,1)S(1)}, bf16[4,9,8,256]{3,2,1,0:T(8,128)(2,1)}, u32[]{:S(2)}, u32[]{:S(2)}) collective-permute-start(bf16[4,9,8,256]{3,2,1,0:T(8,128)(2,1)S(1)} %shard_map.97.refs_4_), channel_id=1, source_target_pairs={{0,3},{1,2},{2,1},{3,0},{4,7},{5,6},{6,5},{7,4},{8,11},{9,10},{10,... | collective-permute-start | bytes 442376 | tf_op jit(solution)/shard_map/ppermute | solution.py:400
  52.5 0.7 copy-start.3
  54.9 0.9 copy-start.4
  75.8 0.7 copy-start.11
  76.5 0.7 copy-start.13
  77.2 0.7 copy-start.15
  77.9 3.8 %copy-start.16 = (f32[32,2048]{1,0:T(8,128)S(1)}, f32[32,2048]{1,0:T(8,128)}, u32[]{:S(2)}) copy-start(f32[32,2048]{1,0:T(8,128)} %copy-done.15) | copy-start | bytes 786436
  77.9 4.1 %copy-start.14 = (f32[32,2048]{1,0:T(8,128)S(1)}, f32[32,2048]{1,0:T(8,128)}, u32[]{:S(2)}) copy-start(f32[32,2048]{1,0:T(8,128)} %copy-done.13) | copy-start | bytes 786436
  77.9 5.5 %copy-start.12 = (f32[32,2048]{1,0:T(8,128)S(1)}, f32[32,2048]{1,0:T(8,128)}, u32[]{:S(2)}) copy-start(f32[32,2048]{1,0:T(8,128)} %copy-done.11) | copy-start | bytes 786436
  78.0 32.9 %all-to-all-start.1 = ((s16[8,64,1152]{2,1,0:T(8,128)(2,1)}), s16[8,64,1152]{2,1,0:T(8,128)(2,1)S(1)}, u32[]{:S(2)}, u32[]{:S(2)}) async-start(s16[8,64,1152]{2,1,0:T(8,128)(2,1)} %get-tuple-element.21), calls=%async_computation.1 | async-start | bytes 2359296 | tf_op jit(solution)/shard_map/all_to_all | solution.py:526
  81.8 1.9 %collective-permute-start.6 = (f32[32,2048]{1,0:T(8,128)S(1)}, f32[32,2048]{1,0:T(8,128)S(1)}, u32[]{:S(2)}, u32[]{:S(2)}) collective-permute-start(f32[32,2048]{1,0:T(8,128)S(1)} %copy-done.16), channel_id=1, source_target_pairs={{0,1},{1,0},{2,3},{3,2},{4,5},{5,4},{6,7},{7,6},{8,9},{9,8},{10,11... | collective-permute-start | bytes 786440 | tf_op jit(solution)/shard_map/ppermute | solution.py:400
  82.0 9.1 %collective-permute-start.7 = (f32[32,2048]{1,0:T(8,128)S(1)}, f32[32,2048]{1,0:T(8,128)S(1)}, u32[]{:S(2)}, u32[]{:S(2)}) collective-permute-start(f32[32,2048]{1,0:T(8,128)S(1)} %copy-done.14), channel_id=1, source_target_pairs={{0,2},{1,3},{2,0},{3,1},{4,6},{5,7},{6,4},{7,5},{8,10},{9,11},{10,... | collective-permute-start | bytes 786440 | tf_op jit(solution)/shard_map/ppermute | solution.py:400
  83.5 12.1 %collective-permute-start.8 = (f32[32,2048]{1,0:T(8,128)S(1)}, f32[32,2048]{1,0:T(8,128)S(1)}, u32[]{:S(2)}, u32[]{:S(2)}) collective-permute-start(f32[32,2048]{1,0:T(8,128)S(1)} %copy-done.12), channel_id=1, source_target_pairs={{0,3},{1,2},{2,1},{3,0},{4,7},{5,6},{6,5},{7,4},{8,11},{9,10},{10,... | collective-permute-start | bytes 786440 | tf_op jit(solution)/shard_map/ppermute | solution.py:400
  95.7 8.8 %collective-permute-start.10 = (f32[8,2048]{1,0:T(8,128)S(1)}, f32[8,2048]{1,0:T(8,128)S(1)}, u32[]{:S(2)}, u32[]{:S(2)}) collective-permute-start(f32[8,2048]{1,0:T(8,128)S(1)} %get-tuple-element.24), channel_id=1, source_target_pairs={{0,8},{4,12},{8,0},{12,4},{16,24},{20,28},{24,16},{28,20},{1,9},{5... | collective-permute-start | bytes 196616 | tf_op jit(solution)/shard_map/ppermute | solution.py:400
  97.9 8.0 %collective-permute-start.11 = (f32[8,2048]{1,0:T(8,128)S(1)}, f32[8,2048]{1,0:T(8,128)S(1)}, u32[]{:S(2)}, u32[]{:S(2)}) collective-permute-start(f32[8,2048]{1,0:T(8,128)S(1)} %get-tuple-element.23), channel_id=1, source_target_pairs={{0,12},{4,8},{8,4},{12,0},{16,28},{20,24},{24,20},{28,16},{1,13},{... | collective-permute-start | bytes 196616 | tf_op jit(solution)/shard_map/ppermute | solution.py:400
  99.3 6.9 %collective-permute-start.9 = (f32[8,2048]{1,0:T(8,128)S(1)}, f32[8,2048]{1,0:T(8,128)S(1)}, u32[]{:S(2)}, u32[]{:S(2)}) collective-permute-start(f32[8,2048]{1,0:T(8,128)S(1)} %get-tuple-element.22), channel_id=1, source_target_pairs={{0,4},{4,0},{8,12},{12,8},{16,20},{20,16},{24,28},{28,24},{1,5},{5... | collective-permute-start | bytes 196616 | tf_op jit(solution)/shard_map/ppermute | solution.py:400

commit v5 on v4

--- a/solution.py
+++ b/solution.py
@@ -18,7 +18,8 @@
 GROUP = 4
 LANES = 128
 FB = LANES // (2 * S)
-WIDTH = 8
+WIDTH = 16
+CHUNKS = 2
 FIXED = 32000.0
 
 
@@ -53,16 +54,21 @@
     return jnp.where(rows == lanes, 1.0, 0.0).astype(jnp.bfloat16)
 
 
-def turn_kernel(spectra_from, counts_from, v_to, spectra_ref, counts_ref, turned_ref, sems):
+def turn_kernel(rcounts_ref, spectra_from, counts_from, rspectra_from, *refs):
+    u_to, *v_to = refs[: 1 + CHUNKS]
+    spectra_ref, counts_ref, rspectra_ref, turned_ref, u_ref, sems, out_sems = refs[1 + CHUNKS :]
     k_own, col_total = spectra_ref.shape
-    rcv_total, cols, _ = v_to.shape
-    members = col_total // cols
+    rcv_total, cols, _ = v_to[0].shape
+    members = col_total // (cols * CHUNKS)
     width = min(k_own, 2 * LANES)
-    copies = [pltpu.make_async_copy(counts_from, counts_ref, sems.at[0])]
+    copies = [
+        pltpu.make_async_copy(counts_from, counts_ref, sems.at[0]),
+        pltpu.make_async_copy(rspectra_from, rspectra_ref, sems.at[1]),
+    ]
     for n, begin in enumerate(range(0, k_own, width)):
         rows = pl.ds(begin, width)
         copies.append(
-            pltpu.make_async_copy(spectra_from.at[rows], spectra_ref.at[rows], sems.at[1 + n])
+            pltpu.make_async_copy(spectra_from.at[rows], spectra_ref.at[rows], sems.at[2 + n])
         )
     for copy in copies:
         copy.start()
@@ -71,51 +77,63 @@
     copies[0].wait()
     inside = seg_ids < counts_ref[...]
     for n, begin in enumerate(range(0, k_own, width)):
-        copies[1 + n].wait()
+        copies[2 + n].wait()
         part = spectra_ref[begin : begin + width, :].astype(jnp.float32)
         part = jnp.where(inside, part, 0.0).astype(jnp.bfloat16)
         turned_ref[:, begin : begin + width] = nt(eye, part).astype(jnp.bfloat16)
-    copies = [
-        pltpu.make_async_copy(
-            turned_ref.at[pl.ds(dest % members * cols, cols)], v_to.at[dest], sems.at[dest]
-        )
-        for dest in range(rcv_total)
-    ]
-    for copy in copies:
-        copy.start()
-    for copy in copies:
-        copy.wait()
-
-
-def fold_kernel(c_ref, rcounts_ref, observed_from, rspectra_from, window_from, order_from, *rest):
-    *out_to, observed_ref, rspectra_ref, window_ref, order_ref, line_ref, out_ref, sems, out_sems = (
-        rest
-    )
+    outs = []
+    for c in range(CHUNKS):
+        for dest in range(rcv_total):
+            first = (dest % members * CHUNKS + c) * cols
+            outs.append(
+                pltpu.make_async_copy(
+                    turned_ref.at[pl.ds(first, cols)],
+                    v_to[c].at[dest],
+                    out_sems.at[c * rcv_total + dest],
+                )
+            )
+            outs[-1].start()
+    copies[1].wait()
+    pieces, rows, half = u_ref.shape
+    row_ids = lax.broadcasted_iota(jnp.int32, (rows, half), 0)
+    counts = jnp.zeros((rows, half), jnp.int32)
+    for i in range(rows):
+        counts = jnp.where(row_ids == i, rcounts_ref[i], counts)
+    seg_ids = lax.broadcasted_iota(jnp.int32, (rows, half), 1) % S
+    for n in range(pieces - 1):
+        part = rspectra_ref[:, n * half : (n + 1) * half].astype(jnp.float32)
+        u_ref[n] = jnp.where(seg_ids < counts, part, 0.0).astype(jnp.bfloat16)
+    u_ref[pieces - 1] = counts.astype(jnp.float32).astype(jnp.bfloat16)
+    outs.append(pltpu.make_async_copy(u_ref, u_to, out_sems.at[CHUNKS * rcv_total]))
+    outs[-1].start()
+    for copy in outs:
+        copy.wait()
+
+
+def fold_kernel(c_ref, observed_from, window_from, order_from, *rest):
+    *out_to, observed_ref, window_ref, order_ref, line_ref, out_ref, sems, out_sems = rest
     row_total, col_total, lag_total = observed_ref.shape
     half = lag_total // 2
-    members = len(out_to)
-    cols = col_total // members
+    members = len(out_to) // CHUNKS
+    cols = col_total // len(out_to)
     lines = col_total * row_total
-    quarter = rspectra_ref.shape[1]
     copies = [
-        pltpu.make_async_copy(src, dst, sems.at[row_total + n])
-        for n, (src, dst) in enumerate(
-            [(window_from, window_ref), (order_from, order_ref), (rspectra_from, rspectra_ref)]
-        )
+        pltpu.make_async_copy(window_from, window_ref, sems.at[row_total]),
+        pltpu.make_async_copy(order_from, order_ref, sems.at[row_total + 1]),
     ] + [
         pltpu.make_async_copy(observed_from.at[i], observed_ref.at[i], sems.at[i])
         for i in range(row_total)
     ]
     for copy in copies:
         copy.start()
-    for copy in copies[:3]:
+    for copy in copies[:2]:
         copy.wait()
     window = jnp.concatenate([window_ref[0], window_ref[1]], axis=0).astype(jnp.float32).T
     station = lax.broadcasted_iota(jnp.int32, (col_total, col_total), 0) + c_ref[1]
     pick = jnp.where(station == order_ref[...], 1.0, 0.0).astype(jnp.bfloat16)
     lag_ids = lax.broadcasted_iota(jnp.int32, (col_total, half), 1).astype(jnp.float32)
     for i in range(row_total):
-        copies[3 + i].wait()
+        copies[2 + i].wait()
         begin = window[:, i : i + 1]
         end = begin + window[:, row_total + i : row_total + i + 1]
         values = observed_ref[i].astype(jnp.float32)
@@ -127,53 +145,44 @@
             line_ref[pl.ds(h * lines + i, col_total, stride=row_total), :] = moved[
                 :, h * LANES : (h + 1) * LANES
             ]
-    row_ids = lax.broadcasted_iota(jnp.int32, (row_total, half), 0)
-    counts = jnp.zeros((row_total, half), jnp.int32)
-    for i in range(row_total):
-        counts = jnp.where(row_ids == i, rcounts_ref[i], counts)
-    seg_ids = lax.broadcasted_iota(jnp.int32, (row_total, half), 1) % S
-    pieces = quarter // half
-    for k in range(members):
-        for n in range(pieces):
-            part = rspectra_ref[:, n * half : (n + 1) * half].astype(jnp.float32)
-            out_ref[k, cols + n] = jnp.where(seg_ids < counts, part, 0.0).astype(jnp.bfloat16)
-        out_ref[k, cols + pieces] = counts.astype(jnp.float32).astype(jnp.bfloat16)
     mine = c_ref[0]
     copies = []
-    for k in range(members):
-        first = (mine ^ k) * (cols * row_total)
-        for h in range(half // LANES):
-            begin = pl.multiple_of(h * lines + first, cols * row_total)
-            rows = line_ref[pl.ds(begin, cols * row_total), :]
-            out_ref[k, :cols, :, h * LANES : (h + 1) * LANES] = rows.reshape(
-                cols, row_total, LANES
-            ).astype(jnp.bfloat16)
-        copies.append(pltpu.make_async_copy(out_ref.at[k], out_to[k], out_sems.at[k]))
-        copies[-1].start()
+    for c in range(CHUNKS):
+        for k in range(members):
+            n = c * members + k
+            first = ((mine ^ k) * CHUNKS + c) * (cols * row_total)
+            for h in range(half // LANES):
+                begin = pl.multiple_of(h * lines + first, cols * row_total)
+                rows = line_ref[pl.ds(begin, cols * row_total), :]
+                out_ref[n, :, :, h * LANES : (h + 1) * LANES] = rows.reshape(
+                    cols, row_total, LANES
+                ).astype(jnp.bfloat16)
+            copies.append(pltpu.make_async_copy(out_ref.at[n], out_to[n], out_sems.at[n]))
+            copies[-1].start()
     for copy in copies:
         copy.wait()
 
 
 def near_kernel(*refs):
     *parts, out_ref, sems = refs
-    extra = out_ref.shape[1]
-    copies = []
-    for k, ref in enumerate(parts):
-        rows = ref.at[pl.ds(ref.shape[0] - extra, extra)]
-        copies.append(pltpu.make_async_copy(rows, out_ref.at[k], sems.at[k]))
-        copies[-1].start()
+    copies = [
+        pltpu.make_async_copy(ref, out_ref.at[k], sems.at[k]) for k, ref in enumerate(parts)
+    ]
     for copy in copies:
-        copy.wait()
-
-
-def pair_kernel(n_e, n_r, c_ref, invn_ref, table_ref, v_from, *refs):
+        copy.start()
+    for copy in copies:
+        copy.wait()
+
+
+def pair_kernel(n_e, n_r, n_in, c_ref, invn_ref, table_ref, v_from, *refs):
     refs = list(refs)
     e_from, u_from = refs[:n_e], refs[n_e : n_e + n_r]
-    w_to, *r_to = refs[n_e + n_r : n_e + 2 * n_r + 1]
+    r_from = refs[n_e + n_r : n_e + n_r + n_in]
+    w_to, *r_to = refs[n_e + n_r + n_in : n_e + 2 * n_r + n_in + 1]
     (
         x_ref, z_ref, plain_ref, turned_ref, code_ref, u_ref, v_ref, e_ref, r_ref, w_ref,
         sems, w_sems,
-    ) = refs[n_e + 2 * n_r + 1 :]
+    ) = refs[n_e + 2 * n_r + n_in + 1 :]
 
     src_total, col_total, k_own = v_ref.shape
     ref_total, irec, k_quarter = r_ref.shape
@@ -191,10 +200,14 @@
     for k, ref in enumerate(u_from):
         early.append(pltpu.make_async_copy(ref, u_ref.at[quarter_me ^ k], sems.at[1 + k]))
     late = [
-        pltpu.make_async_copy(ref.at[pl.ds(0, col_total)], e_ref.at[k], sems.at[1 + n_r + k])
+        pltpu.make_async_copy(ref, e_ref.at[k], sems.at[1 + n_r + k])
         for k, ref in enumerate(e_from)
     ]
-    for copy in early + late:
+    last = [
+        pltpu.make_async_copy(ref, r_ref.at[quarter_me ^ k], sems.at[1 + n_r + n_e + k])
+        for k, ref in enumerate(r_from)
+    ]
+    for copy in early + late + last:
         copy.start()
     half = e_ref.shape[-1]
     eye = eye_of(half)
@@ -257,7 +270,7 @@
 
     for copy in early:
         copy.wait()
-    lax.fori_loop(0, blocks, forward, 0, unroll=16)
+    lax.fori_loop(0, blocks, forward, 0, unroll=64)
 
     lane_ids = lax.broadcasted_iota(jnp.int32, (1, LANES), 1)
     sign = jnp.where(lane_ids < LANES // 2, -1.0, 1.0).astype(jnp.float32)
@@ -308,7 +321,7 @@
 
     for copy in late:
         copy.wait()
-    lax.fori_loop(0, jp_total // WIDTH, pairs, 0)
+    lax.fori_loop(0, jp_total // WIDTH, pairs, 0, unroll=2)
 
     def backward(fb):
         z = jnp.concatenate([z_ref[place(fb, f), :] for f in range(FB)], axis=0)
@@ -344,7 +357,7 @@
         quarter, off = lanes_of(fb, quarter_blocks)
         lanes = pl.ds(off, LANES)
         total = sums[0] + crossed
-        r_ref[quarter, :, lanes] = total
+        r_ref[quarter, :, lanes] = r_ref[quarter, :, lanes] + total if r_from else total
 
     def w_copy(src):
         return pltpu.make_async_copy(w_ref.at[src], w_to.at[src], w_sems.at[src])
@@ -360,38 +373,45 @@
         w_copy(src).start()
         return 0
 
-    owners = src_total // ref_total
-    outs = []
-    for k, ref in enumerate(r_to):
-        begin = (quarter_me ^ k) * owners
-        lax.fori_loop(begin, begin + owners, from_owner, 0)
-        outs.append(pltpu.make_async_copy(r_ref.at[quarter_me ^ k], ref, sems.at[k]))
-        outs[-1].start()
+    for copy in last:
+        copy.wait()
+    lax.fori_loop(0, src_total, from_owner, 0, unroll=4)
+    outs = [
+        pltpu.make_async_copy(r_ref.at[quarter_me ^ k], ref, sems.at[k])
+        for k, ref in enumerate(r_to)
+    ]
+    for copy in outs:
+        copy.start()
     for copy in outs:
         copy.wait()
     for src in range(src_total):
         w_copy(src).wait()
 
 
-def join_kernel(count_ref, got_ref, out_ref):
-    src_total, cols, _ = got_ref.shape
+def join_kernel(count_ref, *refs):
+    *got_refs, out_ref = refs
+    src_total, cols, _ = got_refs[0].shape
     k_own, col_total = out_ref.shape
-    members = col_total // cols
+    members = col_total // (cols * len(got_refs))
     seg_ids = lax.broadcasted_iota(jnp.int32, (LANES, col_total), 0) % S
     inside = seg_ids < count_ref[...]
     scales = [
-        jnp.exp2(got_ref[src, :16, k_own:].astype(jnp.int32).astype(jnp.float32)) * (1.0 / FIXED)
-        for src in range(src_total)
+        [
+            jnp.exp2(ref[src, :16, k_own:].astype(jnp.int32).astype(jnp.float32)) * (1.0 / FIXED)
+            for src in range(src_total)
+        ]
+        for ref in got_refs
     ]
     for b in range(k_own // LANES):
         rows = []
         for m in range(members):
-            total = None
-            for src in range(m, src_total, members):
-                part = got_ref[src, :, b * LANES : (b + 1) * LANES]
-                part = part.astype(jnp.int32).astype(jnp.float32) * scales[src][b : b + 1]
-                total = part if total is None else total + part
-            rows.append(total)
+            for ref, scale in zip(got_refs, scales):
+                total = None
+                for src in range(m, src_total, members):
+                    part = ref[src, :, b * LANES : (b + 1) * LANES]
+                    part = part.astype(jnp.int32).astype(jnp.float32) * scale[src][b : b + 1]
+                    total = part if total is None else total + part
+                rows.append(total)
         whole = jnp.concatenate(rows, axis=0).T
         out_ref[b * LANES : (b + 1) * LANES, :] = jnp.where(inside, whole, 0.0)
 
@@ -419,7 +439,7 @@
     half = lag_total // 2
     members = math.gcd(GROUP, rcv_total)
     irec = row_total * members
-    cols = col_total // members
+    cols = col_total // (members * CHUNKS)
     jj_total = LANES // (2 * irec)
     jp_total = cols // jj_total
     extra = k_quarter // half + 1
@@ -431,53 +451,64 @@
     smem = pl.BlockSpec(memory_space=pltpu.SMEM)
     hbm = pl.BlockSpec(memory_space=pl.ANY)
     scalars = jnp.stack([mine, quarter * col_total, place, quarter]).astype(jnp.int32)
-    params = pltpu.CompilerParams(vmem_limit_bytes=32 * 1024 * 1024)
-    free = pl.CostEstimate(flops=0, bytes_accessed=0, transcendentals=0)
-
-    sent = pl.pallas_call(
+
+    def params(mib):
+        return pltpu.CompilerParams(vmem_limit_bytes=mib * 1024 * 1024)
+
+    def cost(us):
+        return pl.CostEstimate(flops=us * 10**9, bytes_accessed=0, transcendentals=0)
+
+    def after(x, *others):
+        return lax.optimization_barrier((x,) + others)[0]
+
+    u_own, *sent = pl.pallas_call(
         turn_kernel,
-        out_shape=jax.ShapeDtypeStruct((rcv_total, cols, k_own), bf16),
-        in_specs=[hbm] * 2,
-        out_specs=hbm,
+        out_shape=[jax.ShapeDtypeStruct((extra, row_total, half), bf16)]
+        + [jax.ShapeDtypeStruct((rcv_total, cols, k_own), bf16)] * CHUNKS,
+        in_specs=[smem] + [hbm] * 3,
+        out_specs=[hbm] * (1 + CHUNKS),
         scratch_shapes=[
             pltpu.VMEM((k_own, col_total), bf16),
             pltpu.VMEM((1, col_total), jnp.int32),
+            pltpu.VMEM(receiver_spectra.shape, bf16),
             pltpu.VMEM((col_total, k_own), bf16),
-            pltpu.SemaphoreType.DMA((max(rcv_total, 1 + k_own // min(k_own, 2 * LANES)),)),
+            pltpu.VMEM((extra, row_total, half), bf16),
+            pltpu.SemaphoreType.DMA((2 + k_own // min(k_own, 2 * LANES),)),
+            pltpu.SemaphoreType.DMA((CHUNKS * rcv_total + 1,)),
         ],
-        compiler_params=params,
-        cost_estimate=free,
-    )(reference_spectra, reference_counts.reshape(1, col_total))
-    v_all = lax.all_to_all(sent, "rcv", split_axis=0, concat_axis=0, tiled=True)
-
-    _, observed = lax.optimization_barrier((sent, observed))
-    shape = (cols + extra, row_total, half)
+        compiler_params=params(62),
+        cost_estimate=cost(0),
+    )(receiver_counts, reference_spectra, reference_counts.reshape(1, col_total), receiver_spectra)
+    v_all = []
+    for x in sent:
+        x = after(x, *v_all[-1:])
+        v_all.append(lax.all_to_all(x, "rcv", split_axis=0, concat_axis=0, tiled=True))
+
+    shape = (cols, row_total, half)
     folded = pl.pallas_call(
         fold_kernel,
-        out_shape=[jax.ShapeDtypeStruct(shape, bf16)] * members,
-        in_specs=[smem] * 2 + [hbm] * 4,
-        out_specs=[hbm] * members,
+        out_shape=[jax.ShapeDtypeStruct(shape, bf16)] * (CHUNKS * members),
+        in_specs=[smem] + [hbm] * 3,
+        out_specs=[hbm] * (CHUNKS * members),
         scratch_shapes=[
             pltpu.VMEM(observed.shape, bf16),
-            pltpu.VMEM(receiver_spectra.shape, bf16),
             pltpu.VMEM(lag_window.shape, jnp.int32),
             pltpu.VMEM((1, col_total), jnp.int32),
             pltpu.VMEM((half // LANES * col_total * row_total, LANES), jnp.float32),
-            pltpu.VMEM((members,) + shape, bf16),
-            pltpu.SemaphoreType.DMA((row_total + 3,)),
-            pltpu.SemaphoreType.DMA((members,)),
+            pltpu.VMEM((CHUNKS * members,) + shape, bf16),
+            pltpu.SemaphoreType.DMA((row_total + 2,)),
+            pltpu.SemaphoreType.DMA((CHUNKS * members,)),
         ],
-        compiler_params=params,
-        cost_estimate=free,
-    )(
-        scalars,
-        receiver_counts,
-        observed,
-        receiver_spectra,
-        lag_window,
-        column_station.reshape(1, col_total),
-    )
-    e_all = [folded[0]] + [swap(folded[k], "rcv", rcv_total, k) for k in range(1, members)]
+        compiler_params=params(32),
+        cost_estimate=cost(0),
+    )(scalars, after(observed, u_own), lag_window, column_station.reshape(1, col_total))
+    e_all = [
+        [
+            x if k == 0 else swap(x, "rcv", rcv_total, k)
+            for k, x in enumerate(folded[c * members : (c + 1) * members])
+        ]
+        for c in range(CHUNKS)
+    ]
 
     near = pl.pallas_call(
         near_kernel,
@@ -485,53 +516,58 @@
         in_specs=[hbm] * members,
         out_specs=hbm,
         scratch_shapes=[pltpu.SemaphoreType.DMA((members,))],
-        compiler_params=params,
-        cost_estimate=free,
-    )(*e_all)
+        compiler_params=params(16),
+        cost_estimate=cost(0),
+    )(u_own, *[swap(u_own, "rcv", rcv_total, k) for k in range(1, members)])
     u_all = [near] + [swap(near, "ref", ref_total, k) for k in range(1, ref_total)]
-
     group_counts = near[:, extra - 1, :, 0].reshape(irec).astype(jnp.float32)
-    own_counts = lax.dynamic_slice_in_dim(reference_counts, mine * cols, cols).astype(jnp.float32)
-    counts = own_counts.reshape(jj_total, jp_total).T
-    least = jnp.minimum(counts[:, :, None], group_counts[None, None, :])
-    inverse = (1.0 / least).reshape(jp_total, jj_total * irec)
-    inverse = jnp.concatenate([inverse, inverse], axis=1)
+    own_counts = lax.dynamic_slice_in_dim(
+        reference_counts, mine * (cols * CHUNKS), cols * CHUNKS
+    ).astype(jnp.float32)
 
     table = lag_tables(k_total // (2 * S), lag_total)
     lines = jp_total * k_total // (2 * S)
-    w_part, *r_all = pl.pallas_call(
-        functools.partial(pair_kernel, members, ref_total),
-        out_shape=[jax.ShapeDtypeStruct((rcv_total, cols, k_own + LANES), jnp.int16)]
-        + [jax.ShapeDtypeStruct((irec, k_quarter), jnp.float32)] * ref_total,
-        in_specs=[smem] + [vmem] * 2 + [hbm] * (1 + members + ref_total),
-        out_specs=[hbm] * (1 + ref_total),
-        scratch_shapes=[
-            pltpu.VMEM((lines, LANES), jnp.float32),
-            pltpu.VMEM((lines, LANES), jnp.float32),
-            pltpu.VMEM((irec, k_total), bf16),
-            pltpu.VMEM((irec, k_total), bf16),
-            pltpu.VMEM((k_total // LANES, LANES), jnp.float32),
-            pltpu.VMEM((ref_total,) + near.shape, bf16),
-            pltpu.VMEM((rcv_total, cols, k_own), bf16),
-            pltpu.VMEM((members, cols, row_total, half), bf16),
-            pltpu.VMEM((ref_total, irec, k_quarter), jnp.float32),
-            pltpu.VMEM((rcv_total, cols, k_own + LANES), jnp.int16),
-            pltpu.SemaphoreType.DMA((1 + members + ref_total,)),
-            pltpu.SemaphoreType.DMA((rcv_total,)),
-        ],
-        compiler_params=params,
-        cost_estimate=free,
-    )(scalars, inverse, table, v_all, *e_all, *u_all)
-
-    got = lax.all_to_all(w_part, "rcv", split_axis=0, concat_axis=0, tiled=True)
+    r_all, got = [], []
+    for c in range(CHUNKS):
+        counts = own_counts[c * cols : (c + 1) * cols].reshape(jj_total, jp_total).T
+        least = jnp.minimum(counts[:, :, None], group_counts[None, None, :])
+        inverse = (1.0 / least).reshape(jp_total, jj_total * irec)
+        inverse = jnp.concatenate([inverse, inverse], axis=1)
+        operands = [v_all[c], *e_all[c], *u_all, *r_all]
+        w_part, *r_all = pl.pallas_call(
+            functools.partial(pair_kernel, members, ref_total, len(r_all)),
+            out_shape=[jax.ShapeDtypeStruct((rcv_total, cols, k_own + LANES), jnp.int16)]
+            + [jax.ShapeDtypeStruct((irec, k_quarter), jnp.float32)] * ref_total,
+            in_specs=[smem] + [vmem] * 2 + [hbm] * len(operands),
+            out_specs=[hbm] * (1 + ref_total),
+            scratch_shapes=[
+                pltpu.VMEM((lines, LANES), jnp.float32),
+                pltpu.VMEM((lines, LANES), jnp.float32),
+                pltpu.VMEM((irec, k_total), bf16),
+                pltpu.VMEM((irec, k_total), bf16),
+                pltpu.VMEM((k_total // LANES, LANES), jnp.float32),
+                pltpu.VMEM((ref_total,) + near.shape, bf16),
+                pltpu.VMEM((rcv_total, cols, k_own), bf16),
+                pltpu.VMEM((members, cols, row_total, half), bf16),
+                pltpu.VMEM((ref_total, irec, k_quarter), jnp.float32),
+                pltpu.VMEM((rcv_total, cols, k_own + LANES), jnp.int16),
+                pltpu.SemaphoreType.DMA((len(operands),)),
+                pltpu.SemaphoreType.DMA((rcv_total,)),
+            ],
+            compiler_params=params(32),
+            cost_estimate=cost(10),
+        )(scalars, inverse, table, *operands)
+        w_part = after(w_part, *got[-1:])
+        got.append(lax.all_to_all(w_part, "rcv", split_axis=0, concat_axis=0, tiled=True))
+
     reference_grad = pl.pallas_call(
         join_kernel,
         out_shape=jax.ShapeDtypeStruct((k_own, col_total), jnp.float32),
-        in_specs=[vmem] * 2,
+        in_specs=[vmem] * (1 + CHUNKS),
         out_specs=vmem,
-        compiler_params=params,
-        cost_estimate=free,
-    )(reference_counts.reshape(1, col_total), got)
+        compiler_params=params(32),
+        cost_estimate=cost(1),
+    )(reference_counts.reshape(1, col_total), *got)
 
     r_sum = r_all[0]
     for k in range(1, ref_total):

time: 113 us -> 104 us (0.920)
  waiting for transfers between devices: 52.6 us -> 13.4 us
  starting transfers between devices: 22.4 us -> 42.3 us
  local copies, waits for them, and re-layouts: 5.96 us -> 12 us
  Pallas kernels: 29.3 us -> 33.7 us
    ppermute x12 -> x18, waiting for transfers between devices: 48.6 us -> 13.4 us  [swap(): return lax.ppermute(x, axis, [(r, r ^ k) for r in range(total)])]
    all_to_all x2 -> x4, starting transfers between devices: 11.2 us -> 23.3 us  [the longest x2 11.9 us: shards(): lax.all_to_all(w_part, 'rcv', split_axis=0, concat_axis=0, tiled=True)]
    ppermute x12 -> x18, starting transfers between devices: 11.2 us -> 19 us  [swap(): return lax.ppermute(x, axis, [(r, r ^ k) for r in range(total)])]
    unnamed x34 -> x32, local copies, waits for them, and re-layouts: 5.42 us -> 11 us
    all_to_all x2 -> x4, waiting for transfers between devices: 3.95 us -> 0.01 us  [the longest x2 0.01 us: shards(): lax.all_to_all(x, 'rcv', split_axis=0, concat_axis=0, tiled=True)]
    pallas_call x2 -> x3, Pallas kernels: 22.8 us -> 26.7 us  [the longest x2 22.8 us: shards(): pl.pallas_call(functools.partial(pair_kernel, members, ref_total, len(r_a...]
  transfers between devices with their start and end apart: 14 -> 22, of which waited for: 11 -> 6; matrix products, arithmetic and copies ran while one was open for 1% -> 2% of each run, Pallas kernels for 5% -> 28%
where the time goes in v5:
time: 104 us; the launch traced here: 103 us
  starting transfers between devices  42.3 us (41%)
  Pallas kernels  33.7 us (32%)
  waiting for transfers between devices  13.4 us (13%)
  local copies, waits for them, and re-layouts  12 us (12%)
  other arithmetic  1.18 us (1%)
    pallas_call x2, Pallas kernels, shards(): pl.pallas_call(functools.partial(pair_kernel, members, ref_total, len(r_a...  22.8 us
    ppermute x18, starting transfers between devices, swap(): return lax.ppermute(x, axis, [(r, r ^ k) for r in range(total)])  19 us
    ppermute x18, waiting for transfers between devices, swap(): return lax.ppermute(x, axis, [(r, r ^ k) for r in range(total)])  13.4 us
    all_to_all x2, starting transfers between devices, shards(): lax.all_to_all(w_part, 'rcv', split_axis=0, concat_axis=0, tiled=True)  11.9 us
    all_to_all x2, starting transfers between devices, shards(): lax.all_to_all(x, 'rcv', split_axis=0, concat_axis=0, tiled=True)  11.4 us
    unnamed x32, local copies, waits for them, and re-layouts  11 us
    pallas_call x1, Pallas kernels, shards(): pl.pallas_call(fold_kernel, out_shape=[jax.ShapeDtypeStruct(shape, bf16)]...  5.41 us
    pallas_call x1, Pallas kernels, shards(): pl.pallas_call(turn_kernel, out_shape=[jax.ShapeDtypeStruct((extra, row_t...  3.9 us
  transfers between devices with their start and end apart: 22, of which 6 were waited for; matrix products, arithmetic and copies ran while one was open for 2% of the time, Pallas kernels for 28%

profile of v5, /device:TPU:0, one launch (start us, length us, event | category | flops | bytes accessed | tf_op | source)
XLA Modules:
  0.0 103.3 jit_solution(16209434981767488025)
XLA Ops:
  0.6 3.9 %shard_map.95 = (bf16[9,8,256]{2,1,0:T(8,128)(2,1)}, bf16[8,32,1024]{2,1,0:T(8,128)(2,1)}, bf16[8,32,1024]{2,1,0:T(8,128)(2,1)}) custom-call(s32[8]{0:T(128)} %rcounts_ref.1, bf16[1024,256]{1,0:T(8,128)(2,1)} %spectra_from.1, s32[1,256]{1,0:T(1,128)} %bitcast.9, bf16[8,2048]{1,0:T(8,128)(2,1)} %rspectra_from.1), custom_call_target="tpu_custom_call" | custom-call | tf_op jit(solution)/shard_map/pallas_call | solution.py:464
  4.5 0.0 copy-start.1
  4.6 3.0 %collective-permute-start = (bf16[9,8,256]{2,1,0:T(8,128)(2,1)}, bf16[9,8,256]{2,1,0:T(8,128)(2,1)S(1)}, u32[]{:S(2)}, u32[]{:S(2)}) collective-permute-start(bf16[9,8,256]{2,1,0:T(8,128)(2,1)} %get-tuple-element.26.refs_0_), channel_id=1, source_target_pairs={{0,4},{4,0},{8,12},{12,8},{16,20},{20,16},{24,28},{28,24},{1,5},{5... | collective-permute-start | bytes 110600 | tf_op jit(solution)/shard_map/ppermute | solution.py:420
  7.6 1.6 %collective-permute-start.1 = (bf16[9,8,256]{2,1,0:T(8,128)(2,1)}, bf16[9,8,256]{2,1,0:T(8,128)(2,1)S(1)}, u32[]{:S(2)}, u32[]{:S(2)}) collective-permute-start(bf16[9,8,256]{2,1,0:T(8,128)(2,1)} %get-tuple-element.26.refs_0_), channel_id=1, source_target_pairs={{0,8},{4,12},{8,0},{12,4},{16,24},{20,28},{24,16},{28,20},{1,9},{5... | collective-permute-start | bytes 110600 | tf_op jit(solution)/shard_map/ppermute | solution.py:420
  9.2 6.2 %all-to-all-start = ((bf16[8,32,1024]{2,1,0:T(8,128)(2,1)}), bf16[8,32,1024]{2,1,0:T(8,128)(2,1)S(1)}, u32[]{:S(2)}, u32[]{:S(2)}) async-start(bf16[8,32,1024]{2,1,0:T(8,128)(2,1)} %get-tuple-element.28), calls=%async_computation | async-start | bytes 1048576 | tf_op jit(solution)/shard_map/all_to_all | solution.py:485
  15.4 0.1 pad_add_fusion.c_ref
  15.5 1.6 %copy-done = bf16[8,256,512]{2,1,0:T(8,128)(2,1)S(1)} copy-done((bf16[8,256,512]{2,1,0:T(8,128)(2,1)S(1)}, bf16[8,256,512]{2,1,0:T(8,128)(2,1)}, u32[]{:S(2)}) %copy-start) | copy-done | bytes 2097176
  17.1 0.7 copy-done.2
  17.8 0.7 copy-done.3
  18.5 5.4 %shard_map.97 = (bf16[32,8,256]{2,1,0:T(8,128)(2,1)S(1)}, bf16[32,8,256]{2,1,0:T(8,128)(2,1)S(1)}, bf16[32,8,256]{2,1,0:T(8,128)(2,1)S(1)}, bf16[32,8,256]{2,1,0...) custom-call(s32[4]{0:T(128)S(1)} %pad_add_fusion.c_ref, ...), custom_call_target="tpu_custom_call" | custom-call | tf_op jit(solution)/shard_map/pallas_call | solution.py:488
  23.9 2.1 %collective-permute-start.10 = (bf16[32,8,256]{2,1,0:T(8,128)(2,1)S(1)}, bf16[32,8,256]{2,1,0:T(8,128)(2,1)S(1)}, u32[]{:S(2)}, u32[]{:S(2)}) collective-permute-start(bf16[32,8,256]{2,1,0:T(8,128)(2,1)S(1)} %get-tuple-element.37), channel_id=1, source_target_pairs={{0,8},{4,12},{8,0},{12,4},{16,24},{20,28},{24,16},{28,20},{1,9},{5... | collective-permute-start | bytes 393224 | tf_op jit(solution)/shard_map/ppermute | solution.py:420
  26.0 1.5 %collective-permute-start.11 = (bf16[32,8,256]{2,1,0:T(8,128)(2,1)S(1)}, bf16[32,8,256]{2,1,0:T(8,128)(2,1)S(1)}, u32[]{:S(2)}, u32[]{:S(2)}) collective-permute-start(bf16[32,8,256]{2,1,0:T(8,128)(2,1)S(1)} %get-tuple-element.38), channel_id=1, source_target_pairs={{0,12},{4,8},{8,4},{12,0},{16,28},{20,24},{24,20},{28,16},{1,13},{... | collective-permute-start | bytes 393224 | tf_op jit(solution)/shard_map/ppermute | solution.py:420
  27.4 0.1 dynamic-slice_convert_fusion
  27.5 0.1 fusion.7
  27.6 0.1 slice.42
  27.7 0.1 copy.12
  27.7 0.1 min.34
  27.8 0.1 min.35
  27.9 0.1 slice.45
  28.0 0.1 copy.13
  28.1 0.1 min.40
  28.1 0.1 min.41
  28.2 0.1 collective-permute-start.9
  28.4 0.2 shard_map.96.refs_4_
  28.6 0.1 collective-permute-start.6
  28.7 1.6 %collective-permute-start.7 = (bf16[4,9,8,256]{3,2,1,0:T(8,128)(2,1)S(1)}, bf16[4,9,8,256]{3,2,1,0:T(8,128)(2,1)S(1)}, u32[]{:S(2)}, u32[]{:S(2)}) collective-permute-start(bf16[4,9,8,256]{3,2,1,0:T(8,128)(2,1)S(1)} %shard_map.96.refs_4_), channel_id=1, source_target_pairs={{0,2},{1,3},{2,0},{3,1},{4,6},{5,7},{6,4},{7,5},{8,10},{9,11},{10,... | collective-permute-start | bytes 442376 | tf_op jit(solution)/shard_map/ppermute | solution.py:420
  30.2 0.1 convert_reduce_fusion
  30.3 0.1 reshape.56
  30.4 0.1 min.37
  30.5 1.1 %collective-permute-done.10.refs_2_ = bf16[32,8,256]{2,1,0:T(8,128)(2,1)S(1)} collective-permute-done((bf16[32,8,256]{2,1,0:T(8,128)(2,1)S(1)}, bf16[32,8,256]{2,1,0:T(8,128)(2,1)S(1)}, u32[]{:S(2)}, u32[]{:S(2)}) %collective-permute-start.10) | collective-permute-done | bytes 131104 | tf_op jit(solution)/shard_map/ppermute | solution.py:420
  31.6 0.1 pad_maximum_fusion.1.invn_ref
  31.7 0.1 pad_maximum_fusion.invn_ref
  31.8 5.2 %all-to-all-start.1 = ((bf16[8,32,1024]{2,1,0:T(8,128)(2,1)}), bf16[8,32,1024]{2,1,0:T(8,128)(2,1)S(1)}, u32[]{:S(2)}, u32[]{:S(2)}) async-start(bf16[8,32,1024]{2,1,0:T(8,128)(2,1)} %get-tuple-element.29), calls=%async_computation.1 | async-start | bytes 1048576 | tf_op jit(solution)/shard_map/all_to_all | solution.py:485
  37.0 2.0 %collective-permute-start.3 = (bf16[32,8,256]{2,1,0:T(8,128)(2,1)S(1)}, bf16[32,8,256]{2,1,0:T(8,128)(2,1)S(1)}, u32[]{:S(2)}, u32[]{:S(2)}) collective-permute-start(bf16[32,8,256]{2,1,0:T(8,128)(2,1)S(1)} %get-tuple-element.32), channel_id=1, source_target_pairs={{0,4},{4,0},{8,12},{12,8},{16,20},{20,16},{24,28},{28,24},{1,5},{5... | collective-permute-start | bytes 393224 | tf_op jit(solution)/shard_map/ppermute | solution.py:420
  39.0 1.5 %collective-permute-start.4 = (bf16[32,8,256]{2,1,0:T(8,128)(2,1)S(1)}, bf16[32,8,256]{2,1,0:T(8,128)(2,1)S(1)}, u32[]{:S(2)}, u32[]{:S(2)}) collective-permute-start(bf16[32,8,256]{2,1,0:T(8,128)(2,1)S(1)} %get-tuple-element.33), channel_id=1, source_target_pairs={{0,8},{4,12},{8,0},{12,4},{16,24},{20,28},{24,16},{28,20},{1,9},{5... | collective-permute-start | bytes 393224 | tf_op jit(solution)/shard_map/ppermute | solution.py:420
  40.5 0.1 collective-permute-start.5
  40.6 1.0 %copy-done.5 = bf16[1024,256]{1,0:T(8,128)(2,1)S(1)} copy-done((bf16[1024,256]{1,0:T(8,128)(2,1)S(1)}, bf16[1024,256]{1,0:T(8,128)(2,1)}, u32[]{:S(2)}) %copy-start.5) | copy-done | bytes 524312
  41.6 11.3 %shard_map.98 = (s16[8,32,1152]{2,1,0:T(8,128)(2,1)}, f32[32,2048]{1,0:T(8,128)S(1)}, f32[32,2048]{1,0:T(8,128)S(1)}, f32[32,2048]{1,0:T(8,128)S(1)}, f32[32,2048]{1,0:T(8,128)S(1)}) custom-call(s32[4]{0:T(128)S(1)} %pad_add_fusion.c_ref, f32[16,128]{1,0:T(8,128)S(1)} %pad_maximum_fusion.1.invn_ref, bf16[1024,256]{1,0:T(8,128)(2,1)S(1)} %copy-done.5, ...), custom_call_target="tpu_custom_call" | custom-call | flops 10000000000 | tf_op jit(solution)/shard_map/pallas_call | solution.py:537
  52.9 0.7 copy-done.7
  53.6 0.7 copy-done.9
  54.4 0.7 copy-done.11
  55.1 5.9 %all-to-all-start.2 = ((s16[8,32,1152]{2,1,0:T(8,128)(2,1)}), s16[8,32,1152]{2,1,0:T(8,128)(2,1)S(1)}, u32[]{:S(2)}, u32[]{:S(2)}) async-start(s16[8,32,1152]{2,1,0:T(8,128)(2,1)} %get-tuple-element.47), calls=%async_computation.2 | async-start | bytes 1179648 | tf_op jit(solution)/shard_map/all_to_all | solution.py:561
  61.0 0.0 copy-start.6
  61.1 1.0 copy-done.6
  62.1 0.9 copy-done.8
  63.0 0.9 copy-done.10
  64.0 0.9 copy-done.12
  64.9 0.9 copy-done.14
  65.9 11.5 %shard_map.99 = (s16[8,32,1152]{2,1,0:T(8,128)(2,1)}, f32[32,2048]{1,0:T(8,128)S(1)}, f32[32,2048]{1,0:T(8,128)S(1)}, f32[32,2048]{1,0:T(8,128)S(1)}, f32[32,2048]{1,0:T(8,128)S(1)}) custom-call(s32[4]{0:T(128)S(1)} %pad_add_fusion.c_ref, f32[16,128]{1,0:T(8,128)S(1)} %pad_maximum_fusion.invn_ref, bf16[1024,256]{1,0:T(8,128)(2,1)S(1)} %copy-done.6, ...), custom_call_target="tpu_custom_call" | custom-call | flops 10000000000 | tf_op jit(solution)/shard_map/pallas_call | solution.py:537
  77.4 0.1 collective-permute-start.12
  77.5 1.6 %collective-permute-start.13 = (f32[32,2048]{1,0:T(8,128)S(1)}, f32[32,2048]{1,0:T(8,128)S(1)}, u32[]{:S(2)}, u32[]{:S(2)}) collective-permute-start(f32[32,2048]{1,0:T(8,128)S(1)} %get-tuple-element.45), channel_id=1, source_target_pairs={{0,2},{1,3},{2,0},{3,1},{4,6},{5,7},{6,4},{7,5},{8,10},{9,11},{10,... | collective-permute-start | bytes 786440 | tf_op jit(solution)/shard_map/ppermute | solution.py:420
  79.0 0.3 collective-permute-start.14
  79.3 6.0 %all-to-all-start.3 = ((s16[8,32,1152]{2,1,0:T(8,128)(2,1)}), s16[8,32,1152]{2,1,0:T(8,128)(2,1)S(1)}, u32[]{:S(2)}, u32[]{:S(2)}) async-start(s16[8,32,1152]{2,1,0:T(8,128)(2,1)} %get-tuple-element.49), calls=%async_computation.3 | async-start | bytes 1179648 | tf_op jit(solution)/shard_map/all_to_all | solution.py:561
  85.3 1.3 %collective-permute-done.13 = f32[32,2048]{1,0:T(8,128)S(1)} collective-permute-done((f32[32,2048]{1,0:T(8,128)S(1)}, f32[32,2048]{1,0:T(8,128)S(1)}, u32[]{:S(2)}, u32[]{:S(2)}) %collective-permute-start.13) | collective-permute-done | bytes 262176 | tf_op jit(solution)/shard_map/ppermute | solution.py:420
  86.6 4.7 %collective-permute-done.14 = f32[32,2048]{1,0:T(8,128)S(1)} collective-permute-done((f32[32,2048]{1,0:T(8,128)S(1)}, f32[32,2048]{1,0:T(8,128)S(1)}, u32[]{:S(2)}, u32[]{:S(2)}) %collective-permute-start.14) | collective-permute-done | bytes 262176 | tf_op jit(solution)/shard_map/ppermute | solution.py:420
  91.3 0.1 add_add_fusion
  91.4 2.1 %collective-permute-start.15 = (f32[8,2048]{1,0:T(8,128)S(1)}, f32[8,2048]{1,0:T(8,128)S(1)}, u32[]{:S(2)}, u32[]{:S(2)}) collective-permute-start(f32[8,2048]{1,0:T(8,128)S(1)} %get-tuple-element.50), channel_id=1, source_target_pairs={{0,4},{4,0},{8,12},{12,8},{16,20},{20,16},{24,28},{28,24},{1,5},{5... | collective-permute-start | bytes 196616 | tf_op jit(solution)/shard_map/ppermute | solution.py:420
  93.5 1.5 %collective-permute-start.16 = (f32[8,2048]{1,0:T(8,128)S(1)}, f32[8,2048]{1,0:T(8,128)S(1)}, u32[]{:S(2)}, u32[]{:S(2)}) collective-permute-start(f32[8,2048]{1,0:T(8,128)S(1)} %get-tuple-element.52), channel_id=1, source_target_pairs={{0,8},{4,12},{8,0},{12,4},{16,24},{20,28},{24,16},{28,20},{1,9},{5... | collective-permute-start | bytes 196616 | tf_op jit(solution)/shard_map/ppermute | solution.py:420
  95.0 0.1 collective-permute-start.17
  95.1 1.1 %collective-permute-done.15 = f32[8,2048]{1,0:T(8,128)S(1)} collective-permute-done((f32[8,2048]{1,0:T(8,128)S(1)}, f32[8,2048]{1,0:T(8,128)S(1)}, u32[]{:S(2)}, u32[]{:S(2)}) %collective-permute-start.15) | collective-permute-done | bytes 65568 | tf_op jit(solution)/shard_map/ppermute | solution.py:420
  96.1 2.4 %collective-permute-done.16 = f32[8,2048]{1,0:T(8,128)S(1)} collective-permute-done((f32[8,2048]{1,0:T(8,128)S(1)}, f32[8,2048]{1,0:T(8,128)S(1)}, u32[]{:S(2)}, u32[]{:S(2)}) %collective-permute-start.16) | collective-permute-done | bytes 65568 | tf_op jit(solution)/shard_map/ppermute | solution.py:420
  98.5 2.7 %collective-permute-done.17 = f32[8,2048]{1,0:T(8,128)S(1)} collective-permute-done((f32[8,2048]{1,0:T(8,128)S(1)}, f32[8,2048]{1,0:T(8,128)S(1)}, u32[]{:S(2)}, u32[]{:S(2)}) %collective-permute-start.17) | collective-permute-done | bytes 65568 | tf_op jit(solution)/shard_map/ppermute | solution.py:420
  101.3 0.7 fusion.2
  102.0 1.4 %shard_map.100 = f32[1024,256]{1,0:T(8,128)} custom-call(s32[1,256]{1,0:T(1,128)S(1)} %bitcast.10, s16[8,32,1152]{2,1,0:T(8,128)(2,1)S(1)} %all-to-all-done.2.refs_0_, s16[8,32,1152]{2,1,0:T(8,128)(2,1)S(1)} %all-to-all-done.3.refs_1_), custom_call_target="tpu_custom_call" | custom-call | flops 1000000000 | tf_op jit(solution)/shard_map/pallas_call | solution.py:563
  (40 shorter events, 0.1 us)
Async XLA Ops:
  0.6 26.8 %copy-start.4 = (s32[256]{0:T(256)S(1)}, s32[256]{0:T(256)}, u32[]{:S(2)}) copy-start(s32[256]{0:T(256)} %param.11) | copy-start | bytes 3076
  4.5 23.8 %copy-start.1 = (bf16[9,8,256]{2,1,0:T(8,128)(2,1)S(1)}, bf16[9,8,256]{2,1,0:T(8,128)(2,1)}, u32[]{:S(2)}) copy-start(bf16[9,8,256]{2,1,0:T(8,128)(2,1)} %get-tuple-element.26.refs_0_) | copy-start | bytes 110596
  4.6 23.7 %collective-permute-start = (bf16[9,8,256]{2,1,0:T(8,128)(2,1)}, bf16[9,8,256]{2,1,0:T(8,128)(2,1)S(1)}, u32[]{:S(2)}, u32[]{:S(2)}) collective-permute-start(bf16[9,8,256]{2,1,0:T(8,128)(2,1)} %get-tuple-element.26.refs_0_), channel_id=1, source_target_pairs={{0,4},{4,0},{8,12},{12,8},{16,20},{20,16},{24,28},{28,24},{1,5},{5... | collective-permute-start | bytes 110600 | tf_op jit(solution)/shard_map/ppermute | solution.py:420
  7.6 20.8 %collective-permute-start.1 = (bf16[9,8,256]{2,1,0:T(8,128)(2,1)}, bf16[9,8,256]{2,1,0:T(8,128)(2,1)S(1)}, u32[]{:S(2)}, u32[]{:S(2)}) collective-permute-start(bf16[9,8,256]{2,1,0:T(8,128)(2,1)} %get-tuple-element.26.refs_0_), channel_id=1, source_target_pairs={{0,8},{4,12},{8,0},{12,4},{16,24},{20,28},{24,16},{28,20},{1,9},{5... | collective-permute-start | bytes 110600 | tf_op jit(solution)/shard_map/ppermute | solution.py:420
  9.2 19.2 %collective-permute-start.2 = (bf16[9,8,256]{2,1,0:T(8,128)(2,1)}, bf16[9,8,256]{2,1,0:T(8,128)(2,1)S(1)}, u32[]{:S(2)}, u32[]{:S(2)}) collective-permute-start(bf16[9,8,256]{2,1,0:T(8,128)(2,1)} %get-tuple-element.26.refs_0_), channel_id=1, source_target_pairs={{0,12},{4,8},{8,4},{12,0},{16,28},{20,24},{24,20},{28,16},{1,13},{... | collective-permute-start | bytes 110600 | tf_op jit(solution)/shard_map/ppermute | solution.py:420
  9.2 22.6 %all-to-all-start = ((bf16[8,32,1024]{2,1,0:T(8,128)(2,1)}), bf16[8,32,1024]{2,1,0:T(8,128)(2,1)S(1)}, u32[]{:S(2)}, u32[]{:S(2)}) async-start(bf16[8,32,1024]{2,1,0:T(8,128)(2,1)} %get-tuple-element.28), calls=%async_computation | async-start | bytes 1048576 | tf_op jit(solution)/shard_map/all_to_all | solution.py:485
  15.5 1.6 %copy-start = (bf16[8,256,512]{2,1,0:T(8,128)(2,1)S(1)}, bf16[8,256,512]{2,1,0:T(8,128)(2,1)}, u32[]{:S(2)}) copy-start(bf16[8,256,512]{2,1,0:T(8,128)(2,1)} %observed_from) | copy-start | bytes 6291460
  17.1 0.7 copy-start.2
  17.8 0.7 copy-start.3
  23.9 7.7 %collective-permute-start.10 = (bf16[32,8,256]{2,1,0:T(8,128)(2,1)S(1)}, bf16[32,8,256]{2,1,0:T(8,128)(2,1)S(1)}, u32[]{:S(2)}, u32[]{:S(2)}) collective-permute-start(bf16[32,8,256]{2,1,0:T(8,128)(2,1)S(1)} %get-tuple-element.37), channel_id=1, source_target_pairs={{0,8},{4,12},{8,0},{12,4},{16,24},{20,28},{24,16},{28,20},{1,9},{5... | collective-permute-start | bytes 393224 | tf_op jit(solution)/shard_map/ppermute | solution.py:420
  26.0 11.0 %collective-permute-start.11 = (bf16[32,8,256]{2,1,0:T(8,128)(2,1)S(1)}, bf16[32,8,256]{2,1,0:T(8,128)(2,1)S(1)}, u32[]{:S(2)}, u32[]{:S(2)}) collective-permute-start(bf16[32,8,256]{2,1,0:T(8,128)(2,1)S(1)} %get-tuple-element.38), channel_id=1, source_target_pairs={{0,12},{4,8},{8,4},{12,0},{16,28},{20,24},{24,20},{28,16},{1,13},{... | collective-permute-start | bytes 393224 | tf_op jit(solution)/shard_map/ppermute | solution.py:420
  28.2 10.8 %collective-permute-start.9 = (bf16[32,8,256]{2,1,0:T(8,128)(2,1)S(1)}, bf16[32,8,256]{2,1,0:T(8,128)(2,1)S(1)}, u32[]{:S(2)}, u32[]{:S(2)}) collective-permute-start(bf16[32,8,256]{2,1,0:T(8,128)(2,1)S(1)} %get-tuple-element.36), channel_id=1, source_target_pairs={{0,4},{4,0},{8,12},{12,8},{16,20},{20,16},{24,28},{28,24},{1,5},{5... | collective-permute-start | bytes 393224 | tf_op jit(solution)/shard_map/ppermute | solution.py:420
  28.6 11.9 %collective-permute-start.6 = (bf16[4,9,8,256]{3,2,1,0:T(8,128)(2,1)S(1)}, bf16[4,9,8,256]{3,2,1,0:T(8,128)(2,1)S(1)}, u32[]{:S(2)}, u32[]{:S(2)}) collective-permute-start(bf16[4,9,8,256]{3,2,1,0:T(8,128)(2,1)S(1)} %shard_map.96.refs_4_), channel_id=1, source_target_pairs={{0,1},{1,0},{2,3},{3,2},{4,5},{5,4},{6,7},{7,6},{8,9},{9,8},{10,11... | collective-permute-start | bytes 442376 | tf_op jit(solution)/shard_map/ppermute | solution.py:420
  28.7 11.9 %collective-permute-start.7 = (bf16[4,9,8,256]{3,2,1,0:T(8,128)(2,1)S(1)}, bf16[4,9,8,256]{3,2,1,0:T(8,128)(2,1)S(1)}, u32[]{:S(2)}, u32[]{:S(2)}) collective-permute-start(bf16[4,9,8,256]{3,2,1,0:T(8,128)(2,1)S(1)} %shard_map.96.refs_4_), channel_id=1, source_target_pairs={{0,2},{1,3},{2,0},{3,1},{4,6},{5,7},{6,4},{7,5},{8,10},{9,11},{10,... | collective-permute-start | bytes 442376 | tf_op jit(solution)/shard_map/ppermute | solution.py:420
  31.6 8.9 %collective-permute-start.8 = (bf16[4,9,8,256]{3,2,1,0:T(8,128)(2,1)S(1)}, bf16[4,9,8,256]{3,2,1,0:T(8,128)(2,1)S(1)}, u32[]{:S(2)}, u32[]{:S(2)}) collective-permute-start(bf16[4,9,8,256]{3,2,1,0:T(8,128)(2,1)S(1)} %shard_map.96.refs_4_), channel_id=1, source_target_pairs={{0,3},{1,2},{2,1},{3,0},{4,7},{5,6},{6,5},{7,4},{8,11},{9,10},{10,... | collective-permute-start | bytes 442376 | tf_op jit(solution)/shard_map/ppermute | solution.py:420
  31.8 23.3 %all-to-all-start.1 = ((bf16[8,32,1024]{2,1,0:T(8,128)(2,1)}), bf16[8,32,1024]{2,1,0:T(8,128)(2,1)S(1)}, u32[]{:S(2)}, u32[]{:S(2)}) async-start(bf16[8,32,1024]{2,1,0:T(8,128)(2,1)} %get-tuple-element.29), calls=%async_computation.1 | async-start | bytes 1048576 | tf_op jit(solution)/shard_map/all_to_all | solution.py:485
  37.0 24.0 %collective-permute-start.3 = (bf16[32,8,256]{2,1,0:T(8,128)(2,1)S(1)}, bf16[32,8,256]{2,1,0:T(8,128)(2,1)S(1)}, u32[]{:S(2)}, u32[]{:S(2)}) collective-permute-start(bf16[32,8,256]{2,1,0:T(8,128)(2,1)S(1)} %get-tuple-element.32), channel_id=1, source_target_pairs={{0,4},{4,0},{8,12},{12,8},{16,20},{20,16},{24,28},{28,24},{1,5},{5... | collective-permute-start | bytes 393224 | tf_op jit(solution)/shard_map/ppermute | solution.py:420
  39.0 22.0 %collective-permute-start.4 = (bf16[32,8,256]{2,1,0:T(8,128)(2,1)S(1)}, bf16[32,8,256]{2,1,0:T(8,128)(2,1)S(1)}, u32[]{:S(2)}, u32[]{:S(2)}) collective-permute-start(bf16[32,8,256]{2,1,0:T(8,128)(2,1)S(1)} %get-tuple-element.33), channel_id=1, source_target_pairs={{0,8},{4,12},{8,0},{12,4},{16,24},{20,28},{24,16},{28,20},{1,9},{5... | collective-permute-start | bytes 393224 | tf_op jit(solution)/shard_map/ppermute | solution.py:420
  40.5 20.6 %collective-permute-start.5 = (bf16[32,8,256]{2,1,0:T(8,128)(2,1)S(1)}, bf16[32,8,256]{2,1,0:T(8,128)(2,1)S(1)}, u32[]{:S(2)}, u32[]{:S(2)}) collective-permute-start(bf16[32,8,256]{2,1,0:T(8,128)(2,1)S(1)} %get-tuple-element.34), channel_id=1, source_target_pairs={{0,12},{4,8},{8,4},{12,0},{16,28},{20,24},{24,20},{28,16},{1,13},{... | collective-permute-start | bytes 393224 | tf_op jit(solution)/shard_map/ppermute | solution.py:420
  40.5 1.0 %copy-start.5 = (bf16[1024,256]{1,0:T(8,128)(2,1)S(1)}, bf16[1024,256]{1,0:T(8,128)(2,1)}, u32[]{:S(2)}) copy-start(bf16[1024,256]{1,0:T(8,128)(2,1)} %constant.49.table_ref) | copy-start | bytes 1572868
  52.9 0.7 copy-start.7
  53.6 0.7 copy-start.9
  54.4 0.7 copy-start.11
  55.1 6.0 %copy-start.13 = (f32[32,2048]{1,0:T(8,128)}, f32[32,2048]{1,0:T(8,128)S(1)}, u32[]{:S(2)}) copy-start(f32[32,2048]{1,0:T(8,128)S(1)} %get-tuple-element.42.refs_11_) | copy-start | bytes 786436
  55.1 24.2 %all-to-all-start.2 = ((s16[8,32,1152]{2,1,0:T(8,128)(2,1)}), s16[8,32,1152]{2,1,0:T(8,128)(2,1)S(1)}, u32[]{:S(2)}, u32[]{:S(2)}) async-start(s16[8,32,1152]{2,1,0:T(8,128)(2,1)} %get-tuple-element.47), calls=%async_computation.2 | async-start | bytes 1179648 | tf_op jit(solution)/shard_map/all_to_all | solution.py:561
  61.0 1.0 %copy-start.6 = (bf16[1024,256]{1,0:T(8,128)(2,1)S(1)}, bf16[1024,256]{1,0:T(8,128)(2,1)}, u32[]{:S(2)}) copy-start(bf16[1024,256]{1,0:T(8,128)(2,1)} %constant.49.table_ref) | copy-start | bytes 1572868
  62.1 0.9 copy-start.8
  63.0 0.9 copy-start.10
  64.0 0.9 copy-start.12
  64.9 0.9 copy-start.14
  77.4 23.9 %copy-start.15 = (s32[8]{0:T(128)S(1)}, s32[8]{0:T(128)}, u32[]{:S(2)}) copy-start(s32[8]{0:T(128)} %rcounts_ref.1) | copy-start | bytes 100
  77.4 7.9 %collective-permute-start.12 = (f32[32,2048]{1,0:T(8,128)S(1)}, f32[32,2048]{1,0:T(8,128)S(1)}, u32[]{:S(2)}, u32[]{:S(2)}) collective-permute-start(f32[32,2048]{1,0:T(8,128)S(1)} %get-tuple-element.44), channel_id=1, source_target_pairs={{0,1},{1,0},{2,3},{3,2},{4,5},{5,4},{6,7},{7,6},{8,9},{9,8},{10,11... | collective-permute-start | bytes 786440 | tf_op jit(solution)/shard_map/ppermute | solution.py:420
  77.5 9.2 %collective-permute-start.13 = (f32[32,2048]{1,0:T(8,128)S(1)}, f32[32,2048]{1,0:T(8,128)S(1)}, u32[]{:S(2)}, u32[]{:S(2)}) collective-permute-start(f32[32,2048]{1,0:T(8,128)S(1)} %get-tuple-element.45), channel_id=1, source_target_pairs={{0,2},{1,3},{2,0},{3,1},{4,6},{5,7},{6,4},{7,5},{8,10},{9,11},{10,... | collective-permute-start | bytes 786440 | tf_op jit(solution)/shard_map/ppermute | solution.py:420
  79.0 12.3 %collective-permute-start.14 = (f32[32,2048]{1,0:T(8,128)S(1)}, f32[32,2048]{1,0:T(8,128)S(1)}, u32[]{:S(2)}, u32[]{:S(2)}) collective-permute-start(f32[32,2048]{1,0:T(8,128)S(1)} %get-tuple-element.46), channel_id=1, source_target_pairs={{0,3},{1,2},{2,1},{3,0},{4,7},{5,6},{6,5},{7,4},{8,11},{9,10},{10,... | collective-permute-start | bytes 786440 | tf_op jit(solution)/shard_map/ppermute | solution.py:420
  79.3 22.6 %all-to-all-start.3 = ((s16[8,32,1152]{2,1,0:T(8,128)(2,1)}), s16[8,32,1152]{2,1,0:T(8,128)(2,1)S(1)}, u32[]{:S(2)}, u32[]{:S(2)}) async-start(s16[8,32,1152]{2,1,0:T(8,128)(2,1)} %get-tuple-element.49), calls=%async_computation.3 | async-start | bytes 1179648 | tf_op jit(solution)/shard_map/all_to_all | solution.py:561
  91.4 4.7 %collective-permute-start.15 = (f32[8,2048]{1,0:T(8,128)S(1)}, f32[8,2048]{1,0:T(8,128)S(1)}, u32[]{:S(2)}, u32[]{:S(2)}) collective-permute-start(f32[8,2048]{1,0:T(8,128)S(1)} %get-tuple-element.50), channel_id=1, source_target_pairs={{0,4},{4,0},{8,12},{12,8},{16,20},{20,16},{24,28},{28,24},{1,5},{5... | collective-permute-start | bytes 196616 | tf_op jit(solution)/shard_map/ppermute | solution.py:420
  93.5 5.0 %collective-permute-start.16 = (f32[8,2048]{1,0:T(8,128)S(1)}, f32[8,2048]{1,0:T(8,128)S(1)}, u32[]{:S(2)}, u32[]{:S(2)}) collective-permute-start(f32[8,2048]{1,0:T(8,128)S(1)} %get-tuple-element.52), channel_id=1, source_target_pairs={{0,8},{4,12},{8,0},{12,4},{16,24},{20,28},{24,16},{28,20},{1,9},{5... | collective-permute-start | bytes 196616 | tf_op jit(solution)/shard_map/ppermute | solution.py:420
  95.0 6.3 %collective-permute-start.17 = (f32[8,2048]{1,0:T(8,128)S(1)}, f32[8,2048]{1,0:T(8,128)S(1)}, u32[]{:S(2)}, u32[]{:S(2)}) collective-permute-start(f32[8,2048]{1,0:T(8,128)S(1)} %get-tuple-element.51), channel_id=1, source_target_pairs={{0,12},{4,8},{8,4},{12,0},{16,28},{20,24},{24,20},{28,16},{1,13},{... | collective-permute-start | bytes 196616 | tf_op jit(solution)/shard_map/ppermute | solution.py:420

commit v6 on v5

--- a/solution.py
+++ b/solution.py
@@ -54,86 +54,71 @@
     return jnp.where(rows == lanes, 1.0, 0.0).astype(jnp.bfloat16)
 
 
-def turn_kernel(rcounts_ref, spectra_from, counts_from, rspectra_from, *refs):
-    u_to, *v_to = refs[: 1 + CHUNKS]
-    spectra_ref, counts_ref, rspectra_ref, turned_ref, u_ref, sems, out_sems = refs[1 + CHUNKS :]
+def prepare_kernel(c_ref, rcounts_ref, *refs):
+    spectra_from, counts_from, rspectra_from, observed_from, window_from, order_from = refs[:6]
+    v_to, e_to = refs[6 : 6 + CHUNKS], refs[6 + CHUNKS : -11]
+    (
+        spectra_ref, counts_ref, rspectra_ref, observed_ref, window_ref, order_ref,
+        turned_ref, line_ref, out_ref, sems, out_sems,
+    ) = refs[-11:]
     k_own, col_total = spectra_ref.shape
-    rcv_total, cols, _ = v_to[0].shape
-    members = col_total // (cols * CHUNKS)
+    rcv_total, chunk, _ = v_to[0].shape
+    row_total, _, lag_total = observed_ref.shape
+    half = lag_total // 2
+    members = len(e_to)
+    cols = col_total // members
     width = min(k_own, 2 * LANES)
-    copies = [
-        pltpu.make_async_copy(counts_from, counts_ref, sems.at[0]),
-        pltpu.make_async_copy(rspectra_from, rspectra_ref, sems.at[1]),
+    n_in, n_out = 0, 0
+
+    def fetch(src, dst):
+        nonlocal n_in
+        copy = pltpu.make_async_copy(src, dst, sems.at[n_in])
+        copy.start()
+        n_in += 1
+        return copy
+
+    def send(src, dst):
+        nonlocal n_out
+        copy = pltpu.make_async_copy(src, dst, out_sems.at[n_out])
+        copy.start()
+        n_out += 1
+        return copy
+
+    small = [
+        fetch(counts_from, counts_ref),
+        fetch(window_from, window_ref),
+        fetch(order_from, order_ref),
+        fetch(rspectra_from, rspectra_ref),
     ]
-    for n, begin in enumerate(range(0, k_own, width)):
+    spectra = []
+    for begin in range(0, k_own, width):
         rows = pl.ds(begin, width)
-        copies.append(
-            pltpu.make_async_copy(spectra_from.at[rows], spectra_ref.at[rows], sems.at[2 + n])
-        )
-    for copy in copies:
-        copy.start()
+        spectra.append(fetch(spectra_from.at[rows], spectra_ref.at[rows]))
+    seen = [fetch(observed_from.at[i], observed_ref.at[i]) for i in range(row_total)]
+
     eye = eye_of(col_total)
     seg_ids = lax.broadcasted_iota(jnp.int32, (width, col_total), 0) % S
-    copies[0].wait()
+    for copy in small:
+        copy.wait()
     inside = seg_ids < counts_ref[...]
     for n, begin in enumerate(range(0, k_own, width)):
-        copies[2 + n].wait()
+        spectra[n].wait()
         part = spectra_ref[begin : begin + width, :].astype(jnp.float32)
         part = jnp.where(inside, part, 0.0).astype(jnp.bfloat16)
         turned_ref[:, begin : begin + width] = nt(eye, part).astype(jnp.bfloat16)
     outs = []
     for c in range(CHUNKS):
         for dest in range(rcv_total):
-            first = (dest % members * CHUNKS + c) * cols
-            outs.append(
-                pltpu.make_async_copy(
-                    turned_ref.at[pl.ds(first, cols)],
-                    v_to[c].at[dest],
-                    out_sems.at[c * rcv_total + dest],
-                )
-            )
-            outs[-1].start()
-    copies[1].wait()
-    pieces, rows, half = u_ref.shape
-    row_ids = lax.broadcasted_iota(jnp.int32, (rows, half), 0)
-    counts = jnp.zeros((rows, half), jnp.int32)
-    for i in range(rows):
-        counts = jnp.where(row_ids == i, rcounts_ref[i], counts)
-    seg_ids = lax.broadcasted_iota(jnp.int32, (rows, half), 1) % S
-    for n in range(pieces - 1):
-        part = rspectra_ref[:, n * half : (n + 1) * half].astype(jnp.float32)
-        u_ref[n] = jnp.where(seg_ids < counts, part, 0.0).astype(jnp.bfloat16)
-    u_ref[pieces - 1] = counts.astype(jnp.float32).astype(jnp.bfloat16)
-    outs.append(pltpu.make_async_copy(u_ref, u_to, out_sems.at[CHUNKS * rcv_total]))
-    outs[-1].start()
-    for copy in outs:
-        copy.wait()
-
-
-def fold_kernel(c_ref, observed_from, window_from, order_from, *rest):
-    *out_to, observed_ref, window_ref, order_ref, line_ref, out_ref, sems, out_sems = rest
-    row_total, col_total, lag_total = observed_ref.shape
-    half = lag_total // 2
-    members = len(out_to) // CHUNKS
-    cols = col_total // len(out_to)
-    lines = col_total * row_total
-    copies = [
-        pltpu.make_async_copy(window_from, window_ref, sems.at[row_total]),
-        pltpu.make_async_copy(order_from, order_ref, sems.at[row_total + 1]),
-    ] + [
-        pltpu.make_async_copy(observed_from.at[i], observed_ref.at[i], sems.at[i])
-        for i in range(row_total)
-    ]
-    for copy in copies:
-        copy.start()
-    for copy in copies[:2]:
-        copy.wait()
+            first = dest % members * cols + c * chunk
+            outs.append(send(turned_ref.at[pl.ds(first, chunk)], v_to[c].at[dest]))
+
     window = jnp.concatenate([window_ref[0], window_ref[1]], axis=0).astype(jnp.float32).T
     station = lax.broadcasted_iota(jnp.int32, (col_total, col_total), 0) + c_ref[1]
     pick = jnp.where(station == order_ref[...], 1.0, 0.0).astype(jnp.bfloat16)
     lag_ids = lax.broadcasted_iota(jnp.int32, (col_total, half), 1).astype(jnp.float32)
+    lines = col_total * row_total
     for i in range(row_total):
-        copies[2 + i].wait()
+        seen[i].wait()
         begin = window[:, i : i + 1]
         end = begin + window[:, row_total + i : row_total + i + 1]
         values = observed_ref[i].astype(jnp.float32)
@@ -145,44 +130,53 @@
             line_ref[pl.ds(h * lines + i, col_total, stride=row_total), :] = moved[
                 :, h * LANES : (h + 1) * LANES
             ]
-    mine = c_ref[0]
-    copies = []
-    for c in range(CHUNKS):
-        for k in range(members):
-            n = c * members + k
-            first = ((mine ^ k) * CHUNKS + c) * (cols * row_total)
-            for h in range(half // LANES):
-                begin = pl.multiple_of(h * lines + first, cols * row_total)
-                rows = line_ref[pl.ds(begin, cols * row_total), :]
-                out_ref[n, :, :, h * LANES : (h + 1) * LANES] = rows.reshape(
-                    cols, row_total, LANES
-                ).astype(jnp.bfloat16)
-            copies.append(pltpu.make_async_copy(out_ref.at[n], out_to[n], out_sems.at[n]))
-            copies[-1].start()
-    for copy in copies:
+    row_ids = lax.broadcasted_iota(jnp.int32, (row_total, half), 0)
+    counts = jnp.zeros((row_total, half), jnp.int32)
+    for i in range(row_total):
+        counts = jnp.where(row_ids == i, rcounts_ref[i], counts)
+    seg_ids = lax.broadcasted_iota(jnp.int32, (row_total, half), 1) % S
+    pieces = rspectra_ref.shape[1] // half
+    extra = []
+    for n in range(pieces):
+        part = rspectra_ref[:, n * half : (n + 1) * half].astype(jnp.float32)
+        extra.append(jnp.where(seg_ids < counts, part, 0.0).astype(jnp.bfloat16))
+    extra.append(counts.astype(jnp.float32).astype(jnp.bfloat16))
+    for k in range(members):
+        for n, part in enumerate(extra):
+            out_ref[k, cols + n] = part
+        first = (c_ref[0] ^ k) * (cols * row_total)
+        for h in range(half // LANES):
+            begin = pl.multiple_of(h * lines + first, cols * row_total)
+            rows = line_ref[pl.ds(begin, cols * row_total), :]
+            out_ref[k, :cols, :, h * LANES : (h + 1) * LANES] = rows.reshape(
+                cols, row_total, LANES
+            ).astype(jnp.bfloat16)
+        outs.append(send(out_ref.at[k], e_to[k]))
+    for copy in outs:
         copy.wait()
 
 
 def near_kernel(*refs):
     *parts, out_ref, sems = refs
-    copies = [
-        pltpu.make_async_copy(ref, out_ref.at[k], sems.at[k]) for k, ref in enumerate(parts)
-    ]
+    extra = out_ref.shape[1]
+    copies = []
+    for k, ref in enumerate(parts):
+        rows = ref.at[pl.ds(ref.shape[0] - extra, extra)]
+        copies.append(pltpu.make_async_copy(rows, out_ref.at[k], sems.at[k]))
+        copies[-1].start()
     for copy in copies:
-        copy.start()
-    for copy in copies:
-        copy.wait()
-
-
-def pair_kernel(n_e, n_r, n_in, c_ref, invn_ref, table_ref, v_from, *refs):
+        copy.wait()
+
+
+def pair_kernel(chunk, n_e, n_r, n_in, n_out, c_ref, invn_ref, table_ref, v_from, *refs):
     refs = list(refs)
     e_from, u_from = refs[:n_e], refs[n_e : n_e + n_r]
     r_from = refs[n_e + n_r : n_e + n_r + n_in]
-    w_to, *r_to = refs[n_e + n_r + n_in : n_e + 2 * n_r + n_in + 1]
+    w_to, *r_to = refs[n_e + n_r + n_in : n_e + n_r + n_in + n_out + 1]
     (
         x_ref, z_ref, plain_ref, turned_ref, code_ref, u_ref, v_ref, e_ref, r_ref, w_ref,
         sems, w_sems,
-    ) = refs[n_e + 2 * n_r + n_in + 1 :]
+    ) = refs[n_e + n_r + n_in + n_out + 1 :]
 
     src_total, col_total, k_own = v_ref.shape
     ref_total, irec, k_quarter = r_ref.shape
@@ -200,12 +194,13 @@
     for k, ref in enumerate(u_from):
         early.append(pltpu.make_async_copy(ref, u_ref.at[quarter_me ^ k], sems.at[1 + k]))
     late = [
-        pltpu.make_async_copy(ref, e_ref.at[k], sems.at[1 + n_r + k])
+        pltpu.make_async_copy(
+            ref.at[pl.ds(chunk * col_total, col_total)], e_ref.at[k], sems.at[1 + n_r + k]
+        )
         for k, ref in enumerate(e_from)
     ]
     last = [
-        pltpu.make_async_copy(ref, r_ref.at[quarter_me ^ k], sems.at[1 + n_r + n_e + k])
-        for k, ref in enumerate(r_from)
+        pltpu.make_async_copy(ref, r_ref, sems.at[1 + n_r + n_e]) for ref in r_from
     ]
     for copy in early + late + last:
         copy.start()
@@ -377,7 +372,7 @@
         copy.wait()
     lax.fori_loop(0, src_total, from_owner, 0, unroll=4)
     outs = [
-        pltpu.make_async_copy(r_ref.at[quarter_me ^ k], ref, sems.at[k])
+        pltpu.make_async_copy(r_ref if n_out == 1 else r_ref.at[quarter_me ^ k], ref, sems.at[k])
         for k, ref in enumerate(r_to)
     ]
     for copy in outs:
@@ -461,54 +456,44 @@
     def after(x, *others):
         return lax.optimization_barrier((x,) + others)[0]
 
-    u_own, *sent = pl.pallas_call(
-        turn_kernel,
-        out_shape=[jax.ShapeDtypeStruct((extra, row_total, half), bf16)]
-        + [jax.ShapeDtypeStruct((rcv_total, cols, k_own), bf16)] * CHUNKS,
-        in_specs=[smem] + [hbm] * 3,
-        out_specs=[hbm] * (1 + CHUNKS),
+    shape = (cols * CHUNKS + extra, row_total, half)
+    prepared = pl.pallas_call(
+        prepare_kernel,
+        out_shape=[jax.ShapeDtypeStruct((rcv_total, cols, k_own), bf16)] * CHUNKS
+        + [jax.ShapeDtypeStruct(shape, bf16)] * members,
+        in_specs=[smem] * 2 + [hbm] * 6,
+        out_specs=[hbm] * (CHUNKS + members),
         scratch_shapes=[
             pltpu.VMEM((k_own, col_total), bf16),
             pltpu.VMEM((1, col_total), jnp.int32),
             pltpu.VMEM(receiver_spectra.shape, bf16),
+            pltpu.VMEM(observed.shape, bf16),
+            pltpu.VMEM(lag_window.shape, jnp.int32),
+            pltpu.VMEM((1, col_total), jnp.int32),
             pltpu.VMEM((col_total, k_own), bf16),
-            pltpu.VMEM((extra, row_total, half), bf16),
-            pltpu.SemaphoreType.DMA((2 + k_own // min(k_own, 2 * LANES),)),
-            pltpu.SemaphoreType.DMA((CHUNKS * rcv_total + 1,)),
+            pltpu.VMEM((half // LANES * col_total * row_total, LANES), jnp.float32),
+            pltpu.VMEM((members,) + shape, bf16),
+            pltpu.SemaphoreType.DMA((4 + k_own // min(k_own, 2 * LANES) + row_total,)),
+            pltpu.SemaphoreType.DMA((CHUNKS * rcv_total + members,)),
         ],
         compiler_params=params(62),
         cost_estimate=cost(0),
-    )(receiver_counts, reference_spectra, reference_counts.reshape(1, col_total), receiver_spectra)
+    )(
+        scalars,
+        receiver_counts,
+        reference_spectra,
+        reference_counts.reshape(1, col_total),
+        receiver_spectra,
+        observed,
+        lag_window,
+        column_station.reshape(1, col_total),
+    )
+    sent, folded = prepared[:CHUNKS], prepared[CHUNKS:]
     v_all = []
     for x in sent:
         x = after(x, *v_all[-1:])
         v_all.append(lax.all_to_all(x, "rcv", split_axis=0, concat_axis=0, tiled=True))
-
-    shape = (cols, row_total, half)
-    folded = pl.pallas_call(
-        fold_kernel,
-        out_shape=[jax.ShapeDtypeStruct(shape, bf16)] * (CHUNKS * members),
-        in_specs=[smem] + [hbm] * 3,
-        out_specs=[hbm] * (CHUNKS * members),
-        scratch_shapes=[
-            pltpu.VMEM(observed.shape, bf16),
-            pltpu.VMEM(lag_window.shape, jnp.int32),
-            pltpu.VMEM((1, col_total), jnp.int32),
-            pltpu.VMEM((half // LANES * col_total * row_total, LANES), jnp.float32),
-            pltpu.VMEM((CHUNKS * members,) + shape, bf16),
-            pltpu.SemaphoreType.DMA((row_total + 2,)),
-            pltpu.SemaphoreType.DMA((CHUNKS * members,)),
-        ],
-        compiler_params=params(32),
-        cost_estimate=cost(0),
-    )(scalars, after(observed, u_own), lag_window, column_station.reshape(1, col_total))
-    e_all = [
-        [
-            x if k == 0 else swap(x, "rcv", rcv_total, k)
-            for k, x in enumerate(folded[c * members : (c + 1) * members])
-        ]
-        for c in range(CHUNKS)
-    ]
+    e_all = [folded[0]] + [swap(folded[k], "rcv", rcv_total, k) for k in range(1, members)]
 
     near = pl.pallas_call(
         near_kernel,
@@ -518,7 +503,7 @@
         scratch_shapes=[pltpu.SemaphoreType.DMA((members,))],
         compiler_params=params(16),
         cost_estimate=cost(0),
-    )(u_own, *[swap(u_own, "rcv", rcv_total, k) for k in range(1, members)])
+    )(*e_all)
     u_all = [near] + [swap(near, "ref", ref_total, k) for k in range(1, ref_total)]
     group_counts = near[:, extra - 1, :, 0].reshape(irec).astype(jnp.float32)
     own_counts = lax.dynamic_slice_in_dim(
@@ -533,13 +518,17 @@
         least = jnp.minimum(counts[:, :, None], group_counts[None, None, :])
         inverse = (1.0 / least).reshape(jp_total, jj_total * irec)
         inverse = jnp.concatenate([inverse, inverse], axis=1)
-        operands = [v_all[c], *e_all[c], *u_all, *r_all]
+        operands = [v_all[c], *e_all, *u_all, *r_all]
+        if c < CHUNKS - 1:
+            r_shapes = [jax.ShapeDtypeStruct((ref_total, irec, k_quarter), jnp.float32)]
+        else:
+            r_shapes = [jax.ShapeDtypeStruct((irec, k_quarter), jnp.float32)] * ref_total
         w_part, *r_all = pl.pallas_call(
-            functools.partial(pair_kernel, members, ref_total, len(r_all)),
+            functools.partial(pair_kernel, c, members, ref_total, len(r_all), len(r_shapes)),
             out_shape=[jax.ShapeDtypeStruct((rcv_total, cols, k_own + LANES), jnp.int16)]
-            + [jax.ShapeDtypeStruct((irec, k_quarter), jnp.float32)] * ref_total,
+            + r_shapes,
             in_specs=[smem] + [vmem] * 2 + [hbm] * len(operands),
-            out_specs=[hbm] * (1 + ref_total),
+            out_specs=[hbm] * (1 + len(r_shapes)),
             scratch_shapes=[
                 pltpu.VMEM((lines, LANES), jnp.float32),
                 pltpu.VMEM((lines, LANES), jnp.float32),

time: 104 us -> 109 us (1.048)
  waiting for transfers between devices: 13.4 us -> 35.2 us
  starting transfers between devices: 42.3 us -> 32 us
  local copies, waits for them, and re-layouts: 12 us -> 7.88 us
  Pallas kernels: 33.7 us -> 31.3 us
    ppermute x18 -> x12, waiting for transfers between devices: 13.4 us -> 35.2 us  [swap(): return lax.ppermute(x, axis, [(r, r ^ k) for r in range(total)])]
    ppermute x18 -> x12, starting transfers between devices: 19 us -> 11.2 us  [swap(): return lax.ppermute(x, axis, [(r, r ^ k) for r in range(total)])]
    unnamed x32 -> x30, local copies, waits for them, and re-layouts: 11 us -> 6.95 us
    pallas_call x4 -> x3, Pallas kernels: 32.1 us -> 29.7 us  [the longest x2 22.7 us: shards(): pl.pallas_call(functools.partial(pair_kernel, c, members, ref_total, len(...]
    all_to_all x2, starting transfers between devices: 11.9 us -> 9.69 us  [shards(): lax.all_to_all(w_part, 'rcv', split_axis=0, concat_axis=0, tiled=True)]
  transfers between devices with their start and end apart: 22 -> 16, of which waited for: 6 -> 10; matrix products, arithmetic and copies ran while one was open for 2% -> 2% of each run, Pallas kernels for 28% -> 21%
where the time goes in v6:
time: 109 us
  waiting for transfers between devices  35.2 us (32%)
  starting transfers between devices  32 us (29%)
  Pallas kernels  31.3 us (29%)
  local copies, waits for them, and re-layouts  7.88 us (7%)
  other arithmetic  1.67 us (2%)
    ppermute x12, waiting for transfers between devices, swap(): return lax.ppermute(x, axis, [(r, r ^ k) for r in range(total)])  35.2 us
    pallas_call x2, Pallas kernels, shards(): pl.pallas_call(functools.partial(pair_kernel, c, members, ref_total, len(...  22.7 us
    ppermute x12, starting transfers between devices, swap(): return lax.ppermute(x, axis, [(r, r ^ k) for r in range(total)])  11.2 us
    all_to_all x2, starting transfers between devices, shards(): lax.all_to_all(x, 'rcv', split_axis=0, concat_axis=0, tiled=True)  11.1 us
    all_to_all x2, starting transfers between devices, shards(): lax.all_to_all(w_part, 'rcv', split_axis=0, concat_axis=0, tiled=True)  9.69 us
    pallas_call x1, Pallas kernels, shards(): pl.pallas_call(prepare_kernel, out_shape=[jax.ShapeDtypeStruct((rcv_total...  6.97 us
    unnamed x30, local copies, waits for them, and re-layouts  6.95 us
  transfers between devices with their start and end apart: 16, of which 10 were waited for; matrix products, arithmetic and copies ran while one was open for 2% of the time, Pallas kernels for 21%

profile of v6, /device:TPU:0, one launch (start us, length us, event | category | flops | bytes accessed | tf_op | source)
XLA Modules:
  0.0 108.8 jit_solution(3197553850526445492)
XLA Ops:
  0.6 0.0 copy-start.3
  0.7 0.6 pad_add_fusion.c_ref
  1.2 7.0 %shard_map.95 = (bf16[8,32,1024]{2,1,0:T(8,128)(2,1)}, bf16[8,32,1024]{2,1,0:T(8,128)(2,1)}, bf16[73,8,256]{2,1,0:T(8,128)(2,1)}, bf16[73,8,256]{2,1,0:T(8,128)(...) custom-call(s32[4]{0:T(128)} %pad_add_fusion.c_ref, s32[8]{0:T(128)} %rcounts_ref.1, ...), custom_call_target="tpu_custom_call" | custom-call | tf_op jit(solution)/shard_map/pallas_call | solution.py:460
  8.2 0.0 copy-start.10
  8.2 7.4 %all-to-all-start = ((bf16[8,32,1024]{2,1,0:T(8,128)(2,1)}), bf16[8,32,1024]{2,1,0:T(8,128)(2,1)S(1)}, u32[]{:S(2)}, u32[]{:S(2)}) async-start(bf16[8,32,1024]{2,1,0:T(8,128)(2,1)} %get-tuple-element.22), calls=%async_computation | async-start | bytes 1048576 | tf_op jit(solution)/shard_map/all_to_all | solution.py:495
  15.7 2.0 %collective-permute-start = (bf16[73,8,256]{2,1,0:T(8,128)(2,1)}, bf16[73,8,256]{2,1,0:T(8,128)(2,1)S(1)}, u32[]{:S(2)}, u32[]{:S(2)}) collective-permute-start(bf16[73,8,256]{2,1,0:T(8,128)(2,1)} %get-tuple-element.18), channel_id=1, source_target_pairs={{0,4},{4,0},{8,12},{12,8},{16,20},{20,16},{24,28},{28,24},{1,5},{5... | collective-permute-start | bytes 897032 | tf_op jit(solution)/shard_map/ppermute | solution.py:415
  17.7 1.5 %collective-permute-start.1 = (bf16[73,8,256]{2,1,0:T(8,128)(2,1)}, bf16[73,8,256]{2,1,0:T(8,128)(2,1)S(1)}, u32[]{:S(2)}, u32[]{:S(2)}) collective-permute-start(bf16[73,8,256]{2,1,0:T(8,128)(2,1)} %get-tuple-element.19), channel_id=1, source_target_pairs={{0,8},{4,12},{8,0},{12,4},{16,24},{20,28},{24,16},{28,20},{1,9},{5... | collective-permute-start | bytes 897032 | tf_op jit(solution)/shard_map/ppermute | solution.py:415
  19.2 0.0 collective-permute-start.2
  19.2 0.1 dynamic-slice_convert_fusion
  19.3 0.1 fusion.7
  19.3 0.1 slice.42
  19.4 0.1 copy.12
  19.5 0.1 min.34
  19.6 0.1 min.35
  19.7 0.1 slice.45
  19.8 0.1 copy.13
  19.8 0.1 min.40
  19.9 0.1 min.41
  20.0 10.0 %collective-permute-done.refs_1_ = bf16[73,8,256]{2,1,0:T(8,128)(2,1)S(1)} collective-permute-done((bf16[73,8,256]{2,1,0:T(8,128)(2,1)}, bf16[73,8,256]{2,1,0:T(8,128)(2,1)S(1)}, u32[]{:S(2)}, u32[]{:S(2)}) %collective-permute-start) | collective-permute-done | bytes 299040 | tf_op jit(solution)/shard_map/ppermute | solution.py:415
  30.0 4.2 %collective-permute-done.1.refs_2_ = bf16[73,8,256]{2,1,0:T(8,128)(2,1)S(1)} collective-permute-done((bf16[73,8,256]{2,1,0:T(8,128)(2,1)}, bf16[73,8,256]{2,1,0:T(8,128)(2,1)S(1)}, u32[]{:S(2)}, u32[]{:S(2)}) %collective-permute-start.1) | collective-permute-done | bytes 299040 | tf_op jit(solution)/shard_map/ppermute | solution.py:415
  34.2 6.0 %collective-permute-done.2.refs_3_ = bf16[73,8,256]{2,1,0:T(8,128)(2,1)S(1)} collective-permute-done((bf16[73,8,256]{2,1,0:T(8,128)(2,1)}, bf16[73,8,256]{2,1,0:T(8,128)(2,1)S(1)}, u32[]{:S(2)}, u32[]{:S(2)}) %collective-permute-start.2) | collective-permute-done | bytes 299040 | tf_op jit(solution)/shard_map/ppermute | solution.py:415
  40.2 1.0 copy-done
  41.2 0.2 shard_map.96.refs_4_
  41.4 0.1 collective-permute-start.3
  41.5 1.6 %collective-permute-start.4 = (bf16[4,9,8,256]{3,2,1,0:T(8,128)(2,1)S(1)}, bf16[4,9,8,256]{3,2,1,0:T(8,128)(2,1)S(1)}, u32[]{:S(2)}, u32[]{:S(2)}) collective-permute-start(bf16[4,9,8,256]{3,2,1,0:T(8,128)(2,1)S(1)} %shard_map.96.refs_4_), channel_id=1, source_target_pairs={{0,2},{1,3},{2,0},{3,1},{4,6},{5,7},{6,4},{7,5},{8,10},{9,11},{10,... | collective-permute-start | bytes 442376 | tf_op jit(solution)/shard_map/ppermute | solution.py:415
  43.0 0.3 collective-permute-start.5
  43.3 0.1 convert_reduce_fusion
  43.4 0.1 reshape.56
  43.5 0.1 min.37
  43.6 0.1 pad_maximum_fusion.1.invn_ref
  43.7 0.1 pad_maximum_fusion.invn_ref
  43.8 0.0 all-to-all-done.v_from
  43.8 3.7 %all-to-all-start.1 = ((bf16[8,32,1024]{2,1,0:T(8,128)(2,1)}), bf16[8,32,1024]{2,1,0:T(8,128)(2,1)S(1)}, u32[]{:S(2)}, u32[]{:S(2)}) async-start(bf16[8,32,1024]{2,1,0:T(8,128)(2,1)} %get-tuple-element.23), calls=%async_computation.1 | async-start | bytes 1048576 | tf_op jit(solution)/shard_map/all_to_all | solution.py:495
  47.5 0.0 collective-permute-done.3.refs_5_
  47.5 0.7 collective-permute-done.4.refs_6_
  48.2 2.3 %collective-permute-done.5.refs_7_ = bf16[4,9,8,256]{3,2,1,0:T(8,128)(2,1)S(1)} collective-permute-done((bf16[4,9,8,256]{3,2,1,0:T(8,128)(2,1)S(1)}, bf16[4,9,8,256]{3,2,1,0:T(8,128)(2,1)S(1)}, u32[]{:S(2)}, u32[]{:S(2)}) %collective-permute-start.5) | collective-permute-done | bytes 147488 | tf_op jit(solution)/shard_map/ppermute | solution.py:415
  50.5 11.3 %shard_map.97 = (s16[8,32,1152]{2,1,0:T(8,128)(2,1)}, f32[4,32,2048]{2,1,0:T(8,128)S(1)}) custom-call(s32[4]{0:T(128)S(1)} %copy-done.2, f32[16,128]{1,0:T(8,128)S(1)} %pad_maximum_fusion.1.invn_ref, bf16[1024,256]{1,0:T(8,128)(2,1)S(1)} %copy-done.10, bf16[8,32,1024]{2,1,0:T(8,128)(2,1)S(1)} %all-to-all-done.v_from, bf16[73,8,256]{2,1,0:T(8,128)(2,1)S(1)} %copy-done.1, ...), custom_call_target="tpu_custom_call" | custom-call | flops 10000000000 | tf_op jit(solution)/shard_map/pallas_call | solution.py:526
  61.8 0.0 copy-start.12
  61.8 1.0 copy-done.12
  62.8 0.0 all-to-all-done.1.v_from
  62.8 3.7 %all-to-all-start.2 = ((s16[8,32,1152]{2,1,0:T(8,128)(2,1)}), s16[8,32,1152]{2,1,0:T(8,128)(2,1)S(1)}, u32[]{:S(2)}, u32[]{:S(2)}) async-start(s16[8,32,1152]{2,1,0:T(8,128)(2,1)} %get-tuple-element.29), calls=%async_computation.2 | async-start | bytes 1179648 | tf_op jit(solution)/shard_map/all_to_all | solution.py:550
  66.5 0.9 copy-done.5
  67.4 0.9 copy-done.7
  68.3 0.9 copy-done.9
  69.2 1.0 copy-done.11
  70.3 1.2 %copy-done.13 = f32[4,32,2048]{2,1,0:T(8,128)S(1)} copy-done((f32[4,32,2048]{2,1,0:T(8,128)S(1)}, f32[4,32,2048]{2,1,0:T(8,128)}, u32[]{:S(2)}) %copy-start.13) | copy-done | bytes 1048600
  71.5 11.4 %shard_map.98 = (s16[8,32,1152]{2,1,0:T(8,128)(2,1)}, f32[32,2048]{1,0:T(8,128)S(1)}, f32[32,2048]{1,0:T(8,128)S(1)}, f32[32,2048]{1,0:T(8,128)S(1)}, f32[32,2048]{1,0:T(8,128)S(1)}) custom-call(s32[4]{0:T(128)S(1)} %copy-done.2, f32[16,128]{1,0:T(8,128)S(1)} %pad_maximum_fusion.invn_ref, bf16[1024,256]{1,0:T(8,128)(2,1)S(1)} %copy-done.11, ...), custom_call_target="tpu_custom_call" | custom-call | flops 10000000000 | tf_op jit(solution)/shard_map/pallas_call | solution.py:526
  82.9 0.0 copy-start.14
  82.9 0.3 collective-permute-start.6
  83.3 1.5 %collective-permute-start.7 = (f32[32,2048]{1,0:T(8,128)S(1)}, f32[32,2048]{1,0:T(8,128)S(1)}, u32[]{:S(2)}, u32[]{:S(2)}) collective-permute-start(f32[32,2048]{1,0:T(8,128)S(1)} %get-tuple-element.27), channel_id=1, source_target_pairs={{0,2},{1,3},{2,0},{3,1},{4,6},{5,7},{6,4},{7,5},{8,10},{9,11},{10,... | collective-permute-start | bytes 786440 | tf_op jit(solution)/shard_map/ppermute | solution.py:415
  84.8 0.1 collective-permute-start.8
  84.9 0.0 all-to-all-done.2.refs_0_
  84.9 6.0 %all-to-all-start.3 = ((s16[8,32,1152]{2,1,0:T(8,128)(2,1)}), s16[8,32,1152]{2,1,0:T(8,128)(2,1)S(1)}, u32[]{:S(2)}, u32[]{:S(2)}) async-start(s16[8,32,1152]{2,1,0:T(8,128)(2,1)} %get-tuple-element.31), calls=%async_computation.3 | async-start | bytes 1179648 | tf_op jit(solution)/shard_map/all_to_all | solution.py:550
  90.8 1.6 %collective-permute-done.7 = f32[32,2048]{1,0:T(8,128)S(1)} collective-permute-done((f32[32,2048]{1,0:T(8,128)S(1)}, f32[32,2048]{1,0:T(8,128)S(1)}, u32[]{:S(2)}, u32[]{:S(2)}) %collective-permute-start.7) | collective-permute-done | bytes 262176 | tf_op jit(solution)/shard_map/ppermute | solution.py:415
  92.4 4.2 %collective-permute-done.8 = f32[32,2048]{1,0:T(8,128)S(1)} collective-permute-done((f32[32,2048]{1,0:T(8,128)S(1)}, f32[32,2048]{1,0:T(8,128)S(1)}, u32[]{:S(2)}, u32[]{:S(2)}) %collective-permute-start.8) | collective-permute-done | bytes 262176 | tf_op jit(solution)/shard_map/ppermute | solution.py:415
  96.7 0.1 add_add_fusion
  96.7 2.3 %collective-permute-start.10 = (f32[8,2048]{1,0:T(8,128)S(1)}, f32[8,2048]{1,0:T(8,128)S(1)}, u32[]{:S(2)}, u32[]{:S(2)}) collective-permute-start(f32[8,2048]{1,0:T(8,128)S(1)} %get-tuple-element.34), channel_id=1, source_target_pairs={{0,8},{4,12},{8,0},{12,4},{16,24},{20,28},{24,16},{28,20},{1,9},{5... | collective-permute-start | bytes 196616 | tf_op jit(solution)/shard_map/ppermute | solution.py:415
  99.0 1.5 %collective-permute-start.11 = (f32[8,2048]{1,0:T(8,128)S(1)}, f32[8,2048]{1,0:T(8,128)S(1)}, u32[]{:S(2)}, u32[]{:S(2)}) collective-permute-start(f32[8,2048]{1,0:T(8,128)S(1)} %get-tuple-element.33), channel_id=1, source_target_pairs={{0,12},{4,8},{8,4},{12,0},{16,28},{20,24},{24,20},{28,16},{1,13},{... | collective-permute-start | bytes 196616 | tf_op jit(solution)/shard_map/ppermute | solution.py:415
  100.5 0.1 collective-permute-start.9
  100.6 2.5 %collective-permute-done.10 = f32[8,2048]{1,0:T(8,128)S(1)} collective-permute-done((f32[8,2048]{1,0:T(8,128)S(1)}, f32[8,2048]{1,0:T(8,128)S(1)}, u32[]{:S(2)}, u32[]{:S(2)}) %collective-permute-start.10) | collective-permute-done | bytes 65568 | tf_op jit(solution)/shard_map/ppermute | solution.py:415
  103.1 3.5 %collective-permute-done.11 = f32[8,2048]{1,0:T(8,128)S(1)} collective-permute-done((f32[8,2048]{1,0:T(8,128)S(1)}, f32[8,2048]{1,0:T(8,128)S(1)}, u32[]{:S(2)}, u32[]{:S(2)}) %collective-permute-start.11) | collective-permute-done | bytes 65568 | tf_op jit(solution)/shard_map/ppermute | solution.py:415
  106.6 0.2 collective-permute-done.9
  106.8 0.7 fusion.2
  107.5 1.4 %shard_map.99 = f32[1024,256]{1,0:T(8,128)} custom-call(s32[1,256]{1,0:T(1,128)S(1)} %bitcast.9, s16[8,32,1152]{2,1,0:T(8,128)(2,1)S(1)} %all-to-all-done.2.refs_0_, s16[8,32,1152]{2,1,0:T(8,128)(2,1)S(1)} %all-to-all-done.3.refs_1_), custom_call_target="tpu_custom_call" | custom-call | flops 1000000000 | tf_op jit(solution)/shard_map/pallas_call | solution.py:552
  (25 shorter events, 0.1 us)
Async XLA Ops:
  0.6 18.6 %copy-start.3 = (s32[256]{0:T(256)S(1)}, s32[256]{0:T(256)}, u32[]{:S(2)}) copy-start(s32[256]{0:T(256)} %param.11) | copy-start | bytes 3076
  8.2 42.2 %copy-start.1 = (bf16[73,8,256]{2,1,0:T(8,128)(2,1)S(1)}, bf16[73,8,256]{2,1,0:T(8,128)(2,1)}, u32[]{:S(2)}) copy-start(bf16[73,8,256]{2,1,0:T(8,128)(2,1)} %get-tuple-element.17.refs_0_) | copy-start | bytes 897028
  8.2 42.2 %copy-start.2 = (s32[4]{0:T(128)S(1)}, s32[4]{0:T(128)}, u32[]{:S(2)}) copy-start(s32[4]{0:T(128)} %pad_add_fusion.c_ref) | copy-start | bytes 52
  8.2 42.2 %copy-start.10 = (bf16[1024,256]{1,0:T(8,128)(2,1)S(1)}, bf16[1024,256]{1,0:T(8,128)(2,1)}, u32[]{:S(2)}) copy-start(bf16[1024,256]{1,0:T(8,128)(2,1)} %constant.49.table_ref) | copy-start | bytes 1572868
  8.2 35.5 %all-to-all-start = ((bf16[8,32,1024]{2,1,0:T(8,128)(2,1)}), bf16[8,32,1024]{2,1,0:T(8,128)(2,1)S(1)}, u32[]{:S(2)}, u32[]{:S(2)}) async-start(bf16[8,32,1024]{2,1,0:T(8,128)(2,1)} %get-tuple-element.22), calls=%async_computation | async-start | bytes 1048576 | tf_op jit(solution)/shard_map/all_to_all | solution.py:495
  15.7 14.4 %collective-permute-start = (bf16[73,8,256]{2,1,0:T(8,128)(2,1)}, bf16[73,8,256]{2,1,0:T(8,128)(2,1)S(1)}, u32[]{:S(2)}, u32[]{:S(2)}) collective-permute-start(bf16[73,8,256]{2,1,0:T(8,128)(2,1)} %get-tuple-element.18), channel_id=1, source_target_pairs={{0,4},{4,0},{8,12},{12,8},{16,20},{20,16},{24,28},{28,24},{1,5},{5... | collective-permute-start | bytes 897032 | tf_op jit(solution)/shard_map/ppermute | solution.py:415
  17.7 16.5 %collective-permute-start.1 = (bf16[73,8,256]{2,1,0:T(8,128)(2,1)}, bf16[73,8,256]{2,1,0:T(8,128)(2,1)S(1)}, u32[]{:S(2)}, u32[]{:S(2)}) collective-permute-start(bf16[73,8,256]{2,1,0:T(8,128)(2,1)} %get-tuple-element.19), channel_id=1, source_target_pairs={{0,8},{4,12},{8,0},{12,4},{16,24},{20,28},{24,16},{28,20},{1,9},{5... | collective-permute-start | bytes 897032 | tf_op jit(solution)/shard_map/ppermute | solution.py:415
  19.2 21.1 %collective-permute-start.2 = (bf16[73,8,256]{2,1,0:T(8,128)(2,1)}, bf16[73,8,256]{2,1,0:T(8,128)(2,1)S(1)}, u32[]{:S(2)}, u32[]{:S(2)}) collective-permute-start(bf16[73,8,256]{2,1,0:T(8,128)(2,1)} %get-tuple-element.20), channel_id=1, source_target_pairs={{0,12},{4,8},{8,4},{12,0},{16,28},{20,24},{24,20},{28,16},{1,13},{... | collective-permute-start | bytes 897032 | tf_op jit(solution)/shard_map/ppermute | solution.py:415
  40.2 1.0 copy-start
  41.4 6.1 %collective-permute-start.3 = (bf16[4,9,8,256]{3,2,1,0:T(8,128)(2,1)S(1)}, bf16[4,9,8,256]{3,2,1,0:T(8,128)(2,1)S(1)}, u32[]{:S(2)}, u32[]{:S(2)}) collective-permute-start(bf16[4,9,8,256]{3,2,1,0:T(8,128)(2,1)S(1)} %shard_map.96.refs_4_), channel_id=1, source_target_pairs={{0,1},{1,0},{2,3},{3,2},{4,5},{5,4},{6,7},{7,6},{8,9},{9,8},{10,11... | collective-permute-start | bytes 442376 | tf_op jit(solution)/shard_map/ppermute | solution.py:415
  41.5 6.7 %collective-permute-start.4 = (bf16[4,9,8,256]{3,2,1,0:T(8,128)(2,1)S(1)}, bf16[4,9,8,256]{3,2,1,0:T(8,128)(2,1)S(1)}, u32[]{:S(2)}, u32[]{:S(2)}) collective-permute-start(bf16[4,9,8,256]{3,2,1,0:T(8,128)(2,1)S(1)} %shard_map.96.refs_4_), channel_id=1, source_target_pairs={{0,2},{1,3},{2,0},{3,1},{4,6},{5,7},{6,4},{7,5},{8,10},{9,11},{10,... | collective-permute-start | bytes 442376 | tf_op jit(solution)/shard_map/ppermute | solution.py:415
  43.0 7.4 %collective-permute-start.5 = (bf16[4,9,8,256]{3,2,1,0:T(8,128)(2,1)S(1)}, bf16[4,9,8,256]{3,2,1,0:T(8,128)(2,1)S(1)}, u32[]{:S(2)}, u32[]{:S(2)}) collective-permute-start(bf16[4,9,8,256]{3,2,1,0:T(8,128)(2,1)S(1)} %shard_map.96.refs_4_), channel_id=1, source_target_pairs={{0,3},{1,2},{2,1},{3,0},{4,7},{5,6},{6,5},{7,4},{8,11},{9,10},{10,... | collective-permute-start | bytes 442376 | tf_op jit(solution)/shard_map/ppermute | solution.py:415
  43.8 19.0 %all-to-all-start.1 = ((bf16[8,32,1024]{2,1,0:T(8,128)(2,1)}), bf16[8,32,1024]{2,1,0:T(8,128)(2,1)S(1)}, u32[]{:S(2)}, u32[]{:S(2)}) async-start(bf16[8,32,1024]{2,1,0:T(8,128)(2,1)} %get-tuple-element.23), calls=%async_computation.1 | async-start | bytes 1048576 | tf_op jit(solution)/shard_map/all_to_all | solution.py:495
  47.5 14.3 %copy-start.4 = (bf16[4,9,8,256]{3,2,1,0:T(8,128)(2,1)}, bf16[4,9,8,256]{3,2,1,0:T(8,128)(2,1)S(1)}, u32[]{:S(2)}) copy-start(bf16[4,9,8,256]{3,2,1,0:T(8,128)(2,1)S(1)} %collective-permute-done.3.refs_5_) | copy-start | bytes 442372
  48.2 13.6 %copy-start.6 = (bf16[4,9,8,256]{3,2,1,0:T(8,128)(2,1)}, bf16[4,9,8,256]{3,2,1,0:T(8,128)(2,1)S(1)}, u32[]{:S(2)}) copy-start(bf16[4,9,8,256]{3,2,1,0:T(8,128)(2,1)S(1)} %collective-permute-done.4.refs_6_) | copy-start | bytes 442372
  50.4 11.4 %copy-start.8 = (bf16[4,9,8,256]{3,2,1,0:T(8,128)(2,1)}, bf16[4,9,8,256]{3,2,1,0:T(8,128)(2,1)S(1)}, u32[]{:S(2)}) copy-start(bf16[4,9,8,256]{3,2,1,0:T(8,128)(2,1)S(1)} %collective-permute-done.5.refs_7_) | copy-start | bytes 442372
  61.8 1.0 copy-start.12
  62.8 22.1 %all-to-all-start.2 = ((s16[8,32,1152]{2,1,0:T(8,128)(2,1)}), s16[8,32,1152]{2,1,0:T(8,128)(2,1)S(1)}, u32[]{:S(2)}, u32[]{:S(2)}) async-start(s16[8,32,1152]{2,1,0:T(8,128)(2,1)} %get-tuple-element.29), calls=%async_computation.2 | async-start | bytes 1179648 | tf_op jit(solution)/shard_map/all_to_all | solution.py:550
  66.5 0.9 copy-start.5
  67.4 0.9 copy-start.7
  68.3 0.9 copy-start.9
  69.2 1.0 copy-start.11
  70.3 1.2 %copy-start.13 = (f32[4,32,2048]{2,1,0:T(8,128)S(1)}, f32[4,32,2048]{2,1,0:T(8,128)}, u32[]{:S(2)}) copy-start(f32[4,32,2048]{2,1,0:T(8,128)} %copy-done.12) | copy-start | bytes 3145732
  82.9 23.8 %copy-start.14 = (s32[8]{0:T(128)S(1)}, s32[8]{0:T(128)}, u32[]{:S(2)}) copy-start(s32[8]{0:T(128)} %rcounts_ref.1) | copy-start | bytes 100
  82.9 7.9 %collective-permute-start.6 = (f32[32,2048]{1,0:T(8,128)S(1)}, f32[32,2048]{1,0:T(8,128)S(1)}, u32[]{:S(2)}, u32[]{:S(2)}) collective-permute-start(f32[32,2048]{1,0:T(8,128)S(1)} %get-tuple-element.26), channel_id=1, source_target_pairs={{0,1},{1,0},{2,3},{3,2},{4,5},{5,4},{6,7},{7,6},{8,9},{9,8},{10,11... | collective-permute-start | bytes 786440 | tf_op jit(solution)/shard_map/ppermute | solution.py:415
  83.3 9.1 %collective-permute-start.7 = (f32[32,2048]{1,0:T(8,128)S(1)}, f32[32,2048]{1,0:T(8,128)S(1)}, u32[]{:S(2)}, u32[]{:S(2)}) collective-permute-start(f32[32,2048]{1,0:T(8,128)S(1)} %get-tuple-element.27), channel_id=1, source_target_pairs={{0,2},{1,3},{2,0},{3,1},{4,6},{5,7},{6,4},{7,5},{8,10},{9,11},{10,... | collective-permute-start | bytes 786440 | tf_op jit(solution)/shard_map/ppermute | solution.py:415
  84.8 11.9 %collective-permute-start.8 = (f32[32,2048]{1,0:T(8,128)S(1)}, f32[32,2048]{1,0:T(8,128)S(1)}, u32[]{:S(2)}, u32[]{:S(2)}) collective-permute-start(f32[32,2048]{1,0:T(8,128)S(1)} %get-tuple-element.28), channel_id=1, source_target_pairs={{0,3},{1,2},{2,1},{3,0},{4,7},{5,6},{6,5},{7,4},{8,11},{9,10},{10,... | collective-permute-start | bytes 786440 | tf_op jit(solution)/shard_map/ppermute | solution.py:415
  84.9 22.6 %all-to-all-start.3 = ((s16[8,32,1152]{2,1,0:T(8,128)(2,1)}), s16[8,32,1152]{2,1,0:T(8,128)(2,1)S(1)}, u32[]{:S(2)}, u32[]{:S(2)}) async-start(s16[8,32,1152]{2,1,0:T(8,128)(2,1)} %get-tuple-element.31), calls=%async_computation.3 | async-start | bytes 1179648 | tf_op jit(solution)/shard_map/all_to_all | solution.py:550
  96.7 6.4 %collective-permute-start.10 = (f32[8,2048]{1,0:T(8,128)S(1)}, f32[8,2048]{1,0:T(8,128)S(1)}, u32[]{:S(2)}, u32[]{:S(2)}) collective-permute-start(f32[8,2048]{1,0:T(8,128)S(1)} %get-tuple-element.34), channel_id=1, source_target_pairs={{0,8},{4,12},{8,0},{12,4},{16,24},{20,28},{24,16},{28,20},{1,9},{5... | collective-permute-start | bytes 196616 | tf_op jit(solution)/shard_map/ppermute | solution.py:415
  99.0 7.6 %collective-permute-start.11 = (f32[8,2048]{1,0:T(8,128)S(1)}, f32[8,2048]{1,0:T(8,128)S(1)}, u32[]{:S(2)}, u32[]{:S(2)}) collective-permute-start(f32[8,2048]{1,0:T(8,128)S(1)} %get-tuple-element.33), channel_id=1, source_target_pairs={{0,12},{4,8},{8,4},{12,0},{16,28},{20,24},{24,20},{28,16},{1,13},{... | collective-permute-start | bytes 196616 | tf_op jit(solution)/shard_map/ppermute | solution.py:415
  100.5 6.3 %collective-permute-start.9 = (f32[8,2048]{1,0:T(8,128)S(1)}, f32[8,2048]{1,0:T(8,128)S(1)}, u32[]{:S(2)}, u32[]{:S(2)}) collective-permute-start(f32[8,2048]{1,0:T(8,128)S(1)} %get-tuple-element.32), channel_id=1, source_target_pairs={{0,4},{4,0},{8,12},{12,8},{16,20},{20,16},{24,28},{28,24},{1,5},{5... | collective-permute-start | bytes 196616 | tf_op jit(solution)/shard_map/ppermute | solution.py:415

commit v7 on v4

--- a/solution.py
+++ b/solution.py
@@ -18,8 +18,10 @@
 GROUP = 4
 LANES = 128
 FB = LANES // (2 * S)
-WIDTH = 8
+WIDTH = 16
 FIXED = 32000.0
+PAD = 8
+CODES = 16
 
 
 def lag_tables(freq_total, lag_total):
@@ -88,9 +90,10 @@
 
 
 def fold_kernel(c_ref, rcounts_ref, observed_from, rspectra_from, window_from, order_from, *rest):
-    *out_to, observed_ref, rspectra_ref, window_ref, order_ref, line_ref, out_ref, sems, out_sems = (
-        rest
-    )
+    u_to, *out_to = rest[:-9]
+    (
+        observed_ref, rspectra_ref, window_ref, order_ref, line_ref, out_ref, u_ref, sems, out_sems,
+    ) = rest[-9:]
     row_total, col_total, lag_total = observed_ref.shape
     half = lag_total // 2
     members = len(out_to)
@@ -110,6 +113,18 @@
         copy.start()
     for copy in copies[:3]:
         copy.wait()
+    row_ids = lax.broadcasted_iota(jnp.int32, (row_total, half), 0)
+    counts = jnp.zeros((row_total, half), jnp.int32)
+    for i in range(row_total):
+        counts = jnp.where(row_ids == i, rcounts_ref[i], counts)
+    seg_ids = lax.broadcasted_iota(jnp.int32, (row_total, half), 1) % S
+    pieces = quarter // half
+    for n in range(pieces):
+        part = rspectra_ref[:, n * half : (n + 1) * half].astype(jnp.float32)
+        u_ref[n] = jnp.where(seg_ids < counts, part, 0.0).astype(jnp.bfloat16)
+    u_ref[pieces] = counts.astype(jnp.float32).astype(jnp.bfloat16)
+    u_copy = pltpu.make_async_copy(u_ref, u_to, out_sems.at[members])
+    u_copy.start()
     window = jnp.concatenate([window_ref[0], window_ref[1]], axis=0).astype(jnp.float32).T
     station = lax.broadcasted_iota(jnp.int32, (col_total, col_total), 0) + c_ref[1]
     pick = jnp.where(station == order_ref[...], 1.0, 0.0).astype(jnp.bfloat16)
@@ -127,17 +142,6 @@
             line_ref[pl.ds(h * lines + i, col_total, stride=row_total), :] = moved[
                 :, h * LANES : (h + 1) * LANES
             ]
-    row_ids = lax.broadcasted_iota(jnp.int32, (row_total, half), 0)
-    counts = jnp.zeros((row_total, half), jnp.int32)
-    for i in range(row_total):
-        counts = jnp.where(row_ids == i, rcounts_ref[i], counts)
-    seg_ids = lax.broadcasted_iota(jnp.int32, (row_total, half), 1) % S
-    pieces = quarter // half
-    for k in range(members):
-        for n in range(pieces):
-            part = rspectra_ref[:, n * half : (n + 1) * half].astype(jnp.float32)
-            out_ref[k, cols + n] = jnp.where(seg_ids < counts, part, 0.0).astype(jnp.bfloat16)
-        out_ref[k, cols + pieces] = counts.astype(jnp.float32).astype(jnp.bfloat16)
     mine = c_ref[0]
     copies = []
     for k in range(members):
@@ -145,23 +149,22 @@
         for h in range(half // LANES):
             begin = pl.multiple_of(h * lines + first, cols * row_total)
             rows = line_ref[pl.ds(begin, cols * row_total), :]
-            out_ref[k, :cols, :, h * LANES : (h + 1) * LANES] = rows.reshape(
+            out_ref[k, :, :, h * LANES : (h + 1) * LANES] = rows.reshape(
                 cols, row_total, LANES
             ).astype(jnp.bfloat16)
         copies.append(pltpu.make_async_copy(out_ref.at[k], out_to[k], out_sems.at[k]))
         copies[-1].start()
-    for copy in copies:
+    for copy in copies + [u_copy]:
         copy.wait()
 
 
 def near_kernel(*refs):
     *parts, out_ref, sems = refs
-    extra = out_ref.shape[1]
-    copies = []
-    for k, ref in enumerate(parts):
-        rows = ref.at[pl.ds(ref.shape[0] - extra, extra)]
-        copies.append(pltpu.make_async_copy(rows, out_ref.at[k], sems.at[k]))
-        copies[-1].start()
+    copies = [
+        pltpu.make_async_copy(ref, out_ref.at[k], sems.at[k]) for k, ref in enumerate(parts)
+    ]
+    for copy in copies:
+        copy.start()
     for copy in copies:
         copy.wait()
 
@@ -182,6 +185,7 @@
     k_total = src_total * k_own
     half_f = k_total // (4 * S)
     freq_total = 2 * half_f
+    pitch = freq_total + PAD
     blocks = k_total // LANES
     own_blocks = k_own // LANES
     quarter_blocks = k_quarter // LANES
@@ -191,7 +195,7 @@
     for k, ref in enumerate(u_from):
         early.append(pltpu.make_async_copy(ref, u_ref.at[quarter_me ^ k], sems.at[1 + k]))
     late = [
-        pltpu.make_async_copy(ref.at[pl.ds(0, col_total)], e_ref.at[k], sems.at[1 + n_r + k])
+        pltpu.make_async_copy(ref, e_ref.at[k], sems.at[1 + n_r + k])
         for k, ref in enumerate(e_from)
     ]
     for copy in early + late:
@@ -236,7 +240,7 @@
         )
 
     def place(fb, f):
-        return pl.ds((f % 2) * half_f + fb * (FB // 2) + f // 2, jp_total, stride=freq_total)
+        return pl.ds((f % 2) * half_f + fb * (FB // 2) + f // 2, jp_total, stride=pitch)
 
     def forward(fb, _):
         lanes = pl.ds(pl.multiple_of(fb * LANES, LANES), LANES)
@@ -257,7 +261,7 @@
 
     for copy in early:
         copy.wait()
-    lax.fori_loop(0, blocks, forward, 0, unroll=16)
+    lax.fori_loop(0, blocks, forward, 0, unroll=64)
 
     lane_ids = lax.broadcasted_iota(jnp.int32, (1, LANES), 1)
     sign = jnp.where(lane_ids < LANES // 2, -1.0, 1.0).astype(jnp.float32)
@@ -268,7 +272,7 @@
         cols = [step * WIDTH + k for k in range(WIDTH)]
         rhs_e, rhs_o, obs = [], [], []
         for jp in cols:
-            x = x_ref[pl.ds(pl.multiple_of(jp * freq_total, freq_total), freq_total), :]
+            x = x_ref[pl.ds(pl.multiple_of(jp * pitch, PAD), freq_total), :]
             plain = x.astype(jnp.bfloat16)
             turned = pltpu.roll(x, LANES // 2, 1).astype(jnp.bfloat16) * sign
             rhs_e.append(jnp.concatenate([plain[:half_f], turned[:half_f]], axis=0))
@@ -301,16 +305,17 @@
         for k, jp in enumerate(cols):
             lanes = slice(k * LANES, (k + 1) * LANES)
             scale = invn_ref[pl.ds(jp, 1), :] * misfit_scale
-            base = pl.multiple_of(jp * freq_total, freq_total)
+            base = pl.multiple_of(jp * pitch, PAD)
             z_ref[pl.ds(base, half_f), :] = z_e[:, lanes] * scale
             z_ref[pl.ds(base + half_f, half_f), :] = z_o[:, lanes] * scale
         return 0
 
     for copy in late:
         copy.wait()
-    lax.fori_loop(0, jp_total // WIDTH, pairs, 0)
-
-    def backward(fb):
+    lax.fori_loop(0, jp_total // WIDTH, pairs, 0, unroll=2)
+
+    def backward(src, b):
+        fb = src * own_blocks + b
         z = jnp.concatenate([z_ref[place(fb, f), :] for f in range(FB)], axis=0)
         z = z.astype(jnp.bfloat16)
         lanes = pl.ds(pl.multiple_of(fb * LANES, LANES), LANES)
@@ -327,8 +332,7 @@
         power = jnp.ceil(jnp.log2(jnp.maximum(largest, 1e-30)))
         code_ref[pl.ds(fb, 1), :] = power
         fixed = jnp.round(total * (jnp.exp2(-power) * FIXED)).astype(jnp.int32)
-        src, off = lanes_of(fb, own_blocks)
-        w_ref[src, :, pl.ds(off, LANES)] = fixed.astype(jnp.int16)
+        w_ref[src, b * col_total : (b + 1) * col_total, :] = fixed.astype(jnp.int16)
         r = tn(z, v_block(fb))
         sums = []
         for q in range(2):
@@ -351,22 +355,22 @@
 
     def from_owner(src, _):
         for b in range(own_blocks):
-            backward(src * own_blocks + b)
+            backward(src, b)
         codes = code_ref[pl.ds(src * own_blocks, own_blocks), :]
         codes = jnp.concatenate(
-            [codes, jnp.zeros((col_total - own_blocks, LANES), jnp.float32)], axis=0
+            [codes, jnp.zeros((CODES - own_blocks, LANES), jnp.float32)], axis=0
         )
-        w_ref[src, :, k_own:] = codes.astype(jnp.int32).astype(jnp.int16)
+        w_ref[src, own_blocks * col_total :, :] = codes.astype(jnp.int32).astype(jnp.int16)
         w_copy(src).start()
         return 0
 
-    owners = src_total // ref_total
-    outs = []
-    for k, ref in enumerate(r_to):
-        begin = (quarter_me ^ k) * owners
-        lax.fori_loop(begin, begin + owners, from_owner, 0)
-        outs.append(pltpu.make_async_copy(r_ref.at[quarter_me ^ k], ref, sems.at[k]))
-        outs[-1].start()
+    lax.fori_loop(0, src_total, from_owner, 0, unroll=4)
+    outs = [
+        pltpu.make_async_copy(r_ref.at[quarter_me ^ k], ref, sems.at[k])
+        for k, ref in enumerate(r_to)
+    ]
+    for copy in outs:
+        copy.start()
     for copy in outs:
         copy.wait()
     for src in range(src_total):
@@ -374,21 +378,23 @@
 
 
 def join_kernel(count_ref, got_ref, out_ref):
-    src_total, cols, _ = got_ref.shape
+    src_total, rows_total, _ = got_ref.shape
     k_own, col_total = out_ref.shape
+    own_blocks = k_own // LANES
+    cols = (rows_total - CODES) // own_blocks
     members = col_total // cols
     seg_ids = lax.broadcasted_iota(jnp.int32, (LANES, col_total), 0) % S
     inside = seg_ids < count_ref[...]
-    scales = [
-        jnp.exp2(got_ref[src, :16, k_own:].astype(jnp.int32).astype(jnp.float32)) * (1.0 / FIXED)
-        for src in range(src_total)
-    ]
-    for b in range(k_own // LANES):
+    scales = []
+    for src in range(src_total):
+        codes = got_ref[src, own_blocks * cols :, :].astype(jnp.int32).astype(jnp.float32)
+        scales.append(jnp.exp2(codes) * (1.0 / FIXED))
+    for b in range(own_blocks):
         rows = []
         for m in range(members):
             total = None
             for src in range(m, src_total, members):
-                part = got_ref[src, :, b * LANES : (b + 1) * LANES]
+                part = got_ref[src, b * cols : (b + 1) * cols, :]
                 part = part.astype(jnp.int32).astype(jnp.float32) * scales[src][b : b + 1]
                 total = part if total is None else total + part
             rows.append(total)
@@ -431,7 +437,9 @@
     smem = pl.BlockSpec(memory_space=pltpu.SMEM)
     hbm = pl.BlockSpec(memory_space=pl.ANY)
     scalars = jnp.stack([mine, quarter * col_total, place, quarter]).astype(jnp.int32)
-    params = pltpu.CompilerParams(vmem_limit_bytes=32 * 1024 * 1024)
+    def params(mib):
+        return pltpu.CompilerParams(vmem_limit_bytes=mib * 1024 * 1024)
+
     free = pl.CostEstimate(flops=0, bytes_accessed=0, transcendentals=0)
 
     sent = pl.pallas_call(
@@ -445,18 +453,19 @@
             pltpu.VMEM((col_total, k_own), bf16),
             pltpu.SemaphoreType.DMA((max(rcv_total, 1 + k_own // min(k_own, 2 * LANES)),)),
         ],
-        compiler_params=params,
+        compiler_params=params(62),
         cost_estimate=free,
     )(reference_spectra, reference_counts.reshape(1, col_total))
     v_all = lax.all_to_all(sent, "rcv", split_axis=0, concat_axis=0, tiled=True)
 
     _, observed = lax.optimization_barrier((sent, observed))
-    shape = (cols + extra, row_total, half)
-    folded = pl.pallas_call(
+    shape = (cols, row_total, half)
+    u_own, *folded = pl.pallas_call(
         fold_kernel,
-        out_shape=[jax.ShapeDtypeStruct(shape, bf16)] * members,
+        out_shape=[jax.ShapeDtypeStruct((extra, row_total, half), bf16)]
+        + [jax.ShapeDtypeStruct(shape, bf16)] * members,
         in_specs=[smem] * 2 + [hbm] * 4,
-        out_specs=[hbm] * members,
+        out_specs=[hbm] * (1 + members),
         scratch_shapes=[
             pltpu.VMEM(observed.shape, bf16),
             pltpu.VMEM(receiver_spectra.shape, bf16),
@@ -464,10 +473,11 @@
             pltpu.VMEM((1, col_total), jnp.int32),
             pltpu.VMEM((half // LANES * col_total * row_total, LANES), jnp.float32),
             pltpu.VMEM((members,) + shape, bf16),
+            pltpu.VMEM((extra, row_total, half), bf16),
             pltpu.SemaphoreType.DMA((row_total + 3,)),
-            pltpu.SemaphoreType.DMA((members,)),
+            pltpu.SemaphoreType.DMA((members + 1,)),
         ],
-        compiler_params=params,
+        compiler_params=params(32),
         cost_estimate=free,
     )(
         scalars,
@@ -485,9 +495,9 @@
         in_specs=[hbm] * members,
         out_specs=hbm,
         scratch_shapes=[pltpu.SemaphoreType.DMA((members,))],
-        compiler_params=params,
+        compiler_params=params(16),
         cost_estimate=free,
-    )(*e_all)
+    )(u_own, *[swap(u_own, "rcv", rcv_total, k) for k in range(1, members)])
     u_all = [near] + [swap(near, "ref", ref_total, k) for k in range(1, ref_total)]
 
     group_counts = near[:, extra - 1, :, 0].reshape(irec).astype(jnp.float32)
@@ -498,10 +508,11 @@
     inverse = jnp.concatenate([inverse, inverse], axis=1)
 
     table = lag_tables(k_total // (2 * S), lag_total)
-    lines = jp_total * k_total // (2 * S)
+    w_rows = k_own // LANES * cols + CODES
+    lines = jp_total * (k_total // (2 * S) + PAD)
     w_part, *r_all = pl.pallas_call(
         functools.partial(pair_kernel, members, ref_total),
-        out_shape=[jax.ShapeDtypeStruct((rcv_total, cols, k_own + LANES), jnp.int16)]
+        out_shape=[jax.ShapeDtypeStruct((rcv_total, w_rows, LANES), jnp.int16)]
         + [jax.ShapeDtypeStruct((irec, k_quarter), jnp.float32)] * ref_total,
         in_specs=[smem] + [vmem] * 2 + [hbm] * (1 + members + ref_total),
         out_specs=[hbm] * (1 + ref_total),
@@ -515,11 +526,11 @@
             pltpu.VMEM((rcv_total, cols, k_own), bf16),
             pltpu.VMEM((members, cols, row_total, half), bf16),
             pltpu.VMEM((ref_total, irec, k_quarter), jnp.float32),
-            pltpu.VMEM((rcv_total, cols, k_own + LANES), jnp.int16),
+            pltpu.VMEM((rcv_total, w_rows, LANES), jnp.int16),
             pltpu.SemaphoreType.DMA((1 + members + ref_total,)),
             pltpu.SemaphoreType.DMA((rcv_total,)),
         ],
-        compiler_params=params,
+        compiler_params=params(32),
         cost_estimate=free,
     )(scalars, inverse, table, v_all, *e_all, *u_all)
 
@@ -529,7 +540,7 @@
         out_shape=jax.ShapeDtypeStruct((k_own, col_total), jnp.float32),
         in_specs=[vmem] * 2,
         out_specs=vmem,
-        compiler_params=params,
+        compiler_params=params(32),
         cost_estimate=free,
     )(reference_counts.reshape(1, col_total), got)
 

time: 113 us -> 91 us (0.81)
  waiting for transfers between devices: 52.6 us -> 37.2 us
  Pallas kernels: 29.3 us -> 21.6 us
  starting transfers between devices: 22.4 us -> 26.3 us
  local copies, waits for them, and re-layouts: 5.96 us -> 3.73 us
    ppermute x12 -> x15, waiting for transfers between devices: 48.6 us -> 33.7 us  [swap(): return lax.ppermute(x, axis, [(r, r ^ k) for r in range(total)])]
    pallas_call x1, Pallas kernels: 20.1 us -> 12.3 us  [shards(): pl.pallas_call(functools.partial(pair_kernel, members, ref_total), out_sh...]
    ppermute x12 -> x15, starting transfers between devices: 11.2 us -> 15 us  [swap(): return lax.ppermute(x, axis, [(r, r ^ k) for r in range(total)])]
    unnamed x34 -> x24, local copies, waits for them, and re-layouts: 5.42 us -> 3.19 us
  transfers between devices with their start and end apart: 14 -> 17, of which waited for: 11 -> 11; matrix products, arithmetic and copies ran while one was open for 1% -> 2% of each run, Pallas kernels for 5% -> 6%
where the time goes in v7:
time: 91 us; the launch traced here: 90.7 us
  waiting for transfers between devices  37.2 us (41%)
  starting transfers between devices  26.3 us (29%)
  Pallas kernels  21.6 us (24%)
  local copies, waits for them, and re-layouts  3.73 us (4%)
  other arithmetic  1.09 us (1%)
    ppermute x15, waiting for transfers between devices, swap(): return lax.ppermute(x, axis, [(r, r ^ k) for r in range(total)])  33.7 us
    ppermute x15, starting transfers between devices, swap(): return lax.ppermute(x, axis, [(r, r ^ k) for r in range(total)])  15 us
    pallas_call x1, Pallas kernels, shards(): pl.pallas_call(functools.partial(pair_kernel, members, ref_total), out_sh...  12.3 us
    all_to_all x1, starting transfers between devices, shards(): v_all = lax.all_to_all(sent, 'rcv', split_axis=0, concat_axis=0, tiled=True)  7.43 us
    pallas_call x1, Pallas kernels, shards(): pl.pallas_call(fold_kernel, out_shape=[jax.ShapeDtypeStruct((extra, row_t...  4.86 us
    all_to_all x1, starting transfers between devices, shards(): got = lax.all_to_all(w_part, 'rcv', split_axis=0, concat_axis=0, tiled=True)  3.82 us
    all_to_all x1, waiting for transfers between devices, shards(): got = lax.all_to_all(w_part, 'rcv', split_axis=0, concat_axis=0, tiled=True)  3.49 us
    unnamed x24, local copies, waits for them, and re-layouts  3.19 us
  transfers between devices with their start and end apart: 17, of which 11 were waited for; matrix products, arithmetic and copies ran while one was open for 2% of the time, Pallas kernels for 6%

profile of v7, /device:TPU:0, one launch (start us, length us, event | category | flops | bytes accessed | tf_op | source)
XLA Modules:
  0.0 90.7 jit_solution(11975228111776639217)
XLA Ops:
  0.6 2.9 %shard_map.95 = bf16[8,64,1024]{2,1,0:T(8,128)(2,1)} custom-call(bf16[1024,256]{1,0:T(8,128)(2,1)} %spectra_from.1, s32[1,256]{1,0:T(1,128)} %bitcast.7), custom_call_target="tpu_custom_call" | custom-call | tf_op jit(solution)/shard_map/pallas_call | solution.py:445
  3.6 0.0 copy-start
  3.6 0.0 copy-start.2
  3.6 0.0 copy-start.5
  3.6 0.0 copy-start.6
  3.6 7.4 %all-to-all-start = ((bf16[8,64,1024]{2,1,0:T(8,128)(2,1)}), bf16[8,64,1024]{2,1,0:T(8,128)(2,1)S(1)}, u32[]{:S(2)}, u32[]{:S(2)}) async-start(bf16[8,64,1024]{2,1,0:T(8,128)(2,1)} %shard_map.95), calls=%async_computation | async-start | bytes 2097152 | tf_op jit(solution)/shard_map/all_to_all | solution.py:459
  11.1 0.1 pad_add_fusion.c_ref
  11.2 0.0 copy-done.5
  11.2 0.0 copy-done.6
  11.2 0.0 copy-start.4
  11.2 4.9 %shard_map.96 = (bf16[9,8,256]{2,1,0:T(8,128)(2,1)S(1)}, bf16[64,8,256]{2,1,0:T(8,128)(2,1)S(1)}, bf16[64,8,256]{2,1,0:T(8,128)(2,1)}, bf16[64,8,256]{2,1,0:T(8,128)(2,1)}, bf16[64,8,256]{2,1,0:T(8,128)(2,1)S(1)}) custom-call(s32[4]{0:T(128)S(1)} %pad_add_fusion.c_ref, s32[8]{0:T(128)S(1)} %copy-done.5, bf16[8,256,512]{2,1,0:T(8,128)(2,1)S(1)} %copy-done, ...), custom_call_target="tpu_custom_call" | custom-call | tf_op jit(solution)/shard_map/pallas_call | solution.py:463
  16.1 0.0 copy-start.7
  16.1 0.7 copy-done.7
  16.8 2.0 %collective-permute-start = (bf16[9,8,256]{2,1,0:T(8,128)(2,1)S(1)}, bf16[9,8,256]{2,1,0:T(8,128)(2,1)S(1)}, u32[]{:S(2)}, u32[]{:S(2)}) collective-permute-start(bf16[9,8,256]{2,1,0:T(8,128)(2,1)S(1)} %get-tuple-element.14.refs_0_), channel_id=1, source_target_pairs={{0,4},{4,0},{8,12},{12,8},{16,20},{20,16},{24,28},{28,24},{1,5},{5... | collective-permute-start | bytes 110600 | tf_op jit(solution)/shard_map/ppermute | solution.py:406
  18.8 1.5 %collective-permute-start.1 = (bf16[9,8,256]{2,1,0:T(8,128)(2,1)S(1)}, bf16[9,8,256]{2,1,0:T(8,128)(2,1)S(1)}, u32[]{:S(2)}, u32[]{:S(2)}) collective-permute-start(bf16[9,8,256]{2,1,0:T(8,128)(2,1)S(1)} %get-tuple-element.14.refs_0_), channel_id=1, source_target_pairs={{0,8},{4,12},{8,0},{12,4},{16,24},{20,28},{24,16},{28,20},{1,9},{5... | collective-permute-start | bytes 110600 | tf_op jit(solution)/shard_map/ppermute | solution.py:406
  20.3 0.0 collective-permute-start.2
  20.3 2.0 %collective-permute-start.3 = (bf16[64,8,256]{2,1,0:T(8,128)(2,1)}, bf16[64,8,256]{2,1,0:T(8,128)(2,1)S(1)}, u32[]{:S(2)}, u32[]{:S(2)}) collective-permute-start(bf16[64,8,256]{2,1,0:T(8,128)(2,1)} %get-tuple-element.16), channel_id=1, source_target_pairs={{0,4},{4,0},{8,12},{12,8},{16,20},{20,16},{24,28},{28,24},{1,5},{5... | collective-permute-start | bytes 786440 | tf_op jit(solution)/shard_map/ppermute | solution.py:406
  22.3 1.5 %collective-permute-start.4 = (bf16[64,8,256]{2,1,0:T(8,128)(2,1)}, bf16[64,8,256]{2,1,0:T(8,128)(2,1)S(1)}, u32[]{:S(2)}, u32[]{:S(2)}) collective-permute-start(bf16[64,8,256]{2,1,0:T(8,128)(2,1)} %get-tuple-element.17), channel_id=1, source_target_pairs={{0,8},{4,12},{8,0},{12,4},{16,24},{20,28},{24,16},{28,20},{1,9},{5... | collective-permute-start | bytes 786440 | tf_op jit(solution)/shard_map/ppermute | solution.py:406
  23.8 0.0 collective-permute-done.refs_1_
  23.8 0.4 collective-permute-start.5
  24.1 6.0 %collective-permute-done.1.refs_2_ = bf16[9,8,256]{2,1,0:T(8,128)(2,1)S(1)} collective-permute-done((bf16[9,8,256]{2,1,0:T(8,128)(2,1)S(1)}, bf16[9,8,256]{2,1,0:T(8,128)(2,1)S(1)}, u32[]{:S(2)}, u32[]{:S(2)}) %collective-permute-start.1) | collective-permute-done | bytes 36896 | tf_op jit(solution)/shard_map/ppermute | solution.py:406
  30.1 0.8 collective-permute-done.2.refs_3_
  30.9 0.2 shard_map.97.refs_4_
  31.1 0.1 collective-permute-start.6
  31.2 0.1 dynamic-slice_convert_fusion
  31.3 0.1 reshape.35
  31.3 0.1 copy.11
  31.4 0.1 min.20
  31.5 0.1 min.21
  31.6 1.5 %collective-permute-start.7 = (bf16[4,9,8,256]{3,2,1,0:T(8,128)(2,1)S(1)}, bf16[4,9,8,256]{3,2,1,0:T(8,128)(2,1)S(1)}, u32[]{:S(2)}, u32[]{:S(2)}) collective-permute-start(bf16[4,9,8,256]{3,2,1,0:T(8,128)(2,1)S(1)} %shard_map.97.refs_4_), channel_id=1, source_target_pairs={{0,2},{1,3},{2,0},{3,1},{4,6},{5,7},{6,4},{7,5},{8,10},{9,11},{10,... | collective-permute-start | bytes 442376 | tf_op jit(solution)/shard_map/ppermute | solution.py:406
  33.1 0.1 convert_reduce_fusion
  33.2 0.1 reshape.38
  33.3 0.1 min.23
  33.4 0.0 collective-permute-done.6.refs_5_
  33.4 0.4 collective-permute-start.8
  33.8 0.1 pad_maximum_fusion.invn_ref
  33.9 4.4 %collective-permute-done.7.refs_6_ = bf16[4,9,8,256]{3,2,1,0:T(8,128)(2,1)S(1)} collective-permute-done((bf16[4,9,8,256]{3,2,1,0:T(8,128)(2,1)S(1)}, bf16[4,9,8,256]{3,2,1,0:T(8,128)(2,1)S(1)}, u32[]{:S(2)}, u32[]{:S(2)}) %collective-permute-start.7) | collective-permute-done | bytes 147488 | tf_op jit(solution)/shard_map/ppermute | solution.py:406
  38.3 2.3 %collective-permute-done.8.refs_7_ = bf16[4,9,8,256]{3,2,1,0:T(8,128)(2,1)S(1)} collective-permute-done((bf16[4,9,8,256]{3,2,1,0:T(8,128)(2,1)S(1)}, bf16[4,9,8,256]{3,2,1,0:T(8,128)(2,1)S(1)}, u32[]{:S(2)}, u32[]{:S(2)}) %collective-permute-start.8) | collective-permute-done | bytes 147488 | tf_op jit(solution)/shard_map/ppermute | solution.py:406
  40.6 0.0 collective-permute-done.3.refs_1_
  40.6 0.0 collective-permute-done.4.refs_2_
  40.6 3.4 %collective-permute-done.5.refs_3_ = bf16[64,8,256]{2,1,0:T(8,128)(2,1)S(1)} collective-permute-done((bf16[64,8,256]{2,1,0:T(8,128)(2,1)}, bf16[64,8,256]{2,1,0:T(8,128)(2,1)S(1)}, u32[]{:S(2)}, u32[]{:S(2)}) %collective-permute-start.5) | collective-permute-done | bytes 262176 | tf_op jit(solution)/shard_map/ppermute | solution.py:406
  44.0 0.0 all-to-all-done.v_from
  44.0 1.0 %copy-done.1 = bf16[1024,256]{1,0:T(8,128)(2,1)S(1)} copy-done((bf16[1024,256]{1,0:T(8,128)(2,1)S(1)}, bf16[1024,256]{1,0:T(8,128)(2,1)}, u32[]{:S(2)}) %copy-start.1) | copy-done | bytes 524312
  45.0 12.3 %shard_map.98 = (s16[8,528,128]{2,1,0:T(8,128)(2,1)}, f32[32,2048]{1,0:T(8,128)S(1)}, f32[32,2048]{1,0:T(8,128)S(1)}, f32[32,2048]{1,0:T(8,128)S(1)}, f32[32,2048]{1,0:T(8,128)S(1)}) custom-call(s32[4]{0:T(128)S(1)} %pad_add_fusion.c_ref, f32[32,128]{1,0:T(8,128)S(1)} %pad_maximum_fusion.invn_ref, bf16[1024,256]{1,0:T(8,128)(2,1)S(1)} %copy-done.1, ...), custom_call_target="tpu_custom_call" | custom-call | tf_op jit(solution)/shard_map/pallas_call | solution.py:513
  57.3 0.0 copy-start.8
  57.3 0.7 copy-done.8
  58.0 0.7 copy-done.10
  58.7 3.8 %all-to-all-start.1 = ((s16[8,528,128]{2,1,0:T(8,128)(2,1)}), s16[8,528,128]{2,1,0:T(8,128)(2,1)S(1)}, u32[]{:S(2)}, u32[]{:S(2)}) async-start(s16[8,528,128]{2,1,0:T(8,128)(2,1)} %get-tuple-element.23), calls=%async_computation.1 | async-start | bytes 2162688 | tf_op jit(solution)/shard_map/all_to_all | solution.py:537
  62.5 1.6 %collective-permute-start.10 = (f32[32,2048]{1,0:T(8,128)S(1)}, f32[32,2048]{1,0:T(8,128)S(1)}, u32[]{:S(2)}, u32[]{:S(2)}) collective-permute-start(f32[32,2048]{1,0:T(8,128)S(1)} %copy-done.11), channel_id=1, source_target_pairs={{0,2},{1,3},{2,0},{3,1},{4,6},{5,7},{6,4},{7,5},{8,10},{9,11},{10,... | collective-permute-start | bytes 786440 | tf_op jit(solution)/shard_map/ppermute | solution.py:406
  64.1 0.0 collective-permute-start.11
  64.1 0.6 collective-permute-start.9
  64.8 7.0 %collective-permute-done.10 = f32[32,2048]{1,0:T(8,128)S(1)} collective-permute-done((f32[32,2048]{1,0:T(8,128)S(1)}, f32[32,2048]{1,0:T(8,128)S(1)}, u32[]{:S(2)}, u32[]{:S(2)}) %collective-permute-start.10) | collective-permute-done | bytes 262176 | tf_op jit(solution)/shard_map/ppermute | solution.py:406
  71.8 3.5 %collective-permute-done.11 = f32[32,2048]{1,0:T(8,128)S(1)} collective-permute-done((f32[32,2048]{1,0:T(8,128)S(1)}, f32[32,2048]{1,0:T(8,128)S(1)}, u32[]{:S(2)}, u32[]{:S(2)}) %collective-permute-start.11) | collective-permute-done | bytes 262176 | tf_op jit(solution)/shard_map/ppermute | solution.py:406
  75.3 0.0 collective-permute-done.9
  75.4 0.1 add_add_fusion
  75.4 1.7 %collective-permute-start.12 = (f32[8,2048]{1,0:T(8,128)S(1)}, f32[8,2048]{1,0:T(8,128)S(1)}, u32[]{:S(2)}, u32[]{:S(2)}) collective-permute-start(f32[8,2048]{1,0:T(8,128)S(1)} %get-tuple-element.24), channel_id=1, source_target_pairs={{0,4},{4,0},{8,12},{12,8},{16,20},{20,16},{24,28},{28,24},{1,5},{5... | collective-permute-start | bytes 196616 | tf_op jit(solution)/shard_map/ppermute | solution.py:406
  77.2 1.5 %collective-permute-start.13 = (f32[8,2048]{1,0:T(8,128)S(1)}, f32[8,2048]{1,0:T(8,128)S(1)}, u32[]{:S(2)}, u32[]{:S(2)}) collective-permute-start(f32[8,2048]{1,0:T(8,128)S(1)} %get-tuple-element.26), channel_id=1, source_target_pairs={{0,8},{4,12},{8,0},{12,4},{16,24},{20,28},{24,16},{28,20},{1,9},{5... | collective-permute-start | bytes 196616 | tf_op jit(solution)/shard_map/ppermute | solution.py:406
  78.6 0.4 collective-permute-start.14
  79.0 3.5 %collective-permute-done.12 = f32[8,2048]{1,0:T(8,128)S(1)} collective-permute-done((f32[8,2048]{1,0:T(8,128)S(1)}, f32[8,2048]{1,0:T(8,128)S(1)}, u32[]{:S(2)}, u32[]{:S(2)}) %collective-permute-start.12) | collective-permute-done | bytes 65568 | tf_op jit(solution)/shard_map/ppermute | solution.py:406
  82.4 0.8 collective-permute-done.13
  83.3 1.9 %collective-permute-done.14 = f32[8,2048]{1,0:T(8,128)S(1)} collective-permute-done((f32[8,2048]{1,0:T(8,128)S(1)}, f32[8,2048]{1,0:T(8,128)S(1)}, u32[]{:S(2)}, u32[]{:S(2)}) %collective-permute-start.14) | collective-permute-done | bytes 65568 | tf_op jit(solution)/shard_map/ppermute | solution.py:406
  85.2 0.7 fusion.2
  85.9 3.5 %all-to-all-done.1.got_ref = s16[8,528,128]{2,1,0:T(8,128)(2,1)S(1)} async-done(((s16[8,528,128]{2,1,0:T(8,128)(2,1)}), s16[8,528,128]{2,1,0:T(8,128)(2,1)S(1)}, u32[]{:S(2)}, u32[]{:S(2)}) %all-to-all-start.1) | async-done | bytes 1081376 | tf_op jit(solution)/shard_map/all_to_all | solution.py:537
  89.4 1.3 %shard_map.99 = f32[1024,256]{1,0:T(8,128)} custom-call(s32[1,256]{1,0:T(1,128)S(1)} %bitcast.8, s16[8,528,128]{2,1,0:T(8,128)(2,1)S(1)} %all-to-all-done.1.got_ref), custom_call_target="tpu_custom_call" | custom-call | tf_op jit(solution)/shard_map/pallas_call | solution.py:538
  (15 shorter events, 0.1 us)
Async XLA Ops:
  0.6 10.5 %copy-start.3 = (s32[2,8,256]{2,1,0:T(8,128)S(1)}, s32[2,8,256]{2,1,0:T(8,128)}, u32[]{:S(2)}) copy-start(s32[2,8,256]{2,1,0:T(8,128)} %window_from.1) | copy-start | bytes 49156
  3.6 7.6 %copy-start = (bf16[8,256,512]{2,1,0:T(8,128)(2,1)S(1)}, bf16[8,256,512]{2,1,0:T(8,128)(2,1)}, u32[]{:S(2)}) copy-start(bf16[8,256,512]{2,1,0:T(8,128)(2,1)} %observed_from) | copy-start | bytes 6291460
  3.6 7.5 %copy-start.2 = (bf16[8,2048]{1,0:T(8,128)(2,1)S(1)}, bf16[8,2048]{1,0:T(8,128)(2,1)}, u32[]{:S(2)}) copy-start(bf16[8,2048]{1,0:T(8,128)(2,1)} %rspectra_from.1) | copy-start | bytes 98308
  3.6 7.5 %copy-start.5 = (s32[8]{0:T(128)S(1)}, s32[8]{0:T(128)}, u32[]{:S(2)}) copy-start(s32[8]{0:T(128)} %rcounts_ref.1) | copy-start | bytes 100
  3.6 7.5 %copy-start.6 = (s32[256]{0:T(256)S(1)}, s32[256]{0:T(256)}, u32[]{:S(2)}) copy-start(s32[256]{0:T(256)} %param.12) | copy-start | bytes 3076
  3.6 40.4 %all-to-all-start = ((bf16[8,64,1024]{2,1,0:T(8,128)(2,1)}), bf16[8,64,1024]{2,1,0:T(8,128)(2,1)S(1)}, u32[]{:S(2)}, u32[]{:S(2)}) async-start(bf16[8,64,1024]{2,1,0:T(8,128)(2,1)} %shard_map.95), calls=%async_computation | async-start | bytes 2097152 | tf_op jit(solution)/shard_map/all_to_all | solution.py:459
  11.2 20.0 %copy-start.4 = (s32[256]{0:T(256)S(1)}, s32[256]{0:T(256)}, u32[]{:S(2)}) copy-start(s32[256]{0:T(256)} %param.11) | copy-start | bytes 3076
  16.1 0.7 copy-start.7
  16.8 7.0 %collective-permute-start = (bf16[9,8,256]{2,1,0:T(8,128)(2,1)S(1)}, bf16[9,8,256]{2,1,0:T(8,128)(2,1)S(1)}, u32[]{:S(2)}, u32[]{:S(2)}) collective-permute-start(bf16[9,8,256]{2,1,0:T(8,128)(2,1)S(1)} %get-tuple-element.14.refs_0_), channel_id=1, source_target_pairs={{0,4},{4,0},{8,12},{12,8},{16,20},{20,16},{24,28},{28,24},{1,5},{5... | collective-permute-start | bytes 110600 | tf_op jit(solution)/shard_map/ppermute | solution.py:406
  18.8 11.3 %collective-permute-start.1 = (bf16[9,8,256]{2,1,0:T(8,128)(2,1)S(1)}, bf16[9,8,256]{2,1,0:T(8,128)(2,1)S(1)}, u32[]{:S(2)}, u32[]{:S(2)}) collective-permute-start(bf16[9,8,256]{2,1,0:T(8,128)(2,1)S(1)} %get-tuple-element.14.refs_0_), channel_id=1, source_target_pairs={{0,8},{4,12},{8,0},{12,4},{16,24},{20,28},{24,16},{28,20},{1,9},{5... | collective-permute-start | bytes 110600 | tf_op jit(solution)/shard_map/ppermute | solution.py:406
  20.3 10.6 %collective-permute-start.2 = (bf16[9,8,256]{2,1,0:T(8,128)(2,1)S(1)}, bf16[9,8,256]{2,1,0:T(8,128)(2,1)S(1)}, u32[]{:S(2)}, u32[]{:S(2)}) collective-permute-start(bf16[9,8,256]{2,1,0:T(8,128)(2,1)S(1)} %get-tuple-element.14.refs_0_), channel_id=1, source_target_pairs={{0,12},{4,8},{8,4},{12,0},{16,28},{20,24},{24,20},{28,16},{1,13},{... | collective-permute-start | bytes 110600 | tf_op jit(solution)/shard_map/ppermute | solution.py:406
  20.3 20.4 %collective-permute-start.3 = (bf16[64,8,256]{2,1,0:T(8,128)(2,1)}, bf16[64,8,256]{2,1,0:T(8,128)(2,1)S(1)}, u32[]{:S(2)}, u32[]{:S(2)}) collective-permute-start(bf16[64,8,256]{2,1,0:T(8,128)(2,1)} %get-tuple-element.16), channel_id=1, source_target_pairs={{0,4},{4,0},{8,12},{12,8},{16,20},{20,16},{24,28},{28,24},{1,5},{5... | collective-permute-start | bytes 786440 | tf_op jit(solution)/shard_map/ppermute | solution.py:406
  22.3 18.3 %collective-permute-start.4 = (bf16[64,8,256]{2,1,0:T(8,128)(2,1)}, bf16[64,8,256]{2,1,0:T(8,128)(2,1)S(1)}, u32[]{:S(2)}, u32[]{:S(2)}) collective-permute-start(bf16[64,8,256]{2,1,0:T(8,128)(2,1)} %get-tuple-element.17), channel_id=1, source_target_pairs={{0,8},{4,12},{8,0},{12,4},{16,24},{20,28},{24,16},{28,20},{1,9},{5... | collective-permute-start | bytes 786440 | tf_op jit(solution)/shard_map/ppermute | solution.py:406
  23.8 20.2 %collective-permute-start.5 = (bf16[64,8,256]{2,1,0:T(8,128)(2,1)}, bf16[64,8,256]{2,1,0:T(8,128)(2,1)S(1)}, u32[]{:S(2)}, u32[]{:S(2)}) collective-permute-start(bf16[64,8,256]{2,1,0:T(8,128)(2,1)} %copy-done.7), channel_id=1, source_target_pairs={{0,12},{4,8},{8,4},{12,0},{16,28},{20,24},{24,20},{28,16},{1,13},{... | collective-permute-start | bytes 786440 | tf_op jit(solution)/shard_map/ppermute | solution.py:406
  31.1 2.3 %collective-permute-start.6 = (bf16[4,9,8,256]{3,2,1,0:T(8,128)(2,1)S(1)}, bf16[4,9,8,256]{3,2,1,0:T(8,128)(2,1)S(1)}, u32[]{:S(2)}, u32[]{:S(2)}) collective-permute-start(bf16[4,9,8,256]{3,2,1,0:T(8,128)(2,1)S(1)} %shard_map.97.refs_4_), channel_id=1, source_target_pairs={{0,1},{1,0},{2,3},{3,2},{4,5},{5,4},{6,7},{7,6},{8,9},{9,8},{10,11... | collective-permute-start | bytes 442376 | tf_op jit(solution)/shard_map/ppermute | solution.py:406
  31.6 6.7 %collective-permute-start.7 = (bf16[4,9,8,256]{3,2,1,0:T(8,128)(2,1)S(1)}, bf16[4,9,8,256]{3,2,1,0:T(8,128)(2,1)S(1)}, u32[]{:S(2)}, u32[]{:S(2)}) collective-permute-start(bf16[4,9,8,256]{3,2,1,0:T(8,128)(2,1)S(1)} %shard_map.97.refs_4_), channel_id=1, source_target_pairs={{0,2},{1,3},{2,0},{3,1},{4,6},{5,7},{6,4},{7,5},{8,10},{9,11},{10,... | collective-permute-start | bytes 442376 | tf_op jit(solution)/shard_map/ppermute | solution.py:406
  33.4 7.2 %collective-permute-start.8 = (bf16[4,9,8,256]{3,2,1,0:T(8,128)(2,1)S(1)}, bf16[4,9,8,256]{3,2,1,0:T(8,128)(2,1)S(1)}, u32[]{:S(2)}, u32[]{:S(2)}) collective-permute-start(bf16[4,9,8,256]{3,2,1,0:T(8,128)(2,1)S(1)} %shard_map.97.refs_4_), channel_id=1, source_target_pairs={{0,3},{1,2},{2,1},{3,0},{4,7},{5,6},{6,5},{7,4},{8,11},{9,10},{10,... | collective-permute-start | bytes 442376 | tf_op jit(solution)/shard_map/ppermute | solution.py:406
  44.0 1.0 %copy-start.1 = (bf16[1024,256]{1,0:T(8,128)(2,1)S(1)}, bf16[1024,256]{1,0:T(8,128)(2,1)}, u32[]{:S(2)}) copy-start(bf16[1024,256]{1,0:T(8,128)(2,1)} %constant.49.table_ref) | copy-start | bytes 1572868
  57.3 0.7 copy-start.8
  58.0 0.7 copy-start.10
  58.7 3.8 %copy-start.11 = (f32[32,2048]{1,0:T(8,128)S(1)}, f32[32,2048]{1,0:T(8,128)}, u32[]{:S(2)}) copy-start(f32[32,2048]{1,0:T(8,128)} %copy-done.10) | copy-start | bytes 786436
  58.7 5.4 %copy-start.9 = (f32[32,2048]{1,0:T(8,128)S(1)}, f32[32,2048]{1,0:T(8,128)}, u32[]{:S(2)}) copy-start(f32[32,2048]{1,0:T(8,128)} %copy-done.8) | copy-start | bytes 786436
  58.7 30.6 %all-to-all-start.1 = ((s16[8,528,128]{2,1,0:T(8,128)(2,1)}), s16[8,528,128]{2,1,0:T(8,128)(2,1)S(1)}, u32[]{:S(2)}, u32[]{:S(2)}) async-start(s16[8,528,128]{2,1,0:T(8,128)(2,1)} %get-tuple-element.23), calls=%async_computation.1 | async-start | bytes 2162688 | tf_op jit(solution)/shard_map/all_to_all | solution.py:537
  62.5 9.3 %collective-permute-start.10 = (f32[32,2048]{1,0:T(8,128)S(1)}, f32[32,2048]{1,0:T(8,128)S(1)}, u32[]{:S(2)}, u32[]{:S(2)}) collective-permute-start(f32[32,2048]{1,0:T(8,128)S(1)} %copy-done.11), channel_id=1, source_target_pairs={{0,2},{1,3},{2,0},{3,1},{4,6},{5,7},{6,4},{7,5},{8,10},{9,11},{10,... | collective-permute-start | bytes 786440 | tf_op jit(solution)/shard_map/ppermute | solution.py:406
  64.1 11.2 %collective-permute-start.11 = (f32[32,2048]{1,0:T(8,128)S(1)}, f32[32,2048]{1,0:T(8,128)S(1)}, u32[]{:S(2)}, u32[]{:S(2)}) collective-permute-start(f32[32,2048]{1,0:T(8,128)S(1)} %copy-done.9), channel_id=1, source_target_pairs={{0,3},{1,2},{2,1},{3,0},{4,7},{5,6},{6,5},{7,4},{8,11},{9,10},{10,... | collective-permute-start | bytes 786440 | tf_op jit(solution)/shard_map/ppermute | solution.py:406
  64.1 11.2 %collective-permute-start.9 = (f32[32,2048]{1,0:T(8,128)S(1)}, f32[32,2048]{1,0:T(8,128)S(1)}, u32[]{:S(2)}, u32[]{:S(2)}) collective-permute-start(f32[32,2048]{1,0:T(8,128)S(1)} %get-tuple-element.20), channel_id=1, source_target_pairs={{0,1},{1,0},{2,3},{3,2},{4,5},{5,4},{6,7},{7,6},{8,9},{9,8},{10,11... | collective-permute-start | bytes 786440 | tf_op jit(solution)/shard_map/ppermute | solution.py:406
  75.4 7.0 %collective-permute-start.12 = (f32[8,2048]{1,0:T(8,128)S(1)}, f32[8,2048]{1,0:T(8,128)S(1)}, u32[]{:S(2)}, u32[]{:S(2)}) collective-permute-start(f32[8,2048]{1,0:T(8,128)S(1)} %get-tuple-element.24), channel_id=1, source_target_pairs={{0,4},{4,0},{8,12},{12,8},{16,20},{20,16},{24,28},{28,24},{1,5},{5... | collective-permute-start | bytes 196616 | tf_op jit(solution)/shard_map/ppermute | solution.py:406
  77.2 6.1 %collective-permute-start.13 = (f32[8,2048]{1,0:T(8,128)S(1)}, f32[8,2048]{1,0:T(8,128)S(1)}, u32[]{:S(2)}, u32[]{:S(2)}) collective-permute-start(f32[8,2048]{1,0:T(8,128)S(1)} %get-tuple-element.26), channel_id=1, source_target_pairs={{0,8},{4,12},{8,0},{12,4},{16,24},{20,28},{24,16},{28,20},{1,9},{5... | collective-permute-start | bytes 196616 | tf_op jit(solution)/shard_map/ppermute | solution.py:406
  78.6 6.5 %collective-permute-start.14 = (f32[8,2048]{1,0:T(8,128)S(1)}, f32[8,2048]{1,0:T(8,128)S(1)}, u32[]{:S(2)}, u32[]{:S(2)}) collective-permute-start(f32[8,2048]{1,0:T(8,128)S(1)} %get-tuple-element.25), channel_id=1, source_target_pairs={{0,12},{4,8},{8,4},{12,0},{16,28},{20,24},{24,20},{28,16},{1,13},{... | collective-permute-start | bytes 196616 | tf_op jit(solution)/shard_map/ppermute | solution.py:406

commit v8 on v7

--- a/solution.py
+++ b/solution.py
@@ -169,13 +169,13 @@
         copy.wait()
 
 
-def pair_kernel(n_e, n_r, c_ref, invn_ref, table_ref, v_from, *refs):
+def pair_kernel(n_e, n_r, c_ref, invn_ref, v_from, table_from, *refs):
     refs = list(refs)
     e_from, u_from = refs[:n_e], refs[n_e : n_e + n_r]
     w_to, *r_to = refs[n_e + n_r : n_e + 2 * n_r + 1]
     (
         x_ref, z_ref, plain_ref, turned_ref, code_ref, u_ref, v_ref, e_ref, r_ref, w_ref,
-        sems, w_sems,
+        table_ref, sems, w_sems,
     ) = refs[n_e + 2 * n_r + 1 :]
 
     src_total, col_total, k_own = v_ref.shape
@@ -198,17 +198,11 @@
         pltpu.make_async_copy(ref, e_ref.at[k], sems.at[1 + n_r + k])
         for k, ref in enumerate(e_from)
     ]
+    late.append(pltpu.make_async_copy(table_from, table_ref, sems.at[1 + n_r + n_e]))
     for copy in early + late:
         copy.start()
     half = e_ref.shape[-1]
     eye = eye_of(half)
-    table_y = [table_ref[p * half : (p + 1) * half, :] for p in range(2)]
-    table_z = []
-    for p in range(2):
-        begin = 2 * half + p * 2 * half_f
-        parts = [table_ref[begin + n * half_f : begin + (n + 1) * half_f, :] for n in range(2)]
-        table_z.append(jnp.concatenate(parts, axis=1))
-
     group_ids = lax.broadcasted_iota(jnp.int32, (jp_total, LANES), 1) // (2 * S)
     first_part = lax.broadcasted_iota(jnp.int32, (irec, LANES), 1) % (2 * S) < S
 
@@ -312,6 +306,12 @@
 
     for copy in late:
         copy.wait()
+    table_y = [table_ref[p * half : (p + 1) * half, :] for p in range(2)]
+    table_z = []
+    for p in range(2):
+        begin = 2 * half + p * 2 * half_f
+        parts = [table_ref[begin + n * half_f : begin + (n + 1) * half_f, :] for n in range(2)]
+        table_z.append(jnp.concatenate(parts, axis=1))
     lax.fori_loop(0, jp_total // WIDTH, pairs, 0, unroll=2)
 
     def backward(src, b):
@@ -377,7 +377,7 @@
         w_copy(src).wait()
 
 
-def join_kernel(count_ref, got_ref, out_ref):
+def join_kernel(count_ref, got_ref, out_to, out_ref, sems):
     src_total, rows_total, _ = got_ref.shape
     k_own, col_total = out_ref.shape
     own_blocks = k_own // LANES
@@ -389,6 +389,7 @@
     for src in range(src_total):
         codes = got_ref[src, own_blocks * cols :, :].astype(jnp.int32).astype(jnp.float32)
         scales.append(jnp.exp2(codes) * (1.0 / FIXED))
+    copies = []
     for b in range(own_blocks):
         rows = []
         for m in range(members):
@@ -399,7 +400,12 @@
                 total = part if total is None else total + part
             rows.append(total)
         whole = jnp.concatenate(rows, axis=0).T
-        out_ref[b * LANES : (b + 1) * LANES, :] = jnp.where(inside, whole, 0.0)
+        rows = pl.ds(b * LANES, LANES)
+        out_ref[rows, :] = jnp.where(inside, whole, 0.0)
+        copies.append(pltpu.make_async_copy(out_ref.at[rows], out_to.at[rows], sems.at[b]))
+        copies[-1].start()
+    for copy in copies:
+        copy.wait()
 
 
 def swap(x, axis, total, k):
@@ -514,7 +520,7 @@
         functools.partial(pair_kernel, members, ref_total),
         out_shape=[jax.ShapeDtypeStruct((rcv_total, w_rows, LANES), jnp.int16)]
         + [jax.ShapeDtypeStruct((irec, k_quarter), jnp.float32)] * ref_total,
-        in_specs=[smem] + [vmem] * 2 + [hbm] * (1 + members + ref_total),
+        in_specs=[smem, vmem] + [hbm] * (2 + members + ref_total),
         out_specs=[hbm] * (1 + ref_total),
         scratch_shapes=[
             pltpu.VMEM((lines, LANES), jnp.float32),
@@ -527,19 +533,24 @@
             pltpu.VMEM((members, cols, row_total, half), bf16),
             pltpu.VMEM((ref_total, irec, k_quarter), jnp.float32),
             pltpu.VMEM((rcv_total, w_rows, LANES), jnp.int16),
-            pltpu.SemaphoreType.DMA((1 + members + ref_total,)),
+            pltpu.VMEM(table.shape, bf16),
+            pltpu.SemaphoreType.DMA((2 + members + ref_total,)),
             pltpu.SemaphoreType.DMA((rcv_total,)),
         ],
-        compiler_params=params(32),
+        compiler_params=params(62),
         cost_estimate=free,
-    )(scalars, inverse, table, v_all, *e_all, *u_all)
+    )(scalars, inverse, v_all, table, *e_all, *u_all)
 
     got = lax.all_to_all(w_part, "rcv", split_axis=0, concat_axis=0, tiled=True)
     reference_grad = pl.pallas_call(
         join_kernel,
         out_shape=jax.ShapeDtypeStruct((k_own, col_total), jnp.float32),
         in_specs=[vmem] * 2,
-        out_specs=vmem,
+        out_specs=hbm,
+        scratch_shapes=[
+            pltpu.VMEM((k_own, col_total), jnp.float32),
+            pltpu.SemaphoreType.DMA((k_own // LANES,)),
+        ],
         compiler_params=params(32),
         cost_estimate=free,
     )(reference_counts.reshape(1, col_total), got)

time: 91 us -> 90.4 us (level)
  local copies, waits for them, and re-layouts: 3.73 us -> 1.97 us
  starting transfers between devices: 26.3 us -> 27.6 us
  waiting for transfers between devices: 37.2 us -> 36.1 us
    unnamed x24 -> x38, local copies, waits for them, and re-layouts: 3.19 us -> 1.43 us
    ppermute x15, starting transfers between devices: 15 us -> 16.2 us  [swap(): return lax.ppermute(x, axis, [(r, r ^ k) for r in range(total)])]
    ppermute x15, waiting for transfers between devices: 33.7 us -> 32.6 us  [swap(): return lax.ppermute(x, axis, [(r, r ^ k) for r in range(total)])]
    pallas_call x1, Pallas kernels: 12.3 us -> 13.3 us  [shards(): pl.pallas_call(functools.partial(pair_kernel, members, ref_total), out_sh...]
  transfers between devices with their start and end apart: 17 -> 17, of which waited for: 11 -> 11; matrix products, arithmetic and copies ran while one was open for 2% -> 2% of each run, Pallas kernels for 6% -> 5%
where the time goes in v8:
time: 90.4 us; the launch traced here: 90.1 us
  waiting for transfers between devices  36.1 us (40%)
  starting transfers between devices  27.6 us (31%)
  Pallas kernels  21.8 us (24%)
  local copies, waits for them, and re-layouts  1.97 us (2%)
  other arithmetic  1.71 us (2%)
  between operations  0.91 us (1%)
    ppermute x15, waiting for transfers between devices, swap(): return lax.ppermute(x, axis, [(r, r ^ k) for r in range(total)])  32.6 us
    ppermute x15, starting transfers between devices, swap(): return lax.ppermute(x, axis, [(r, r ^ k) for r in range(total)])  16.2 us
    pallas_call x1, Pallas kernels, shards(): pl.pallas_call(functools.partial(pair_kernel, members, ref_total), out_sh...  13.3 us
    all_to_all x1, starting transfers between devices, shards(): v_all = lax.all_to_all(sent, 'rcv', split_axis=0, concat_axis=0, tiled=True)  7.43 us
    pallas_call x1, Pallas kernels, shards(): pl.pallas_call(fold_kernel, out_shape=[jax.ShapeDtypeStruct((extra, row_t...  4.19 us
    all_to_all x1, starting transfers between devices, shards(): got = lax.all_to_all(w_part, 'rcv', split_axis=0, concat_axis=0, tiled=True)  4 us
    all_to_all x1, waiting for transfers between devices, shards(): got = lax.all_to_all(w_part, 'rcv', split_axis=0, concat_axis=0, tiled=True)  3.46 us
    pallas_call x1, Pallas kernels, shards(): pl.pallas_call(turn_kernel, out_shape=jax.ShapeDtypeStruct((rcv_total, co...  2.95 us
  transfers between devices with their start and end apart: 17, of which 11 were waited for; matrix products, arithmetic and copies ran while one was open for 2% of the time, Pallas kernels for 5%

profile of v8, /device:TPU:0, one launch (start us, length us, event | category | flops | bytes accessed | tf_op | source)
XLA Modules:
  0.0 90.1 jit_solution(4015387934471442271)
XLA Ops:
  0.6 0.0 copy-start.4
  0.6 2.9 %shard_map.95 = bf16[8,64,1024]{2,1,0:T(8,128)(2,1)} custom-call(bf16[1024,256]{1,0:T(8,128)(2,1)} %spectra_from.1, s32[1,256]{1,0:T(1,128)} %bitcast.7), custom_call_target="tpu_custom_call" | custom-call | tf_op jit(solution)/shard_map/pallas_call | solution.py:451
  3.6 0.0 copy-start
  3.6 0.0 copy-start.3
  3.6 0.0 copy-start.7
  3.6 0.0 copy-start.8
  3.6 7.4 %all-to-all-start = ((bf16[8,64,1024]{2,1,0:T(8,128)(2,1)}), bf16[8,64,1024]{2,1,0:T(8,128)(2,1)}, u32[]{:S(2)}, u32[]{:S(2)}) async-start(bf16[8,64,1024]{2,1,0:T(8,128)(2,1)} %shard_map.95), calls=%async_computation | async-start | bytes 2097152 | tf_op jit(solution)/shard_map/all_to_all | solution.py:465
  11.1 0.1 pad_add_fusion.c_ref
  11.2 0.0 copy-done.4
  11.2 0.0 copy-done
  11.2 0.0 copy-start.6
  11.2 4.2 %shard_map.96 = (bf16[9,8,256]{2,1,0:T(8,128)(2,1)S(1)}, bf16[64,8,256]{2,1,0:T(8,128)(2,1)S(1)}, bf16[64,8,256]{2,1,0:T(8,128)(2,1)S(1)}, bf16[64,8,256]{2,1,0:T(8,128)(2,1)S(1)}, bf16[64,8,256]{2,1,0:T(8,128)(2,1)S(1)}) custom-call(s32[4]{0:T(128)S(1)} %pad_add_fusion.c_ref, s32[8]{0:T(128)S(1)} %copy-done.7, bf16[8,256,512]{2,1,0:T(8,128)(2,1)S(1)} %copy-done, ...), custom_call_target="tpu_custom_call" | custom-call | tf_op jit(solution)/shard_map/pallas_call | solution.py:469
  15.4 0.7 copy-done.2
  16.1 2.0 %collective-permute-start = (bf16[9,8,256]{2,1,0:T(8,128)(2,1)S(1)}, bf16[9,8,256]{2,1,0:T(8,128)(2,1)S(1)}, u32[]{:S(2)}, u32[]{:S(2)}) collective-permute-start(bf16[9,8,256]{2,1,0:T(8,128)(2,1)S(1)} %get-tuple-element.14.refs_0_), channel_id=1, source_target_pairs={{0,4},{4,0},{8,12},{12,8},{16,20},{20,16},{24,28},{28,24},{1,5},{5... | collective-permute-start | bytes 110600 | tf_op jit(solution)/shard_map/ppermute | solution.py:412
  18.1 1.5 %collective-permute-start.1 = (bf16[9,8,256]{2,1,0:T(8,128)(2,1)S(1)}, bf16[9,8,256]{2,1,0:T(8,128)(2,1)S(1)}, u32[]{:S(2)}, u32[]{:S(2)}) collective-permute-start(bf16[9,8,256]{2,1,0:T(8,128)(2,1)S(1)} %get-tuple-element.14.refs_0_), channel_id=1, source_target_pairs={{0,8},{4,12},{8,0},{12,4},{16,24},{20,28},{24,16},{28,20},{1,9},{5... | collective-permute-start | bytes 110600 | tf_op jit(solution)/shard_map/ppermute | solution.py:412
  19.6 0.0 collective-permute-start.2
  19.6 2.0 %collective-permute-start.3 = (bf16[64,8,256]{2,1,0:T(8,128)(2,1)S(1)}, bf16[64,8,256]{2,1,0:T(8,128)(2,1)S(1)}, u32[]{:S(2)}, u32[]{:S(2)}) collective-permute-start(bf16[64,8,256]{2,1,0:T(8,128)(2,1)S(1)} %get-tuple-element.16), channel_id=1, source_target_pairs={{0,4},{4,0},{8,12},{12,8},{16,20},{20,16},{24,28},{28,24},{1,5},{5... | collective-permute-start | bytes 786440 | tf_op jit(solution)/shard_map/ppermute | solution.py:412
  21.6 1.5 %collective-permute-start.4 = (bf16[64,8,256]{2,1,0:T(8,128)(2,1)S(1)}, bf16[64,8,256]{2,1,0:T(8,128)(2,1)S(1)}, u32[]{:S(2)}, u32[]{:S(2)}) collective-permute-start(bf16[64,8,256]{2,1,0:T(8,128)(2,1)S(1)} %get-tuple-element.17), channel_id=1, source_target_pairs={{0,8},{4,12},{8,0},{12,4},{16,24},{20,28},{24,16},{28,20},{1,9},{5... | collective-permute-start | bytes 786440 | tf_op jit(solution)/shard_map/ppermute | solution.py:412
  23.1 0.0 collective-permute-done.refs_1_
  23.1 1.5 %collective-permute-start.5 = (bf16[64,8,256]{2,1,0:T(8,128)(2,1)S(1)}, bf16[64,8,256]{2,1,0:T(8,128)(2,1)S(1)}, u32[]{:S(2)}, u32[]{:S(2)}) collective-permute-start(bf16[64,8,256]{2,1,0:T(8,128)(2,1)S(1)} %get-tuple-element.18), channel_id=1, source_target_pairs={{0,12},{4,8},{8,4},{12,0},{16,28},{20,24},{24,20},{28,16},{1,13},{... | collective-permute-start | bytes 786440 | tf_op jit(solution)/shard_map/ppermute | solution.py:412
  24.6 5.5 %collective-permute-done.1.refs_2_ = bf16[9,8,256]{2,1,0:T(8,128)(2,1)S(1)} collective-permute-done((bf16[9,8,256]{2,1,0:T(8,128)(2,1)S(1)}, bf16[9,8,256]{2,1,0:T(8,128)(2,1)S(1)}, u32[]{:S(2)}, u32[]{:S(2)}) %collective-permute-start.1) | collective-permute-done | bytes 36896 | tf_op jit(solution)/shard_map/ppermute | solution.py:412
  30.1 0.8 collective-permute-done.2.refs_3_
  30.9 0.2 shard_map.97.refs_4_
  31.1 0.0 copy-start.1
  31.1 0.1 collective-permute-start.6
  31.2 0.1 dynamic-slice_convert_fusion
  31.3 0.1 reshape.35
  31.4 0.1 copy.11
  31.4 0.1 min.20
  31.5 0.1 min.21
  31.6 1.5 %collective-permute-start.7 = (bf16[4,9,8,256]{3,2,1,0:T(8,128)(2,1)S(1)}, bf16[4,9,8,256]{3,2,1,0:T(8,128)(2,1)S(1)}, u32[]{:S(2)}, u32[]{:S(2)}) collective-permute-start(bf16[4,9,8,256]{3,2,1,0:T(8,128)(2,1)S(1)} %shard_map.97.refs_4_), channel_id=1, source_target_pairs={{0,2},{1,3},{2,0},{3,1},{4,6},{5,7},{6,4},{7,5},{8,10},{9,11},{10,... | collective-permute-start | bytes 442376 | tf_op jit(solution)/shard_map/ppermute | solution.py:412
  33.1 0.1 convert_reduce_fusion
  33.2 0.1 reshape.38
  33.3 0.1 min.23
  33.4 0.0 collective-permute-done.6.refs_5_
  33.4 0.4 collective-permute-start.8
  33.8 0.7 pad_maximum_fusion.invn_ref
  34.5 3.8 %collective-permute-done.7.refs_6_ = bf16[4,9,8,256]{3,2,1,0:T(8,128)(2,1)S(1)} collective-permute-done((bf16[4,9,8,256]{3,2,1,0:T(8,128)(2,1)S(1)}, bf16[4,9,8,256]{3,2,1,0:T(8,128)(2,1)S(1)}, u32[]{:S(2)}, u32[]{:S(2)}) %collective-permute-start.7) | collective-permute-done | bytes 147488 | tf_op jit(solution)/shard_map/ppermute | solution.py:412
  38.3 2.3 %collective-permute-done.8.refs_7_ = bf16[4,9,8,256]{3,2,1,0:T(8,128)(2,1)S(1)} collective-permute-done((bf16[4,9,8,256]{3,2,1,0:T(8,128)(2,1)S(1)}, bf16[4,9,8,256]{3,2,1,0:T(8,128)(2,1)S(1)}, u32[]{:S(2)}, u32[]{:S(2)}) %collective-permute-start.8) | collective-permute-done | bytes 147488 | tf_op jit(solution)/shard_map/ppermute | solution.py:412
  40.6 0.0 collective-permute-done.3.refs_1_
  40.6 0.0 collective-permute-done.4.refs_2_
  40.6 3.3 %collective-permute-done.5.refs_3_ = bf16[64,8,256]{2,1,0:T(8,128)(2,1)S(1)} collective-permute-done((bf16[64,8,256]{2,1,0:T(8,128)(2,1)S(1)}, bf16[64,8,256]{2,1,0:T(8,128)(2,1)S(1)}, u32[]{:S(2)}, u32[]{:S(2)}) %collective-permute-start.5) | collective-permute-done | bytes 262176 | tf_op jit(solution)/shard_map/ppermute | solution.py:412
  44.0 0.0 all-to-all-done.v_from
  44.1 0.7 copy-done.12
  44.7 13.3 %shard_map.98 = (s16[8,528,128]{2,1,0:T(8,128)(2,1)}, f32[32,2048]{1,0:T(8,128)}, f32[32,2048]{1,0:T(8,128)}, f32[32,2048]{1,0:T(8,128)}, f32[32,2048]{1,0:T(8,128)}) custom-call(s32[4]{0:T(128)} %copy-done.5, f32[32,128]{1,0:T(8,128)} %pad_maximum_fusion.invn_ref, bf16[8,64,1024]{2,1,0:T(8,128)(2,1)} %all-to-all-done.v_from, ...), custom_call_target="tpu_custom_call" | custom-call | tf_op jit(solution)/shard_map/pallas_call | solution.py:519
  58.0 0.0 copy-start.9
  58.0 4.0 %all-to-all-start.1 = ((s16[8,528,128]{2,1,0:T(8,128)(2,1)}), s16[8,528,128]{2,1,0:T(8,128)(2,1)S(1)}, u32[]{:S(2)}, u32[]{:S(2)}) async-start(s16[8,528,128]{2,1,0:T(8,128)(2,1)} %get-tuple-element.23), calls=%async_computation.1 | async-start | bytes 2162688 | tf_op jit(solution)/shard_map/all_to_all | solution.py:544
  62.0 1.6 %collective-permute-start.10 = (f32[32,2048]{1,0:T(8,128)S(1)}, f32[32,2048]{1,0:T(8,128)S(1)}, u32[]{:S(2)}, u32[]{:S(2)}) collective-permute-start(f32[32,2048]{1,0:T(8,128)S(1)} %copy-done.18), channel_id=1, source_target_pairs={{0,2},{1,3},{2,0},{3,1},{4,6},{5,7},{6,4},{7,5},{8,10},{9,11},{10,... | collective-permute-start | bytes 786440 | tf_op jit(solution)/shard_map/ppermute | solution.py:412
  63.6 0.0 collective-permute-start.11
  63.6 0.0 copy-done.16
  63.6 0.6 collective-permute-start.9
  64.3 7.0 %collective-permute-done.10 = f32[32,2048]{1,0:T(8,128)S(1)} collective-permute-done((f32[32,2048]{1,0:T(8,128)S(1)}, f32[32,2048]{1,0:T(8,128)S(1)}, u32[]{:S(2)}, u32[]{:S(2)}) %collective-permute-start.10) | collective-permute-done | bytes 262176 | tf_op jit(solution)/shard_map/ppermute | solution.py:412
  71.3 3.6 %collective-permute-done.11 = f32[32,2048]{1,0:T(8,128)S(1)} collective-permute-done((f32[32,2048]{1,0:T(8,128)S(1)}, f32[32,2048]{1,0:T(8,128)S(1)}, u32[]{:S(2)}, u32[]{:S(2)}) %collective-permute-start.11) | collective-permute-done | bytes 262176 | tf_op jit(solution)/shard_map/ppermute | solution.py:412
  74.9 0.0 collective-permute-done.9
  74.9 0.1 add_add_fusion
  75.0 1.7 %collective-permute-start.12 = (f32[8,2048]{1,0:T(8,128)S(1)}, f32[8,2048]{1,0:T(8,128)S(1)}, u32[]{:S(2)}, u32[]{:S(2)}) collective-permute-start(f32[8,2048]{1,0:T(8,128)S(1)} %get-tuple-element.24), channel_id=1, source_target_pairs={{0,4},{4,0},{8,12},{12,8},{16,20},{20,16},{24,28},{28,24},{1,5},{5... | collective-permute-start | bytes 196616 | tf_op jit(solution)/shard_map/ppermute | solution.py:412
  76.7 1.5 %collective-permute-start.13 = (f32[8,2048]{1,0:T(8,128)S(1)}, f32[8,2048]{1,0:T(8,128)S(1)}, u32[]{:S(2)}, u32[]{:S(2)}) collective-permute-start(f32[8,2048]{1,0:T(8,128)S(1)} %get-tuple-element.26), channel_id=1, source_target_pairs={{0,8},{4,12},{8,0},{12,4},{16,24},{20,28},{24,16},{28,20},{1,9},{5... | collective-permute-start | bytes 196616 | tf_op jit(solution)/shard_map/ppermute | solution.py:412
  78.2 0.4 collective-permute-start.14
  78.6 3.5 %collective-permute-done.12 = f32[8,2048]{1,0:T(8,128)S(1)} collective-permute-done((f32[8,2048]{1,0:T(8,128)S(1)}, f32[8,2048]{1,0:T(8,128)S(1)}, u32[]{:S(2)}, u32[]{:S(2)}) %collective-permute-start.12) | collective-permute-done | bytes 65568 | tf_op jit(solution)/shard_map/ppermute | solution.py:412
  82.1 0.8 collective-permute-done.13
  82.9 1.8 %collective-permute-done.14 = f32[8,2048]{1,0:T(8,128)S(1)} collective-permute-done((f32[8,2048]{1,0:T(8,128)S(1)}, f32[8,2048]{1,0:T(8,128)S(1)}, u32[]{:S(2)}, u32[]{:S(2)}) %collective-permute-start.14) | collective-permute-done | bytes 65568 | tf_op jit(solution)/shard_map/ppermute | solution.py:412
  84.8 0.7 fusion.2
  85.5 3.5 %all-to-all-done.1.got_ref = s16[8,528,128]{2,1,0:T(8,128)(2,1)S(1)} async-done(((s16[8,528,128]{2,1,0:T(8,128)(2,1)}), s16[8,528,128]{2,1,0:T(8,128)(2,1)S(1)}, u32[]{:S(2)}, u32[]{:S(2)}) %all-to-all-start.1) | async-done | bytes 1081376 | tf_op jit(solution)/shard_map/all_to_all | solution.py:544
  88.9 1.1 %shard_map.99 = f32[1024,256]{1,0:T(8,128)} custom-call(s32[1,256]{1,0:T(1,128)S(1)} %bitcast.8, s16[8,528,128]{2,1,0:T(8,128)(2,1)S(1)} %all-to-all-done.1.got_ref), custom_call_target="tpu_custom_call" | custom-call | tf_op jit(solution)/shard_map/pallas_call | solution.py:545
  (29 shorter events, 0.1 us)
Async XLA Ops:
  0.6 10.5 %copy-start.4 = (s32[2,8,256]{2,1,0:T(8,128)S(1)}, s32[2,8,256]{2,1,0:T(8,128)}, u32[]{:S(2)}) copy-start(s32[2,8,256]{2,1,0:T(8,128)} %window_from.1) | copy-start | bytes 49156
  3.6 7.6 %copy-start = (bf16[8,256,512]{2,1,0:T(8,128)(2,1)S(1)}, bf16[8,256,512]{2,1,0:T(8,128)(2,1)}, u32[]{:S(2)}) copy-start(bf16[8,256,512]{2,1,0:T(8,128)(2,1)} %observed_from) | copy-start | bytes 6291460
  3.6 7.6 %copy-start.3 = (bf16[8,2048]{1,0:T(8,128)(2,1)S(1)}, bf16[8,2048]{1,0:T(8,128)(2,1)}, u32[]{:S(2)}) copy-start(bf16[8,2048]{1,0:T(8,128)(2,1)} %rspectra_from.1) | copy-start | bytes 98308
  3.6 7.5 %copy-start.7 = (s32[8]{0:T(128)S(1)}, s32[8]{0:T(128)}, u32[]{:S(2)}) copy-start(s32[8]{0:T(128)} %rcounts_ref.1) | copy-start | bytes 100
  3.6 7.5 %copy-start.8 = (s32[256]{0:T(256)S(1)}, s32[256]{0:T(256)}, u32[]{:S(2)}) copy-start(s32[256]{0:T(256)} %param.12) | copy-start | bytes 3076
  3.6 40.4 %all-to-all-start = ((bf16[8,64,1024]{2,1,0:T(8,128)(2,1)}), bf16[8,64,1024]{2,1,0:T(8,128)(2,1)}, u32[]{:S(2)}, u32[]{:S(2)}) async-start(bf16[8,64,1024]{2,1,0:T(8,128)(2,1)} %shard_map.95), calls=%async_computation | async-start | bytes 2097152 | tf_op jit(solution)/shard_map/all_to_all | solution.py:465
  11.1 11.9 %copy-start.5 = (s32[4]{0:T(128)}, s32[4]{0:T(128)S(1)}, u32[]{:S(2)}) copy-start(s32[4]{0:T(128)S(1)} %pad_add_fusion.c_ref) | copy-start | bytes 52
  11.2 20.0 %copy-start.6 = (s32[256]{0:T(256)S(1)}, s32[256]{0:T(256)}, u32[]{:S(2)}) copy-start(s32[256]{0:T(256)} %param.11) | copy-start | bytes 3076
  15.4 0.7 copy-start.2
  16.1 7.0 %collective-permute-start = (bf16[9,8,256]{2,1,0:T(8,128)(2,1)S(1)}, bf16[9,8,256]{2,1,0:T(8,128)(2,1)S(1)}, u32[]{:S(2)}, u32[]{:S(2)}) collective-permute-start(bf16[9,8,256]{2,1,0:T(8,128)(2,1)S(1)} %get-tuple-element.14.refs_0_), channel_id=1, source_target_pairs={{0,4},{4,0},{8,12},{12,8},{16,20},{20,16},{24,28},{28,24},{1,5},{5... | collective-permute-start | bytes 110600 | tf_op jit(solution)/shard_map/ppermute | solution.py:412
  18.1 12.0 %collective-permute-start.1 = (bf16[9,8,256]{2,1,0:T(8,128)(2,1)S(1)}, bf16[9,8,256]{2,1,0:T(8,128)(2,1)S(1)}, u32[]{:S(2)}, u32[]{:S(2)}) collective-permute-start(bf16[9,8,256]{2,1,0:T(8,128)(2,1)S(1)} %get-tuple-element.14.refs_0_), channel_id=1, source_target_pairs={{0,8},{4,12},{8,0},{12,4},{16,24},{20,28},{24,16},{28,20},{1,9},{5... | collective-permute-start | bytes 110600 | tf_op jit(solution)/shard_map/ppermute | solution.py:412
  19.6 11.3 %collective-permute-start.2 = (bf16[9,8,256]{2,1,0:T(8,128)(2,1)S(1)}, bf16[9,8,256]{2,1,0:T(8,128)(2,1)S(1)}, u32[]{:S(2)}, u32[]{:S(2)}) collective-permute-start(bf16[9,8,256]{2,1,0:T(8,128)(2,1)S(1)} %get-tuple-element.14.refs_0_), channel_id=1, source_target_pairs={{0,12},{4,8},{8,4},{12,0},{16,28},{20,24},{24,20},{28,16},{1,13},{... | collective-permute-start | bytes 110600 | tf_op jit(solution)/shard_map/ppermute | solution.py:412
  19.6 21.0 %collective-permute-start.3 = (bf16[64,8,256]{2,1,0:T(8,128)(2,1)S(1)}, bf16[64,8,256]{2,1,0:T(8,128)(2,1)S(1)}, u32[]{:S(2)}, u32[]{:S(2)}) collective-permute-start(bf16[64,8,256]{2,1,0:T(8,128)(2,1)S(1)} %get-tuple-element.16), channel_id=1, source_target_pairs={{0,4},{4,0},{8,12},{12,8},{16,20},{20,16},{24,28},{28,24},{1,5},{5... | collective-permute-start | bytes 786440 | tf_op jit(solution)/shard_map/ppermute | solution.py:412
  21.6 19.0 %collective-permute-start.4 = (bf16[64,8,256]{2,1,0:T(8,128)(2,1)S(1)}, bf16[64,8,256]{2,1,0:T(8,128)(2,1)S(1)}, u32[]{:S(2)}, u32[]{:S(2)}) collective-permute-start(bf16[64,8,256]{2,1,0:T(8,128)(2,1)S(1)} %get-tuple-element.17), channel_id=1, source_target_pairs={{0,8},{4,12},{8,0},{12,4},{16,24},{20,28},{24,16},{28,20},{1,9},{5... | collective-permute-start | bytes 786440 | tf_op jit(solution)/shard_map/ppermute | solution.py:412
  23.1 20.9 %collective-permute-start.5 = (bf16[64,8,256]{2,1,0:T(8,128)(2,1)S(1)}, bf16[64,8,256]{2,1,0:T(8,128)(2,1)S(1)}, u32[]{:S(2)}, u32[]{:S(2)}) collective-permute-start(bf16[64,8,256]{2,1,0:T(8,128)(2,1)S(1)} %get-tuple-element.18), channel_id=1, source_target_pairs={{0,12},{4,8},{8,4},{12,0},{16,28},{20,24},{24,20},{28,16},{1,13},{... | collective-permute-start | bytes 786440 | tf_op jit(solution)/shard_map/ppermute | solution.py:412
  31.1 12.9 %copy-start.1 = (bf16[4,9,8,256]{3,2,1,0:T(8,128)(2,1)}, bf16[4,9,8,256]{3,2,1,0:T(8,128)(2,1)S(1)}, u32[]{:S(2)}) copy-start(bf16[4,9,8,256]{3,2,1,0:T(8,128)(2,1)S(1)} %shard_map.97.refs_4_) | copy-start | bytes 442372
  31.1 2.3 %collective-permute-start.6 = (bf16[4,9,8,256]{3,2,1,0:T(8,128)(2,1)S(1)}, bf16[4,9,8,256]{3,2,1,0:T(8,128)(2,1)S(1)}, u32[]{:S(2)}, u32[]{:S(2)}) collective-permute-start(bf16[4,9,8,256]{3,2,1,0:T(8,128)(2,1)S(1)} %shard_map.97.refs_4_), channel_id=1, source_target_pairs={{0,1},{1,0},{2,3},{3,2},{4,5},{5,4},{6,7},{7,6},{8,9},{9,8},{10,11... | collective-permute-start | bytes 442376 | tf_op jit(solution)/shard_map/ppermute | solution.py:412
  31.6 6.7 %collective-permute-start.7 = (bf16[4,9,8,256]{3,2,1,0:T(8,128)(2,1)S(1)}, bf16[4,9,8,256]{3,2,1,0:T(8,128)(2,1)S(1)}, u32[]{:S(2)}, u32[]{:S(2)}) collective-permute-start(bf16[4,9,8,256]{3,2,1,0:T(8,128)(2,1)S(1)} %shard_map.97.refs_4_), channel_id=1, source_target_pairs={{0,2},{1,3},{2,0},{3,1},{4,6},{5,7},{6,4},{7,5},{8,10},{9,11},{10,... | collective-permute-start | bytes 442376 | tf_op jit(solution)/shard_map/ppermute | solution.py:412
  33.4 10.6 %copy-start.13 = (bf16[4,9,8,256]{3,2,1,0:T(8,128)(2,1)}, bf16[4,9,8,256]{3,2,1,0:T(8,128)(2,1)S(1)}, u32[]{:S(2)}) copy-start(bf16[4,9,8,256]{3,2,1,0:T(8,128)(2,1)S(1)} %collective-permute-done.6.refs_5_) | copy-start | bytes 442372
  33.4 7.2 %collective-permute-start.8 = (bf16[4,9,8,256]{3,2,1,0:T(8,128)(2,1)S(1)}, bf16[4,9,8,256]{3,2,1,0:T(8,128)(2,1)S(1)}, u32[]{:S(2)}, u32[]{:S(2)}) collective-permute-start(bf16[4,9,8,256]{3,2,1,0:T(8,128)(2,1)S(1)} %shard_map.97.refs_4_), channel_id=1, source_target_pairs={{0,3},{1,2},{2,1},{3,0},{4,7},{5,6},{6,5},{7,4},{8,11},{9,10},{10,... | collective-permute-start | bytes 442376 | tf_op jit(solution)/shard_map/ppermute | solution.py:412
  38.3 5.7 %copy-start.14 = (bf16[4,9,8,256]{3,2,1,0:T(8,128)(2,1)}, bf16[4,9,8,256]{3,2,1,0:T(8,128)(2,1)S(1)}, u32[]{:S(2)}) copy-start(bf16[4,9,8,256]{3,2,1,0:T(8,128)(2,1)S(1)} %collective-permute-done.7.refs_6_) | copy-start | bytes 442372
  40.6 3.4 %copy-start.15 = (bf16[4,9,8,256]{3,2,1,0:T(8,128)(2,1)}, bf16[4,9,8,256]{3,2,1,0:T(8,128)(2,1)S(1)}, u32[]{:S(2)}) copy-start(bf16[4,9,8,256]{3,2,1,0:T(8,128)(2,1)S(1)} %collective-permute-done.8.refs_7_) | copy-start | bytes 442372
  40.6 3.4 %copy-start.10 = (bf16[64,8,256]{2,1,0:T(8,128)(2,1)}, bf16[64,8,256]{2,1,0:T(8,128)(2,1)S(1)}, u32[]{:S(2)}) copy-start(bf16[64,8,256]{2,1,0:T(8,128)(2,1)S(1)} %collective-permute-done.3.refs_1_) | copy-start | bytes 786436
  40.6 3.4 %copy-start.11 = (bf16[64,8,256]{2,1,0:T(8,128)(2,1)}, bf16[64,8,256]{2,1,0:T(8,128)(2,1)S(1)}, u32[]{:S(2)}) copy-start(bf16[64,8,256]{2,1,0:T(8,128)(2,1)S(1)} %collective-permute-done.4.refs_2_) | copy-start | bytes 786436
  44.0 0.7 copy-start.12
  58.0 4.0 %copy-start.18 = (f32[32,2048]{1,0:T(8,128)S(1)}, f32[32,2048]{1,0:T(8,128)}, u32[]{:S(2)}) copy-start(f32[32,2048]{1,0:T(8,128)} %get-tuple-element.21) | copy-start | bytes 786436
  58.0 5.6 %copy-start.17 = (f32[32,2048]{1,0:T(8,128)S(1)}, f32[32,2048]{1,0:T(8,128)}, u32[]{:S(2)}) copy-start(f32[32,2048]{1,0:T(8,128)} %get-tuple-element.22) | copy-start | bytes 786436
  58.0 5.6 %copy-start.16 = (f32[32,2048]{1,0:T(8,128)S(1)}, f32[32,2048]{1,0:T(8,128)}, u32[]{:S(2)}) copy-start(f32[32,2048]{1,0:T(8,128)} %get-tuple-element.20) | copy-start | bytes 786436
  58.0 16.9 %copy-start.9 = (f32[32,2048]{1,0:T(8,128)S(1)}, f32[32,2048]{1,0:T(8,128)}, u32[]{:S(2)}) copy-start(f32[32,2048]{1,0:T(8,128)} %get-tuple-element.19) | copy-start | bytes 786436
  58.0 30.9 %all-to-all-start.1 = ((s16[8,528,128]{2,1,0:T(8,128)(2,1)}), s16[8,528,128]{2,1,0:T(8,128)(2,1)S(1)}, u32[]{:S(2)}, u32[]{:S(2)}) async-start(s16[8,528,128]{2,1,0:T(8,128)(2,1)} %get-tuple-element.23), calls=%async_computation.1 | async-start | bytes 2162688 | tf_op jit(solution)/shard_map/all_to_all | solution.py:544
  62.0 9.2 %collective-permute-start.10 = (f32[32,2048]{1,0:T(8,128)S(1)}, f32[32,2048]{1,0:T(8,128)S(1)}, u32[]{:S(2)}, u32[]{:S(2)}) collective-permute-start(f32[32,2048]{1,0:T(8,128)S(1)} %copy-done.18), channel_id=1, source_target_pairs={{0,2},{1,3},{2,0},{3,1},{4,6},{5,7},{6,4},{7,5},{8,10},{9,11},{10,... | collective-permute-start | bytes 786440 | tf_op jit(solution)/shard_map/ppermute | solution.py:412
  63.6 11.3 %collective-permute-start.11 = (f32[32,2048]{1,0:T(8,128)S(1)}, f32[32,2048]{1,0:T(8,128)S(1)}, u32[]{:S(2)}, u32[]{:S(2)}) collective-permute-start(f32[32,2048]{1,0:T(8,128)S(1)} %copy-done.17), channel_id=1, source_target_pairs={{0,3},{1,2},{2,1},{3,0},{4,7},{5,6},{6,5},{7,4},{8,11},{9,10},{10,... | collective-permute-start | bytes 786440 | tf_op jit(solution)/shard_map/ppermute | solution.py:412
  63.6 11.3 %collective-permute-start.9 = (f32[32,2048]{1,0:T(8,128)S(1)}, f32[32,2048]{1,0:T(8,128)S(1)}, u32[]{:S(2)}, u32[]{:S(2)}) collective-permute-start(f32[32,2048]{1,0:T(8,128)S(1)} %copy-done.16), channel_id=1, source_target_pairs={{0,1},{1,0},{2,3},{3,2},{4,5},{5,4},{6,7},{7,6},{8,9},{9,8},{10,11... | collective-permute-start | bytes 786440 | tf_op jit(solution)/shard_map/ppermute | solution.py:412
  75.0 7.1 %collective-permute-start.12 = (f32[8,2048]{1,0:T(8,128)S(1)}, f32[8,2048]{1,0:T(8,128)S(1)}, u32[]{:S(2)}, u32[]{:S(2)}) collective-permute-start(f32[8,2048]{1,0:T(8,128)S(1)} %get-tuple-element.24), channel_id=1, source_target_pairs={{0,4},{4,0},{8,12},{12,8},{16,20},{20,16},{24,28},{28,24},{1,5},{5... | collective-permute-start | bytes 196616 | tf_op jit(solution)/shard_map/ppermute | solution.py:412
  76.7 6.2 %collective-permute-start.13 = (f32[8,2048]{1,0:T(8,128)S(1)}, f32[8,2048]{1,0:T(8,128)S(1)}, u32[]{:S(2)}, u32[]{:S(2)}) collective-permute-start(f32[8,2048]{1,0:T(8,128)S(1)} %get-tuple-element.26), channel_id=1, source_target_pairs={{0,8},{4,12},{8,0},{12,4},{16,24},{20,28},{24,16},{28,20},{1,9},{5... | collective-permute-start | bytes 196616 | tf_op jit(solution)/shard_map/ppermute | solution.py:412
  78.2 6.5 %collective-permute-start.14 = (f32[8,2048]{1,0:T(8,128)S(1)}, f32[8,2048]{1,0:T(8,128)S(1)}, u32[]{:S(2)}, u32[]{:S(2)}) collective-permute-start(f32[8,2048]{1,0:T(8,128)S(1)} %get-tuple-element.25), channel_id=1, source_target_pairs={{0,12},{4,8},{8,4},{12,0},{16,28},{20,24},{24,20},{28,16},{1,13},{... | collective-permute-start | bytes 196616 | tf_op jit(solution)/shard_map/ppermute | solution.py:412

commit v9 on v8

--- a/solution.py
+++ b/solution.py
@@ -172,14 +172,14 @@
 def pair_kernel(n_e, n_r, c_ref, invn_ref, v_from, table_from, *refs):
     refs = list(refs)
     e_from, u_from = refs[:n_e], refs[n_e : n_e + n_r]
-    w_to, *r_to = refs[n_e + n_r : n_e + 2 * n_r + 1]
+    w_to, z_to = refs[n_e + n_r : n_e + n_r + 2]
     (
-        x_ref, z_ref, plain_ref, turned_ref, code_ref, u_ref, v_ref, e_ref, r_ref, w_ref,
-        table_ref, sems, w_sems,
-    ) = refs[n_e + 2 * n_r + 1 :]
+        x_ref, z_ref, plain_ref, turned_ref, code_ref, u_ref, v_ref, e_ref, z_out_ref, w_ref,
+        table_ref, sems, w_sems, z_sems,
+    ) = refs[n_e + n_r + 2 :]
 
     src_total, col_total, k_own = v_ref.shape
-    ref_total, irec, k_quarter = r_ref.shape
+    irec, k_quarter = plain_ref.shape[0], (u_ref.shape[2] - 1) * u_ref.shape[4]
     jj_total = LANES // (2 * irec)
     jp_total = col_total // jj_total
     k_total = src_total * k_own
@@ -333,6 +333,70 @@
         code_ref[pl.ds(fb, 1), :] = power
         fixed = jnp.round(total * (jnp.exp2(-power) * FIXED)).astype(jnp.int32)
         w_ref[src, b * col_total : (b + 1) * col_total, :] = fixed.astype(jnp.int16)
+        z_out_ref[fb] = z
+
+    def w_copy(src):
+        return pltpu.make_async_copy(w_ref.at[src], w_to.at[src], w_sems.at[src])
+
+    def z_copy(src):
+        rows = pl.ds(src * own_blocks, own_blocks)
+        return pltpu.make_async_copy(z_out_ref.at[rows], z_to.at[rows], z_sems.at[src])
+
+    def from_owner(src, _):
+        for b in range(own_blocks):
+            backward(src, b)
+        codes = code_ref[pl.ds(src * own_blocks, own_blocks), :]
+        codes = jnp.concatenate(
+            [codes, jnp.zeros((CODES - own_blocks, LANES), jnp.float32)], axis=0
+        )
+        w_ref[src, own_blocks * col_total :, :] = codes.astype(jnp.int32).astype(jnp.int16)
+        w_copy(src).start()
+        z_copy(src).start()
+        return 0
+
+    lax.fori_loop(0, src_total, from_owner, 0, unroll=4)
+    for src in range(src_total):
+        w_copy(src).wait()
+        z_copy(src).wait()
+
+
+def receiver_sum_kernel(c_ref, v_from, z_from, *refs):
+    *r_to, v_ref, z_ref, r_ref, code_ref, sems = refs
+    src_total, col_total, k_own = v_ref.shape
+    ref_total = r_ref.shape[0]
+    blocks = z_ref.shape[0]
+    quarter_blocks = blocks // ref_total
+    irec = (r_ref.shape[1] - CODES) // quarter_blocks
+    jj_total = LANES // (2 * irec)
+    jp_total = col_total // jj_total
+    own_blocks = k_own // LANES
+    copies = [
+        pltpu.make_async_copy(v_from, v_ref, sems.at[0]),
+        pltpu.make_async_copy(z_from, z_ref, sems.at[1]),
+    ]
+    for copy in copies:
+        copy.start()
+    group_ids = lax.broadcasted_iota(jnp.int32, (jp_total, LANES), 1) // (2 * S)
+    first_part = lax.broadcasted_iota(jnp.int32, (irec, LANES), 1) % (2 * S) < S
+
+    def lanes_of(fb, per):
+        return fb // per, pl.multiple_of(fb % per * LANES, LANES)
+
+    def v_block(fb):
+        src, off = lanes_of(fb, own_blocks)
+        parts = [
+            v_ref[src, jj * jp_total : (jj + 1) * jp_total, pl.ds(off, LANES)]
+            for jj in range(jj_total)
+        ]
+        zero = jnp.zeros((jp_total, LANES), jnp.bfloat16)
+        rows = [
+            jnp.concatenate([jnp.where(group_ids == f, part, zero) for part in parts], axis=1)
+            for f in range(FB)
+        ]
+        return jnp.concatenate(rows, axis=0)
+
+    def step(fb, _):
+        z = z_ref[fb]
         r = tn(z, v_block(fb))
         sums = []
         for q in range(2):
@@ -345,36 +409,52 @@
         crossed = jnp.where(
             first_part, -pltpu.roll(sums[1], LANES - S, 1), pltpu.roll(sums[1], S, 1)
         )
-        quarter, off = lanes_of(fb, quarter_blocks)
-        lanes = pl.ds(off, LANES)
         total = sums[0] + crossed
-        r_ref[quarter, :, lanes] = total
-
-    def w_copy(src):
-        return pltpu.make_async_copy(w_ref.at[src], w_to.at[src], w_sems.at[src])
-
-    def from_owner(src, _):
-        for b in range(own_blocks):
-            backward(src, b)
-        codes = code_ref[pl.ds(src * own_blocks, own_blocks), :]
+        largest = jnp.max(jnp.abs(total), axis=0, keepdims=True)
+        power = jnp.ceil(jnp.log2(jnp.maximum(largest, 1e-30)))
+        code_ref[pl.ds(fb, 1), :] = power
+        fixed = jnp.round(total * (jnp.exp2(-power) * FIXED)).astype(jnp.int32)
+        rows = pl.ds(pl.multiple_of(fb % quarter_blocks * irec, irec), irec)
+        r_ref[fb // quarter_blocks, rows, :] = fixed.astype(jnp.int16)
+        return 0
+
+    for copy in copies:
+        copy.wait()
+    lax.fori_loop(0, blocks, step, 0, unroll=32)
+    for quarter in range(ref_total):
+        codes = code_ref[quarter * quarter_blocks : (quarter + 1) * quarter_blocks, :]
         codes = jnp.concatenate(
-            [codes, jnp.zeros((CODES - own_blocks, LANES), jnp.float32)], axis=0
-        )
-        w_ref[src, own_blocks * col_total :, :] = codes.astype(jnp.int32).astype(jnp.int16)
-        w_copy(src).start()
-        return 0
-
-    lax.fori_loop(0, src_total, from_owner, 0, unroll=4)
+            [codes, jnp.zeros((CODES - quarter_blocks, LANES), jnp.float32)], axis=0
+        ) if quarter_blocks < CODES else codes
+        r_ref[quarter, quarter_blocks * irec :, :] = codes.astype(jnp.int32).astype(jnp.int16)
     outs = [
-        pltpu.make_async_copy(r_ref.at[quarter_me ^ k], ref, sems.at[k])
+        pltpu.make_async_copy(r_ref.at[c_ref[3] ^ k], ref, sems.at[2 + k])
         for k, ref in enumerate(r_to)
     ]
     for copy in outs:
         copy.start()
     for copy in outs:
         copy.wait()
-    for src in range(src_total):
-        w_copy(src).wait()
+
+
+def add_kernel(n_in, *refs):
+    got_refs, out_refs = refs[:n_in], refs[n_in:]
+    members = len(out_refs)
+    rows, k_quarter = out_refs[0].shape
+    blocks = k_quarter // LANES
+    irec = rows * members
+    scales = [
+        jnp.exp2(ref[blocks * irec :, :].astype(jnp.int32).astype(jnp.float32)) * (1.0 / FIXED)
+        for ref in got_refs
+    ]
+    for b in range(blocks):
+        total = None
+        for ref, scale in zip(got_refs, scales):
+            part = ref[b * irec : (b + 1) * irec, :].astype(jnp.int32).astype(jnp.float32)
+            part = part * scale[b : b + 1]
+            total = part if total is None else total + part
+        for m in range(members):
+            out_refs[m][:, b * LANES : (b + 1) * LANES] = total[m * rows : (m + 1) * rows]
 
 
 def join_kernel(count_ref, got_ref, out_to, out_ref, sems):
@@ -516,12 +596,14 @@
     table = lag_tables(k_total // (2 * S), lag_total)
     w_rows = k_own // LANES * cols + CODES
     lines = jp_total * (k_total // (2 * S) + PAD)
-    w_part, *r_all = pl.pallas_call(
+    w_part, z_part = pl.pallas_call(
         functools.partial(pair_kernel, members, ref_total),
-        out_shape=[jax.ShapeDtypeStruct((rcv_total, w_rows, LANES), jnp.int16)]
-        + [jax.ShapeDtypeStruct((irec, k_quarter), jnp.float32)] * ref_total,
+        out_shape=[
+            jax.ShapeDtypeStruct((rcv_total, w_rows, LANES), jnp.int16),
+            jax.ShapeDtypeStruct((k_total // LANES, FB * jp_total, LANES), bf16),
+        ],
         in_specs=[smem, vmem] + [hbm] * (2 + members + ref_total),
-        out_specs=[hbm] * (1 + ref_total),
+        out_specs=[hbm] * 2,
         scratch_shapes=[
             pltpu.VMEM((lines, LANES), jnp.float32),
             pltpu.VMEM((lines, LANES), jnp.float32),
@@ -531,10 +613,11 @@
             pltpu.VMEM((ref_total,) + near.shape, bf16),
             pltpu.VMEM((rcv_total, cols, k_own), bf16),
             pltpu.VMEM((members, cols, row_total, half), bf16),
-            pltpu.VMEM((ref_total, irec, k_quarter), jnp.float32),
+            pltpu.VMEM((k_total // LANES, FB * jp_total, LANES), bf16),
             pltpu.VMEM((rcv_total, w_rows, LANES), jnp.int16),
             pltpu.VMEM(table.shape, bf16),
             pltpu.SemaphoreType.DMA((2 + members + ref_total,)),
+            pltpu.SemaphoreType.DMA((rcv_total,)),
             pltpu.SemaphoreType.DMA((rcv_total,)),
         ],
         compiler_params=params(62),
@@ -555,10 +638,31 @@
         cost_estimate=free,
     )(reference_counts.reshape(1, col_total), got)
 
-    r_sum = r_all[0]
-    for k in range(1, ref_total):
-        r_sum = r_sum + swap(r_all[k], "ref", ref_total, k)
-    parts = [r_sum[k * row_total : (k + 1) * row_total] for k in range(members)]
+    r_rows = k_quarter // LANES * irec + CODES
+    r_all = pl.pallas_call(
+        receiver_sum_kernel,
+        out_shape=[jax.ShapeDtypeStruct((r_rows, LANES), jnp.int16)] * ref_total,
+        in_specs=[smem] + [hbm] * 2,
+        out_specs=[hbm] * ref_total,
+        scratch_shapes=[
+            pltpu.VMEM((rcv_total, cols, k_own), bf16),
+            pltpu.VMEM(z_part.shape, bf16),
+            pltpu.VMEM((ref_total, r_rows, LANES), jnp.int16),
+            pltpu.VMEM((k_total // LANES, LANES), jnp.float32),
+            pltpu.SemaphoreType.DMA((2 + ref_total,)),
+        ],
+        compiler_params=params(62),
+        cost_estimate=free,
+    )(scalars, v_all, z_part)
+
+    parts = pl.pallas_call(
+        functools.partial(add_kernel, ref_total),
+        out_shape=[jax.ShapeDtypeStruct((row_total, k_quarter), jnp.float32)] * members,
+        in_specs=[vmem] * ref_total,
+        out_specs=[vmem] * members,
+        compiler_params=params(16),
+        cost_estimate=free,
+    )(r_all[0], *[swap(r_all[k], "ref", ref_total, k) for k in range(1, ref_total)])
     r_sum = parts[0]
     for k in range(1, members):
         r_sum = r_sum + swap(parts[k], "rcv", rcv_total, k)

time: 90.4 us -> 88.6 us (0.980)
  waiting for transfers between devices: 36.1 us -> 29.9 us
  Pallas kernels: 21.8 us -> 25.5 us
  local copies, waits for them, and re-layouts: 1.97 us -> 2.92 us
    ppermute x15, waiting for transfers between devices: 32.6 us -> 26.7 us  [swap(): return lax.ppermute(x, axis, [(r, r ^ k) for r in range(total)])]
    pallas_call x0 -> x2, Pallas kernels: none -> 5.28 us  [the longest x1 5.14 us: shards(): pl.pallas_call(receiver_sum_kernel, out_shape=[jax.ShapeDtypeStruct((r_ro...]
    pallas_call x1, Pallas kernels: 13.3 us -> 11.7 us  [shards(): pl.pallas_call(functools.partial(pair_kernel, members, ref_total), out_sh...]
    unnamed x38 -> x32, local copies, waits for them, and re-layouts: 1.43 us -> 2.4 us
  transfers between devices with their start and end apart: 17 -> 17, of which waited for: 11 -> 10; matrix products, arithmetic and copies ran while one was open for 2% -> 2% of each run, Pallas kernels for 5% -> 11%
where the time goes in v9:
time: 88.6 us; the launch traced here: 88.3 us
  waiting for transfers between devices  29.9 us (34%)
  starting transfers between devices  27.4 us (31%)
  Pallas kernels  25.5 us (29%)
  local copies, waits for them, and re-layouts  2.92 us (3%)
  other arithmetic  1.64 us (2%)
    ppermute x15, waiting for transfers between devices, swap(): return lax.ppermute(x, axis, [(r, r ^ k) for r in range(total)])  26.7 us
    ppermute x15, starting transfers between devices, swap(): return lax.ppermute(x, axis, [(r, r ^ k) for r in range(total)])  16.2 us
    pallas_call x1, Pallas kernels, shards(): pl.pallas_call(functools.partial(pair_kernel, members, ref_total), out_sh...  11.7 us
    all_to_all x1, starting transfers between devices, shards(): v_all = lax.all_to_all(sent, 'rcv', split_axis=0, concat_axis=0, tiled=True)  7.42 us
    pallas_call x1, Pallas kernels, shards(): pl.pallas_call(receiver_sum_kernel, out_shape=[jax.ShapeDtypeStruct((r_ro...  5.14 us
    pallas_call x1, Pallas kernels, shards(): pl.pallas_call(fold_kernel, out_shape=[jax.ShapeDtypeStruct((extra, row_t...  4.19 us
    all_to_all x1, starting transfers between devices, shards(): got = lax.all_to_all(w_part, 'rcv', split_axis=0, concat_axis=0, tiled=True)  3.81 us
    all_to_all x1, waiting for transfers between devices, shards(): got = lax.all_to_all(w_part, 'rcv', split_axis=0, concat_axis=0, tiled=True)  3.28 us
  transfers between devices with their start and end apart: 17, of which 10 were waited for; matrix products, arithmetic and copies ran while one was open for 2% of the time, Pallas kernels for 11%

profile of v9, /device:TPU:0, one launch (start us, length us, event | category | flops | bytes accessed | tf_op | source)
XLA Modules:
  0.0 88.3 jit_solution(7449809705177833109)
XLA Ops:
  0.6 0.0 copy-start.9
  0.6 0.0 copy-start.8
  0.7 0.0 copy-start.5
  0.7 0.0 copy-start.4
  0.7 3.0 %shard_map.95 = bf16[8,64,1024]{2,1,0:T(8,128)(2,1)} custom-call(bf16[1024,256]{1,0:T(8,128)(2,1)} %spectra_from.1, s32[1,256]{1,0:T(1,128)} %bitcast.7), custom_call_target="tpu_custom_call" | custom-call | tf_op jit(solution)/shard_map/pallas_call | solution.py:531
  3.6 0.0 copy-start
  3.7 0.0 copy-start.7
  3.7 7.4 %all-to-all-start = ((bf16[8,64,1024]{2,1,0:T(8,128)(2,1)}), bf16[8,64,1024]{2,1,0:T(8,128)(2,1)}, u32[]{:S(2)}, u32[]{:S(2)}) async-start(bf16[8,64,1024]{2,1,0:T(8,128)(2,1)} %shard_map.95), calls=%async_computation | async-start | bytes 2097152 | tf_op jit(solution)/shard_map/all_to_all | solution.py:545
  11.1 0.1 pad_add_fusion.c_ref
  11.2 0.0 copy-done.9
  11.2 4.2 %shard_map.96 = (bf16[9,8,256]{2,1,0:T(8,128)(2,1)S(1)}, bf16[64,8,256]{2,1,0:T(8,128)(2,1)S(1)}, bf16[64,8,256]{2,1,0:T(8,128)(2,1)S(1)}, bf16[64,8,256]{2,1,0:T(8,128)(2,1)S(1)}, bf16[64,8,256]{2,1,0:T(8,128)(2,1)S(1)}) custom-call(s32[4]{0:T(128)S(1)} %pad_add_fusion.c_ref, s32[8]{0:T(128)S(1)} %copy-done.8, bf16[8,256,512]{2,1,0:T(8,128)(2,1)S(1)} %copy-done, ...), custom_call_target="tpu_custom_call" | custom-call | tf_op jit(solution)/shard_map/pallas_call | solution.py:549
  15.4 0.7 copy-done.2
  16.1 2.0 %collective-permute-start = (bf16[9,8,256]{2,1,0:T(8,128)(2,1)S(1)}, bf16[9,8,256]{2,1,0:T(8,128)(2,1)S(1)}, u32[]{:S(2)}, u32[]{:S(2)}) collective-permute-start(bf16[9,8,256]{2,1,0:T(8,128)(2,1)S(1)} %get-tuple-element.19.refs_0_), channel_id=1, source_target_pairs={{0,4},{4,0},{8,12},{12,8},{16,20},{20,16},{24,28},{28,24},{1,5},{5... | collective-permute-start | bytes 110600 | tf_op jit(solution)/shard_map/ppermute | solution.py:492
  18.2 1.5 %collective-permute-start.1 = (bf16[9,8,256]{2,1,0:T(8,128)(2,1)S(1)}, bf16[9,8,256]{2,1,0:T(8,128)(2,1)S(1)}, u32[]{:S(2)}, u32[]{:S(2)}) collective-permute-start(bf16[9,8,256]{2,1,0:T(8,128)(2,1)S(1)} %get-tuple-element.19.refs_0_), channel_id=1, source_target_pairs={{0,8},{4,12},{8,0},{12,4},{16,24},{20,28},{24,16},{28,20},{1,9},{5... | collective-permute-start | bytes 110600 | tf_op jit(solution)/shard_map/ppermute | solution.py:492
  19.6 0.0 collective-permute-start.2
  19.6 2.0 %collective-permute-start.3 = (bf16[64,8,256]{2,1,0:T(8,128)(2,1)S(1)}, bf16[64,8,256]{2,1,0:T(8,128)(2,1)S(1)}, u32[]{:S(2)}, u32[]{:S(2)}) collective-permute-start(bf16[64,8,256]{2,1,0:T(8,128)(2,1)S(1)} %get-tuple-element.21), channel_id=1, source_target_pairs={{0,4},{4,0},{8,12},{12,8},{16,20},{20,16},{24,28},{28,24},{1,5},{5... | collective-permute-start | bytes 786440 | tf_op jit(solution)/shard_map/ppermute | solution.py:492
  21.6 1.5 %collective-permute-start.4 = (bf16[64,8,256]{2,1,0:T(8,128)(2,1)S(1)}, bf16[64,8,256]{2,1,0:T(8,128)(2,1)S(1)}, u32[]{:S(2)}, u32[]{:S(2)}) collective-permute-start(bf16[64,8,256]{2,1,0:T(8,128)(2,1)S(1)} %get-tuple-element.22), channel_id=1, source_target_pairs={{0,8},{4,12},{8,0},{12,4},{16,24},{20,28},{24,16},{28,20},{1,9},{5... | collective-permute-start | bytes 786440 | tf_op jit(solution)/shard_map/ppermute | solution.py:492
  23.1 0.0 collective-permute-done.refs_1_
  23.1 1.5 %collective-permute-start.5 = (bf16[64,8,256]{2,1,0:T(8,128)(2,1)S(1)}, bf16[64,8,256]{2,1,0:T(8,128)(2,1)S(1)}, u32[]{:S(2)}, u32[]{:S(2)}) collective-permute-start(bf16[64,8,256]{2,1,0:T(8,128)(2,1)S(1)} %get-tuple-element.23), channel_id=1, source_target_pairs={{0,12},{4,8},{8,4},{12,0},{16,28},{20,24},{24,20},{28,16},{1,13},{... | collective-permute-start | bytes 786440 | tf_op jit(solution)/shard_map/ppermute | solution.py:492
  24.6 5.5 %collective-permute-done.1.refs_2_ = bf16[9,8,256]{2,1,0:T(8,128)(2,1)S(1)} collective-permute-done((bf16[9,8,256]{2,1,0:T(8,128)(2,1)S(1)}, bf16[9,8,256]{2,1,0:T(8,128)(2,1)S(1)}, u32[]{:S(2)}, u32[]{:S(2)}) %collective-permute-start.1) | collective-permute-done | bytes 36896 | tf_op jit(solution)/shard_map/ppermute | solution.py:492
  30.1 0.8 collective-permute-done.2.refs_3_
  30.9 0.2 shard_map.97.refs_4_
  31.1 0.1 collective-permute-start.6
  31.2 0.0 copy-done.7
  31.2 0.1 dynamic-slice_convert_fusion
  31.3 0.1 reshape.36
  31.4 0.1 copy.11
  31.5 0.1 min.20
  31.6 0.1 min.21
  31.7 1.5 %collective-permute-start.7 = (bf16[4,9,8,256]{3,2,1,0:T(8,128)(2,1)S(1)}, bf16[4,9,8,256]{3,2,1,0:T(8,128)(2,1)S(1)}, u32[]{:S(2)}, u32[]{:S(2)}) collective-permute-start(bf16[4,9,8,256]{3,2,1,0:T(8,128)(2,1)S(1)} %shard_map.97.refs_4_), channel_id=1, source_target_pairs={{0,2},{1,3},{2,0},{3,1},{4,6},{5,7},{6,4},{7,5},{8,10},{9,11},{10,... | collective-permute-start | bytes 442376 | tf_op jit(solution)/shard_map/ppermute | solution.py:492
  33.2 0.1 convert_reduce_fusion
  33.2 0.1 reshape.38
  33.3 0.1 min.23
  33.4 0.0 collective-permute-done.6.refs_5_
  33.4 0.4 collective-permute-start.8
  33.8 0.7 pad_maximum_fusion.invn_ref
  34.5 3.8 %collective-permute-done.7.refs_6_ = bf16[4,9,8,256]{3,2,1,0:T(8,128)(2,1)S(1)} collective-permute-done((bf16[4,9,8,256]{3,2,1,0:T(8,128)(2,1)S(1)}, bf16[4,9,8,256]{3,2,1,0:T(8,128)(2,1)S(1)}, u32[]{:S(2)}, u32[]{:S(2)}) %collective-permute-start.7) | collective-permute-done | bytes 147488 | tf_op jit(solution)/shard_map/ppermute | solution.py:492
  38.3 2.3 %collective-permute-done.8.refs_7_ = bf16[4,9,8,256]{3,2,1,0:T(8,128)(2,1)S(1)} collective-permute-done((bf16[4,9,8,256]{3,2,1,0:T(8,128)(2,1)S(1)}, bf16[4,9,8,256]{3,2,1,0:T(8,128)(2,1)S(1)}, u32[]{:S(2)}, u32[]{:S(2)}) %collective-permute-start.8) | collective-permute-done | bytes 147488 | tf_op jit(solution)/shard_map/ppermute | solution.py:492
  40.6 0.0 collective-permute-done.3.refs_1_
  40.7 0.0 collective-permute-done.4.refs_2_
  40.7 0.0 copy-start.11
  40.7 3.3 %collective-permute-done.5.refs_3_ = bf16[64,8,256]{2,1,0:T(8,128)(2,1)S(1)} collective-permute-done((bf16[64,8,256]{2,1,0:T(8,128)(2,1)S(1)}, bf16[64,8,256]{2,1,0:T(8,128)(2,1)S(1)}, u32[]{:S(2)}, u32[]{:S(2)}) %collective-permute-start.5) | collective-permute-done | bytes 262176 | tf_op jit(solution)/shard_map/ppermute | solution.py:492
  44.0 0.7 copy-done.12
  44.7 0.0 all-to-all-done.v_from
  44.8 11.7 %shard_map.98 = (s16[8,528,128]{2,1,0:T(8,128)(2,1)}, bf16[64,128,128]{2,1,0:T(8,128)(2,1)}) custom-call(s32[4]{0:T(128)} %copy-done.6, f32[32,128]{1,0:T(8,128)} %pad_maximum_fusion.invn_ref, bf16[8,64,1024]{2,1,0:T(8,128)(2,1)} %all-to-all-done.v_from, bf16[1024,256]{1,0:T(8,128)(2,1)} %constant.49.table_from, bf16[64,8,256]{2,1,0:T(8,128)(2,1)} %copy-done.2, ...), custom_call_target="tpu_custom_call" | custom-call | tf_op jit(solution)/shard_map/pallas_call | solution.py:599
  56.5 3.8 %all-to-all-start.1 = ((s16[8,528,128]{2,1,0:T(8,128)(2,1)}), s16[8,528,128]{2,1,0:T(8,128)(2,1)S(1)}, u32[]{:S(2)}, u32[]{:S(2)}) async-start(s16[8,528,128]{2,1,0:T(8,128)(2,1)} %get-tuple-element.33), calls=%async_computation.1 | async-start | bytes 2162688 | tf_op jit(solution)/shard_map/all_to_all | solution.py:627
  60.3 5.1 %shard_map.99 = (s16[528,128]{1,0:T(8,128)(2,1)}, s16[528,128]{1,0:T(8,128)(2,1)}, s16[528,128]{1,0:T(8,128)(2,1)}, s16[528,128]{1,0:T(8,128)(2,1)}) custom-call(s32[4]{0:T(128)} %copy-done.6, bf16[8,64,1024]{2,1,0:T(8,128)(2,1)} %all-to-all-done.v_from, bf16[64,128,128]{2,1,0:T(8,128)(2,1)} %get-tuple-element.24.z_from), custom_call_target="tpu_custom_call" | custom-call | tf_op jit(solution)/shard_map/pallas_call | solution.py:642
  65.4 1.6 %collective-permute-start.10 = (s16[528,128]{1,0:T(8,128)(2,1)}, s16[528,128]{1,0:T(8,128)(2,1)S(1)}, u32[]{:S(2)}, u32[]{:S(2)}) collective-permute-start(s16[528,128]{1,0:T(8,128)(2,1)} %get-tuple-element.27), channel_id=1, source_target_pairs={{0,2},{1,3},{2,0},{3,1},{4,6},{5,7},{6,4},{7,5},{8,10},{9,11},{10,... | collective-permute-start | bytes 405512 | tf_op jit(solution)/shard_map/ppermute | solution.py:492
  67.0 0.0 collective-permute-start.11
  67.0 0.6 collective-permute-start.9
  67.7 4.4 %collective-permute-done.10.refs_2_ = s16[528,128]{1,0:T(8,128)(2,1)S(1)} collective-permute-done((s16[528,128]{1,0:T(8,128)(2,1)}, s16[528,128]{1,0:T(8,128)(2,1)S(1)}, u32[]{:S(2)}, u32[]{:S(2)}) %collective-permute-start.10) | collective-permute-done | bytes 135200 | tf_op jit(solution)/shard_map/ppermute | solution.py:492
  72.1 1.1 %collective-permute-done.11.refs_3_ = s16[528,128]{1,0:T(8,128)(2,1)S(1)} collective-permute-done((s16[528,128]{1,0:T(8,128)(2,1)}, s16[528,128]{1,0:T(8,128)(2,1)S(1)}, u32[]{:S(2)}, u32[]{:S(2)}) %collective-permute-start.11) | collective-permute-done | bytes 135200 | tf_op jit(solution)/shard_map/ppermute | solution.py:492
  73.2 0.0 collective-permute-done.9.refs_1_
  73.2 0.9 %copy-done.3 = s16[528,128]{1,0:T(8,128)(2,1)S(1)} copy-done((s16[528,128]{1,0:T(8,128)(2,1)S(1)}, s16[528,128]{1,0:T(8,128)(2,1)}, u32[]{:S(2)}) %copy-start.3) | copy-done | bytes 135192
  74.1 0.1 shard_map.100
  74.2 2.0 %collective-permute-start.12 = (f32[8,2048]{1,0:T(8,128)S(1)}, f32[8,2048]{1,0:T(8,128)S(1)}, u32[]{:S(2)}, u32[]{:S(2)}) collective-permute-start(f32[8,2048]{1,0:T(8,128)S(1)} %get-tuple-element.30), channel_id=1, source_target_pairs={{0,4},{4,0},{8,12},{12,8},{16,20},{20,16},{24,28},{28,24},{1,5},{5... | collective-permute-start | bytes 196616 | tf_op jit(solution)/shard_map/ppermute | solution.py:492
  76.3 1.5 %collective-permute-start.13 = (f32[8,2048]{1,0:T(8,128)S(1)}, f32[8,2048]{1,0:T(8,128)S(1)}, u32[]{:S(2)}, u32[]{:S(2)}) collective-permute-start(f32[8,2048]{1,0:T(8,128)S(1)} %get-tuple-element.31), channel_id=1, source_target_pairs={{0,8},{4,12},{8,0},{12,4},{16,24},{20,28},{24,16},{28,20},{1,9},{5... | collective-permute-start | bytes 196616 | tf_op jit(solution)/shard_map/ppermute | solution.py:492
  77.7 0.1 collective-permute-start.14
  77.8 3.6 %collective-permute-done.12 = f32[8,2048]{1,0:T(8,128)S(1)} collective-permute-done((f32[8,2048]{1,0:T(8,128)S(1)}, f32[8,2048]{1,0:T(8,128)S(1)}, u32[]{:S(2)}, u32[]{:S(2)}) %collective-permute-start.12) | collective-permute-done | bytes 65568 | tf_op jit(solution)/shard_map/ppermute | solution.py:492
  81.4 0.0 collective-permute-done.13
  81.4 1.8 %collective-permute-done.14 = f32[8,2048]{1,0:T(8,128)S(1)} collective-permute-done((f32[8,2048]{1,0:T(8,128)S(1)}, f32[8,2048]{1,0:T(8,128)S(1)}, u32[]{:S(2)}, u32[]{:S(2)}) %collective-permute-start.14) | collective-permute-done | bytes 65568 | tf_op jit(solution)/shard_map/ppermute | solution.py:492
  83.2 0.7 add_select_fusion
  83.9 3.3 %all-to-all-done.1.got_ref = s16[8,528,128]{2,1,0:T(8,128)(2,1)S(1)} async-done(((s16[8,528,128]{2,1,0:T(8,128)(2,1)}), s16[8,528,128]{2,1,0:T(8,128)(2,1)S(1)}, u32[]{:S(2)}, u32[]{:S(2)}) %all-to-all-start.1) | async-done | bytes 1081376 | tf_op jit(solution)/shard_map/all_to_all | solution.py:627
  87.1 1.1 %shard_map.101 = f32[1024,256]{1,0:T(8,128)} custom-call(s32[1,256]{1,0:T(1,128)S(1)} %bitcast.8, s16[8,528,128]{2,1,0:T(8,128)(2,1)S(1)} %all-to-all-done.1.got_ref), custom_call_target="tpu_custom_call" | custom-call | tf_op jit(solution)/shard_map/pallas_call | solution.py:628
  (23 shorter events, 0.1 us)
Async XLA Ops:
  0.6 10.5 %copy-start.9 = (s32[256]{0:T(256)S(1)}, s32[256]{0:T(256)}, u32[]{:S(2)}) copy-start(s32[256]{0:T(256)} %param.12) | copy-start | bytes 3076
  0.6 10.5 %copy-start.8 = (s32[8]{0:T(128)S(1)}, s32[8]{0:T(128)}, u32[]{:S(2)}) copy-start(s32[8]{0:T(128)} %rcounts_ref.1) | copy-start | bytes 100
  0.7 10.5 %copy-start.5 = (s32[2,8,256]{2,1,0:T(8,128)S(1)}, s32[2,8,256]{2,1,0:T(8,128)}, u32[]{:S(2)}) copy-start(s32[2,8,256]{2,1,0:T(8,128)} %window_from.1) | copy-start | bytes 49156
  0.7 10.5 %copy-start.4 = (bf16[8,2048]{1,0:T(8,128)(2,1)S(1)}, bf16[8,2048]{1,0:T(8,128)(2,1)}, u32[]{:S(2)}) copy-start(bf16[8,2048]{1,0:T(8,128)(2,1)} %rspectra_from.1) | copy-start | bytes 98308
  3.6 7.6 %copy-start = (bf16[8,256,512]{2,1,0:T(8,128)(2,1)S(1)}, bf16[8,256,512]{2,1,0:T(8,128)(2,1)}, u32[]{:S(2)}) copy-start(bf16[8,256,512]{2,1,0:T(8,128)(2,1)} %observed_from) | copy-start | bytes 6291460
  3.7 27.5 %copy-start.7 = (s32[256]{0:T(256)S(1)}, s32[256]{0:T(256)}, u32[]{:S(2)}) copy-start(s32[256]{0:T(256)} %param.11) | copy-start | bytes 3076
  3.7 41.1 %all-to-all-start = ((bf16[8,64,1024]{2,1,0:T(8,128)(2,1)}), bf16[8,64,1024]{2,1,0:T(8,128)(2,1)}, u32[]{:S(2)}, u32[]{:S(2)}) async-start(bf16[8,64,1024]{2,1,0:T(8,128)(2,1)} %shard_map.95), calls=%async_computation | async-start | bytes 2097152 | tf_op jit(solution)/shard_map/all_to_all | solution.py:545
  11.2 33.6 %copy-start.6 = (s32[4]{0:T(128)}, s32[4]{0:T(128)S(1)}, u32[]{:S(2)}) copy-start(s32[4]{0:T(128)S(1)} %pad_add_fusion.c_ref) | copy-start | bytes 52
  15.4 0.7 copy-start.2
  16.1 7.0 %collective-permute-start = (bf16[9,8,256]{2,1,0:T(8,128)(2,1)S(1)}, bf16[9,8,256]{2,1,0:T(8,128)(2,1)S(1)}, u32[]{:S(2)}, u32[]{:S(2)}) collective-permute-start(bf16[9,8,256]{2,1,0:T(8,128)(2,1)S(1)} %get-tuple-element.19.refs_0_), channel_id=1, source_target_pairs={{0,4},{4,0},{8,12},{12,8},{16,20},{20,16},{24,28},{28,24},{1,5},{5... | collective-permute-start | bytes 110600 | tf_op jit(solution)/shard_map/ppermute | solution.py:492
  18.2 12.0 %collective-permute-start.1 = (bf16[9,8,256]{2,1,0:T(8,128)(2,1)S(1)}, bf16[9,8,256]{2,1,0:T(8,128)(2,1)S(1)}, u32[]{:S(2)}, u32[]{:S(2)}) collective-permute-start(bf16[9,8,256]{2,1,0:T(8,128)(2,1)S(1)} %get-tuple-element.19.refs_0_), channel_id=1, source_target_pairs={{0,8},{4,12},{8,0},{12,4},{16,24},{20,28},{24,16},{28,20},{1,9},{5... | collective-permute-start | bytes 110600 | tf_op jit(solution)/shard_map/ppermute | solution.py:492
  19.6 11.3 %collective-permute-start.2 = (bf16[9,8,256]{2,1,0:T(8,128)(2,1)S(1)}, bf16[9,8,256]{2,1,0:T(8,128)(2,1)S(1)}, u32[]{:S(2)}, u32[]{:S(2)}) collective-permute-start(bf16[9,8,256]{2,1,0:T(8,128)(2,1)S(1)} %get-tuple-element.19.refs_0_), channel_id=1, source_target_pairs={{0,12},{4,8},{8,4},{12,0},{16,28},{20,24},{24,20},{28,16},{1,13},{... | collective-permute-start | bytes 110600 | tf_op jit(solution)/shard_map/ppermute | solution.py:492
  19.6 21.0 %collective-permute-start.3 = (bf16[64,8,256]{2,1,0:T(8,128)(2,1)S(1)}, bf16[64,8,256]{2,1,0:T(8,128)(2,1)S(1)}, u32[]{:S(2)}, u32[]{:S(2)}) collective-permute-start(bf16[64,8,256]{2,1,0:T(8,128)(2,1)S(1)} %get-tuple-element.21), channel_id=1, source_target_pairs={{0,4},{4,0},{8,12},{12,8},{16,20},{20,16},{24,28},{28,24},{1,5},{5... | collective-permute-start | bytes 786440 | tf_op jit(solution)/shard_map/ppermute | solution.py:492
  21.6 19.0 %collective-permute-start.4 = (bf16[64,8,256]{2,1,0:T(8,128)(2,1)S(1)}, bf16[64,8,256]{2,1,0:T(8,128)(2,1)S(1)}, u32[]{:S(2)}, u32[]{:S(2)}) collective-permute-start(bf16[64,8,256]{2,1,0:T(8,128)(2,1)S(1)} %get-tuple-element.22), channel_id=1, source_target_pairs={{0,8},{4,12},{8,0},{12,4},{16,24},{20,28},{24,16},{28,20},{1,9},{5... | collective-permute-start | bytes 786440 | tf_op jit(solution)/shard_map/ppermute | solution.py:492
  23.1 20.9 %collective-permute-start.5 = (bf16[64,8,256]{2,1,0:T(8,128)(2,1)S(1)}, bf16[64,8,256]{2,1,0:T(8,128)(2,1)S(1)}, u32[]{:S(2)}, u32[]{:S(2)}) collective-permute-start(bf16[64,8,256]{2,1,0:T(8,128)(2,1)S(1)} %get-tuple-element.23), channel_id=1, source_target_pairs={{0,12},{4,8},{8,4},{12,0},{16,28},{20,24},{24,20},{28,16},{1,13},{... | collective-permute-start | bytes 786440 | tf_op jit(solution)/shard_map/ppermute | solution.py:492
  31.1 13.6 %copy-start.1 = (bf16[4,9,8,256]{3,2,1,0:T(8,128)(2,1)}, bf16[4,9,8,256]{3,2,1,0:T(8,128)(2,1)S(1)}, u32[]{:S(2)}) copy-start(bf16[4,9,8,256]{3,2,1,0:T(8,128)(2,1)S(1)} %shard_map.97.refs_4_) | copy-start | bytes 442372
  31.1 2.3 %collective-permute-start.6 = (bf16[4,9,8,256]{3,2,1,0:T(8,128)(2,1)S(1)}, bf16[4,9,8,256]{3,2,1,0:T(8,128)(2,1)S(1)}, u32[]{:S(2)}, u32[]{:S(2)}) collective-permute-start(bf16[4,9,8,256]{3,2,1,0:T(8,128)(2,1)S(1)} %shard_map.97.refs_4_), channel_id=1, source_target_pairs={{0,1},{1,0},{2,3},{3,2},{4,5},{5,4},{6,7},{7,6},{8,9},{9,8},{10,11... | collective-permute-start | bytes 442376 | tf_op jit(solution)/shard_map/ppermute | solution.py:492
  31.7 6.7 %collective-permute-start.7 = (bf16[4,9,8,256]{3,2,1,0:T(8,128)(2,1)S(1)}, bf16[4,9,8,256]{3,2,1,0:T(8,128)(2,1)S(1)}, u32[]{:S(2)}, u32[]{:S(2)}) collective-permute-start(bf16[4,9,8,256]{3,2,1,0:T(8,128)(2,1)S(1)} %shard_map.97.refs_4_), channel_id=1, source_target_pairs={{0,2},{1,3},{2,0},{3,1},{4,6},{5,7},{6,4},{7,5},{8,10},{9,11},{10,... | collective-permute-start | bytes 442376 | tf_op jit(solution)/shard_map/ppermute | solution.py:492
  33.4 11.3 %copy-start.13 = (bf16[4,9,8,256]{3,2,1,0:T(8,128)(2,1)}, bf16[4,9,8,256]{3,2,1,0:T(8,128)(2,1)S(1)}, u32[]{:S(2)}) copy-start(bf16[4,9,8,256]{3,2,1,0:T(8,128)(2,1)S(1)} %collective-permute-done.6.refs_5_) | copy-start | bytes 442372
  33.4 7.2 %collective-permute-start.8 = (bf16[4,9,8,256]{3,2,1,0:T(8,128)(2,1)S(1)}, bf16[4,9,8,256]{3,2,1,0:T(8,128)(2,1)S(1)}, u32[]{:S(2)}, u32[]{:S(2)}) collective-permute-start(bf16[4,9,8,256]{3,2,1,0:T(8,128)(2,1)S(1)} %shard_map.97.refs_4_), channel_id=1, source_target_pairs={{0,3},{1,2},{2,1},{3,0},{4,7},{5,6},{6,5},{7,4},{8,11},{9,10},{10,... | collective-permute-start | bytes 442376 | tf_op jit(solution)/shard_map/ppermute | solution.py:492
  38.3 6.5 %copy-start.14 = (bf16[4,9,8,256]{3,2,1,0:T(8,128)(2,1)}, bf16[4,9,8,256]{3,2,1,0:T(8,128)(2,1)S(1)}, u32[]{:S(2)}) copy-start(bf16[4,9,8,256]{3,2,1,0:T(8,128)(2,1)S(1)} %collective-permute-done.7.refs_6_) | copy-start | bytes 442372
  40.6 4.1 %copy-start.15 = (bf16[4,9,8,256]{3,2,1,0:T(8,128)(2,1)}, bf16[4,9,8,256]{3,2,1,0:T(8,128)(2,1)S(1)}, u32[]{:S(2)}) copy-start(bf16[4,9,8,256]{3,2,1,0:T(8,128)(2,1)S(1)} %collective-permute-done.8.refs_7_) | copy-start | bytes 442372
  40.7 4.1 %copy-start.10 = (bf16[64,8,256]{2,1,0:T(8,128)(2,1)}, bf16[64,8,256]{2,1,0:T(8,128)(2,1)S(1)}, u32[]{:S(2)}) copy-start(bf16[64,8,256]{2,1,0:T(8,128)(2,1)S(1)} %collective-permute-done.3.refs_1_) | copy-start | bytes 786436
  40.7 4.1 %copy-start.11 = (bf16[64,8,256]{2,1,0:T(8,128)(2,1)}, bf16[64,8,256]{2,1,0:T(8,128)(2,1)S(1)}, u32[]{:S(2)}) copy-start(bf16[64,8,256]{2,1,0:T(8,128)(2,1)S(1)} %collective-permute-done.4.refs_2_) | copy-start | bytes 786436
  44.0 0.7 copy-start.12
  56.5 30.7 %all-to-all-start.1 = ((s16[8,528,128]{2,1,0:T(8,128)(2,1)}), s16[8,528,128]{2,1,0:T(8,128)(2,1)S(1)}, u32[]{:S(2)}, u32[]{:S(2)}) async-start(s16[8,528,128]{2,1,0:T(8,128)(2,1)} %get-tuple-element.33), calls=%async_computation.1 | async-start | bytes 2162688 | tf_op jit(solution)/shard_map/all_to_all | solution.py:627
  65.4 6.7 %collective-permute-start.10 = (s16[528,128]{1,0:T(8,128)(2,1)}, s16[528,128]{1,0:T(8,128)(2,1)S(1)}, u32[]{:S(2)}, u32[]{:S(2)}) collective-permute-start(s16[528,128]{1,0:T(8,128)(2,1)} %get-tuple-element.27), channel_id=1, source_target_pairs={{0,2},{1,3},{2,0},{3,1},{4,6},{5,7},{6,4},{7,5},{8,10},{9,11},{10,... | collective-permute-start | bytes 405512 | tf_op jit(solution)/shard_map/ppermute | solution.py:492
  67.0 6.1 %collective-permute-start.11 = (s16[528,128]{1,0:T(8,128)(2,1)}, s16[528,128]{1,0:T(8,128)(2,1)S(1)}, u32[]{:S(2)}, u32[]{:S(2)}) collective-permute-start(s16[528,128]{1,0:T(8,128)(2,1)} %get-tuple-element.28), channel_id=1, source_target_pairs={{0,3},{1,2},{2,1},{3,0},{4,7},{5,6},{6,5},{7,4},{8,11},{9,10},{10,... | collective-permute-start | bytes 405512 | tf_op jit(solution)/shard_map/ppermute | solution.py:492
  67.0 6.1 %collective-permute-start.9 = (s16[528,128]{1,0:T(8,128)(2,1)}, s16[528,128]{1,0:T(8,128)(2,1)S(1)}, u32[]{:S(2)}, u32[]{:S(2)}) collective-permute-start(s16[528,128]{1,0:T(8,128)(2,1)} %get-tuple-element.26), channel_id=1, source_target_pairs={{0,1},{1,0},{2,3},{3,2},{4,5},{5,4},{6,7},{7,6},{8,9},{9,8},{10,11... | collective-permute-start | bytes 405512 | tf_op jit(solution)/shard_map/ppermute | solution.py:492
  73.2 0.9 %copy-start.3 = (s16[528,128]{1,0:T(8,128)(2,1)S(1)}, s16[528,128]{1,0:T(8,128)(2,1)}, u32[]{:S(2)}) copy-start(s16[528,128]{1,0:T(8,128)(2,1)} %get-tuple-element.25.refs_0_) | copy-start | bytes 405508
  74.2 7.2 %collective-permute-start.12 = (f32[8,2048]{1,0:T(8,128)S(1)}, f32[8,2048]{1,0:T(8,128)S(1)}, u32[]{:S(2)}, u32[]{:S(2)}) collective-permute-start(f32[8,2048]{1,0:T(8,128)S(1)} %get-tuple-element.30), channel_id=1, source_target_pairs={{0,4},{4,0},{8,12},{12,8},{16,20},{20,16},{24,28},{28,24},{1,5},{5... | collective-permute-start | bytes 196616 | tf_op jit(solution)/shard_map/ppermute | solution.py:492
  76.3 5.1 %collective-permute-start.13 = (f32[8,2048]{1,0:T(8,128)S(1)}, f32[8,2048]{1,0:T(8,128)S(1)}, u32[]{:S(2)}, u32[]{:S(2)}) collective-permute-start(f32[8,2048]{1,0:T(8,128)S(1)} %get-tuple-element.31), channel_id=1, source_target_pairs={{0,8},{4,12},{8,0},{12,4},{16,24},{20,28},{24,16},{28,20},{1,9},{5... | collective-permute-start | bytes 196616 | tf_op jit(solution)/shard_map/ppermute | solution.py:492
  77.7 5.4 %collective-permute-start.14 = (f32[8,2048]{1,0:T(8,128)S(1)}, f32[8,2048]{1,0:T(8,128)S(1)}, u32[]{:S(2)}, u32[]{:S(2)}) collective-permute-start(f32[8,2048]{1,0:T(8,128)S(1)} %get-tuple-element.32), channel_id=1, source_target_pairs={{0,12},{4,8},{8,4},{12,0},{16,28},{20,24},{24,20},{28,16},{1,13},{... | collective-permute-start | bytes 196616 | tf_op jit(solution)/shard_map/ppermute | solution.py:492

commit v10 on v9

--- a/solution.py
+++ b/solution.py
@@ -557,7 +557,7 @@
             pltpu.VMEM(receiver_spectra.shape, bf16),
             pltpu.VMEM(lag_window.shape, jnp.int32),
             pltpu.VMEM((1, col_total), jnp.int32),
-            pltpu.VMEM((half // LANES * col_total * row_total, LANES), jnp.float32),
+            pltpu.VMEM(((half // LANES * col_total + 1) * row_total, LANES), jnp.float32),
             pltpu.VMEM((members,) + shape, bf16),
             pltpu.VMEM((extra, row_total, half), bf16),
             pltpu.SemaphoreType.DMA((row_total + 3,)),
@@ -595,7 +595,7 @@
 
     table = lag_tables(k_total // (2 * S), lag_total)
     w_rows = k_own // LANES * cols + CODES
-    lines = jp_total * (k_total // (2 * S) + PAD)
+    lines = (jp_total + 1) * (k_total // (2 * S) + PAD)
     w_part, z_part = pl.pallas_call(
         functools.partial(pair_kernel, members, ref_total),
         out_shape=[

time: 88.6 us -> 88.6 us (level)
  no operation moved by 1% of the time
where the time goes in v10:
time: 88.6 us; the launch traced here: 88.3 us
  waiting for transfers between devices  30 us (34%)
  starting transfers between devices  27.4 us (31%)
  Pallas kernels  25.5 us (29%)
  local copies, waits for them, and re-layouts  2.92 us (3%)
  other arithmetic  1.64 us (2%)
    ppermute x15, waiting for transfers between devices, swap(): return lax.ppermute(x, axis, [(r, r ^ k) for r in range(total)])  26.7 us
    ppermute x15, starting transfers between devices, swap(): return lax.ppermute(x, axis, [(r, r ^ k) for r in range(total)])  16.2 us
    pallas_call x1, Pallas kernels, shards(): pl.pallas_call(functools.partial(pair_kernel, members, ref_total), out_sh...  11.7 us
    all_to_all x1, starting transfers between devices, shards(): v_all = lax.all_to_all(sent, 'rcv', split_axis=0, concat_axis=0, tiled=True)  7.42 us
    pallas_call x1, Pallas kernels, shards(): pl.pallas_call(receiver_sum_kernel, out_shape=[jax.ShapeDtypeStruct((r_ro...  5.14 us
    pallas_call x1, Pallas kernels, shards(): pl.pallas_call(fold_kernel, out_shape=[jax.ShapeDtypeStruct((extra, row_t...  4.19 us
    all_to_all x1, starting transfers between devices, shards(): got = lax.all_to_all(w_part, 'rcv', split_axis=0, concat_axis=0, tiled=True)  3.8 us
    all_to_all x1, waiting for transfers between devices, shards(): got = lax.all_to_all(w_part, 'rcv', split_axis=0, concat_axis=0, tiled=True)  3.28 us
  transfers between devices with their start and end apart: 17, of which 10 were waited for; matrix products, arithmetic and copies ran while one was open for 2% of the time, Pallas kernels for 11%

profile of v10, /device:TPU:0, one launch (start us, length us, event | category | flops | bytes accessed | tf_op | source)
XLA Modules:
  0.0 88.3 jit_solution(567629383167458543)
XLA Ops:
  0.6 0.0 copy-start.9
  0.6 0.0 copy-start.8
  0.7 0.0 copy-start.5
  0.7 0.0 copy-start.4
  0.7 3.0 %shard_map.95 = bf16[8,64,1024]{2,1,0:T(8,128)(2,1)} custom-call(bf16[1024,256]{1,0:T(8,128)(2,1)} %spectra_from.1, s32[1,256]{1,0:T(1,128)} %bitcast.7), custom_call_target="tpu_custom_call" | custom-call | tf_op jit(solution)/shard_map/pallas_call | solution.py:531
  3.6 0.0 copy-start
  3.7 0.0 copy-start.7
  3.7 7.4 %all-to-all-start = ((bf16[8,64,1024]{2,1,0:T(8,128)(2,1)}), bf16[8,64,1024]{2,1,0:T(8,128)(2,1)}, u32[]{:S(2)}, u32[]{:S(2)}) async-start(bf16[8,64,1024]{2,1,0:T(8,128)(2,1)} %shard_map.95), calls=%async_computation | async-start | bytes 2097152 | tf_op jit(solution)/shard_map/all_to_all | solution.py:545
  11.1 0.1 pad_add_fusion.c_ref
  11.2 0.0 copy-done.9
  11.2 0.0 copy-done.8
  11.2 4.2 %shard_map.96 = (bf16[9,8,256]{2,1,0:T(8,128)(2,1)S(1)}, bf16[64,8,256]{2,1,0:T(8,128)(2,1)S(1)}, bf16[64,8,256]{2,1,0:T(8,128)(2,1)S(1)}, bf16[64,8,256]{2,1,0:T(8,128)(2,1)S(1)}, bf16[64,8,256]{2,1,0:T(8,128)(2,1)S(1)}) custom-call(s32[4]{0:T(128)S(1)} %pad_add_fusion.c_ref, s32[8]{0:T(128)S(1)} %copy-done.8, bf16[8,256,512]{2,1,0:T(8,128)(2,1)S(1)} %copy-done, ...), custom_call_target="tpu_custom_call" | custom-call | tf_op jit(solution)/shard_map/pallas_call | solution.py:549
  15.4 0.7 copy-done.2
  16.1 2.0 %collective-permute-start = (bf16[9,8,256]{2,1,0:T(8,128)(2,1)S(1)}, bf16[9,8,256]{2,1,0:T(8,128)(2,1)S(1)}, u32[]{:S(2)}, u32[]{:S(2)}) collective-permute-start(bf16[9,8,256]{2,1,0:T(8,128)(2,1)S(1)} %get-tuple-element.19.refs_0_), channel_id=1, source_target_pairs={{0,4},{4,0},{8,12},{12,8},{16,20},{20,16},{24,28},{28,24},{1,5},{5... | collective-permute-start | bytes 110600 | tf_op jit(solution)/shard_map/ppermute | solution.py:492
  18.2 1.5 %collective-permute-start.1 = (bf16[9,8,256]{2,1,0:T(8,128)(2,1)S(1)}, bf16[9,8,256]{2,1,0:T(8,128)(2,1)S(1)}, u32[]{:S(2)}, u32[]{:S(2)}) collective-permute-start(bf16[9,8,256]{2,1,0:T(8,128)(2,1)S(1)} %get-tuple-element.19.refs_0_), channel_id=1, source_target_pairs={{0,8},{4,12},{8,0},{12,4},{16,24},{20,28},{24,16},{28,20},{1,9},{5... | collective-permute-start | bytes 110600 | tf_op jit(solution)/shard_map/ppermute | solution.py:492
  19.6 0.0 collective-permute-start.2
  19.6 2.0 %collective-permute-start.3 = (bf16[64,8,256]{2,1,0:T(8,128)(2,1)S(1)}, bf16[64,8,256]{2,1,0:T(8,128)(2,1)S(1)}, u32[]{:S(2)}, u32[]{:S(2)}) collective-permute-start(bf16[64,8,256]{2,1,0:T(8,128)(2,1)S(1)} %get-tuple-element.21), channel_id=1, source_target_pairs={{0,4},{4,0},{8,12},{12,8},{16,20},{20,16},{24,28},{28,24},{1,5},{5... | collective-permute-start | bytes 786440 | tf_op jit(solution)/shard_map/ppermute | solution.py:492
  21.6 1.5 %collective-permute-start.4 = (bf16[64,8,256]{2,1,0:T(8,128)(2,1)S(1)}, bf16[64,8,256]{2,1,0:T(8,128)(2,1)S(1)}, u32[]{:S(2)}, u32[]{:S(2)}) collective-permute-start(bf16[64,8,256]{2,1,0:T(8,128)(2,1)S(1)} %get-tuple-element.22), channel_id=1, source_target_pairs={{0,8},{4,12},{8,0},{12,4},{16,24},{20,28},{24,16},{28,20},{1,9},{5... | collective-permute-start | bytes 786440 | tf_op jit(solution)/shard_map/ppermute | solution.py:492
  23.1 0.0 collective-permute-done.refs_1_
  23.1 1.5 %collective-permute-start.5 = (bf16[64,8,256]{2,1,0:T(8,128)(2,1)S(1)}, bf16[64,8,256]{2,1,0:T(8,128)(2,1)S(1)}, u32[]{:S(2)}, u32[]{:S(2)}) collective-permute-start(bf16[64,8,256]{2,1,0:T(8,128)(2,1)S(1)} %get-tuple-element.23), channel_id=1, source_target_pairs={{0,12},{4,8},{8,4},{12,0},{16,28},{20,24},{24,20},{28,16},{1,13},{... | collective-permute-start | bytes 786440 | tf_op jit(solution)/shard_map/ppermute | solution.py:492
  24.6 5.5 %collective-permute-done.1.refs_2_ = bf16[9,8,256]{2,1,0:T(8,128)(2,1)S(1)} collective-permute-done((bf16[9,8,256]{2,1,0:T(8,128)(2,1)S(1)}, bf16[9,8,256]{2,1,0:T(8,128)(2,1)S(1)}, u32[]{:S(2)}, u32[]{:S(2)}) %collective-permute-start.1) | collective-permute-done | bytes 36896 | tf_op jit(solution)/shard_map/ppermute | solution.py:492
  30.1 0.8 collective-permute-done.2.refs_3_
  30.9 0.2 shard_map.97.refs_4_
  31.1 0.1 collective-permute-start.6
  31.2 0.1 dynamic-slice_convert_fusion
  31.3 0.1 reshape.36
  31.4 0.1 copy.11
  31.5 0.1 min.20
  31.6 0.1 min.21
  31.7 1.5 %collective-permute-start.7 = (bf16[4,9,8,256]{3,2,1,0:T(8,128)(2,1)S(1)}, bf16[4,9,8,256]{3,2,1,0:T(8,128)(2,1)S(1)}, u32[]{:S(2)}, u32[]{:S(2)}) collective-permute-start(bf16[4,9,8,256]{3,2,1,0:T(8,128)(2,1)S(1)} %shard_map.97.refs_4_), channel_id=1, source_target_pairs={{0,2},{1,3},{2,0},{3,1},{4,6},{5,7},{6,4},{7,5},{8,10},{9,11},{10,... | collective-permute-start | bytes 442376 | tf_op jit(solution)/shard_map/ppermute | solution.py:492
  33.2 0.1 convert_reduce_fusion
  33.2 0.1 reshape.38
  33.3 0.1 min.23
  33.4 0.0 collective-permute-done.6.refs_5_
  33.4 0.4 collective-permute-start.8
  33.8 0.7 pad_maximum_fusion.invn_ref
  34.5 3.8 %collective-permute-done.7.refs_6_ = bf16[4,9,8,256]{3,2,1,0:T(8,128)(2,1)S(1)} collective-permute-done((bf16[4,9,8,256]{3,2,1,0:T(8,128)(2,1)S(1)}, bf16[4,9,8,256]{3,2,1,0:T(8,128)(2,1)S(1)}, u32[]{:S(2)}, u32[]{:S(2)}) %collective-permute-start.7) | collective-permute-done | bytes 147488 | tf_op jit(solution)/shard_map/ppermute | solution.py:492
  38.3 2.3 %collective-permute-done.8.refs_7_ = bf16[4,9,8,256]{3,2,1,0:T(8,128)(2,1)S(1)} collective-permute-done((bf16[4,9,8,256]{3,2,1,0:T(8,128)(2,1)S(1)}, bf16[4,9,8,256]{3,2,1,0:T(8,128)(2,1)S(1)}, u32[]{:S(2)}, u32[]{:S(2)}) %collective-permute-start.8) | collective-permute-done | bytes 147488 | tf_op jit(solution)/shard_map/ppermute | solution.py:492
  40.6 0.0 collective-permute-done.3.refs_1_
  40.7 0.0 collective-permute-done.4.refs_2_
  40.7 3.3 %collective-permute-done.5.refs_3_ = bf16[64,8,256]{2,1,0:T(8,128)(2,1)S(1)} collective-permute-done((bf16[64,8,256]{2,1,0:T(8,128)(2,1)S(1)}, bf16[64,8,256]{2,1,0:T(8,128)(2,1)S(1)}, u32[]{:S(2)}, u32[]{:S(2)}) %collective-permute-start.5) | collective-permute-done | bytes 262176 | tf_op jit(solution)/shard_map/ppermute | solution.py:492
  44.0 0.7 copy-done.12
  44.7 0.0 all-to-all-done.v_from
  44.7 0.0 copy-done.6
  44.8 11.7 %shard_map.98 = (s16[8,528,128]{2,1,0:T(8,128)(2,1)}, bf16[64,128,128]{2,1,0:T(8,128)(2,1)}) custom-call(s32[4]{0:T(128)} %copy-done.6, f32[32,128]{1,0:T(8,128)} %pad_maximum_fusion.invn_ref, bf16[8,64,1024]{2,1,0:T(8,128)(2,1)} %all-to-all-done.v_from, bf16[1024,256]{1,0:T(8,128)(2,1)} %constant.49.table_from, bf16[64,8,256]{2,1,0:T(8,128)(2,1)} %copy-done.2, ...), custom_call_target="tpu_custom_call" | custom-call | tf_op jit(solution)/shard_map/pallas_call | solution.py:599
  56.5 3.8 %all-to-all-start.1 = ((s16[8,528,128]{2,1,0:T(8,128)(2,1)}), s16[8,528,128]{2,1,0:T(8,128)(2,1)S(1)}, u32[]{:S(2)}, u32[]{:S(2)}) async-start(s16[8,528,128]{2,1,0:T(8,128)(2,1)} %get-tuple-element.33), calls=%async_computation.1 | async-start | bytes 2162688 | tf_op jit(solution)/shard_map/all_to_all | solution.py:627
  60.3 5.1 %shard_map.99 = (s16[528,128]{1,0:T(8,128)(2,1)}, s16[528,128]{1,0:T(8,128)(2,1)}, s16[528,128]{1,0:T(8,128)(2,1)}, s16[528,128]{1,0:T(8,128)(2,1)}) custom-call(s32[4]{0:T(128)} %copy-done.6, bf16[8,64,1024]{2,1,0:T(8,128)(2,1)} %all-to-all-done.v_from, bf16[64,128,128]{2,1,0:T(8,128)(2,1)} %get-tuple-element.24.z_from), custom_call_target="tpu_custom_call" | custom-call | tf_op jit(solution)/shard_map/pallas_call | solution.py:642
  65.4 1.6 %collective-permute-start.10 = (s16[528,128]{1,0:T(8,128)(2,1)}, s16[528,128]{1,0:T(8,128)(2,1)S(1)}, u32[]{:S(2)}, u32[]{:S(2)}) collective-permute-start(s16[528,128]{1,0:T(8,128)(2,1)} %get-tuple-element.27), channel_id=1, source_target_pairs={{0,2},{1,3},{2,0},{3,1},{4,6},{5,7},{6,4},{7,5},{8,10},{9,11},{10,... | collective-permute-start | bytes 405512 | tf_op jit(solution)/shard_map/ppermute | solution.py:492
  67.0 0.0 collective-permute-start.11
  67.0 0.6 collective-permute-start.9
  67.6 4.5 %collective-permute-done.10.refs_2_ = s16[528,128]{1,0:T(8,128)(2,1)S(1)} collective-permute-done((s16[528,128]{1,0:T(8,128)(2,1)}, s16[528,128]{1,0:T(8,128)(2,1)S(1)}, u32[]{:S(2)}, u32[]{:S(2)}) %collective-permute-start.10) | collective-permute-done | bytes 135200 | tf_op jit(solution)/shard_map/ppermute | solution.py:492
  72.1 1.1 %collective-permute-done.11.refs_3_ = s16[528,128]{1,0:T(8,128)(2,1)S(1)} collective-permute-done((s16[528,128]{1,0:T(8,128)(2,1)}, s16[528,128]{1,0:T(8,128)(2,1)S(1)}, u32[]{:S(2)}, u32[]{:S(2)}) %collective-permute-start.11) | collective-permute-done | bytes 135200 | tf_op jit(solution)/shard_map/ppermute | solution.py:492
  73.2 0.0 collective-permute-done.9.refs_1_
  73.2 0.9 %copy-done.3 = s16[528,128]{1,0:T(8,128)(2,1)S(1)} copy-done((s16[528,128]{1,0:T(8,128)(2,1)S(1)}, s16[528,128]{1,0:T(8,128)(2,1)}, u32[]{:S(2)}) %copy-start.3) | copy-done | bytes 135192
  74.1 0.1 shard_map.100
  74.2 2.0 %collective-permute-start.12 = (f32[8,2048]{1,0:T(8,128)S(1)}, f32[8,2048]{1,0:T(8,128)S(1)}, u32[]{:S(2)}, u32[]{:S(2)}) collective-permute-start(f32[8,2048]{1,0:T(8,128)S(1)} %get-tuple-element.30), channel_id=1, source_target_pairs={{0,4},{4,0},{8,12},{12,8},{16,20},{20,16},{24,28},{28,24},{1,5},{5... | collective-permute-start | bytes 196616 | tf_op jit(solution)/shard_map/ppermute | solution.py:492
  76.2 1.5 %collective-permute-start.13 = (f32[8,2048]{1,0:T(8,128)S(1)}, f32[8,2048]{1,0:T(8,128)S(1)}, u32[]{:S(2)}, u32[]{:S(2)}) collective-permute-start(f32[8,2048]{1,0:T(8,128)S(1)} %get-tuple-element.31), channel_id=1, source_target_pairs={{0,8},{4,12},{8,0},{12,4},{16,24},{20,28},{24,16},{28,20},{1,9},{5... | collective-permute-start | bytes 196616 | tf_op jit(solution)/shard_map/ppermute | solution.py:492
  77.7 0.1 collective-permute-start.14
  77.8 3.6 %collective-permute-done.12 = f32[8,2048]{1,0:T(8,128)S(1)} collective-permute-done((f32[8,2048]{1,0:T(8,128)S(1)}, f32[8,2048]{1,0:T(8,128)S(1)}, u32[]{:S(2)}, u32[]{:S(2)}) %collective-permute-start.12) | collective-permute-done | bytes 65568 | tf_op jit(solution)/shard_map/ppermute | solution.py:492
  81.4 0.0 collective-permute-done.13
  81.4 1.8 %collective-permute-done.14 = f32[8,2048]{1,0:T(8,128)S(1)} collective-permute-done((f32[8,2048]{1,0:T(8,128)S(1)}, f32[8,2048]{1,0:T(8,128)S(1)}, u32[]{:S(2)}, u32[]{:S(2)}) %collective-permute-start.14) | collective-permute-done | bytes 65568 | tf_op jit(solution)/shard_map/ppermute | solution.py:492
  83.2 0.7 add_select_fusion
  83.9 3.3 %all-to-all-done.1.got_ref = s16[8,528,128]{2,1,0:T(8,128)(2,1)S(1)} async-done(((s16[8,528,128]{2,1,0:T(8,128)(2,1)}), s16[8,528,128]{2,1,0:T(8,128)(2,1)S(1)}, u32[]{:S(2)}, u32[]{:S(2)}) %all-to-all-start.1) | async-done | bytes 1081376 | tf_op jit(solution)/shard_map/all_to_all | solution.py:627
  87.1 1.1 %shard_map.101 = f32[1024,256]{1,0:T(8,128)} custom-call(s32[1,256]{1,0:T(1,128)S(1)} %bitcast.8, s16[8,528,128]{2,1,0:T(8,128)(2,1)S(1)} %all-to-all-done.1.got_ref), custom_call_target="tpu_custom_call" | custom-call | tf_op jit(solution)/shard_map/pallas_call | solution.py:628
  (23 shorter events, 0.1 us)
Async XLA Ops:
  0.6 10.5 %copy-start.9 = (s32[256]{0:T(256)S(1)}, s32[256]{0:T(256)}, u32[]{:S(2)}) copy-start(s32[256]{0:T(256)} %param.12) | copy-start | bytes 3076
  0.6 10.5 %copy-start.8 = (s32[8]{0:T(128)S(1)}, s32[8]{0:T(128)}, u32[]{:S(2)}) copy-start(s32[8]{0:T(128)} %rcounts_ref.1) | copy-start | bytes 100
  0.7 10.5 %copy-start.5 = (s32[2,8,256]{2,1,0:T(8,128)S(1)}, s32[2,8,256]{2,1,0:T(8,128)}, u32[]{:S(2)}) copy-start(s32[2,8,256]{2,1,0:T(8,128)} %window_from.1) | copy-start | bytes 49156
  0.7 10.5 %copy-start.4 = (bf16[8,2048]{1,0:T(8,128)(2,1)S(1)}, bf16[8,2048]{1,0:T(8,128)(2,1)}, u32[]{:S(2)}) copy-start(bf16[8,2048]{1,0:T(8,128)(2,1)} %rspectra_from.1) | copy-start | bytes 98308
  3.6 7.6 %copy-start = (bf16[8,256,512]{2,1,0:T(8,128)(2,1)S(1)}, bf16[8,256,512]{2,1,0:T(8,128)(2,1)}, u32[]{:S(2)}) copy-start(bf16[8,256,512]{2,1,0:T(8,128)(2,1)} %observed_from) | copy-start | bytes 6291460
  3.7 27.5 %copy-start.7 = (s32[256]{0:T(256)S(1)}, s32[256]{0:T(256)}, u32[]{:S(2)}) copy-start(s32[256]{0:T(256)} %param.11) | copy-start | bytes 3076
  3.7 41.1 %all-to-all-start = ((bf16[8,64,1024]{2,1,0:T(8,128)(2,1)}), bf16[8,64,1024]{2,1,0:T(8,128)(2,1)}, u32[]{:S(2)}, u32[]{:S(2)}) async-start(bf16[8,64,1024]{2,1,0:T(8,128)(2,1)} %shard_map.95), calls=%async_computation | async-start | bytes 2097152 | tf_op jit(solution)/shard_map/all_to_all | solution.py:545
  11.2 33.6 %copy-start.6 = (s32[4]{0:T(128)}, s32[4]{0:T(128)S(1)}, u32[]{:S(2)}) copy-start(s32[4]{0:T(128)S(1)} %pad_add_fusion.c_ref) | copy-start | bytes 52
  15.4 0.7 copy-start.2
  16.1 7.0 %collective-permute-start = (bf16[9,8,256]{2,1,0:T(8,128)(2,1)S(1)}, bf16[9,8,256]{2,1,0:T(8,128)(2,1)S(1)}, u32[]{:S(2)}, u32[]{:S(2)}) collective-permute-start(bf16[9,8,256]{2,1,0:T(8,128)(2,1)S(1)} %get-tuple-element.19.refs_0_), channel_id=1, source_target_pairs={{0,4},{4,0},{8,12},{12,8},{16,20},{20,16},{24,28},{28,24},{1,5},{5... | collective-permute-start | bytes 110600 | tf_op jit(solution)/shard_map/ppermute | solution.py:492
  18.2 12.0 %collective-permute-start.1 = (bf16[9,8,256]{2,1,0:T(8,128)(2,1)S(1)}, bf16[9,8,256]{2,1,0:T(8,128)(2,1)S(1)}, u32[]{:S(2)}, u32[]{:S(2)}) collective-permute-start(bf16[9,8,256]{2,1,0:T(8,128)(2,1)S(1)} %get-tuple-element.19.refs_0_), channel_id=1, source_target_pairs={{0,8},{4,12},{8,0},{12,4},{16,24},{20,28},{24,16},{28,20},{1,9},{5... | collective-permute-start | bytes 110600 | tf_op jit(solution)/shard_map/ppermute | solution.py:492
  19.6 11.3 %collective-permute-start.2 = (bf16[9,8,256]{2,1,0:T(8,128)(2,1)S(1)}, bf16[9,8,256]{2,1,0:T(8,128)(2,1)S(1)}, u32[]{:S(2)}, u32[]{:S(2)}) collective-permute-start(bf16[9,8,256]{2,1,0:T(8,128)(2,1)S(1)} %get-tuple-element.19.refs_0_), channel_id=1, source_target_pairs={{0,12},{4,8},{8,4},{12,0},{16,28},{20,24},{24,20},{28,16},{1,13},{... | collective-permute-start | bytes 110600 | tf_op jit(solution)/shard_map/ppermute | solution.py:492
  19.6 21.0 %collective-permute-start.3 = (bf16[64,8,256]{2,1,0:T(8,128)(2,1)S(1)}, bf16[64,8,256]{2,1,0:T(8,128)(2,1)S(1)}, u32[]{:S(2)}, u32[]{:S(2)}) collective-permute-start(bf16[64,8,256]{2,1,0:T(8,128)(2,1)S(1)} %get-tuple-element.21), channel_id=1, source_target_pairs={{0,4},{4,0},{8,12},{12,8},{16,20},{20,16},{24,28},{28,24},{1,5},{5... | collective-permute-start | bytes 786440 | tf_op jit(solution)/shard_map/ppermute | solution.py:492
  21.6 19.0 %collective-permute-start.4 = (bf16[64,8,256]{2,1,0:T(8,128)(2,1)S(1)}, bf16[64,8,256]{2,1,0:T(8,128)(2,1)S(1)}, u32[]{:S(2)}, u32[]{:S(2)}) collective-permute-start(bf16[64,8,256]{2,1,0:T(8,128)(2,1)S(1)} %get-tuple-element.22), channel_id=1, source_target_pairs={{0,8},{4,12},{8,0},{12,4},{16,24},{20,28},{24,16},{28,20},{1,9},{5... | collective-permute-start | bytes 786440 | tf_op jit(solution)/shard_map/ppermute | solution.py:492
  23.1 20.9 %collective-permute-start.5 = (bf16[64,8,256]{2,1,0:T(8,128)(2,1)S(1)}, bf16[64,8,256]{2,1,0:T(8,128)(2,1)S(1)}, u32[]{:S(2)}, u32[]{:S(2)}) collective-permute-start(bf16[64,8,256]{2,1,0:T(8,128)(2,1)S(1)} %get-tuple-element.23), channel_id=1, source_target_pairs={{0,12},{4,8},{8,4},{12,0},{16,28},{20,24},{24,20},{28,16},{1,13},{... | collective-permute-start | bytes 786440 | tf_op jit(solution)/shard_map/ppermute | solution.py:492
  31.1 13.6 %copy-start.1 = (bf16[4,9,8,256]{3,2,1,0:T(8,128)(2,1)}, bf16[4,9,8,256]{3,2,1,0:T(8,128)(2,1)S(1)}, u32[]{:S(2)}) copy-start(bf16[4,9,8,256]{3,2,1,0:T(8,128)(2,1)S(1)} %shard_map.97.refs_4_) | copy-start | bytes 442372
  31.1 2.3 %collective-permute-start.6 = (bf16[4,9,8,256]{3,2,1,0:T(8,128)(2,1)S(1)}, bf16[4,9,8,256]{3,2,1,0:T(8,128)(2,1)S(1)}, u32[]{:S(2)}, u32[]{:S(2)}) collective-permute-start(bf16[4,9,8,256]{3,2,1,0:T(8,128)(2,1)S(1)} %shard_map.97.refs_4_), channel_id=1, source_target_pairs={{0,1},{1,0},{2,3},{3,2},{4,5},{5,4},{6,7},{7,6},{8,9},{9,8},{10,11... | collective-permute-start | bytes 442376 | tf_op jit(solution)/shard_map/ppermute | solution.py:492
  31.7 6.7 %collective-permute-start.7 = (bf16[4,9,8,256]{3,2,1,0:T(8,128)(2,1)S(1)}, bf16[4,9,8,256]{3,2,1,0:T(8,128)(2,1)S(1)}, u32[]{:S(2)}, u32[]{:S(2)}) collective-permute-start(bf16[4,9,8,256]{3,2,1,0:T(8,128)(2,1)S(1)} %shard_map.97.refs_4_), channel_id=1, source_target_pairs={{0,2},{1,3},{2,0},{3,1},{4,6},{5,7},{6,4},{7,5},{8,10},{9,11},{10,... | collective-permute-start | bytes 442376 | tf_op jit(solution)/shard_map/ppermute | solution.py:492
  33.4 11.3 %copy-start.13 = (bf16[4,9,8,256]{3,2,1,0:T(8,128)(2,1)}, bf16[4,9,8,256]{3,2,1,0:T(8,128)(2,1)S(1)}, u32[]{:S(2)}) copy-start(bf16[4,9,8,256]{3,2,1,0:T(8,128)(2,1)S(1)} %collective-permute-done.6.refs_5_) | copy-start | bytes 442372
  33.4 7.2 %collective-permute-start.8 = (bf16[4,9,8,256]{3,2,1,0:T(8,128)(2,1)S(1)}, bf16[4,9,8,256]{3,2,1,0:T(8,128)(2,1)S(1)}, u32[]{:S(2)}, u32[]{:S(2)}) collective-permute-start(bf16[4,9,8,256]{3,2,1,0:T(8,128)(2,1)S(1)} %shard_map.97.refs_4_), channel_id=1, source_target_pairs={{0,3},{1,2},{2,1},{3,0},{4,7},{5,6},{6,5},{7,4},{8,11},{9,10},{10,... | collective-permute-start | bytes 442376 | tf_op jit(solution)/shard_map/ppermute | solution.py:492
  38.3 6.5 %copy-start.14 = (bf16[4,9,8,256]{3,2,1,0:T(8,128)(2,1)}, bf16[4,9,8,256]{3,2,1,0:T(8,128)(2,1)S(1)}, u32[]{:S(2)}) copy-start(bf16[4,9,8,256]{3,2,1,0:T(8,128)(2,1)S(1)} %collective-permute-done.7.refs_6_) | copy-start | bytes 442372
  40.6 4.1 %copy-start.15 = (bf16[4,9,8,256]{3,2,1,0:T(8,128)(2,1)}, bf16[4,9,8,256]{3,2,1,0:T(8,128)(2,1)S(1)}, u32[]{:S(2)}) copy-start(bf16[4,9,8,256]{3,2,1,0:T(8,128)(2,1)S(1)} %collective-permute-done.8.refs_7_) | copy-start | bytes 442372
  40.7 4.1 %copy-start.10 = (bf16[64,8,256]{2,1,0:T(8,128)(2,1)}, bf16[64,8,256]{2,1,0:T(8,128)(2,1)S(1)}, u32[]{:S(2)}) copy-start(bf16[64,8,256]{2,1,0:T(8,128)(2,1)S(1)} %collective-permute-done.3.refs_1_) | copy-start | bytes 786436
  40.7 4.1 %copy-start.11 = (bf16[64,8,256]{2,1,0:T(8,128)(2,1)}, bf16[64,8,256]{2,1,0:T(8,128)(2,1)S(1)}, u32[]{:S(2)}) copy-start(bf16[64,8,256]{2,1,0:T(8,128)(2,1)S(1)} %collective-permute-done.4.refs_2_) | copy-start | bytes 786436
  44.0 0.7 copy-start.12
  56.5 30.7 %all-to-all-start.1 = ((s16[8,528,128]{2,1,0:T(8,128)(2,1)}), s16[8,528,128]{2,1,0:T(8,128)(2,1)S(1)}, u32[]{:S(2)}, u32[]{:S(2)}) async-start(s16[8,528,128]{2,1,0:T(8,128)(2,1)} %get-tuple-element.33), calls=%async_computation.1 | async-start | bytes 2162688 | tf_op jit(solution)/shard_map/all_to_all | solution.py:627
  65.4 6.7 %collective-permute-start.10 = (s16[528,128]{1,0:T(8,128)(2,1)}, s16[528,128]{1,0:T(8,128)(2,1)S(1)}, u32[]{:S(2)}, u32[]{:S(2)}) collective-permute-start(s16[528,128]{1,0:T(8,128)(2,1)} %get-tuple-element.27), channel_id=1, source_target_pairs={{0,2},{1,3},{2,0},{3,1},{4,6},{5,7},{6,4},{7,5},{8,10},{9,11},{10,... | collective-permute-start | bytes 405512 | tf_op jit(solution)/shard_map/ppermute | solution.py:492
  67.0 6.2 %collective-permute-start.11 = (s16[528,128]{1,0:T(8,128)(2,1)}, s16[528,128]{1,0:T(8,128)(2,1)S(1)}, u32[]{:S(2)}, u32[]{:S(2)}) collective-permute-start(s16[528,128]{1,0:T(8,128)(2,1)} %get-tuple-element.28), channel_id=1, source_target_pairs={{0,3},{1,2},{2,1},{3,0},{4,7},{5,6},{6,5},{7,4},{8,11},{9,10},{10,... | collective-permute-start | bytes 405512 | tf_op jit(solution)/shard_map/ppermute | solution.py:492
  67.0 6.2 %collective-permute-start.9 = (s16[528,128]{1,0:T(8,128)(2,1)}, s16[528,128]{1,0:T(8,128)(2,1)S(1)}, u32[]{:S(2)}, u32[]{:S(2)}) collective-permute-start(s16[528,128]{1,0:T(8,128)(2,1)} %get-tuple-element.26), channel_id=1, source_target_pairs={{0,1},{1,0},{2,3},{3,2},{4,5},{5,4},{6,7},{7,6},{8,9},{9,8},{10,11... | collective-permute-start | bytes 405512 | tf_op jit(solution)/shard_map/ppermute | solution.py:492
  73.2 0.9 %copy-start.3 = (s16[528,128]{1,0:T(8,128)(2,1)S(1)}, s16[528,128]{1,0:T(8,128)(2,1)}, u32[]{:S(2)}) copy-start(s16[528,128]{1,0:T(8,128)(2,1)} %get-tuple-element.25.refs_0_) | copy-start | bytes 405508
  74.2 7.2 %collective-permute-start.12 = (f32[8,2048]{1,0:T(8,128)S(1)}, f32[8,2048]{1,0:T(8,128)S(1)}, u32[]{:S(2)}, u32[]{:S(2)}) collective-permute-start(f32[8,2048]{1,0:T(8,128)S(1)} %get-tuple-element.30), channel_id=1, source_target_pairs={{0,4},{4,0},{8,12},{12,8},{16,20},{20,16},{24,28},{28,24},{1,5},{5... | collective-permute-start | bytes 196616 | tf_op jit(solution)/shard_map/ppermute | solution.py:492
  76.2 5.2 %collective-permute-start.13 = (f32[8,2048]{1,0:T(8,128)S(1)}, f32[8,2048]{1,0:T(8,128)S(1)}, u32[]{:S(2)}, u32[]{:S(2)}) collective-permute-start(f32[8,2048]{1,0:T(8,128)S(1)} %get-tuple-element.31), channel_id=1, source_target_pairs={{0,8},{4,12},{8,0},{12,4},{16,24},{20,28},{24,16},{28,20},{1,9},{5... | collective-permute-start | bytes 196616 | tf_op jit(solution)/shard_map/ppermute | solution.py:492
  77.7 5.5 %collective-permute-start.14 = (f32[8,2048]{1,0:T(8,128)S(1)}, f32[8,2048]{1,0:T(8,128)S(1)}, u32[]{:S(2)}, u32[]{:S(2)}) collective-permute-start(f32[8,2048]{1,0:T(8,128)S(1)} %get-tuple-element.32), channel_id=1, source_target_pairs={{0,12},{4,8},{8,4},{12,0},{16,28},{20,24},{24,20},{28,16},{1,13},{... | collective-permute-start | bytes 196616 | tf_op jit(solution)/shard_map/ppermute | solution.py:492

commit v11 on v10

--- a/solution.py
+++ b/solution.py
@@ -59,7 +59,7 @@
     k_own, col_total = spectra_ref.shape
     rcv_total, cols, _ = v_to.shape
     members = col_total // cols
-    width = min(k_own, 2 * LANES)
+    width = min(k_own, 4 * LANES)
     copies = [pltpu.make_async_copy(counts_from, counts_ref, sems.at[0])]
     for n, begin in enumerate(range(0, k_own, width)):
         rows = pl.ds(begin, width)
@@ -71,11 +71,10 @@
     eye = eye_of(col_total)
     seg_ids = lax.broadcasted_iota(jnp.int32, (width, col_total), 0) % S
     copies[0].wait()
-    inside = seg_ids < counts_ref[...]
+    inside = jnp.where(seg_ids < counts_ref[...], 1.0, 0.0).astype(jnp.bfloat16)
     for n, begin in enumerate(range(0, k_own, width)):
         copies[1 + n].wait()
-        part = spectra_ref[begin : begin + width, :].astype(jnp.float32)
-        part = jnp.where(inside, part, 0.0).astype(jnp.bfloat16)
+        part = spectra_ref[begin : begin + width, :] * inside
         turned_ref[:, begin : begin + width] = nt(eye, part).astype(jnp.bfloat16)
     copies = [
         pltpu.make_async_copy(
@@ -537,7 +536,7 @@
             pltpu.VMEM((k_own, col_total), bf16),
             pltpu.VMEM((1, col_total), jnp.int32),
             pltpu.VMEM((col_total, k_own), bf16),
-            pltpu.SemaphoreType.DMA((max(rcv_total, 1 + k_own // min(k_own, 2 * LANES)),)),
+            pltpu.SemaphoreType.DMA((max(rcv_total, 1 + k_own // min(k_own, 4 * LANES)),)),
         ],
         compiler_params=params(62),
         cost_estimate=free,

time: 88.6 us -> 88.2 us (level)
  no operation moved by 1% of the time
where the time goes in v11:
time: 88.2 us; the launch traced here: 87.9 us
  waiting for transfers between devices  30 us (34%)
  starting transfers between devices  27.4 us (31%)
  Pallas kernels  25.1 us (28%)
  local copies, waits for them, and re-layouts  2.92 us (3%)
  other arithmetic  1.64 us (2%)
    ppermute x15, waiting for transfers between devices, swap(): return lax.ppermute(x, axis, [(r, r ^ k) for r in range(total)])  26.7 us
    ppermute x15, starting transfers between devices, swap(): return lax.ppermute(x, axis, [(r, r ^ k) for r in range(total)])  16.2 us
    pallas_call x1, Pallas kernels, shards(): pl.pallas_call(functools.partial(pair_kernel, members, ref_total), out_sh...  11.7 us
    all_to_all x1, starting transfers between devices, shards(): v_all = lax.all_to_all(sent, 'rcv', split_axis=0, concat_axis=0, tiled=True)  7.43 us
    pallas_call x1, Pallas kernels, shards(): pl.pallas_call(receiver_sum_kernel, out_shape=[jax.ShapeDtypeStruct((r_ro...  5.14 us
    pallas_call x1, Pallas kernels, shards(): pl.pallas_call(fold_kernel, out_shape=[jax.ShapeDtypeStruct((extra, row_t...  4.19 us
    all_to_all x1, starting transfers between devices, shards(): got = lax.all_to_all(w_part, 'rcv', split_axis=0, concat_axis=0, tiled=True)  3.81 us
    all_to_all x1, waiting for transfers between devices, shards(): got = lax.all_to_all(w_part, 'rcv', split_axis=0, concat_axis=0, tiled=True)  3.28 us
  transfers between devices with their start and end apart: 17, of which 10 were waited for; matrix products, arithmetic and copies ran while one was open for 2% of the time, Pallas kernels for 11%

profile of v11, /device:TPU:0, one launch (start us, length us, event | category | flops | bytes accessed | tf_op | source)
XLA Modules:
  0.0 87.9 jit_solution(6617989526876082618)
XLA Ops:
  0.6 0.0 copy-start.9
  0.6 0.0 copy-start.8
  0.7 2.5 %shard_map.95 = bf16[8,64,1024]{2,1,0:T(8,128)(2,1)} custom-call(bf16[1024,256]{1,0:T(8,128)(2,1)} %spectra_from.1, s32[1,256]{1,0:T(1,128)} %bitcast.7), custom_call_target="tpu_custom_call" | custom-call | tf_op jit(solution)/shard_map/pallas_call | solution.py:530
  3.2 0.0 copy-start
  3.2 0.0 copy-start.7
  3.2 7.4 %all-to-all-start = ((bf16[8,64,1024]{2,1,0:T(8,128)(2,1)}), bf16[8,64,1024]{2,1,0:T(8,128)(2,1)}, u32[]{:S(2)}, u32[]{:S(2)}) async-start(bf16[8,64,1024]{2,1,0:T(8,128)(2,1)} %shard_map.95), calls=%async_computation | async-start | bytes 2097152 | tf_op jit(solution)/shard_map/all_to_all | solution.py:544
  10.7 0.1 pad_add_fusion.c_ref
  10.8 0.0 copy-done.5
  10.8 0.0 copy-done.4
  10.8 0.0 copy-done
  10.8 4.2 %shard_map.96 = (bf16[9,8,256]{2,1,0:T(8,128)(2,1)S(1)}, bf16[64,8,256]{2,1,0:T(8,128)(2,1)S(1)}, bf16[64,8,256]{2,1,0:T(8,128)(2,1)S(1)}, bf16[64,8,256]{2,1,0:T(8,128)(2,1)S(1)}, bf16[64,8,256]{2,1,0:T(8,128)(2,1)S(1)}) custom-call(s32[4]{0:T(128)S(1)} %pad_add_fusion.c_ref, s32[8]{0:T(128)S(1)} %copy-done.8, bf16[8,256,512]{2,1,0:T(8,128)(2,1)S(1)} %copy-done, ...), custom_call_target="tpu_custom_call" | custom-call | tf_op jit(solution)/shard_map/pallas_call | solution.py:548
  15.0 0.7 copy-done.2
  15.7 2.0 %collective-permute-start = (bf16[9,8,256]{2,1,0:T(8,128)(2,1)S(1)}, bf16[9,8,256]{2,1,0:T(8,128)(2,1)S(1)}, u32[]{:S(2)}, u32[]{:S(2)}) collective-permute-start(bf16[9,8,256]{2,1,0:T(8,128)(2,1)S(1)} %get-tuple-element.19.refs_0_), channel_id=1, source_target_pairs={{0,4},{4,0},{8,12},{12,8},{16,20},{20,16},{24,28},{28,24},{1,5},{5... | collective-permute-start | bytes 110600 | tf_op jit(solution)/shard_map/ppermute | solution.py:491
  17.7 1.5 %collective-permute-start.1 = (bf16[9,8,256]{2,1,0:T(8,128)(2,1)S(1)}, bf16[9,8,256]{2,1,0:T(8,128)(2,1)S(1)}, u32[]{:S(2)}, u32[]{:S(2)}) collective-permute-start(bf16[9,8,256]{2,1,0:T(8,128)(2,1)S(1)} %get-tuple-element.19.refs_0_), channel_id=1, source_target_pairs={{0,8},{4,12},{8,0},{12,4},{16,24},{20,28},{24,16},{28,20},{1,9},{5... | collective-permute-start | bytes 110600 | tf_op jit(solution)/shard_map/ppermute | solution.py:491
  19.2 0.0 collective-permute-start.2
  19.2 2.0 %collective-permute-start.3 = (bf16[64,8,256]{2,1,0:T(8,128)(2,1)S(1)}, bf16[64,8,256]{2,1,0:T(8,128)(2,1)S(1)}, u32[]{:S(2)}, u32[]{:S(2)}) collective-permute-start(bf16[64,8,256]{2,1,0:T(8,128)(2,1)S(1)} %get-tuple-element.21), channel_id=1, source_target_pairs={{0,4},{4,0},{8,12},{12,8},{16,20},{20,16},{24,28},{28,24},{1,5},{5... | collective-permute-start | bytes 786440 | tf_op jit(solution)/shard_map/ppermute | solution.py:491
  21.2 1.5 %collective-permute-start.4 = (bf16[64,8,256]{2,1,0:T(8,128)(2,1)S(1)}, bf16[64,8,256]{2,1,0:T(8,128)(2,1)S(1)}, u32[]{:S(2)}, u32[]{:S(2)}) collective-permute-start(bf16[64,8,256]{2,1,0:T(8,128)(2,1)S(1)} %get-tuple-element.22), channel_id=1, source_target_pairs={{0,8},{4,12},{8,0},{12,4},{16,24},{20,28},{24,16},{28,20},{1,9},{5... | collective-permute-start | bytes 786440 | tf_op jit(solution)/shard_map/ppermute | solution.py:491
  22.7 0.0 collective-permute-done.refs_1_
  22.7 1.5 %collective-permute-start.5 = (bf16[64,8,256]{2,1,0:T(8,128)(2,1)S(1)}, bf16[64,8,256]{2,1,0:T(8,128)(2,1)S(1)}, u32[]{:S(2)}, u32[]{:S(2)}) collective-permute-start(bf16[64,8,256]{2,1,0:T(8,128)(2,1)S(1)} %get-tuple-element.23), channel_id=1, source_target_pairs={{0,12},{4,8},{8,4},{12,0},{16,28},{20,24},{24,20},{28,16},{1,13},{... | collective-permute-start | bytes 786440 | tf_op jit(solution)/shard_map/ppermute | solution.py:491
  24.2 5.5 %collective-permute-done.1.refs_2_ = bf16[9,8,256]{2,1,0:T(8,128)(2,1)S(1)} collective-permute-done((bf16[9,8,256]{2,1,0:T(8,128)(2,1)S(1)}, bf16[9,8,256]{2,1,0:T(8,128)(2,1)S(1)}, u32[]{:S(2)}, u32[]{:S(2)}) %collective-permute-start.1) | collective-permute-done | bytes 36896 | tf_op jit(solution)/shard_map/ppermute | solution.py:491
  29.7 0.8 collective-permute-done.2.refs_3_
  30.5 0.2 shard_map.97.refs_4_
  30.7 0.0 copy-start.1
  30.7 0.1 collective-permute-start.6
  30.8 0.1 dynamic-slice_convert_fusion
  30.9 0.1 reshape.36
  31.0 0.1 copy.11
  31.1 0.1 min.20
  31.1 0.1 min.21
  31.2 1.5 %collective-permute-start.7 = (bf16[4,9,8,256]{3,2,1,0:T(8,128)(2,1)S(1)}, bf16[4,9,8,256]{3,2,1,0:T(8,128)(2,1)S(1)}, u32[]{:S(2)}, u32[]{:S(2)}) collective-permute-start(bf16[4,9,8,256]{3,2,1,0:T(8,128)(2,1)S(1)} %shard_map.97.refs_4_), channel_id=1, source_target_pairs={{0,2},{1,3},{2,0},{3,1},{4,6},{5,7},{6,4},{7,5},{8,10},{9,11},{10,... | collective-permute-start | bytes 442376 | tf_op jit(solution)/shard_map/ppermute | solution.py:491
  32.7 0.1 convert_reduce_fusion
  32.8 0.1 reshape.38
  32.9 0.1 min.23
  33.0 0.0 collective-permute-done.6.refs_5_
  33.0 0.4 collective-permute-start.8
  33.4 0.7 pad_maximum_fusion.invn_ref
  34.1 3.8 %collective-permute-done.7.refs_6_ = bf16[4,9,8,256]{3,2,1,0:T(8,128)(2,1)S(1)} collective-permute-done((bf16[4,9,8,256]{3,2,1,0:T(8,128)(2,1)S(1)}, bf16[4,9,8,256]{3,2,1,0:T(8,128)(2,1)S(1)}, u32[]{:S(2)}, u32[]{:S(2)}) %collective-permute-start.7) | collective-permute-done | bytes 147488 | tf_op jit(solution)/shard_map/ppermute | solution.py:491
  37.9 2.3 %collective-permute-done.8.refs_7_ = bf16[4,9,8,256]{3,2,1,0:T(8,128)(2,1)S(1)} collective-permute-done((bf16[4,9,8,256]{3,2,1,0:T(8,128)(2,1)S(1)}, bf16[4,9,8,256]{3,2,1,0:T(8,128)(2,1)S(1)}, u32[]{:S(2)}, u32[]{:S(2)}) %collective-permute-start.8) | collective-permute-done | bytes 147488 | tf_op jit(solution)/shard_map/ppermute | solution.py:491
  40.2 0.0 collective-permute-done.3.refs_1_
  40.2 0.0 collective-permute-done.4.refs_2_
  40.3 3.3 %collective-permute-done.5.refs_3_ = bf16[64,8,256]{2,1,0:T(8,128)(2,1)S(1)} collective-permute-done((bf16[64,8,256]{2,1,0:T(8,128)(2,1)S(1)}, bf16[64,8,256]{2,1,0:T(8,128)(2,1)S(1)}, u32[]{:S(2)}, u32[]{:S(2)}) %collective-permute-start.5) | collective-permute-done | bytes 262176 | tf_op jit(solution)/shard_map/ppermute | solution.py:491
  43.6 0.7 copy-done.12
  44.3 0.0 all-to-all-done.v_from
  44.3 0.0 copy-done.15
  44.4 11.7 %shard_map.98 = (s16[8,528,128]{2,1,0:T(8,128)(2,1)}, bf16[64,128,128]{2,1,0:T(8,128)(2,1)}) custom-call(s32[4]{0:T(128)} %copy-done.6, f32[32,128]{1,0:T(8,128)} %pad_maximum_fusion.invn_ref, bf16[8,64,1024]{2,1,0:T(8,128)(2,1)} %all-to-all-done.v_from, bf16[1024,256]{1,0:T(8,128)(2,1)} %constant.49.table_from, bf16[64,8,256]{2,1,0:T(8,128)(2,1)} %copy-done.2, ...), custom_call_target="tpu_custom_call" | custom-call | tf_op jit(solution)/shard_map/pallas_call | solution.py:598
  56.1 3.8 %all-to-all-start.1 = ((s16[8,528,128]{2,1,0:T(8,128)(2,1)}), s16[8,528,128]{2,1,0:T(8,128)(2,1)S(1)}, u32[]{:S(2)}, u32[]{:S(2)}) async-start(s16[8,528,128]{2,1,0:T(8,128)(2,1)} %get-tuple-element.33), calls=%async_computation.1 | async-start | bytes 2162688 | tf_op jit(solution)/shard_map/all_to_all | solution.py:626
  59.9 5.1 %shard_map.99 = (s16[528,128]{1,0:T(8,128)(2,1)}, s16[528,128]{1,0:T(8,128)(2,1)}, s16[528,128]{1,0:T(8,128)(2,1)}, s16[528,128]{1,0:T(8,128)(2,1)}) custom-call(s32[4]{0:T(128)} %copy-done.6, bf16[8,64,1024]{2,1,0:T(8,128)(2,1)} %all-to-all-done.v_from, bf16[64,128,128]{2,1,0:T(8,128)(2,1)} %get-tuple-element.24.z_from), custom_call_target="tpu_custom_call" | custom-call | tf_op jit(solution)/shard_map/pallas_call | solution.py:641
  65.0 1.6 %collective-permute-start.10 = (s16[528,128]{1,0:T(8,128)(2,1)}, s16[528,128]{1,0:T(8,128)(2,1)S(1)}, u32[]{:S(2)}, u32[]{:S(2)}) collective-permute-start(s16[528,128]{1,0:T(8,128)(2,1)} %get-tuple-element.27), channel_id=1, source_target_pairs={{0,2},{1,3},{2,0},{3,1},{4,6},{5,7},{6,4},{7,5},{8,10},{9,11},{10,... | collective-permute-start | bytes 405512 | tf_op jit(solution)/shard_map/ppermute | solution.py:491
  66.6 0.0 collective-permute-start.11
  66.6 0.6 collective-permute-start.9
  67.2 4.4 %collective-permute-done.10.refs_2_ = s16[528,128]{1,0:T(8,128)(2,1)S(1)} collective-permute-done((s16[528,128]{1,0:T(8,128)(2,1)}, s16[528,128]{1,0:T(8,128)(2,1)S(1)}, u32[]{:S(2)}, u32[]{:S(2)}) %collective-permute-start.10) | collective-permute-done | bytes 135200 | tf_op jit(solution)/shard_map/ppermute | solution.py:491
  71.7 1.1 %collective-permute-done.11.refs_3_ = s16[528,128]{1,0:T(8,128)(2,1)S(1)} collective-permute-done((s16[528,128]{1,0:T(8,128)(2,1)}, s16[528,128]{1,0:T(8,128)(2,1)S(1)}, u32[]{:S(2)}, u32[]{:S(2)}) %collective-permute-start.11) | collective-permute-done | bytes 135200 | tf_op jit(solution)/shard_map/ppermute | solution.py:491
  72.7 0.0 collective-permute-done.9.refs_1_
  72.7 0.9 %copy-done.3 = s16[528,128]{1,0:T(8,128)(2,1)S(1)} copy-done((s16[528,128]{1,0:T(8,128)(2,1)S(1)}, s16[528,128]{1,0:T(8,128)(2,1)}, u32[]{:S(2)}) %copy-start.3) | copy-done | bytes 135192
  73.6 0.1 shard_map.100
  73.8 2.0 %collective-permute-start.12 = (f32[8,2048]{1,0:T(8,128)S(1)}, f32[8,2048]{1,0:T(8,128)S(1)}, u32[]{:S(2)}, u32[]{:S(2)}) collective-permute-start(f32[8,2048]{1,0:T(8,128)S(1)} %get-tuple-element.30), channel_id=1, source_target_pairs={{0,4},{4,0},{8,12},{12,8},{16,20},{20,16},{24,28},{28,24},{1,5},{5... | collective-permute-start | bytes 196616 | tf_op jit(solution)/shard_map/ppermute | solution.py:491
  75.8 1.5 %collective-permute-start.13 = (f32[8,2048]{1,0:T(8,128)S(1)}, f32[8,2048]{1,0:T(8,128)S(1)}, u32[]{:S(2)}, u32[]{:S(2)}) collective-permute-start(f32[8,2048]{1,0:T(8,128)S(1)} %get-tuple-element.31), channel_id=1, source_target_pairs={{0,8},{4,12},{8,0},{12,4},{16,24},{20,28},{24,16},{28,20},{1,9},{5... | collective-permute-start | bytes 196616 | tf_op jit(solution)/shard_map/ppermute | solution.py:491
  77.3 0.1 collective-permute-start.14
  77.4 3.6 %collective-permute-done.12 = f32[8,2048]{1,0:T(8,128)S(1)} collective-permute-done((f32[8,2048]{1,0:T(8,128)S(1)}, f32[8,2048]{1,0:T(8,128)S(1)}, u32[]{:S(2)}, u32[]{:S(2)}) %collective-permute-start.12) | collective-permute-done | bytes 65568 | tf_op jit(solution)/shard_map/ppermute | solution.py:491
  81.0 0.0 collective-permute-done.13
  81.0 1.8 %collective-permute-done.14 = f32[8,2048]{1,0:T(8,128)S(1)} collective-permute-done((f32[8,2048]{1,0:T(8,128)S(1)}, f32[8,2048]{1,0:T(8,128)S(1)}, u32[]{:S(2)}, u32[]{:S(2)}) %collective-permute-start.14) | collective-permute-done | bytes 65568 | tf_op jit(solution)/shard_map/ppermute | solution.py:491
  82.7 0.7 add_select_fusion
  83.4 3.3 %all-to-all-done.1.got_ref = s16[8,528,128]{2,1,0:T(8,128)(2,1)S(1)} async-done(((s16[8,528,128]{2,1,0:T(8,128)(2,1)}), s16[8,528,128]{2,1,0:T(8,128)(2,1)S(1)}, u32[]{:S(2)}, u32[]{:S(2)}) %all-to-all-start.1) | async-done | bytes 1081376 | tf_op jit(solution)/shard_map/all_to_all | solution.py:626
  86.7 1.1 %shard_map.101 = f32[1024,256]{1,0:T(8,128)} custom-call(s32[1,256]{1,0:T(1,128)S(1)} %bitcast.8, s16[8,528,128]{2,1,0:T(8,128)(2,1)S(1)} %all-to-all-done.1.got_ref), custom_call_target="tpu_custom_call" | custom-call | tf_op jit(solution)/shard_map/pallas_call | solution.py:627
  (23 shorter events, 0.1 us)
Async XLA Ops:
  0.6 10.1 %copy-start.9 = (s32[256]{0:T(256)S(1)}, s32[256]{0:T(256)}, u32[]{:S(2)}) copy-start(s32[256]{0:T(256)} %param.12) | copy-start | bytes 3076
  0.6 10.1 %copy-start.8 = (s32[8]{0:T(128)S(1)}, s32[8]{0:T(128)}, u32[]{:S(2)}) copy-start(s32[8]{0:T(128)} %rcounts_ref.1) | copy-start | bytes 100
  0.7 10.1 %copy-start.5 = (s32[2,8,256]{2,1,0:T(8,128)S(1)}, s32[2,8,256]{2,1,0:T(8,128)}, u32[]{:S(2)}) copy-start(s32[2,8,256]{2,1,0:T(8,128)} %window_from.1) | copy-start | bytes 49156
  0.7 10.1 %copy-start.4 = (bf16[8,2048]{1,0:T(8,128)(2,1)S(1)}, bf16[8,2048]{1,0:T(8,128)(2,1)}, u32[]{:S(2)}) copy-start(bf16[8,2048]{1,0:T(8,128)(2,1)} %rspectra_from.1) | copy-start | bytes 98308
  3.2 7.6 %copy-start = (bf16[8,256,512]{2,1,0:T(8,128)(2,1)S(1)}, bf16[8,256,512]{2,1,0:T(8,128)(2,1)}, u32[]{:S(2)}) copy-start(bf16[8,256,512]{2,1,0:T(8,128)(2,1)} %observed_from) | copy-start | bytes 6291460
  3.2 27.6 %copy-start.7 = (s32[256]{0:T(256)S(1)}, s32[256]{0:T(256)}, u32[]{:S(2)}) copy-start(s32[256]{0:T(256)} %param.11) | copy-start | bytes 3076
  3.2 41.1 %all-to-all-start = ((bf16[8,64,1024]{2,1,0:T(8,128)(2,1)}), bf16[8,64,1024]{2,1,0:T(8,128)(2,1)}, u32[]{:S(2)}, u32[]{:S(2)}) async-start(bf16[8,64,1024]{2,1,0:T(8,128)(2,1)} %shard_map.95), calls=%async_computation | async-start | bytes 2097152 | tf_op jit(solution)/shard_map/all_to_all | solution.py:544
  10.8 33.6 %copy-start.6 = (s32[4]{0:T(128)}, s32[4]{0:T(128)S(1)}, u32[]{:S(2)}) copy-start(s32[4]{0:T(128)S(1)} %pad_add_fusion.c_ref) | copy-start | bytes 52
  15.0 0.7 copy-start.2
  15.7 7.0 %collective-permute-start = (bf16[9,8,256]{2,1,0:T(8,128)(2,1)S(1)}, bf16[9,8,256]{2,1,0:T(8,128)(2,1)S(1)}, u32[]{:S(2)}, u32[]{:S(2)}) collective-permute-start(bf16[9,8,256]{2,1,0:T(8,128)(2,1)S(1)} %get-tuple-element.19.refs_0_), channel_id=1, source_target_pairs={{0,4},{4,0},{8,12},{12,8},{16,20},{20,16},{24,28},{28,24},{1,5},{5... | collective-permute-start | bytes 110600 | tf_op jit(solution)/shard_map/ppermute | solution.py:491
  17.7 12.0 %collective-permute-start.1 = (bf16[9,8,256]{2,1,0:T(8,128)(2,1)S(1)}, bf16[9,8,256]{2,1,0:T(8,128)(2,1)S(1)}, u32[]{:S(2)}, u32[]{:S(2)}) collective-permute-start(bf16[9,8,256]{2,1,0:T(8,128)(2,1)S(1)} %get-tuple-element.19.refs_0_), channel_id=1, source_target_pairs={{0,8},{4,12},{8,0},{12,4},{16,24},{20,28},{24,16},{28,20},{1,9},{5... | collective-permute-start | bytes 110600 | tf_op jit(solution)/shard_map/ppermute | solution.py:491
  19.2 11.3 %collective-permute-start.2 = (bf16[9,8,256]{2,1,0:T(8,128)(2,1)S(1)}, bf16[9,8,256]{2,1,0:T(8,128)(2,1)S(1)}, u32[]{:S(2)}, u32[]{:S(2)}) collective-permute-start(bf16[9,8,256]{2,1,0:T(8,128)(2,1)S(1)} %get-tuple-element.19.refs_0_), channel_id=1, source_target_pairs={{0,12},{4,8},{8,4},{12,0},{16,28},{20,24},{24,20},{28,16},{1,13},{... | collective-permute-start | bytes 110600 | tf_op jit(solution)/shard_map/ppermute | solution.py:491
  19.2 21.0 %collective-permute-start.3 = (bf16[64,8,256]{2,1,0:T(8,128)(2,1)S(1)}, bf16[64,8,256]{2,1,0:T(8,128)(2,1)S(1)}, u32[]{:S(2)}, u32[]{:S(2)}) collective-permute-start(bf16[64,8,256]{2,1,0:T(8,128)(2,1)S(1)} %get-tuple-element.21), channel_id=1, source_target_pairs={{0,4},{4,0},{8,12},{12,8},{16,20},{20,16},{24,28},{28,24},{1,5},{5... | collective-permute-start | bytes 786440 | tf_op jit(solution)/shard_map/ppermute | solution.py:491
  21.2 19.0 %collective-permute-start.4 = (bf16[64,8,256]{2,1,0:T(8,128)(2,1)S(1)}, bf16[64,8,256]{2,1,0:T(8,128)(2,1)S(1)}, u32[]{:S(2)}, u32[]{:S(2)}) collective-permute-start(bf16[64,8,256]{2,1,0:T(8,128)(2,1)S(1)} %get-tuple-element.22), channel_id=1, source_target_pairs={{0,8},{4,12},{8,0},{12,4},{16,24},{20,28},{24,16},{28,20},{1,9},{5... | collective-permute-start | bytes 786440 | tf_op jit(solution)/shard_map/ppermute | solution.py:491
  22.7 20.9 %collective-permute-start.5 = (bf16[64,8,256]{2,1,0:T(8,128)(2,1)S(1)}, bf16[64,8,256]{2,1,0:T(8,128)(2,1)S(1)}, u32[]{:S(2)}, u32[]{:S(2)}) collective-permute-start(bf16[64,8,256]{2,1,0:T(8,128)(2,1)S(1)} %get-tuple-element.23), channel_id=1, source_target_pairs={{0,12},{4,8},{8,4},{12,0},{16,28},{20,24},{24,20},{28,16},{1,13},{... | collective-permute-start | bytes 786440 | tf_op jit(solution)/shard_map/ppermute | solution.py:491
  30.7 13.6 %copy-start.1 = (bf16[4,9,8,256]{3,2,1,0:T(8,128)(2,1)}, bf16[4,9,8,256]{3,2,1,0:T(8,128)(2,1)S(1)}, u32[]{:S(2)}) copy-start(bf16[4,9,8,256]{3,2,1,0:T(8,128)(2,1)S(1)} %shard_map.97.refs_4_) | copy-start | bytes 442372
  30.7 2.3 %collective-permute-start.6 = (bf16[4,9,8,256]{3,2,1,0:T(8,128)(2,1)S(1)}, bf16[4,9,8,256]{3,2,1,0:T(8,128)(2,1)S(1)}, u32[]{:S(2)}, u32[]{:S(2)}) collective-permute-start(bf16[4,9,8,256]{3,2,1,0:T(8,128)(2,1)S(1)} %shard_map.97.refs_4_), channel_id=1, source_target_pairs={{0,1},{1,0},{2,3},{3,2},{4,5},{5,4},{6,7},{7,6},{8,9},{9,8},{10,11... | collective-permute-start | bytes 442376 | tf_op jit(solution)/shard_map/ppermute | solution.py:491
  31.2 6.7 %collective-permute-start.7 = (bf16[4,9,8,256]{3,2,1,0:T(8,128)(2,1)S(1)}, bf16[4,9,8,256]{3,2,1,0:T(8,128)(2,1)S(1)}, u32[]{:S(2)}, u32[]{:S(2)}) collective-permute-start(bf16[4,9,8,256]{3,2,1,0:T(8,128)(2,1)S(1)} %shard_map.97.refs_4_), channel_id=1, source_target_pairs={{0,2},{1,3},{2,0},{3,1},{4,6},{5,7},{6,4},{7,5},{8,10},{9,11},{10,... | collective-permute-start | bytes 442376 | tf_op jit(solution)/shard_map/ppermute | solution.py:491
  33.0 11.3 %copy-start.13 = (bf16[4,9,8,256]{3,2,1,0:T(8,128)(2,1)}, bf16[4,9,8,256]{3,2,1,0:T(8,128)(2,1)S(1)}, u32[]{:S(2)}) copy-start(bf16[4,9,8,256]{3,2,1,0:T(8,128)(2,1)S(1)} %collective-permute-done.6.refs_5_) | copy-start | bytes 442372
  33.0 7.2 %collective-permute-start.8 = (bf16[4,9,8,256]{3,2,1,0:T(8,128)(2,1)S(1)}, bf16[4,9,8,256]{3,2,1,0:T(8,128)(2,1)S(1)}, u32[]{:S(2)}, u32[]{:S(2)}) collective-permute-start(bf16[4,9,8,256]{3,2,1,0:T(8,128)(2,1)S(1)} %shard_map.97.refs_4_), channel_id=1, source_target_pairs={{0,3},{1,2},{2,1},{3,0},{4,7},{5,6},{6,5},{7,4},{8,11},{9,10},{10,... | collective-permute-start | bytes 442376 | tf_op jit(solution)/shard_map/ppermute | solution.py:491
  37.9 6.5 %copy-start.14 = (bf16[4,9,8,256]{3,2,1,0:T(8,128)(2,1)}, bf16[4,9,8,256]{3,2,1,0:T(8,128)(2,1)S(1)}, u32[]{:S(2)}) copy-start(bf16[4,9,8,256]{3,2,1,0:T(8,128)(2,1)S(1)} %collective-permute-done.7.refs_6_) | copy-start | bytes 442372
  40.2 4.1 %copy-start.15 = (bf16[4,9,8,256]{3,2,1,0:T(8,128)(2,1)}, bf16[4,9,8,256]{3,2,1,0:T(8,128)(2,1)S(1)}, u32[]{:S(2)}) copy-start(bf16[4,9,8,256]{3,2,1,0:T(8,128)(2,1)S(1)} %collective-permute-done.8.refs_7_) | copy-start | bytes 442372
  40.2 4.1 %copy-start.10 = (bf16[64,8,256]{2,1,0:T(8,128)(2,1)}, bf16[64,8,256]{2,1,0:T(8,128)(2,1)S(1)}, u32[]{:S(2)}) copy-start(bf16[64,8,256]{2,1,0:T(8,128)(2,1)S(1)} %collective-permute-done.3.refs_1_) | copy-start | bytes 786436
  40.2 4.1 %copy-start.11 = (bf16[64,8,256]{2,1,0:T(8,128)(2,1)}, bf16[64,8,256]{2,1,0:T(8,128)(2,1)S(1)}, u32[]{:S(2)}) copy-start(bf16[64,8,256]{2,1,0:T(8,128)(2,1)S(1)} %collective-permute-done.4.refs_2_) | copy-start | bytes 786436
  43.6 0.7 copy-start.12
  56.1 30.6 %all-to-all-start.1 = ((s16[8,528,128]{2,1,0:T(8,128)(2,1)}), s16[8,528,128]{2,1,0:T(8,128)(2,1)S(1)}, u32[]{:S(2)}, u32[]{:S(2)}) async-start(s16[8,528,128]{2,1,0:T(8,128)(2,1)} %get-tuple-element.33), calls=%async_computation.1 | async-start | bytes 2162688 | tf_op jit(solution)/shard_map/all_to_all | solution.py:626
  65.0 6.7 %collective-permute-start.10 = (s16[528,128]{1,0:T(8,128)(2,1)}, s16[528,128]{1,0:T(8,128)(2,1)S(1)}, u32[]{:S(2)}, u32[]{:S(2)}) collective-permute-start(s16[528,128]{1,0:T(8,128)(2,1)} %get-tuple-element.27), channel_id=1, source_target_pairs={{0,2},{1,3},{2,0},{3,1},{4,6},{5,7},{6,4},{7,5},{8,10},{9,11},{10,... | collective-permute-start | bytes 405512 | tf_op jit(solution)/shard_map/ppermute | solution.py:491
  66.6 6.2 %collective-permute-start.11 = (s16[528,128]{1,0:T(8,128)(2,1)}, s16[528,128]{1,0:T(8,128)(2,1)S(1)}, u32[]{:S(2)}, u32[]{:S(2)}) collective-permute-start(s16[528,128]{1,0:T(8,128)(2,1)} %get-tuple-element.28), channel_id=1, source_target_pairs={{0,3},{1,2},{2,1},{3,0},{4,7},{5,6},{6,5},{7,4},{8,11},{9,10},{10,... | collective-permute-start | bytes 405512 | tf_op jit(solution)/shard_map/ppermute | solution.py:491
  66.6 6.2 %collective-permute-start.9 = (s16[528,128]{1,0:T(8,128)(2,1)}, s16[528,128]{1,0:T(8,128)(2,1)S(1)}, u32[]{:S(2)}, u32[]{:S(2)}) collective-permute-start(s16[528,128]{1,0:T(8,128)(2,1)} %get-tuple-element.26), channel_id=1, source_target_pairs={{0,1},{1,0},{2,3},{3,2},{4,5},{5,4},{6,7},{7,6},{8,9},{9,8},{10,11... | collective-permute-start | bytes 405512 | tf_op jit(solution)/shard_map/ppermute | solution.py:491
  72.7 0.9 %copy-start.3 = (s16[528,128]{1,0:T(8,128)(2,1)S(1)}, s16[528,128]{1,0:T(8,128)(2,1)}, u32[]{:S(2)}) copy-start(s16[528,128]{1,0:T(8,128)(2,1)} %get-tuple-element.25.refs_0_) | copy-start | bytes 405508
  73.8 7.2 %collective-permute-start.12 = (f32[8,2048]{1,0:T(8,128)S(1)}, f32[8,2048]{1,0:T(8,128)S(1)}, u32[]{:S(2)}, u32[]{:S(2)}) collective-permute-start(f32[8,2048]{1,0:T(8,128)S(1)} %get-tuple-element.30), channel_id=1, source_target_pairs={{0,4},{4,0},{8,12},{12,8},{16,20},{20,16},{24,28},{28,24},{1,5},{5... | collective-permute-start | bytes 196616 | tf_op jit(solution)/shard_map/ppermute | solution.py:491
  75.8 5.2 %collective-permute-start.13 = (f32[8,2048]{1,0:T(8,128)S(1)}, f32[8,2048]{1,0:T(8,128)S(1)}, u32[]{:S(2)}, u32[]{:S(2)}) collective-permute-start(f32[8,2048]{1,0:T(8,128)S(1)} %get-tuple-element.31), channel_id=1, source_target_pairs={{0,8},{4,12},{8,0},{12,4},{16,24},{20,28},{24,16},{28,20},{1,9},{5... | collective-permute-start | bytes 196616 | tf_op jit(solution)/shard_map/ppermute | solution.py:491
  77.3 5.5 %collective-permute-start.14 = (f32[8,2048]{1,0:T(8,128)S(1)}, f32[8,2048]{1,0:T(8,128)S(1)}, u32[]{:S(2)}, u32[]{:S(2)}) collective-permute-start(f32[8,2048]{1,0:T(8,128)S(1)} %get-tuple-element.32), channel_id=1, source_target_pairs={{0,12},{4,8},{8,4},{12,0},{16,28},{20,24},{24,20},{28,16},{1,13},{... | collective-permute-start | bytes 196616 | tf_op jit(solution)/shard_map/ppermute | solution.py:491
